TPU v7x, 32 devices: a whole 2x2x4 slice. The times are simulated.
32 devices in a mesh: section: 2 (over core), dp: 16 (over z, y, x).
Axes of the slice: x: 2, y: 2, z: 4, core: 2. Of those that a mesh axis runs over, the one named last changes fastest.
Arguments:
- patches: bfloat16 [128, 196, 768], P('dp'), may hold values from -6 to 6
- labels: int32 [128], P('dp'), may hold values from 0 to 999
- replay: int32 [128], P('dp'), may hold values from 0 to 1, as said below
- old_logits: float32 [128, 1000], P('dp'), may hold values from -10 to 10
- basis_count: int32 [2], replicated, may hold values from 20 to 200, as said below
- master: float32 [2, 638976], P('section', 'dp')
- first_moment: float32 [2, 638976], P('section', 'dp'), may hold values from -3.0517578e-05 to 3.0517578e-05
- second_moment: float32 [2, 638976], P('section', 'dp'), may hold values from 1.565004e-13 to 2.5040063e-12
- basis: bfloat16 [400, 2, 638976], P(None, 'section', 'dp'), may hold values from -6 to 6
Outputs:
- loss_parts: float32 [3], replicated
- grad_norm: float32 [], replicated
- coefficients: float32 [2, 200], replicated
- new_master: float32 [2, 638976], P('section', 'dp')
- new_first: float32 [2, 638976], P('section', 'dp')
- new_second: float32 [2, 638976], P('section', 'dp')
Inputs may be any that keep to these rules, and one draw needn't show every extreme that they name: `basis_count`: one task has exactly 200 basis vectors. At least one image is a replay example.
All inputs are finite; a program needn't handle non-finite values.
Results may differ from a plain program's by a relative error of at most 0.012.
The roundings to bfloat16 on the way count: a program that leaves them out, or rounds other values in their place, can miss the bound.
Values may be sent and summed in bfloat16 or wider, within the bound.
No kernel may reach another device: no remote copies, remote signals or barrier semaphores. Data moves between devices by JAX's collectives and lax.ppermute only.
A program may use at most 192 MiB of HBM per device.

v0:
```python
import math

import jax
import jax.numpy as jnp
from jax import lax
from jax.sharding import PartitionSpec as P

HEADS = 3
HD = 64
D = 192
FF = 768
PDIM = 768
PATCHES = 196
CLASSES = 1000
MB = 2
TASKS = 2
KMAX = 200
STEP = 10
BLOCK_P = 444672
FIRST_P = 185664
LAST_P = 193384


HIGHEST_PREC = lax.Precision.HIGHEST
NORM_EPS = 1e-06
CLIP_NORM = 0.02
LEARN_RATE = 0.05
BETA_ONE = 0.9
BETA_TWO = 0.999
ADAM_EPS = 1e-08
WEIGHT_DECAY = 0.05


def from_behind(value, axis, steps):
    count = lax.axis_size(axis)
    first, last = (max(0, -steps), min(count, count - steps))
    return lax.ppermute(value, axis, [(source, source + steps) for source in range(first, last)])


def block_shapes():
    return [
        (D,),
        (D,),
        (D, 3 * D),
        (2 * D,),
        (D, D),
        (D,),
        (D,),
        (D,),
        (D, FF),
        (FF,),
        (FF, D),
        (D,),
    ]


def first_shapes():
    return [(PDIM, D), (D,), (D,), (PATCHES + 1, D)]


def last_shapes():
    return [(D,), (D,), (D, CLASSES), (CLASSES,)]


def unpack(flat_vec, shapes):
    pieces = []
    offset = 0
    for dims in shapes:
        entries = math.prod(dims)
        pieces.append(flat_vec[offset : offset + entries].reshape(dims))
        offset += entries
    return pieces


def pack(grads, length):
    flat_vec = jnp.concatenate([piece.reshape(-1) for piece in grads])
    return jnp.pad(flat_vec, (0, length - flat_vec.shape[0]))


def to_low(value):
    return value.astype(jnp.bfloat16)


def as_float(value):
    return value.astype(jnp.float32)


def norm_rows(rows_in, gain_vec, bias_vec):
    mean_row = jnp.mean(rows_in, -1, keepdims=True)
    centred = rows_in - mean_row
    variance = jnp.mean(centred * centred, -1, keepdims=True)
    return centred * lax.rsqrt(variance + NORM_EPS) * gain_vec + bias_vec


def block_forward(residual, params):
    (
        gain_one,
        bias_one,
        w_qkv,
        b_qkv,
        w_out,
        b_out,
        gain_two,
        bias_two,
        w_up,
        b_up,
        w_down,
        b_down,
    ) = params
    images, seq_len, model_width = residual.shape
    flat_in = residual.reshape(-1, model_width)
    normed = to_low(norm_rows(flat_in, as_float(gain_one), as_float(bias_one)))
    bias_full = jnp.concatenate(
        [as_float(b_qkv[:D]), jnp.zeros((D,), jnp.float32), as_float(b_qkv[D:])]
    )
    qkv = to_low(jnp.dot(normed, w_qkv, preferred_element_type=jnp.float32) + bias_full)
    heads = qkv.reshape(images, seq_len, 3, HEADS, HD)
    queries, key_heads, values = (heads[:, :, 0], heads[:, :, 1], heads[:, :, 2])
    scores = jnp.einsum(
        "bqhe,bkhe->bhqk", queries, key_heads, preferred_element_type=jnp.float32
    ) * HD ** (-0.5)
    soft_weights = jax.nn.softmax(scores, -1)
    soft_low = to_low(soft_weights)
    mixed = jnp.einsum("bhqk,bkhe->bqhe", soft_low, values, preferred_element_type=jnp.float32)
    mixed = to_low(mixed.reshape(-1, model_width))
    hidden = flat_in + jnp.dot(mixed, w_out, preferred_element_type=jnp.float32) + as_float(b_out)
    normed_two = to_low(norm_rows(hidden, as_float(gain_two), as_float(bias_two)))
    pre_act = jnp.dot(normed_two, w_up, preferred_element_type=jnp.float32) + as_float(b_up)
    activated = to_low(jax.nn.gelu(pre_act, approximate=False))
    output = (
        hidden + jnp.dot(activated, w_down, preferred_element_type=jnp.float32) + as_float(b_down)
    )
    saved = (
        flat_in,
        normed,
        queries,
        key_heads,
        values,
        soft_weights,
        soft_low,
        mixed,
        hidden,
        normed_two,
        pre_act,
        activated,
    )
    return (output.reshape(residual.shape), saved)


def block_backward(saved, params, grad_out):
    (
        gain_one,
        bias_one,
        w_qkv,
        b_qkv,
        w_out,
        b_out,
        gain_two,
        bias_two,
        w_up,
        b_up,
        w_down,
        b_down,
    ) = params
    (
        flat_in,
        normed,
        queries,
        key_heads,
        values,
        soft_weights,
        soft_low,
        mixed,
        hidden,
        normed_two,
        pre_act,
        activated,
    ) = saved
    images, seq_len, model_width = grad_out.shape
    grad_flat = grad_out.reshape(-1, model_width)
    grad_down = to_low(grad_flat)
    dw_down = jnp.einsum("tf,td->fd", activated, grad_down, preferred_element_type=jnp.float32)
    db_down = jnp.sum(as_float(grad_down), 0)
    grad_act = jnp.einsum("td,fd->tf", grad_down, w_down, preferred_element_type=jnp.float32)
    _, gelu_back = jax.vjp(lambda inner: jax.nn.gelu(inner, approximate=False), pre_act)
    grad_up = to_low(gelu_back(grad_act)[0])
    dw_up = jnp.einsum("td,tf->df", normed_two, grad_up, preferred_element_type=jnp.float32)
    db_up = jnp.sum(as_float(grad_up), 0)
    grad_normed_two = jnp.einsum("tf,df->td", grad_up, w_up, preferred_element_type=jnp.float32)
    _, norm_back_two = jax.vjp(norm_rows, hidden, as_float(gain_two), as_float(bias_two))
    hidden_part, dgain_two, dbias_two = norm_back_two(grad_normed_two)
    grad_hidden = grad_flat + hidden_part
    grad_branch = to_low(grad_hidden)
    dw_out = jnp.einsum("td,te->de", mixed, grad_branch, preferred_element_type=jnp.float32)
    db_out = jnp.sum(as_float(grad_branch), 0)
    grad_mixed = to_low(
        jnp.einsum("te,de->td", grad_branch, w_out, preferred_element_type=jnp.float32)
    )
    grad_mixed = grad_mixed.reshape(images, seq_len, HEADS, HD)
    grad_soft = jnp.einsum(
        "bqhe,bkhe->bhqk", grad_mixed, values, preferred_element_type=jnp.float32
    )
    grad_values = jnp.einsum(
        "bhqk,bqhe->bkhe", soft_low, grad_mixed, preferred_element_type=jnp.float32
    )
    inner_sum = jnp.sum(grad_soft * soft_weights, -1, keepdims=True)
    grad_scores = to_low(soft_weights * (grad_soft - inner_sum))
    grad_queries = jnp.einsum(
        "bhqk,bkhe->bqhe", grad_scores, key_heads, preferred_element_type=jnp.float32
    ) * HD ** (-0.5)
    grad_keys = jnp.einsum(
        "bhqk,bqhe->bkhe", grad_scores, queries, preferred_element_type=jnp.float32
    ) * HD ** (-0.5)
    grad_qkv = to_low(
        jnp.stack([grad_queries, grad_keys, grad_values], 2).reshape(-1, 3 * model_width)
    )
    dw_qkv = jnp.einsum("td,te->de", normed, grad_qkv, preferred_element_type=jnp.float32)
    qkv_sums = jnp.sum(as_float(grad_qkv), 0)
    db_qkv = jnp.concatenate([qkv_sums[:D], qkv_sums[2 * D :]])
    grad_normed = jnp.einsum("te,de->td", grad_qkv, w_qkv, preferred_element_type=jnp.float32)
    _, norm_back_one = jax.vjp(norm_rows, flat_in, as_float(gain_one), as_float(bias_one))
    input_part, dgain_one, dbias_one = norm_back_one(grad_normed)
    grad_in = (grad_hidden + input_part).reshape(grad_out.shape)
    grads = [
        dgain_one,
        dbias_one,
        dw_qkv,
        db_qkv,
        dw_out,
        db_out,
        dgain_two,
        dbias_two,
        dw_up,
        db_up,
        dw_down,
        db_down,
    ]
    return (grad_in, grads)


def embed_forward(patch_blk, first_edge):
    w_patch, b_patch, cls_token, pos_embed = first_edge
    embedded = jnp.einsum(
        "bpc,cd->bpd", patch_blk, w_patch, preferred_element_type=jnp.float32
    ) + as_float(b_patch)
    cls_rows = jnp.broadcast_to(as_float(cls_token)[None, None, :], (patch_blk.shape[0], 1, D))
    return jnp.concatenate([cls_rows, embedded], 1) + as_float(pos_embed)[None]


def embed_backward(patch_blk, grad_tokens):
    grad_embedded = to_low(grad_tokens[:, 1:])
    dw_patch = jnp.einsum(
        "bpc,bpd->cd", patch_blk, grad_embedded, preferred_element_type=jnp.float32
    )
    db_patch = jnp.sum(as_float(grad_embedded), (0, 1))
    dcls_token = jnp.sum(grad_tokens[:, 0], 0)
    dpos_embed = jnp.sum(grad_tokens, 0)
    return [dw_patch, db_patch, dcls_token, dpos_embed]


def head_step(final, last_edge, label_blk, replay_blk, old_blk, image_total, replay_count):
    gain_last, bias_last, w_head, b_head = last_edge
    top_rows = final[:, 0]
    gain_float, bias_float = (as_float(gain_last), as_float(bias_last))
    top_low = to_low(norm_rows(top_rows, gain_float, bias_float))
    logits = jnp.dot(top_low, w_head, preferred_element_type=jnp.float32) + as_float(b_head)
    log_total = jax.nn.logsumexp(logits, -1)
    onehot = (label_blk[:, None] == jnp.arange(CLASSES)[None, :]).astype(jnp.float32)
    entropy_sum = jnp.sum(log_total - jnp.sum(logits * onehot, -1))
    distance = logits - old_blk
    replay_float = as_float(replay_blk)
    replay_sum = jnp.sum(replay_float * jnp.mean(distance * distance, -1))
    grad_logits = (jnp.exp(logits - log_total[:, None]) - onehot) / image_total
    grad_logits = grad_logits + replay_float[:, None] * 2.0 * distance / (CLASSES * replay_count)
    grad_low = to_low(grad_logits)
    dw_head = jnp.einsum("bd,bc->dc", top_low, grad_low, preferred_element_type=jnp.float32)
    db_head = jnp.sum(as_float(grad_low), 0)
    grad_top = jnp.einsum("bc,dc->bd", grad_low, w_head, preferred_element_type=jnp.float32)
    _, norm_back = jax.vjp(norm_rows, top_rows, gain_float, bias_float)
    grad_rows, dgain_last, dbias_last = norm_back(grad_top)
    grad_final = jnp.concatenate([grad_rows[:, None, :], jnp.zeros_like(final[:, 1:])], 1)
    return (entropy_sum, replay_sum, grad_final, [dgain_last, dbias_last, dw_head, db_head])


def body(
    patches, labels, replay, old_logits, basis_count, master, first_moment, second_moment, basis
):
    dp_devices = lax.axis_size("dp")
    shard_len = master.shape[1]
    section_len = shard_len * dp_devices
    image_total = jnp.float32(patches.shape[0] * dp_devices)
    replay_count = lax.psum(jnp.sum(replay).astype(jnp.float32), "dp")
    section_index = lax.axis_index("section")
    per_micro = patches.shape[0] // MB
    act_dims = (per_micro, PATCHES + 1, D)
    zero_scalar = jnp.zeros((), jnp.float32)
    gathered = lax.all_gather(to_low(master[0]), "dp", axis=0, tiled=True)
    block_params = unpack(gathered[:BLOCK_P], block_shapes())
    first_edge = unpack(gathered[BLOCK_P : BLOCK_P + FIRST_P], first_shapes())
    last_edge = unpack(gathered[BLOCK_P : BLOCK_P + LAST_P], last_shapes())
    entropy_total = zero_scalar
    replay_total = zero_scalar
    grad_acc = jnp.zeros((section_len,), jnp.float32)
    for micro in range(MB):
        lower = micro * per_micro
        patch_blk = patches[lower : lower + per_micro]
        label_blk = labels[lower : lower + per_micro]
        replay_blk = replay[lower : lower + per_micro]
        old_blk = old_logits[lower : lower + per_micro]

        def early_forward():
            tokens = embed_forward(patch_blk, first_edge)
            return to_low(block_forward(tokens, block_params)[0])

        def early_none():
            return jnp.zeros(act_dims, jnp.bfloat16)

        sent = lax.cond(section_index == 0, early_forward, early_none)
        received = from_behind(sent, "section", 1)

        def late_step():
            residual = as_float(received)
            final, saved = block_forward(residual, block_params)
            entropy_sum, replay_sum, grad_final, head_grads = head_step(
                final, last_edge, label_blk, replay_blk, old_blk, image_total, replay_count
            )
            grad_in, grads = block_backward(saved, block_params, grad_final)
            return (entropy_sum, replay_sum, to_low(grad_in), pack(grads + head_grads, section_len))

        def late_none():
            return (
                zero_scalar,
                zero_scalar,
                jnp.zeros(act_dims, jnp.bfloat16),
                jnp.zeros((section_len,), jnp.float32),
            )

        entropy_sum, replay_sum, back_sent, late_grads = lax.cond(
            section_index == 1, late_step, late_none
        )
        back_received = from_behind(back_sent, "section", -1)

        def early_backward():
            tokens = embed_forward(patch_blk, first_edge)
            _, saved = block_forward(tokens, block_params)
            grad_tokens, grads = block_backward(saved, block_params, as_float(back_received))
            return pack(grads + embed_backward(patch_blk, grad_tokens), section_len)

        def early_grads_none():
            return jnp.zeros((section_len,), jnp.float32)

        early_grads = lax.cond(section_index == 0, early_backward, early_grads_none)
        entropy_total = entropy_total + entropy_sum
        replay_total = replay_total + replay_sum
        grad_acc = grad_acc + late_grads + early_grads
    grad_shard = lax.psum_scatter(grad_acc, "dp", scatter_dimension=0, tiled=True)
    basis_rows = basis[:, 0, :]
    squares = jnp.sum(grad_shard * grad_shard)
    totals = lax.psum((squares, entropy_total, replay_total), ("section", "dp"))
    grad_norm = jnp.sqrt(totals[0])
    factor = jnp.minimum(1.0, CLIP_NORM / (grad_norm + 1e-06))
    clipped = grad_shard * factor
    raw_local = jnp.dot(
        basis_rows, clipped, precision=HIGHEST_PREC, preferred_element_type=jnp.float32
    )
    raw_coef = lax.psum(raw_local, ("section", "dp"))
    row_mask = (jnp.arange(KMAX)[None, :] < basis_count[:, None]).astype(jnp.float32)
    coefficients = raw_coef.reshape(TASKS, KMAX) * row_mask
    whole_len = jnp.float32(2 * section_len)
    removed = jnp.dot(
        coefficients.reshape(-1),
        basis_rows,
        precision=HIGHEST_PREC,
        preferred_element_type=jnp.float32,
    )
    projected = clipped - removed / whole_len
    new_first = BETA_ONE * first_moment[0] + (1.0 - BETA_ONE) * projected
    new_second = BETA_TWO * second_moment[0] + (1.0 - BETA_TWO) * projected * projected
    ratio = (
        new_first
        / (1.0 - BETA_ONE**STEP)
        / (jnp.sqrt(new_second / (1.0 - BETA_TWO**STEP)) + ADAM_EPS)
    )
    new_master = master[0] - LEARN_RATE * (ratio + WEIGHT_DECAY * master[0])
    loss_parts = jnp.stack([totals[1], totals[2], replay_count])
    return (
        loss_parts,
        grad_norm,
        coefficients,
        new_master[None],
        new_first[None],
        new_second[None],
    )


def solution(mesh):
    in_specs = (
        P("dp", None, None),
        P("dp"),
        P("dp"),
        P("dp", None),
        P(),
        P("section", "dp"),
        P("section", "dp"),
        P("section", "dp"),
        P(None, "section", "dp"),
    )
    out_specs = (P(), P(), P(), P("section", "dp"), P("section", "dp"), P("section", "dp"))
    return jax.shard_map(body, mesh=mesh, in_specs=in_specs, out_specs=out_specs, check_vma=False)
```

profile of v0, /device:TPU:0, one launch (start us, length us, event | category | flops | bytes accessed | tf_op | source)
XLA Modules:
  0.0 842.2 jit_solution(12224191037570304274)
XLA Ops:
  8.9 4.4 fusion.430
  13.4 57.3 %all-gather.2.cloned.1.call-done = bf16[638976]{0:T(1024)(128)(2,1)} async-done(((bf16[39936]{0:T(1024)(128)(2,1)}), bf16[638976]{0:T(1024)(128)(2,1)}) %all-gather.2.cloned.1.call-update) | async-done | bytes 1277968 | tf_op jit(solution)/shard_map/all_gather | solution.py:297
  80.1 42.4 %conditional.6 = (bf16[4,197,192]{1,0,2:T(4,128)(2,1)}) conditional(s32[]{:T(128)} %convert_element_type.668, () %tuple.49, (bf16[192]{0:T(256)(128)(2,1)S(1)}, bf16[4,196,768]{2,1,0:T(8,128)(2,1)S(1)}, bf16[768,192]{1,0:T(8,128)(2,1)S(1)}, bf16[192]{0:T(256)(128)(2,1)S(1)}, bf16[197,192]{1,0:T(8,128)(2,1)S(1)}, ...), branch_computations={%region_0.0_spmd, %region_1.8_spmd} | conditional | flops 1095375872 | bytes 31968580 | solution.py:318
  88.3 5.9 reshape.1088
  94.2 3.6 fusion.406
  97.9 2.1 copy.287
  99.9 2.1 copy.288
  105.7 2.1 fusion.407
  109.3 2.1 convert_element_type.481
  113.7 7.6 fusion.18
  123.8 2.5 copy.308
  126.4 43.5 %conditional.8 = (bf16[4,197,192]{1,0,2:T(4,128)(2,1)}) conditional(s32[]{:T(128)} %convert_element_type.668, () %tuple.53, (bf16[192]{0:T(256)(128)(2,1)S(1)}, bf16[4,196,768]{2,1,0:T(8,128)(2,1)}, bf16[768,192]{1,0:T(8,128)(2,1)S(1)}, bf16[192]{0:T(256)(128)(2,1)S(1)}, bf16[197,192]{1,0:T(8,128)(2,1)S(1)}, ...), branch_computations={%region_44.45_spmd, %region_45.52_spmd} | conditional | flops 1095375872 | bytes 31977880 | solution.py:318
  128.1 2.7 convolution_add_fusion.5
  137.5 5.6 reshape.1090
  143.1 3.6 fusion.409
  146.7 2.1 copy.294
  148.8 2.1 copy.295
  154.6 2.1 fusion.410
  160.9 7.6 fusion.163
  173.3 40.2 %psum.35 = f32[]{:T(128)} all-reduce(f32[]{:T(128)S(6)} %convert_element_type.670), channel_id=1, replica_groups=mesh['section'=2,'dp'=16] {'dp'}, use_global_device_ids=true, to_apply=%region_9.10 | all-reduce | flops 1 | bytes 8 | tf_op jit(solution)/shard_map/psum | solution.py:292
  217.4 10.2 %conditional.7 = (f32[]{:T(128)}, f32[]{:T(128)}, bf16[4,197,192]{1,0,2:T(4,128)(2,1)}, f32[638976]{0:T(1024)}) conditional(s32[]{:T(128)} %convert_element_type.667, () %tuple.48, (bf16[4,197,192]{1,0,2:T(4,128)(2,1)S(1)}, bf16[192]{0:T(256)(128)(2,1)S(1)}, bf16[192]{0:T(256)(128)(2,1)S(1)}, bf16[192,576]{1,0:T(8,128)(2,1)S(1)}, ...), branch_computations={%region_10.0_spmd, %region_11.44_spmd} | conditional | flops 2527613696 | bytes 149209728 | solution.py:338
  228.9 14.8 %conditional.9 = (f32[]{:T(128)}, f32[]{:T(128)}, bf16[4,197,192]{1,0,2:T(4,128)(2,1)}, f32[638976]{0:T(1024)}) conditional(s32[]{:T(128)} %convert_element_type.667, () %tuple.52, (bf16[4,197,192]{1,0,2:T(4,128)(2,1)}, bf16[192]{0:T(256)(128)(2,1)}, bf16[192]{0:T(256)(128)(2,1)}, bf16[192,576]{1,0:T(8,128)(2,1)}, bf16[384]{0:T(512)(128)(2,1)}, ...), branch_computations={%region_52.53_spmd, %region_53.86_spmd} | conditional | flops 2527613696 | bytes 150307328 | solution.py:338
  246.7 50.3 %collective-permute-done.2 = bf16[4,197,192]{1,0,2:T(4,128)(2,1)} collective-permute-done((bf16[4,197,192]{1,0,2:T(4,128)(2,1)}, bf16[4,197,192]{1,0,2:T(4,128)(2,1)}, u32[]{:S(2)}, u32[]{:S(2)}) %collective-permute-start.2) | collective-permute-done | bytes 302624 | tf_op jit(solution)/shard_map/ppermute | solution.py:37
  297.0 126.5 %conditional.10 = (f32[638976]{0:T(1024)}) conditional(s32[]{:T(128)} %convert_element_type.668, () %tuple.56, (bf16[192]{0:T(256)(128)(2,1)}, bf16[4,196,768]{2,1,0:T(8,128)(2,1)S(1)}, bf16[768,192]{1,0:T(8,128)(2,1)}, bf16[192]{0:T(256)(128)(2,1)}, bf16[197,192]{1,0:T(8,128)(2,1)S(1)}, /*index=5*/bf16[192]{0:T(256)(128)(2,1)}, ...), branch_computations={%region_88.0_spmd, %region_89.112_spmd} | conditional | flops 2753529600 | bytes 150505952 | solution.py:352
  300.9 2.6 convert_reduce_fusion.16
  316.5 5.4 reshape.1092
  322.0 3.7 fusion.412
  328.6 2.2 copy.303
  331.4 2.6 fusion.414
  338.2 6.3 fusion.291
  346.2 3.1 convert_reduce_fusion.12
  349.3 2.4 reshape.1055
  351.7 3.7 multiply_reduce_fusion.36
  363.3 2.4 convolution_bitcast_fusion.2
  371.3 3.2 copy.211
  374.5 3.3 convert_element_type.622
  377.8 2.6 fusion.433
  380.4 2.5 multiply_reduce_fusion.35
  382.9 2.1 reshape.1052
  387.3 2.2 add_add_fusion.10
  395.0 24.9 %concatenate.44 = f32[630336]{0:T(1024)} concatenate(f32[192]{0:T(256)S(1)} %copy-done.140, f32[192]{0:T(256)S(1)} %copy-done.141, f32[110592]{0:T(1024)S(1)} %copy-done.57, f32[192]{0:T(256)S(1)} %copy-done.149, f32[192]{0:T(256)S(1)} %copy-done.147, f32[36864]{0:T(1024)S(1)} %reshape.1053, f32[192]{0:T(256)S(1)} %copy-done.137, f32[192]{0:T(256)S(1)} %copy-done.168, ...), dimensions={0} | concatenate | bytes 5042688 | tf_op jit(solution)/shard_map/cond/branch_1_fun/concatenate | solution.py:76
  419.9 3.4 pad.14
  423.5 25.7 %collective-permute-done.3 = bf16[4,197,192]{1,0,2:T(4,128)(2,1)} collective-permute-done((bf16[4,197,192]{1,0,2:T(4,128)(2,1)}, bf16[4,197,192]{1,0,2:T(4,128)(2,1)}, u32[]{:S(2)}, u32[]{:S(2)}) %collective-permute-start.3) | collective-permute-done | bytes 302624 | tf_op jit(solution)/shard_map/ppermute | solution.py:37
  449.2 113.9 %conditional.11 = (f32[638976]{0:T(1024)}) conditional(s32[]{:T(128)} %convert_element_type.668, () %tuple.58, (bf16[192]{0:T(256)(128)(2,1)}, bf16[4,196,768]{2,1,0:T(8,128)(2,1)}, bf16[768,192]{1,0:T(8,128)(2,1)}, bf16[192]{0:T(256)(128)(2,1)}, bf16[197,192]{1,0:T(8,128)(2,1)}, /*index=5*/bf16[192]{0:T(256)(128)(2,1)}, ...), branch_computations={%region_112.113_spmd, %region_113.136_spmd} | conditional | flops 2753529600 | bytes 152795424 | solution.py:352
  453.1 2.6 convert_reduce_fusion.21
  464.6 2.8 reshape.1093
  467.4 3.7 fusion.416
  475.9 2.6 fusion.418
  482.6 5.3 fusion.336
  489.6 3.0 convert_reduce_fusion.17
  492.6 2.3 reshape.1065
  494.9 3.5 multiply_reduce_fusion.44
  507.1 2.5 convolution_bitcast_fusion.4
  515.5 2.7 convert_element_type.655
  520.9 2.1 reshape.1062
  534.7 24.9 %concatenate.47 = f32[630336]{0:T(1024)} concatenate(f32[192]{0:T(256)S(1)} %copy-done.142, f32[192]{0:T(256)S(1)} %copy-done.143, f32[110592]{0:T(1024)S(1)} %copy-done.58, f32[192]{0:T(256)S(1)} %copy-done.150, f32[192]{0:T(256)S(1)} %copy-done.148, f32[36864]{0:T(1024)S(1)} %copy-done.70, f32[192]{0:T(256)S(1)} %copy-done.138, f32[192]{0:T(256)S(1)} %copy-done.170, ...), dimensions={0} | concatenate | bytes 5042688 | tf_op jit(solution)/shard_map/cond/branch_1_fun/concatenate | solution.py:76
  559.6 3.3 pad.15
  563.1 5.9 add_add_fusion.16
  571.5 128.3 %all-reduce.10.cloned.1.call-done = f32[638976]{0:T(1024)} async-done(((f32[638976]{0:T(1024)}), f32[638976]{0:T(1024)}) %all-reduce.10.cloned.1.call-update) | async-done | bytes 2555920
  701.4 40.3 %psum.38 = f32[]{:T(128)} all-reduce(f32[]{:T(128)} %multiply_reduce_fusion.48), channel_id=1, replica_groups=mesh['section'=2,'dp'=16] {'section','dp'}, use_global_device_ids=true, to_apply=%region_138.139 | all-reduce | flops 1 | bytes 8 | tf_op jit(solution)/shard_map/psum | solution.py:359
  743.4 28.4 %fusion.382 = f32[1,400]{1,0:T(1,128)S(1)} fusion(f32[39936,1]{0,1:T(1,128)S(1)} %bitcast.400, bf16[400,1,39936]{2,0,1:T(8,128)(2,1)} %param.29), kind=kOutput, calls=%fused_computation.692 | convolution fusion | flops 191692800 | bytes 32110144 | tf_op jit(solution)/shard_map/dot_general | solution.py:363
  771.8 40.5 %all-reduce.7 = (f32[1]{0:T(128)}, f32[1]{0:T(128)}, f32[400]{0:T(512)S(1)}) all-reduce(f32[1]{0:T(128)} %bitcast.62, f32[1]{0:T(128)} %bitcast.61, f32[400]{0:T(512)S(1)} %bitcast.409), channel_id=1, replica_groups=mesh['section'=2,'dp'=16] {'section','dp'}, use_global_device_ids=true, to_apply=%region_87.0 | all-reduce | flops 402 | bytes 3216 | tf_op jit(solution)/shard_map/psum | solution.py:359
  813.0 16.8 %fusion.380 = f32[1,39936]{1,0:T(1,128)S(1)} fusion(f32[400,1]{0,1:T(1,128)S(1)} %bitcast.410, bf16[400,1,39936]{2,0,1:T(8,128)(2,1)} %param.29), kind=kOutput, calls=%fused_computation.690 | convolution fusion | flops 191692800 | bytes 32110144 | tf_op jit(solution)/shard_map/dot_general | solution.py:370
  829.7 2.5 pad_maximum_fusion.6
  (435 shorter events, 168.1 us)
Async XLA Ops:
  7.2 63.5 %all-gather.2.cloned.1.call-start = ((), (), s32[]{:S(2)}) async-start(), calls=%async_computation | async-start | bytes 1357824 | tf_op jit(solution)/shard_map/all_gather | solution.py:297
  8.8 691.0 %all-reduce.10.cloned.1.call-start = ((), (), s32[]{:S(2)}) async-start(), calls=%async_computation.1 | async-start | bytes 5111808
  72.8 53.6 %copy-start.51 = (bf16[197,192]{1,0:T(8,128)(2,1)}, bf16[197,192]{1,0:T(8,128)(2,1)S(1)}, u32[]{:S(2)}) copy-start(bf16[197,192]{1,0:T(8,128)(2,1)S(1)} %slice.317) | copy-start | bytes 226948
  74.0 143.3 %copy-start.17 = (bf16[192,576]{1,0:T(8,128)(2,1)}, bf16[192,576]{1,0:T(8,128)(2,1)S(1)}, u32[]{:S(2)}) copy-start(bf16[192,576]{1,0:T(8,128)(2,1)S(1)} %reshape.1073) | copy-start | bytes 663556
  75.9 141.4 %copy-start.38 = (bf16[768,192]{1,0:T(8,128)(2,1)}, bf16[768,192]{1,0:T(8,128)(2,1)S(1)}, u32[]{:S(2)}) copy-start(bf16[768,192]{1,0:T(8,128)(2,1)S(1)} %slice.330) | copy-start | bytes 884740
  77.1 49.2 %copy-start.8 = (bf16[768,192]{1,0:T(8,128)(2,1)}, bf16[768,192]{1,0:T(8,128)(2,1)S(1)}, u32[]{:S(2)}) copy-start(bf16[768,192]{1,0:T(8,128)(2,1)S(1)} %slice.314) | copy-start | bytes 884740
  77.8 139.5 %copy-start.96 = (bf16[384]{0:T(512)(128)(2,1)}, bf16[384]{0:T(512)(128)(2,1)S(1)}, u32[]{:S(2)}) copy-start(bf16[384]{0:T(512)(128)(2,1)S(1)} %slice.376) | copy-start | bytes 2308
  80.0 46.3 %copy-start.121 = (bf16[192]{0:T(256)(128)(2,1)}, bf16[192]{0:T(256)(128)(2,1)S(1)}, u32[]{:S(2)}) copy-start(bf16[192]{0:T(256)(128)(2,1)S(1)} %get-tuple-element.729) | copy-start | bytes 1156
  80.0 46.3 %copy-start.180 = (bf16[192]{0:T(256)(128)(2,1)}, bf16[192]{0:T(256)(128)(2,1)S(1)}, u32[]{:S(2)}) copy-start(bf16[192]{0:T(256)(128)(2,1)S(1)} %get-tuple-element.728) | copy-start | bytes 1156
  80.0 46.3 %copy-start.181 = (bf16[192]{0:T(256)(128)(2,1)}, bf16[192]{0:T(256)(128)(2,1)S(1)}, u32[]{:S(2)}) copy-start(bf16[192]{0:T(256)(128)(2,1)S(1)} %get-tuple-element.722) | copy-start | bytes 1156
  80.0 137.3 %copy-start.175 = (bf16[192]{0:T(256)(128)(2,1)}, bf16[192]{0:T(256)(128)(2,1)S(1)}, u32[]{:S(2)}) copy-start(bf16[192]{0:T(256)(128)(2,1)S(1)} %get-tuple-element.723) | copy-start | bytes 1156
  80.0 137.3 %copy-start.176 = (bf16[192]{0:T(256)(128)(2,1)}, bf16[192]{0:T(256)(128)(2,1)S(1)}, u32[]{:S(2)}) copy-start(bf16[192]{0:T(256)(128)(2,1)S(1)} %get-tuple-element.724) | copy-start | bytes 1156
  80.1 137.3 %copy-start.177 = (bf16[192]{0:T(256)(128)(2,1)}, bf16[192]{0:T(256)(128)(2,1)S(1)}, u32[]{:S(2)}) copy-start(bf16[192]{0:T(256)(128)(2,1)S(1)} %get-tuple-element.725) | copy-start | bytes 1156
  80.1 137.3 %copy-start.178 = (bf16[192]{0:T(256)(128)(2,1)}, bf16[192]{0:T(256)(128)(2,1)S(1)}, u32[]{:S(2)}) copy-start(bf16[192]{0:T(256)(128)(2,1)S(1)} %get-tuple-element.726) | copy-start | bytes 1156
  80.1 137.3 %copy-start.179 = (bf16[192]{0:T(256)(128)(2,1)}, bf16[192]{0:T(256)(128)(2,1)S(1)}, u32[]{:S(2)}) copy-start(bf16[192]{0:T(256)(128)(2,1)S(1)} %get-tuple-element.727) | copy-start | bytes 1156
  105.7 2.2 copy-start.81
  122.5 94.8 %collective-permute-start = (bf16[4,197,192]{1,0,2:T(4,128)(2,1)}, bf16[4,197,192]{1,0,2:T(4,128)(2,1)S(1)}, u32[]{:S(2)}, u32[]{:S(2)}) collective-permute-start(bf16[4,197,192]{1,0,2:T(4,128)(2,1)} %get-tuple-element.749), channel_id=1, source_target_pairs={{0,16},{1,17},{2,18},{3,19},{4,20},{5,21},{6,22},{7,23},{8,24},{9,... | collective-permute-start | bytes 907784 | tf_op jit(solution)/shard_map/ppermute | solution.py:37
  126.3 45.6 %copy-start.160 = (s32[8]{0:T(128)S(1)}, s32[8]{0:T(128)}, u32[]{:S(2)}) copy-start(s32[8]{0:T(128)} %param.23) | copy-start | bytes 100
  154.6 2.2 copy-start.82
  157.2 3.7 copy-start.182
  157.2 3.7 copy-start.183
  157.2 3.7 copy-start.184
  169.9 59.0 %collective-permute-start.1 = (bf16[4,197,192]{1,0,2:T(4,128)(2,1)}, bf16[4,197,192]{1,0,2:T(4,128)(2,1)}, u32[]{:S(2)}, u32[]{:S(2)}) collective-permute-start(bf16[4,197,192]{1,0,2:T(4,128)(2,1)} %get-tuple-element.750), channel_id=1, source_target_pairs={{0,16},{1,17},{2,18},{3,19},{4,20},{5,21},{6,22},{7,23},{8,24},{9,... | collective-permute-start | bytes 907784 | tf_op jit(solution)/shard_map/ppermute | solution.py:37
  227.6 69.4 %collective-permute-start.2 = (bf16[4,197,192]{1,0,2:T(4,128)(2,1)}, bf16[4,197,192]{1,0,2:T(4,128)(2,1)}, u32[]{:S(2)}, u32[]{:S(2)}) collective-permute-start(bf16[4,197,192]{1,0,2:T(4,128)(2,1)} %get-tuple-element.367), channel_id=1, source_target_pairs={{16,0},{17,1},{18,2},{19,3},{20,4},{21,5},{22,6},{23,7},{24,8},{25... | collective-permute-start | bytes 907784 | tf_op jit(solution)/shard_map/ppermute | solution.py:37
  228.9 68.1 %copy-start.52 = (bf16[197,192]{1,0:T(8,128)(2,1)S(1)}, bf16[197,192]{1,0:T(8,128)(2,1)}, u32[]{:S(2)}) copy-start(bf16[197,192]{1,0:T(8,128)(2,1)} %copy-done.51) | copy-start | bytes 226948
  243.7 205.5 %collective-permute-start.3 = (bf16[4,197,192]{1,0,2:T(4,128)(2,1)}, bf16[4,197,192]{1,0,2:T(4,128)(2,1)}, u32[]{:S(2)}, u32[]{:S(2)}) collective-permute-start(bf16[4,197,192]{1,0,2:T(4,128)(2,1)} %get-tuple-element.369), channel_id=1, source_target_pairs={{16,0},{17,1},{18,2},{19,3},{20,4},{21,5},{22,6},{23,7},{24,8},{25... | collective-permute-start | bytes 907784 | tf_op jit(solution)/shard_map/ppermute | solution.py:37
  297.0 10.3 %copy-start.122 = (bf16[192]{0:T(256)(128)(2,1)S(1)}, bf16[192]{0:T(256)(128)(2,1)}, u32[]{:S(2)}) copy-start(bf16[192]{0:T(256)(128)(2,1)} %get-tuple-element.314) | copy-start | bytes 1156 | tf_op jit(solution)/shard_map/cond
  297.6 17.3 %copy-start.113 = (f32[192]{0:T(256)}, f32[192]{0:T(256)S(1)}, u32[]{:S(2)}) copy-start(f32[192]{0:T(256)S(1)} %convert_element_type.600) | copy-start | bytes 2308 | tf_op jit(solution)/shard_map/cond
  309.5 5.3 copy-start.20
  327.0 4.3 copy-start.34
  328.6 5.3 copy-start.36
  331.4 2.6 copy-start.77
  344.4 1.7 copy-start.41
  351.7 3.7 copy-start.65
  358.6 3.0 copy-start.47
  363.3 2.6 copy-start.5
  363.3 2.6 copy-start.73
  363.3 2.7 copy-start.78
  363.3 2.7 copy-start.95
  370.0 7.8 copy-start.61
  449.2 11.5 %copy-start.123 = (bf16[192]{0:T(256)(128)(2,1)S(1)}, bf16[192]{0:T(256)(128)(2,1)}, u32[]{:S(2)}) copy-start(bf16[192]{0:T(256)(128)(2,1)} %get-tuple-element.331) | copy-start | bytes 1156 | tf_op jit(solution)/shard_map/cond
  461.6 2.4 copy-start.21
  475.3 3.1 copy-start.79
  479.9 2.8 copy-start.86
  488.0 1.6 copy-start.42
  494.9 3.5 copy-start.66
  501.7 3.0 copy-start.48
  507.1 2.5 copy-start.7
  507.1 2.6 copy-start.74
  507.1 2.7 copy-start.80
  512.3 5.9 copy-start.62
  520.9 4.1 copy-start.9
  520.9 4.1 copy-start.16
  530.9 2.6 copy-start.67
  532.8 1.7 copy-start.54
  532.8 1.7 copy-start.56
  532.8 1.7 copy-start.58
  532.8 1.7 copy-start.70
  532.8 1.7 copy-start.129
  532.8 1.7 copy-start.132
  532.9 1.7 copy-start.138
  532.9 1.7 copy-start.142
  813.0 19.3 %copy-start.68 = (f32[1,39936]{1,0:T(1,128)S(1)}, f32[1,39936]{1,0:T(1,128)}, u32[]{:S(2)}) copy-start(f32[1,39936]{1,0:T(1,128)} %broadcast_multiply_fusion.15) | copy-start | bytes 479236
  813.0 19.3 %copy-start.69 = (f32[1,39936]{1,0:T(1,128)S(1)}, f32[1,39936]{1,0:T(1,128)}, u32[]{:S(2)}) copy-start(f32[1,39936]{1,0:T(1,128)} %param.26) | copy-start | bytes 479236
  (32 other events, 37.4 us)
Sparse Core Ops, SparseCore 0:
  11.3 59.3 all-gather.1
  569.2 130.6 all-reduce.9
where the time goes:
time: 853 us; the launch traced here: 842 us
  waiting for transfers between devices  262 us (31%)
  local copies, waits for them, and re-layouts  211 us (25%)
  matrix products  134 us (16%)
  blocking collectives  121 us (14%)
  other arithmetic  68.7 us (8%)
  loops' own time  22.3 us (3%)
  between operations  17.8 us (2%)
    unnamed x3, waiting for transfers between devices  128 us
    psum x2, blocking collectives, body(): totals = lax.psum((squares, entropy_total, replay_total), ('section', 'dp'))  80.8 us
    ppermute x4, waiting for transfers between devices, from_behind(): lax.ppermute(value, axis, [(source, source + steps) for source in range(f...  75.9 us
    all_gather x1, waiting for transfers between devices, body(): gathered = lax.all_gather(to_low(master[0]), 'dp', axis=0, tiled=True)  57.3 us
    concatenate x2, local copies, waits for them, and re-layouts, pack(): flat_vec = jnp.concatenate([piece.reshape(-1) for piece in grads])  49.8 us
    psum x1, blocking collectives, body(): replay_count = lax.psum(jnp.sum(replay).astype(jnp.float32), 'dp')  40.2 us
    cond x152, local copies, waits for them, and re-layouts  29.3 us
    dot_general x1, matrix products, body(): jnp.dot(basis_rows, clipped, precision=HIGHEST_PREC, preferred_element_ty...  28.4 us
  transfers between devices with their start and end apart: 6, of which 4 were waited for; matrix products, arithmetic and copies ran while one was open for 22% of the time, Pallas kernels for 0%

commit v1 on v0

v1 whole, which is shorter than its diff:
```python
import functools
import math

import jax
import jax.numpy as jnp
from jax import lax
from jax.experimental import pallas as pl
from jax.experimental.pallas import tpu as pltpu
from jax.sharding import PartitionSpec as P

HEADS = 3
HD = 64
D = 192
FF = 768
PDIM = 768
PATCHES = 196
TOKENS = PATCHES + 1
ROWS = 208
CLS = PATCHES
CLASSES = 1000
CPAD = 1024
TASKS = 2
KMAX = 200
KB = TASKS * KMAX
STEP = 10
LANES = 128
HALF = 64
SPARE = 512
SUMS = 512

NORM_EPS = 1e-06
CLIP_NORM = 0.02
LEARN_RATE = 0.05
BETA_ONE = 0.9
BETA_TWO = 0.999
ADAM_EPS = 1e-08
WEIGHT_DECAY = 0.05
SCALE = HD ** (-0.5)
MASKED = -1e30

BLOCK_AT = dict(
    gain_one=0,
    bias_one=3,
    w_qkv=6,
    b_qkv=1734,
    w_out=1740,
    b_out=2316,
    gain_two=2319,
    bias_two=2322,
    w_up=2325,
    b_up=4629,
    w_down=4641,
    b_down=6945,
)
W_PATCH, B_PATCH, CLS_TOKEN, POS_EMBED = 6948, 9252, 9255, 9258
GAIN_LAST, BIAS_LAST, W_HEAD, B_HEAD = 6948, 6951, 6954, 9954
VECTORS = ("gain_one", "bias_one", "b_q", "b_v", "b_out", "gain_two", "bias_two", "b_up", "b_down")
VEC_ROWS = 16

f32 = jnp.float32
bf16 = jnp.bfloat16


def dot(left, right, left_dim=1, right_dim=0):
    return lax.dot_general(
        left, right, (((left_dim,), (right_dim,)), ((), ())), preferred_element_type=f32
    )


def low_lanes(shape):
    return lax.broadcasted_iota(jnp.int32, shape, 1) < HALF


def swap_halves(value):
    return pltpu.roll(value, HALF, 1)


def head_masks():
    lane = lax.broadcasted_iota(jnp.int32, (1, D), 1)
    return [jnp.logical_and(lane >= h * HD, lane < (h + 1) * HD) for h in range(HEADS)]


def by_head(value):
    return jnp.concatenate([jnp.where(m, value, 0.0) for m in head_masks()], 0)


def from_heads(value):
    rows = value.shape[0] // HEADS
    parts = [value[h * rows : (h + 1) * rows] for h in range(HEADS)]
    masks = head_masks()
    return jnp.where(masks[0], parts[0], jnp.where(masks[1], parts[1], parts[2]))


def normalise(rows_in):
    mean = jnp.sum(rows_in, -1, keepdims=True) * (1.0 / D)
    centred = rows_in - mean
    variance = jnp.sum(centred * centred, -1, keepdims=True) * (1.0 / D)
    scale = lax.rsqrt(variance + NORM_EPS)
    return centred * scale, scale


def normalise_back(grad, gain, unit, scale):
    grad_unit = grad * gain
    first = jnp.sum(grad_unit, -1, keepdims=True) * (1.0 / D)
    second = jnp.sum(grad_unit * unit, -1, keepdims=True) * (1.0 / D)
    return scale * (grad_unit - first - unit * second)


def gelu_parts(pre):
    cdf = 0.5 * (1.0 + lax.erf(pre * math.sqrt(0.5)))
    slope = cdf + pre * (jnp.exp(-0.5 * pre * pre) * (1.0 / math.sqrt(2.0 * math.pi)))
    return pre * cdf, slope


def column_sums(value):
    return jnp.sum(value.astype(f32), 0, keepdims=True)


def strided(ref, start, count, stride):
    if count == 1 or stride == 1:
        return ref[pl.ds(start, count), :]
    return ref[pl.ds(start, count, stride=stride), :]


class Flat:
    def __init__(self, even, odd, mix, rows):
        self.even, self.odd, self.mix, self.rows = even, odd, mix, rows

    def shift(self):
        step = 192
        for at in range(0, self.rows, step):
            here = swap_halves(self.even[at : at + step, :])
            after = swap_halves(self.even[at + 1 : at + 1 + step, :])
            self.odd[at : at + step, :] = jnp.where(low_lanes(here.shape), here, after)

    def rows_at(self, half, count, stride):
        return strided(self.odd if half % 2 else self.even, half // 2, count, stride)

    def blocks(self, half, width, rows, cols):
        for at in range(0, cols, LANES):
            start = half + at // HALF
            if rows == 1 or width % 2 == 0:
                value = self.rows_at(start, rows, width // 2)
            else:
                pairs = (rows + 1) // 2
                self.mix[pl.ds(0, pairs, stride=2), :] = self.rows_at(start, pairs, width)
                self.mix[pl.ds(1, pairs, stride=2), :] = self.rows_at(start + width, pairs, width)
                value = self.mix[0:rows, :]
            yield at, min(LANES, cols - at), value

    def read(self, dest, half, width, rows, cols):
        for at, wide, value in self.blocks(half, width, rows, cols):
            dest[0:rows, at : at + wide] = value[:, :wide].astype(dest.dtype)

    def read_row(self, dest, row, half, cols):
        for at, wide, value in self.blocks(half, 2, 1, cols):
            dest[row : row + 1, at : at + wide] = value[:, :wide]

    def clear(self):
        self.even[...] = jnp.zeros(self.even.shape, f32)
        self.odd[...] = jnp.zeros(self.odd.shape, f32)

    def put_rows(self, half, count, stride, value):
        ref, start = (self.odd, half // 2 + 8) if half % 2 else (self.even, half // 2)
        if count == 1 or stride == 1:
            ref[pl.ds(start, count), :] = value
        else:
            ref[pl.ds(start, count, stride=stride), :] = value

    def write(self, value, half, width, cols):
        rows = value.shape[0]
        for at in range(0, cols, LANES):
            wide = min(LANES, cols - at)
            part = value[:, at : at + wide]
            if wide < LANES:
                part = jnp.concatenate([part, jnp.zeros((rows, LANES - wide), f32)], 1)
            start = half + at // HALF
            if rows == 1 or width % 2 == 0:
                self.put_rows(start, rows, width // 2, part)
            else:
                pairs = (rows + 1) // 2
                self.mix[0:rows, :] = part
                self.put_rows(start, pairs, width, self.mix[pl.ds(0, pairs, stride=2), :])
                self.put_rows(start + width, pairs, width, self.mix[pl.ds(1, pairs, stride=2), :])

    def merged(self, at, count):
        here = swap_halves(self.odd[at + 8 : at + 8 + count, :])
        before = swap_halves(self.odd[at + 7 : at + 7 + count, :])
        return self.even[at : at + count, :] + jnp.where(low_lanes(here.shape), before, here)


class Place:
    def __init__(self, dims, shard_rows):
        self.z, self.y, self.x = dims
        self.count = self.z * self.y * self.x
        self.shard_rows = shard_rows
        self.sent_rows = -(-(shard_rows + 1) // 16) * 16

    def split(self, index):
        plane = self.y * self.x
        return index // plane, lax.rem(index, plane) // self.x, lax.rem(index, self.x)

    def turns(self):
        return [(a, b) for a in range(self.y) for b in range(self.x)]


def load_section(place, info, pieces, wanted, flat):
    own, other = pieces
    section = info[0]
    zed, why, ex = place.split(info[1])
    rows = place.shard_rows

    def copy(refs):
        for turn, (a, b) in enumerate(place.turns()):
            for d in range(place.z):
                shard = lax.rem(zed + (place.z - d), place.z) * (place.y * place.x)
                shard = shard + lax.rem(why + (place.y - a), place.y) * place.x
                shard = shard + lax.rem(ex + (place.x - b), place.x)
                start = shard * rows
                if rows % 8 == 0:
                    start = pl.multiple_of(start, 8)
                value = refs[turn][d].astype(f32)
                flat.even[pl.ds(start, rows), :] = value[:rows]

    @pl.when(section == wanted)
    def _():
        copy(own)

    @pl.when(section != wanted)
    def _():
        copy(other)

    flat.shift()


def read_block(flat, weights, vec):
    at = BLOCK_AT
    w_q, w_k, w_v, w_out, w_up, w_down = weights
    for place, dest in enumerate((w_q, w_k, w_v)):
        flat.read(dest, at["w_qkv"] + 3 * place, 9, D, D)
    flat.read(w_out, at["w_out"], 3, D, D)
    flat.read(w_up, at["w_up"], 12, D, FF)
    flat.read(w_down, at["w_down"], 3, FF, D)
    starts = dict(at, b_q=at["b_qkv"], b_v=at["b_qkv"] + 3)
    for row, name in enumerate(VECTORS):
        flat.read_row(vec, row, starts[name], FF if name == "b_up" else D)


def vector(vec, name):
    row = VECTORS.index(name)
    return vec[row : row + 1, 0 : FF if name == "b_up" else D]


def write_vectors(flat, sums):
    at = BLOCK_AT
    starts = dict(at, b_q=at["b_qkv"], b_v=at["b_qkv"] + 3)
    for name, value in sums.items():
        flat.write(value, starts[name], 2, value.shape[1])


def send_out(place, info, flat, out_ref):
    zed, why, ex = place.split(info[1])
    rows, spare = place.shard_rows, place.sent_rows - place.shard_rows
    for shard in range(place.count):
        zk, yk, xk = shard // (place.y * place.x), shard // place.x % place.y, shard % place.x
        d = lax.rem(zk + place.z - zed, place.z)
        a = lax.rem(yk + place.y - why, place.y)
        b = lax.rem(xk + place.x - ex, place.x)
        value = flat.merged(shard * rows, rows)
        value = jnp.concatenate([value, jnp.zeros((spare, LANES), f32)], 0)
        out_ref[(a * place.x + b) * place.z + d] = value.astype(bf16)


def front_kernel(place, info, *refs):
    turns = len(place.turns())
    own, other, refs = refs[:turns], refs[turns : 2 * turns], refs[2 * turns :]
    patches, refs = refs[0], refs[1:]
    (x_out, q_out, k_out, v_out, probs_out, mixed_out, hidden_out, act_out, slope_out, middle_out) = refs[:10]
    w_q, w_k, w_v, w_out, w_up, w_down, vec = refs[10:17]
    even, odd, mix, w_patch, added, tokens = refs[17:]
    flat = Flat(even, odd, mix, place.count * place.shard_rows)

    @pl.when(pl.program_id(0) == 0)
    def _():
        load_section(place, info, (own, other), 0, flat)
        read_block(flat, (w_q, w_k, w_v, w_out, w_up, w_down), vec)
        flat.read(w_patch, W_PATCH, 3, PDIM, D)
        flat.read_row(vec, 9, B_PATCH, D)
        flat.read_row(vec, 10, CLS_TOKEN, D)
        added[...] = jnp.zeros(added.shape, f32)
        tokens[...] = jnp.zeros(tokens.shape, f32)
        for at, wide, value in flat.blocks(POS_EMBED, 3, TOKENS + 1, D):
            bias = vec[9:10, at : at + wide]
            token = vec[10:11, at : at + wide]
            added[0:PATCHES, at : at + wide] = value[1:TOKENS, :wide] + bias
            added[CLS : CLS + 1, at : at + wide] = value[0:1, :wide] + token

    tokens[0:PATCHES, :] = dot(patches[...], w_patch[...])
    x = tokens[...] + added[...]
    x_out[...] = x
    unit, _ = normalise(x)
    normed = (unit * vector(vec, "gain_one") + vector(vec, "bias_one")).astype(bf16)
    q = (dot(normed, w_q[...]) + vector(vec, "b_q")).astype(bf16)
    k = dot(normed, w_k[...]).astype(bf16)
    v = (dot(normed, w_v[...]) + vector(vec, "b_v")).astype(bf16)
    q_out[...], k_out[...], v_out[...] = q, k, v
    scores = dot(by_head(q.astype(f32) * SCALE).astype(bf16), k, 1, 1)
    column = lax.broadcasted_iota(jnp.int32, scores.shape, 1)
    scores = jnp.where(column < TOKENS, scores, MASKED)
    raised = jnp.exp(scores - jnp.max(scores, -1, keepdims=True))
    probs = raised / jnp.sum(raised, -1, keepdims=True)
    probs_out[...] = probs
    mixed = from_heads(dot(probs.astype(bf16), v)).astype(bf16)
    mixed_out[...] = mixed
    hidden = x + dot(mixed, w_out[...]) + vector(vec, "b_out")
    hidden_out[...] = hidden
    unit, _ = normalise(hidden)
    normed = (unit * vector(vec, "gain_two") + vector(vec, "bias_two")).astype(bf16)
    pre = dot(normed, w_up[...]) + vector(vec, "b_up")
    act, slope = gelu_parts(pre)
    act = act.astype(bf16)
    act_out[...], slope_out[...] = act, slope
    middle = hidden + dot(act, w_down[...]) + vector(vec, "b_down")
    middle_out[...] = middle.astype(bf16)


def read_head(flat, wide, w_head, b_head):
    first = W_HEAD // 2
    lane = lax.broadcasted_iota(jnp.int32, (16, LANES), 1)
    for phase in range(16):
        start, off = first + CLASSES * phase // LANES, CLASSES * phase % LANES
        got = [strided(flat.even, start + j, 16, 125) for j in range(9 if off else 8)]
        if off:
            got = [pltpu.roll(g, LANES - off, 1) for g in got]
        for j in range(8):
            value = jnp.where(lane < LANES - off, got[j], got[j + 1]) if off else got[j]
            wide[j, pl.ds(phase, 16, stride=16), :] = value
    lane = lax.broadcasted_iota(jnp.int32, (1, LANES), 1)
    for j in range(8):
        keep = lane + j * LANES < CLASSES
        w_head[:, j * LANES : (j + 1) * LANES] = jnp.where(keep, wide[j, 0:D, :], 0.0).astype(bf16)
        value = flat.even[B_HEAD // 2 + j : B_HEAD // 2 + j + 1, :]
        b_head[0:1, j * LANES : (j + 1) * LANES] = jnp.where(keep, value, 0.0)


def write_head(flat, wide, grad_w, grad_b):
    first = W_HEAD // 2
    for j in range(8):
        wide[j, 0:D, :] = grad_w[:, j * LANES : (j + 1) * LANES]
        wide[j, D:, :] = jnp.zeros((wide.shape[1] - D, LANES), f32)
    lane = lax.broadcasted_iota(jnp.int32, (16, LANES), 1)
    for phase in range(16):
        start, off = first + CLASSES * phase // LANES, CLASSES * phase % LANES
        got = [wide[j, pl.ds(phase, 16, stride=16), :] for j in range(8)]
        if off:
            got = [pltpu.roll(g, off, 1) for g in got]
        for j in range(9 if off else 8):
            if not off:
                value = got[j]
            else:
                before = got[j - 1] if j else jnp.zeros((16, LANES), f32)
                value = jnp.where(lane < off, before, got[j] if j < 8 else 0.0)
            flat.even[pl.ds(start + j, 16, stride=125), :] += value
    for j in range(8):
        row = B_HEAD // 2 + j
        flat.even[row : row + 1, :] += grad_b[:, j * LANES : (j + 1) * LANES]


def late_kernel(place, per, image_total, info, labels, replay, *refs):
    turns = len(place.turns())
    own, other, refs = refs[:turns], refs[turns : 2 * turns], refs[2 * turns :]
    middle, old_logits, back_out, grad_out, loss_out = refs[:5]
    even, odd, mix, wide, w_q, w_k, w_v, w_out, w_up, w_down, vec, w_head, b_head, few, many = refs[5:]
    flat = Flat(even, odd, mix, place.count * place.shard_rows)
    load_section(place, info, (own, other), 1, flat)
    read_block(flat, (w_q, w_k, w_v, w_out, w_up, w_down), vec)
    flat.read_row(vec, 9, GAIN_LAST, D)
    flat.read_row(vec, 10, BIAS_LAST, D)
    read_head(flat, wide, w_head, b_head)
    gain_last, bias_last = vec[9:10, 0:D], vec[10:11, 0:D]
    carried = jnp.zeros((1, LANES), f32)
    for ref in own:
        for d in range(place.z):
            carried = carried + ref[d].astype(f32)[place.shard_rows : place.shard_rows + 1]
    replay_count = carried[:, 0:1]

    x = middle[...].astype(f32)
    unit, scale = normalise(x)
    normed_f = unit * vector(vec, "gain_one") + vector(vec, "bias_one")
    normed = normed_f.astype(bf16)
    k = dot(normed, w_k[...]).astype(bf16)
    v = (dot(normed, w_v[...]) + vector(vec, "b_v")).astype(bf16)

    def class_rows(value):
        few[...] = jnp.zeros(few.shape, f32)
        for i in range(per):
            few[i : i + 1, :] = value[i * ROWS + CLS : i * ROWS + CLS + 1, :]
        return few[...]

    eight = few.shape[0]
    image = lax.broadcasted_iota(jnp.int32, (eight, 1), 0)
    real = image < per
    x_top = class_rows(x)
    top_normed = class_rows(normed_f).astype(bf16)
    q = (dot(top_normed, w_q[...]) + vector(vec, "b_q")).astype(bf16)
    q_heads = by_head(jnp.where(real, q.astype(f32) * SCALE, 0.0)).astype(bf16)
    scores = dot(q_heads, k, 1, 1)
    column = lax.broadcasted_iota(jnp.int32, scores.shape, 1)
    owner = lax.rem(lax.broadcasted_iota(jnp.int32, scores.shape, 0), eight) * ROWS
    inside = jnp.logical_and(column >= owner, column < owner + TOKENS)
    scores = jnp.where(inside, scores, MASKED)
    raised = jnp.where(inside, jnp.exp(scores - jnp.max(scores, -1, keepdims=True)), 0.0)
    total = jnp.sum(raised, -1, keepdims=True)
    probs = raised / jnp.where(total > 0.0, total, 1.0)
    probs_low = probs.astype(bf16)
    mixed = from_heads(dot(probs_low, v)).astype(bf16)
    hidden = x_top + dot(mixed, w_out[...]) + vector(vec, "b_out")
    unit_two, scale_two = normalise(hidden)
    normed_two = (unit_two * vector(vec, "gain_two") + vector(vec, "bias_two")).astype(bf16)
    act, slope = gelu_parts(dot(normed_two, w_up[...]) + vector(vec, "b_up"))
    act = act.astype(bf16)
    final = hidden + dot(act, w_down[...]) + vector(vec, "b_down")

    unit_last, scale_last = normalise(final)
    top = (unit_last * gain_last + bias_last).astype(bf16)
    classes = lax.broadcasted_iota(jnp.int32, (eight, CPAD), 1)
    logits = dot(top, w_head[...]) + b_head[...]
    logits = jnp.where(classes < CLASSES, logits, MASKED)
    highest = jnp.max(logits, -1, keepdims=True)
    log_total = highest + jnp.log(jnp.sum(jnp.exp(logits - highest), -1, keepdims=True))
    label = jnp.zeros((eight, 1), jnp.int32)
    again = jnp.zeros((eight, 1), f32)
    for i in range(per):
        label = jnp.where(image == i, labels[info[0] * per + i], label)
        again = jnp.where(image == i, replay[info[0] * per + i].astype(f32), again)
    picked = jnp.logical_and(classes == label, real)
    entropy = jnp.where(real, log_total, 0.0) - jnp.sum(jnp.where(picked, logits, 0.0), -1, keepdims=True)
    wanted = jnp.where(info[0] == 0, old_logits[0:per, :], old_logits[per : 2 * per, :])
    if per < eight:
        wanted = jnp.concatenate([wanted, jnp.zeros((eight - per, CLASSES), f32)], 0)
    wanted = jnp.concatenate([wanted, jnp.zeros((eight, CPAD - CLASSES), f32)], 1)
    distance = jnp.where(jnp.logical_and(classes < CLASSES, real), logits - wanted, 0.0)
    squares = again * (jnp.sum(distance * distance, -1, keepdims=True) * (1.0 / CLASSES))
    lane = lax.broadcasted_iota(jnp.int32, (1, LANES), 1)
    entropy_sum = jnp.sum(entropy, 0, keepdims=True)
    replay_sum = jnp.sum(squares, 0, keepdims=True)
    loss_out[...] = jnp.where(lane == 0, entropy_sum, jnp.where(lane == 1, replay_sum, replay_count))

    grad = (jnp.exp(logits - log_total) - jnp.where(picked, 1.0, 0.0)) * (1.0 / image_total)
    grad = grad + again * 2.0 * distance / (CLASSES * replay_count)
    grad = jnp.where(jnp.logical_and(classes < CLASSES, real), grad, 0.0)
    grad_low = grad.astype(bf16)
    flat.clear()
    write_head(flat, wide, dot(top, grad_low, 0, 0), column_sums(grad_low))
    sums = {}
    grad = dot(grad_low, w_head[...], 1, 1)
    flat.write(column_sums(grad * unit_last), GAIN_LAST, 2, D)
    flat.write(column_sums(grad), BIAS_LAST, 2, D)
    grad = normalise_back(grad, gain_last, unit_last, scale_last)

    at = BLOCK_AT
    grad_down = grad.astype(bf16)
    flat.write(dot(act, grad_down, 0, 0), at["w_down"], 3, D)
    sums["b_down"] = column_sums(grad_down)
    grad_up = (dot(grad_down, w_down[...], 1, 1) * slope).astype(bf16)
    flat.write(dot(normed_two, grad_up, 0, 0), at["w_up"], 12, FF)
    sums["b_up"] = column_sums(grad_up)
    grad_two = dot(grad_up, w_up[...], 1, 1)
    sums["gain_two"], sums["bias_two"] = column_sums(grad_two * unit_two), column_sums(grad_two)
    grad_hidden = grad + normalise_back(grad_two, vector(vec, "gain_two"), unit_two, scale_two)
    branch = grad_hidden.astype(bf16)
    flat.write(dot(mixed, branch, 0, 0), at["w_out"], 3, D)
    sums["b_out"] = column_sums(branch)
    mixed_heads = by_head(dot(branch, w_out[...], 1, 1).astype(bf16).astype(f32)).astype(bf16)
    grad_probs = dot(mixed_heads, v, 1, 1)
    grad_v = dot(probs_low, mixed_heads, 0, 0).astype(bf16)
    inner = jnp.sum(grad_probs * probs, -1, keepdims=True)
    grad_scores = (probs * (grad_probs - inner)).astype(bf16)
    grad_q = (from_heads(dot(grad_scores, k)) * SCALE).astype(bf16)
    grad_k = dot(grad_scores, q_heads, 0, 0).astype(bf16)
    flat.write(dot(top_normed, grad_q, 0, 0), at["w_qkv"], 9, D)
    flat.write(dot(normed, grad_k, 0, 0), at["w_qkv"] + 3, 9, D)
    flat.write(dot(normed, grad_v, 0, 0), at["w_qkv"] + 6, 9, D)
    sums["b_q"], sums["b_v"] = column_sums(grad_q), column_sums(grad_v)
    many[...] = dot(grad_k, w_k[...], 1, 1) + dot(grad_v, w_v[...], 1, 1)
    top_back = dot(grad_q, w_q[...], 1, 1)
    for i in range(per):
        many[i * ROWS + CLS : i * ROWS + CLS + 1, :] += top_back[i : i + 1, :]
    grad_one = many[...]
    sums["gain_one"], sums["bias_one"] = column_sums(grad_one * unit), column_sums(grad_one)
    many[...] = normalise_back(grad_one, vector(vec, "gain_one"), unit, scale)
    for i in range(per):
        many[i * ROWS + CLS : i * ROWS + CLS + 1, :] += grad_hidden[i : i + 1, :]
    back_out[...] = many[...].astype(bf16)
    write_vectors(flat, sums)
    send_out(place, info, flat, grad_out)


def back_kernel(place, info, *refs):
    (grad_in, x_in, q_in, k_in, v_in, probs_in, mixed_in, hidden_in, act_in, slope_in, patches) = refs[:11]
    w_q, w_k, w_v, w_out, w_up, w_down, vec, grad_out = refs[11:19]
    even, odd, mix, g_q, g_k, g_v, g_out, g_up, g_down, g_patch, g_pos, rows = refs[19:]
    step = pl.program_id(0)
    sums_at = {name: row for row, name in enumerate(VECTORS)}

    @pl.when(step == 0)
    def _():
        for ref in (g_q, g_k, g_v, g_out, g_up, g_down, g_patch, g_pos, rows):
            ref[...] = jnp.zeros(ref.shape, f32)

    def add_row(row, value):
        rows[row : row + 1, 0 : value.shape[1]] += value

    grad_low = grad_in[...]
    g_down[...] += dot(act_in[...], grad_low, 0, 0)
    add_row(sums_at["b_down"], column_sums(grad_low))
    grad_up = (dot(grad_low, w_down[...], 1, 1) * slope_in[...]).astype(bf16)
    unit, scale = normalise(hidden_in[...])
    normed = (unit * vector(vec, "gain_two") + vector(vec, "bias_two")).astype(bf16)
    g_up[...] += dot(normed, grad_up, 0, 0)
    add_row(sums_at["b_up"], column_sums(grad_up))
    grad_two = dot(grad_up, w_up[...], 1, 1)
    add_row(sums_at["gain_two"], column_sums(grad_two * unit))
    add_row(sums_at["bias_two"], column_sums(grad_two))
    grad_hidden = grad_low.astype(f32) + normalise_back(grad_two, vector(vec, "gain_two"), unit, scale)
    branch = grad_hidden.astype(bf16)
    g_out[...] += dot(mixed_in[...], branch, 0, 0)
    add_row(sums_at["b_out"], column_sums(branch))
    mixed_heads = by_head(dot(branch, w_out[...], 1, 1).astype(bf16).astype(f32)).astype(bf16)
    q_heads = by_head(q_in[...].astype(f32) * SCALE).astype(bf16)
    probs = probs_in[...]
    grad_probs = dot(mixed_heads, v_in[...], 1, 1)
    grad_v = dot(probs.astype(bf16), mixed_heads, 0, 0).astype(bf16)
    inner = jnp.sum(grad_probs * probs, -1, keepdims=True)
    grad_scores = (probs * (grad_probs - inner)).astype(bf16)
    grad_q = (from_heads(dot(grad_scores, k_in[...])) * SCALE).astype(bf16)
    grad_k = dot(grad_scores, q_heads, 0, 0).astype(bf16)
    unit, scale = normalise(x_in[...])
    normed = (unit * vector(vec, "gain_one") + vector(vec, "bias_one")).astype(bf16)
    g_q[...] += dot(normed, grad_q, 0, 0)
    g_k[...] += dot(normed, grad_k, 0, 0)
    g_v[...] += dot(normed, grad_v, 0, 0)
    add_row(sums_at["b_q"], column_sums(grad_q))
    add_row(sums_at["b_v"], column_sums(grad_v))
    grad_one = dot(grad_q, w_q[...], 1, 1) + dot(grad_k, w_k[...], 1, 1) + dot(grad_v, w_v[...], 1, 1)
    add_row(sums_at["gain_one"], column_sums(grad_one * unit))
    add_row(sums_at["bias_one"], column_sums(grad_one))
    grad_x = grad_hidden + normalise_back(grad_one, vector(vec, "gain_one"), unit, scale)
    g_pos[...] += grad_x
    grad_emb = grad_x[0:PATCHES].astype(bf16)
    g_patch[...] += dot(patches[...], grad_emb, 0, 0)
    add_row(9, column_sums(grad_emb))

    @pl.when(step == pl.num_programs(0) - 1)
    def _():
        at = BLOCK_AT
        flat = Flat(even, odd, mix, place.count * place.shard_rows)
        flat.clear()
        for part, ref in enumerate((g_q, g_k, g_v)):
            flat.write(ref[...], at["w_qkv"] + 3 * part, 9, D)
        flat.write(g_out[...], at["w_out"], 3, D)
        flat.write(g_up[...], at["w_up"], 12, FF)
        flat.write(g_down[...], at["w_down"], 3, D)
        flat.write(g_patch[...], W_PATCH, 3, D)
        names = {name: rows[row : row + 1, 0 : FF if name == "b_up" else D] for name, row in sums_at.items()}
        write_vectors(flat, names)
        flat.write(rows[9:10, 0:D], B_PATCH, 2, D)
        token = g_pos[CLS : CLS + 1, :]
        flat.write(token, CLS_TOKEN, 2, D)
        natural = jnp.concatenate([token, g_pos[0:PATCHES, :], jnp.zeros((1, D), f32)], 0)
        flat.write(natural, POS_EMBED, 3, D)
        send_out(place, info, flat, grad_out)


def inner_kernel(blocks, first, *refs):
    pieces, basis, loss, grad_out, sums_out, total = refs[:-5], *refs[-5:]
    step = pl.program_id(0)
    shard_rows = grad_out.shape[0]

    @pl.when(step == 0)
    def _():
        value = first[...]
        for ref in pieces:
            value = value + ref[...].astype(f32)
        grad_out[...] = value[:shard_rows]
        total[...] = jnp.zeros(total.shape, f32)

    base = step * blocks
    for at in range(0, KB, 16):
        acc = jnp.zeros((16, LANES), f32)
        for j in range(blocks):
            part = basis[at : at + 16, j * LANES : (j + 1) * LANES].astype(f32)
            acc = acc + part * grad_out[pl.ds(base + j, 1), :]
        total[at : at + 16, :] += acc

    @pl.when(step == pl.num_programs(0) - 1)
    def _():
        coefs = jnp.sum(total[...].T, 0, keepdims=True)
        grad = grad_out[...]
        squares = jnp.sum(jnp.sum(grad * grad, 0, keepdims=True), 1, keepdims=True)
        lane = lax.broadcasted_iota(jnp.int32, (1, SUMS - KB), 1)
        rest = jnp.where(lane == 0, squares, 0.0)
        rest = rest + jnp.where(lane == 1, loss[0:1, 0:1], 0.0) + jnp.where(lane == 2, loss[0:1, 1:2], 0.0)
        sums_out[:, 0:KB] = coefs
        sums_out[:, KB:SUMS] = rest


def update_kernel(blocks, whole_len, counts, sums, basis, grad, loss, master, first, second, *refs):
    loss_out, norm_out, coef_out, master_out, first_out, second_out, coef, removed = refs
    step = pl.program_id(0)

    def clip_factor():
        norm = jnp.sqrt(sums[0:1, KB : KB + 1])
        return norm, jnp.minimum(1.0, CLIP_NORM / (norm + 1e-06))

    @pl.when(step == 0)
    def _():
        norm, factor = clip_factor()
        lane = lax.broadcasted_iota(jnp.int32, (1, KB), 1)
        limit = jnp.where(lane < KMAX, counts[0], counts[1] + KMAX)
        row = jnp.where(lane < limit, sums[:, 0:KB] * factor, 0.0)
        coef_out[0:1, :] = row[:, 0:KMAX]
        coef_out[1:2, :] = row[:, KMAX:KB]
        coef[...] = jnp.broadcast_to(row, (LANES, KB)).T
        norm_out[0] = jnp.sum(norm)
        loss_out[0] = jnp.sum(sums[0:1, KB + 1 : KB + 2])
        loss_out[1] = jnp.sum(sums[0:1, KB + 2 : KB + 3])
        loss_out[2] = jnp.sum(loss[0:1, 2:3])

    acc = [jnp.zeros((8, LANES), f32) for _ in range(blocks)]
    for at in range(0, KB, 16):
        weight = coef[at : at + 16, :]
        for j in range(blocks):
            part = basis[at : at + 16, j * LANES : (j + 1) * LANES].astype(f32) * weight
            acc[j] = acc[j] + (part[0:8] + part[8:16])
    base = step * blocks
    for j in range(blocks):
        removed[pl.ds(base + j, 1), :] = jnp.sum(acc[j], 0, keepdims=True)

    @pl.when(step == pl.num_programs(0) - 1)
    def _():
        _, factor = clip_factor()
        rows = grad.shape[0]
        projected = grad[...] * factor - removed[0:rows, :] * (1.0 / whole_len)
        new_first = BETA_ONE * first[...] + (1.0 - BETA_ONE) * projected
        new_second = BETA_TWO * second[...] + (1.0 - BETA_TWO) * projected * projected
        ratio = (
            new_first
            / (1.0 - BETA_ONE**STEP)
            / (jnp.sqrt(new_second / (1.0 - BETA_TWO**STEP)) + ADAM_EPS)
        )
        old = master[...]
        master_out[...] = old - LEARN_RATE * (ratio + WEIGHT_DECAY * old)
        first_out[...] = new_first
        second_out[...] = new_second


def dp_dims(count):
    zed = 4 if count % 4 == 0 else 1
    plane = count // zed
    ex = max(side for side in range(1, math.isqrt(plane) + 1) if plane % side == 0)
    return zed, plane // ex, ex


def moved(value, place, turn=(0, 0, 0), core=0, sections=(0, 1)):
    pairs = []
    for section in sections:
        for zed in range(place.z):
            for why in range(place.y):
                for ex in range(place.x):
                    source = (section * place.z + zed) * place.y * place.x + why * place.x + ex
                    there = ((section + core) % 2) * place.z + (zed + turn[0]) % place.z
                    target = (there * place.y + (why + turn[1]) % place.y) * place.x
                    pairs.append((source, target + (ex + turn[2]) % place.x))
    return lax.ppermute(value, ("section", "dp"), pairs)


def butterfly(value, place):
    value = value + moved(value, place, core=1)
    for axis, size in ((2, place.x), (1, place.y), (0, place.z)):
        span = 1
        while span < size:
            pairs = []
            for index in range(2 * place.count):
                section, rest = divmod(index, place.count)
                at = [rest // (place.y * place.x), rest // place.x % place.y, rest % place.x]
                at[axis] ^= span
                pairs.append((index, section * place.count + (at[0] * place.y + at[1]) * place.x + at[2]))
            value = value + lax.ppermute(value, ("section", "dp"), pairs)
            span *= 2
    return value


def whole(shape):
    return pl.BlockSpec(shape, lambda *_: (0,) * len(shape))


def params(megabytes):
    return pltpu.CompilerParams(
        vmem_limit_bytes=megabytes * 1024 * 1024, dimension_semantics=("arbitrary",)
    )


def body(
    patches, labels, replay, old_logits, basis_count, master, first_moment, second_moment, basis
):
    chips = lax.axis_size("dp")
    shard_len = master.shape[1]
    shard_rows = shard_len // LANES
    place = Place(dp_dims(chips), shard_rows)
    images = patches.shape[0]
    per = images // 2
    section = lax.axis_index("section")
    info = jnp.stack([section, lax.axis_index("dp")]).astype(jnp.int32)
    flat_rows = chips * shard_rows + SPARE
    turns = place.turns()

    shard = master[0].astype(bf16).reshape(shard_rows, LANES)
    count = jnp.sum(replay).astype(bf16)
    tail = jnp.full((place.sent_rows - shard_rows, LANES), count, bf16)
    shard = jnp.concatenate([shard, tail], 0)
    line = jnp.stack([shard] + [moved(shard, place, (d, 0, 0)) for d in range(1, place.z)])
    own = [moved(line, place, (0, a, b)) if a + b else line for a, b in turns]
    other = [moved(piece, place, core=1) for piece in own]

    flat_scratch = [
        pltpu.VMEM((flat_rows, LANES), f32),
        pltpu.VMEM((flat_rows, LANES), f32),
        pltpu.VMEM((FF + 32, LANES), f32),
    ]
    piece_specs = [whole(piece.shape) for piece in own + other]
    block_shapes = [(D, D)] * 4 + [(D, FF), (FF, D)]
    row_of = lambda i, *_: (i, 0)
    saved = [
        ((ROWS, D), f32),
        ((ROWS, D), bf16),
        ((ROWS, D), bf16),
        ((ROWS, D), bf16),
        ((HEADS * ROWS, ROWS), f32),
        ((ROWS, D), bf16),
        ((ROWS, D), f32),
        ((ROWS, FF), bf16),
        ((ROWS, FF), f32),
    ]
    middle_kind = ((ROWS, D), bf16)
    patch_spec = pl.BlockSpec((None, PATCHES, PDIM), lambda i, info: (info[0] * per + i, 0, 0))
    outs = pl.pallas_call(
        functools.partial(front_kernel, place),
        grid_spec=pltpu.PrefetchScalarGridSpec(
            num_scalar_prefetch=1,
            grid=(per,),
            in_specs=piece_specs + [patch_spec],
            out_specs=[pl.BlockSpec(shape, row_of) for shape, _ in saved + [middle_kind]]
            + [whole(shape) for shape in block_shapes]
            + [whole((VEC_ROWS, FF))],
            scratch_shapes=flat_scratch
            + [pltpu.VMEM((PDIM, D), bf16), pltpu.VMEM((ROWS, D), f32), pltpu.VMEM((ROWS, D), f32)],
        ),
        out_shape=[
            jax.ShapeDtypeStruct((per * shape[0], shape[1]), kind) for shape, kind in saved + [middle_kind]
        ]
        + [jax.ShapeDtypeStruct(shape, bf16) for shape in block_shapes]
        + [jax.ShapeDtypeStruct((VEC_ROWS, FF), f32)],
        compiler_params=params(40),
        name="front",
    )(info, *own, *other, patches)
    kept, middle, weights = outs[:9], outs[9], outs[10:]

    grad_shape = jax.ShapeDtypeStruct((chips, place.sent_rows, LANES), bf16)
    smem = pl.BlockSpec(memory_space=pltpu.SMEM)
    vmem = pl.BlockSpec(memory_space=pltpu.VMEM)
    eight = -(-per // 8) * 8
    back, late_grad, loss = pl.pallas_call(
        functools.partial(late_kernel, place, per, float(images * chips)),
        in_specs=[smem] * 3 + [vmem] * (2 * len(turns) + 2),
        out_specs=[vmem] * 3,
        out_shape=[
            jax.ShapeDtypeStruct((per * ROWS, D), bf16),
            grad_shape,
            jax.ShapeDtypeStruct((1, LANES), f32),
        ],
        scratch_shapes=flat_scratch
        + [pltpu.VMEM((8, 256, LANES), f32)]
        + [pltpu.VMEM(shape, bf16) for shape in block_shapes]
        + [
            pltpu.VMEM((VEC_ROWS, FF), f32),
            pltpu.VMEM((D, CPAD), bf16),
            pltpu.VMEM((1, CPAD), f32),
            pltpu.VMEM((eight, D), f32),
            pltpu.VMEM((per * ROWS, D), f32),
        ],
        compiler_params=pltpu.CompilerParams(vmem_limit_bytes=40 * 1024 * 1024),
        name="late",
    )(info, labels, replay, *own, *other, middle, old_logits)

    early_grad = pl.pallas_call(
        functools.partial(back_kernel, place),
        grid_spec=pltpu.PrefetchScalarGridSpec(
            num_scalar_prefetch=1,
            grid=(per,),
            in_specs=[pl.BlockSpec(shape, row_of) for shape, _ in [middle_kind] + saved]
            + [patch_spec]
            + [whole(shape) for shape in block_shapes]
            + [whole((VEC_ROWS, FF))],
            out_specs=whole(grad_shape.shape),
            scratch_shapes=flat_scratch
            + [pltpu.VMEM(shape, f32) for shape in block_shapes]
            + [
                pltpu.VMEM((PDIM, D), f32),
                pltpu.VMEM((ROWS, D), f32),
                pltpu.VMEM((VEC_ROWS, FF), f32),
            ],
        ),
        out_shape=grad_shape,
        compiler_params=params(48),
        name="back",
    )(info, back, *kept, patches, *weights)

    late_here = moved(late_grad, place, core=1, sections=(0,))
    early_here = moved(early_grad, place, core=1, sections=(1,))

    def paired(turn):
        cut = slice(turn * place.z, (turn + 1) * place.z)
        early = early_grad[cut].astype(f32) + early_here[cut].astype(f32)
        late = late_grad[cut].astype(f32) + late_here[cut].astype(f32)
        return jnp.where(section == 0, early, late)

    summed = paired(0)
    arrived = [
        moved(paired(turn).astype(bf16), place, (0, a, b)) for turn, (a, b) in enumerate(turns) if turn
    ]
    for piece in arrived:
        summed = summed + piece.astype(f32)
    pieces = [moved(summed[d].astype(bf16), place, (d, 0, 0)) for d in range(1, place.z)]

    rows_basis = basis.reshape(KB, shard_len)
    blocks = max(n for n in range(1, 27) if shard_rows % n == 0)
    steps = shard_rows // blocks
    basis_spec = pl.BlockSpec((KB, blocks * LANES), lambda i, *_: (0, i))
    flat_kind = jax.ShapeDtypeStruct((shard_rows, LANES), f32)
    grad, sums = pl.pallas_call(
        functools.partial(inner_kernel, blocks),
        grid=(steps,),
        in_specs=[whole((place.sent_rows, LANES))] * place.z + [basis_spec, whole((1, LANES))],
        out_specs=[whole((shard_rows, LANES)), whole((1, SUMS))],
        out_shape=[flat_kind, jax.ShapeDtypeStruct((1, SUMS), f32)],
        scratch_shapes=[pltpu.VMEM((KB, LANES), f32)],
        compiler_params=params(24),
        name="inner",
    )(summed[0], *pieces, rows_basis, loss)
    sums = butterfly(sums, place)
    flat_spec = whole((shard_rows, LANES))
    padded_rows = -(-shard_rows // 8) * 8
    loss_parts, norm, coefficients, new_master, new_first, new_second = pl.pallas_call(
        functools.partial(update_kernel, blocks, float(2 * shard_len * chips)),
        grid_spec=pltpu.PrefetchScalarGridSpec(
            num_scalar_prefetch=1,
            grid=(steps,),
            in_specs=[whole((1, SUMS)), basis_spec, flat_spec, whole((1, LANES))] + [flat_spec] * 3,
            out_specs=[smem, smem, whole((TASKS, KMAX))] + [flat_spec] * 3,
            scratch_shapes=[pltpu.VMEM((KB, LANES), f32), pltpu.VMEM((padded_rows, LANES), f32)],
        ),
        out_shape=[
            jax.ShapeDtypeStruct((3,), f32),
            jax.ShapeDtypeStruct((1,), f32),
            jax.ShapeDtypeStruct((TASKS, KMAX), f32),
        ]
        + [flat_kind] * 3,
        compiler_params=params(24),
        name="update",
    )(
        basis_count,
        sums,
        rows_basis,
        grad,
        loss,
        master.reshape(shard_rows, LANES),
        first_moment.reshape(shard_rows, LANES),
        second_moment.reshape(shard_rows, LANES),
    )
    return (
        loss_parts,
        norm[0],
        coefficients,
        new_master.reshape(1, shard_len),
        new_first.reshape(1, shard_len),
        new_second.reshape(1, shard_len),
    )


def solution(mesh):
    in_specs = (
        P("dp", None, None),
        P("dp"),
        P("dp"),
        P("dp", None),
        P(),
        P("section", "dp"),
        P("section", "dp"),
        P("section", "dp"),
        P(None, "section", "dp"),
    )
    out_specs = (P(), P(), P(), P("section", "dp"), P("section", "dp"), P("section", "dp"))
    return jax.shard_map(body, mesh=mesh, in_specs=in_specs, out_specs=out_specs, check_vma=False)
```

time: 853 us -> 165 us (0.19); the launches traced: 842 us -> 164 us
  waiting for transfers between devices: 262 us -> 53.3 us
  local copies, waits for them, and re-layouts: 211 us -> 5.45 us
  matrix products: 134 us -> 0 us
  blocking collectives: 121 us -> 0 us
  Pallas kernels: 0 us -> 68.7 us
  other arithmetic: 68.7 us -> 5.74 us
  starting transfers between devices: 6.04 us -> 29.2 us
  loops' own time: 22.3 us -> 0 us
  between operations: 17.8 us -> 1.67 us
    dot_general x52 -> x0, matrix products: 134 us -> none  [the longest x1 28.4 us: body(): jnp.dot(basis_rows, clipped, precision=HIGHEST_PREC, preferred_element_ty...]
    unnamed x3 -> x0, waiting for transfers between devices: 128 us -> none
    psum x3 -> x0, blocking collectives: 121 us -> none  [the longest x2 80.8 us: body(): totals = lax.psum((squares, entropy_total, replay_total), ('section', 'dp'))]
    pallas_call x0 -> x5, Pallas kernels: none -> 68.7 us  [the longest x1 17.5 us: body(): pl.pallas_call(functools.partial(update_kernel, blocks, float(2 * shard_l...]
    all_gather x1 -> x0, waiting for transfers between devices: 57.3 us -> none  [body(): gathered = lax.all_gather(to_low(master[0]), 'dp', axis=0, tiled=True)]
    concatenate x2 -> x0, local copies, waits for them, and re-layouts: 49.8 us -> none  [pack(): flat_vec = jnp.concatenate([piece.reshape(-1) for piece in grads])]
    reshape x26 -> x0, local copies, waits for them, and re-layouts: 45.5 us -> none  [the longest x4 19.8 us: block_forward(): heads = qkv.reshape(images, seq_len, 3, HEADS, HD)]
    slice x26 -> x0, local copies, waits for them, and re-layouts: 32.4 us -> none  [the longest x13 10.4 us: unpack(): pieces.append(flat_vec[offset:offset + entries].reshape(dims))]
  transfers between devices with their start and end apart: 6 -> 23, of which waited for: 4 -> 17; matrix products, arithmetic and copies ran while one was open for 22% -> 1% of each run, Pallas kernels for 0% -> 0%
where the time goes in v1:
time: 165 us; the launch traced here: 164 us
  Pallas kernels  68.7 us (42%)
  waiting for transfers between devices  53.3 us (32%)
  starting transfers between devices  29.2 us (18%)
  other arithmetic  5.74 us (3%)
  local copies, waits for them, and re-layouts  5.45 us (3%)
  between operations  1.67 us (1%)
    ppermute x19, waiting for transfers between devices, moved(): return lax.ppermute(value, ('section', 'dp'), pairs)  41.1 us
    ppermute x19, starting transfers between devices, moved(): return lax.ppermute(value, ('section', 'dp'), pairs)  26.1 us
    pallas_call x1, Pallas kernels, body(): pl.pallas_call(functools.partial(update_kernel, blocks, float(2 * shard_l...  17.5 us
    pallas_call x1, Pallas kernels, body(): pl.pallas_call(functools.partial(inner_kernel, blocks), grid=(steps,), in...  15.9 us
    pallas_call x1, Pallas kernels, body(): pl.pallas_call(functools.partial(back_kernel, place), grid_spec=pltpu.Pre...  15.3 us
    ppermute x4, waiting for transfers between devices, butterfly(): value = value + lax.ppermute(value, ('section', 'dp'), pairs)  12.2 us
    pallas_call x1, Pallas kernels, body(): pl.pallas_call(functools.partial(front_kernel, place), grid_spec=pltpu.Pr...  12.1 us
    pallas_call x1, Pallas kernels, body(): pl.pallas_call(functools.partial(late_kernel, place, per, float(images *...  8.02 us
  transfers between devices with their start and end apart: 23, of which 17 were waited for; matrix products, arithmetic and copies ran while one was open for 1% of the time, Pallas kernels for 0%

profile of v1, /device:TPU:0, one launch (start us, length us, event | category | flops | bytes accessed | tf_op | source)
XLA Modules:
  0.0 164.0 jit_solution(14141899964392159811)
XLA Ops:
  0.6 1.3 reduce_sum.9
  2.6 0.9 convert_element_type.85
  3.5 4.1 %collective-permute-start.1 = (bf16[320,128]{1,0:T(8,128)(2,1)S(1)}, bf16[320,128]{1,0:T(8,128)(2,1)S(1)}, u32[]{:S(2)}, u32[]{:S(2)}) collective-permute-start(bf16[320,128]{1,0:T(8,128)(2,1)S(1)} %get-tuple-element.71), channel_id=1, source_target_pairs={{0,8},{1,9},{2,10},{3,11},{4,12},{5,13},{6,14},{7,15},{8,0},{9,1},... | collective-permute-start | bytes 245768 | tf_op jit(solution)/shard_map/ppermute | solution.py:675
  7.6 1.6 collective-permute-start
  9.2 2.2 %collective-permute-start.2 = (bf16[320,128]{1,0:T(8,128)(2,1)S(1)}, bf16[320,128]{1,0:T(8,128)(2,1)S(1)}, u32[]{:S(2)}, u32[]{:S(2)}) collective-permute-start(bf16[320,128]{1,0:T(8,128)(2,1)S(1)} %get-tuple-element.71), channel_id=1, source_target_pairs={{0,12},{1,13},{2,14},{3,15},{4,0},{5,1},{6,2},{7,3},{8,4},{9,5},{1... | collective-permute-start | bytes 245768 | tf_op jit(solution)/shard_map/ppermute | solution.py:675
  11.5 1.6 %collective-permute-done.1 = bf16[320,128]{1,0:T(8,128)(2,1)S(1)} collective-permute-done((bf16[320,128]{1,0:T(8,128)(2,1)S(1)}, bf16[320,128]{1,0:T(8,128)(2,1)S(1)}, u32[]{:S(2)}, u32[]{:S(2)}) %collective-permute-start.1) | collective-permute-done | bytes 81952 | tf_op jit(solution)/shard_map/ppermute | solution.py:675
  13.1 1.3 collective-permute-done
  14.4 0.7 collective-permute-done.2
  15.1 2.7 %collective-permute-start.5 = (bf16[4,320,128]{2,1,0:T(8,128)(2,1)S(1)}, bf16[4,320,128]{2,1,0:T(8,128)(2,1)S(1)}, u32[]{:S(2)}, u32[]{:S(2)}) collective-permute-start(bf16[4,320,128]{2,1,0:T(8,128)(2,1)S(1)} %pad_maximum_fusion.refs_0_), channel_id=1, source_target_pairs={{0,3},{1,2},{2,1},{3,0},{4,7},{5,6},{6,5},{7,4},{8,11},{9,10},{10,... | collective-permute-start | bytes 983048 | tf_op jit(solution)/shard_map/ppermute | solution.py:675
  17.8 0.5 collective-permute-start.4
  18.3 0.3 collective-permute-start.3
  18.6 0.0 collective-permute-start.6
  18.6 8.1 %collective-permute-done.5.refs_3_ = bf16[4,320,128]{2,1,0:T(8,128)(2,1)S(1)} collective-permute-done((bf16[4,320,128]{2,1,0:T(8,128)(2,1)S(1)}, bf16[4,320,128]{2,1,0:T(8,128)(2,1)S(1)}, u32[]{:S(2)}, u32[]{:S(2)}) %collective-permute-start.5) | collective-permute-done | bytes 327712 | tf_op jit(solution)/shard_map/ppermute | solution.py:675
  26.7 0.0 collective-permute-start.9
  26.7 5.5 %collective-permute-done.4.refs_2_ = bf16[4,320,128]{2,1,0:T(8,128)(2,1)S(1)} collective-permute-done((bf16[4,320,128]{2,1,0:T(8,128)(2,1)S(1)}, bf16[4,320,128]{2,1,0:T(8,128)(2,1)S(1)}, u32[]{:S(2)}, u32[]{:S(2)}) %collective-permute-start.4) | collective-permute-done | bytes 327712 | tf_op jit(solution)/shard_map/ppermute | solution.py:675
  32.2 0.0 collective-permute-start.8
  32.2 0.2 collective-permute-done.3.refs_1_
  32.4 0.3 collective-permute-start.7
  32.7 2.1 %copy.15.refs_8_.refs_10_ = bf16[8,196,768]{2,1,0:T(8,128)(2,1)S(1)} copy(bf16[8,196,768]{2,0,1:T(8,128)(2,1)} %param.9) | data formatting | bytes 4816896 | tf_op args[0]
  34.8 0.1 pad_add_fusion.info
  34.9 0.0 collective-permute-done.6.refs_4_
  34.9 0.0 collective-permute-done.9.refs_7_
  35.0 0.0 collective-permute-done.8.refs_6_
  35.0 0.0 copy-start.2
  35.0 0.0 collective-permute-done.7.refs_5_
  35.0 12.1 %front.1 = (f32[832,192]{1,0:T(8,128)S(1)}, bf16[832,192]{1,0:T(8,128)(2,1)S(1)}, bf16[832,192]{1,0:T(8,128)(2,1)S(1)}, bf16[832,192]{1,0:T(8,128)(2,1)S(1)}, f3...) custom-call(s32[2]{0:T(128)S(1)} %pad_add_fusion.info, ...), custom_call_target="tpu_custom_call" | custom-call | tf_op jit(solution)/shard_map/front/pallas_call | solution.py:747
  47.1 0.0 copy-start.6
  47.1 1.0 copy-done.6
  48.1 0.0 copy-start.3
  48.2 1.2 copy-done.3
  49.4 1.0 copy-done.5
  50.3 8.0 %late.1 = (bf16[832,192]{1,0:T(8,128)(2,1)S(1)}, bf16[16,320,128]{2,1,0:T(8,128)(2,1)S(1)}, f32[1,128]{1,0:T(1,128)S(1)}) custom-call(s32[2]{0:T(128)S(1)} %pad_add_fusion.info, s32[8]{0:T(128)S(1)} %copy-done.11, s32[8]{0:T(128)S(1)} %copy-done.12, bf16[4,320,128]{2,1,0:T(8,128)(2,1)S(1)} %pad_maximum_fusion.refs_0_, ...), custom_call_target="tpu_custom_call" | custom-call | tf_op jit(solution)/shard_map/late/pallas_call | solution.py:773
  58.4 15.3 %back.1 = bf16[16,320,128]{2,1,0:T(8,128)(2,1)} custom-call(s32[2]{0:T(128)S(1)} %pad_add_fusion.info, bf16[832,192]{1,0:T(8,128)(2,1)S(1)} %get-tuple-element.35.refs_0_, f32[832,192]{1,0:T(8,128)S(1)} %get-tuple-element.36.refs_1_, bf16[832,192]{1,0:T(8,128)(2,1)S(1)} %get-tuple-element.37.refs_2_, bf16[832,192]{1,0:T(8,128)(2,1)S(1)} %get-tuple-element.38.refs_3_, ...), custom_call_target="tpu_custom_call" | custom-call | tf_op jit(solution)/shard_map/back/pallas_call | solution.py:796
  73.6 1.3 collective-permute-start.10
  74.9 4.2 %collective-permute-start.11 = (bf16[16,320,128]{2,1,0:T(8,128)(2,1)S(1)}, bf16[16,320,128]{2,1,0:T(8,128)(2,1)}, u32[]{:S(2)}, u32[]{:S(2)}) collective-permute-start(bf16[16,320,128]{2,1,0:T(8,128)(2,1)S(1)} %get-tuple-element.52), channel_id=1, source_target_pairs={{0,16},{1,17},{2,18},{3,19},{4,20},{5,21},{6,22},{7,23},{8,24},{9,... | collective-permute-start | bytes 3932168 | tf_op jit(solution)/shard_map/ppermute | solution.py:675
  79.1 0.0 collective-permute-done.10
  79.1 1.7 %collective-permute-done.11 = bf16[16,320,128]{2,1,0:T(8,128)(2,1)} collective-permute-done((bf16[16,320,128]{2,1,0:T(8,128)(2,1)S(1)}, bf16[16,320,128]{2,1,0:T(8,128)(2,1)}, u32[]{:S(2)}, u32[]{:S(2)}) %collective-permute-start.11) | collective-permute-done | bytes 1310752 | tf_op jit(solution)/shard_map/ppermute | solution.py:675
  80.8 2.0 %select_convert_fusion.2 = (bf16[4,320,128]{2,1,0:T(8,128)(2,1)S(1)}, bf16[4,320,128]{2,1,0:T(8,128)(2,1)S(1)}, bf16[4,320,128]{2,1,0:T(8,128)(2,1)S(1)}) fusion(bf16[16,320,128]{2,1,0:T(8,128)(2,1)} %collective-permute-done.11, bf16[16,320,128]{2,1,0:T(8,128)(2,1)S(1)} %collective-permute-done.10, bf16[16,320,128]{2,1,0:T(8,128)(2,1)} %back.1, ...), kind=kLoop, calls=%fused_computation.3 | loop fusion | flops 3932160 | bytes 4915201 | tf_op jit(solution)/shard_map/convert_element_type | solution.py:830
  82.8 1.7 %collective-permute-start.12 = (bf16[4,320,128]{2,1,0:T(8,128)(2,1)S(1)}, bf16[4,320,128]{2,1,0:T(8,128)(2,1)S(1)}, u32[]{:S(2)}, u32[]{:S(2)}) collective-permute-start(bf16[4,320,128]{2,1,0:T(8,128)(2,1)S(1)} %get-tuple-element.64), channel_id=1, source_target_pairs={{0,1},{1,0},{2,3},{3,2},{4,5},{5,4},{6,7},{7,6},{8,9},{9,8},{10,11... | collective-permute-start | bytes 983048 | tf_op jit(solution)/shard_map/ppermute | solution.py:675
  84.5 1.5 collective-permute-start.14
  86.0 0.4 collective-permute-start.13
  86.4 7.0 %collective-permute-done.12 = bf16[4,320,128]{2,1,0:T(8,128)(2,1)S(1)} collective-permute-done((bf16[4,320,128]{2,1,0:T(8,128)(2,1)S(1)}, bf16[4,320,128]{2,1,0:T(8,128)(2,1)S(1)}, u32[]{:S(2)}, u32[]{:S(2)}) %collective-permute-start.12) | collective-permute-done | bytes 327712 | tf_op jit(solution)/shard_map/ppermute | solution.py:675
  93.4 7.7 %collective-permute-done.14 = bf16[4,320,128]{2,1,0:T(8,128)(2,1)S(1)} collective-permute-done((bf16[4,320,128]{2,1,0:T(8,128)(2,1)S(1)}, bf16[4,320,128]{2,1,0:T(8,128)(2,1)S(1)}, u32[]{:S(2)}, u32[]{:S(2)}) %collective-permute-start.14) | collective-permute-done | bytes 327712 | tf_op jit(solution)/shard_map/ppermute | solution.py:675
  101.1 1.4 collective-permute-done.13
  102.5 1.4 fusion
  103.9 1.8 %collective-permute-start.17 = (bf16[320,128]{1,0:T(8,128)(2,1)S(1)}, bf16[320,128]{1,0:T(8,128)(2,1)S(1)}, u32[]{:S(2)}, u32[]{:S(2)}) collective-permute-start(bf16[320,128]{1,0:T(8,128)(2,1)S(1)} %get-tuple-element.67), channel_id=1, source_target_pairs={{0,12},{1,13},{2,14},{3,15},{4,0},{5,1},{6,2},{7,3},{8,4},{9,5},{1... | collective-permute-start | bytes 245768 | tf_op jit(solution)/shard_map/ppermute | solution.py:675
  105.7 1.5 collective-permute-start.16
  107.2 1.9 %collective-permute-start.15 = (bf16[320,128]{1,0:T(8,128)(2,1)S(1)}, bf16[320,128]{1,0:T(8,128)(2,1)S(1)}, u32[]{:S(2)}, u32[]{:S(2)}) collective-permute-start(bf16[320,128]{1,0:T(8,128)(2,1)S(1)} %get-tuple-element.69), channel_id=1, source_target_pairs={{0,4},{1,5},{2,6},{3,7},{4,8},{5,9},{6,10},{7,11},{8,12},{9,13},{1... | collective-permute-start | bytes 245768 | tf_op jit(solution)/shard_map/ppermute | solution.py:675
  109.1 0.1 collective-permute-done.17.refs_2_
  109.2 4.7 %collective-permute-done.16.refs_1_ = bf16[320,128]{1,0:T(8,128)(2,1)S(1)} collective-permute-done((bf16[320,128]{1,0:T(8,128)(2,1)S(1)}, bf16[320,128]{1,0:T(8,128)(2,1)S(1)}, u32[]{:S(2)}, u32[]{:S(2)}) %collective-permute-start.16) | collective-permute-done | bytes 81952 | tf_op jit(solution)/shard_map/ppermute | solution.py:675
  114.0 0.0 collective-permute-done.15.refs_0_
  114.0 0.0 copy-start.13
  114.0 15.9 %inner.1 = (f32[312,128]{1,0:T(8,128)S(1)}, f32[1,512]{1,0:T(1,128)S(1)}) custom-call(f32[320,128]{1,0:T(8,128)S(1)} %slice_bitcast_fusion.first, bf16[320,128]{1,0:T(8,128)(2,1)S(1)} %collective-permute-done.15.refs_0_, bf16[320,128]{1,0:T(8,128)(2,1)S(1)} %collective-permute-done.16.refs_1_, bf16[320,128]{1,0:T(8,128)(2,1)S(1)} %collective-permute-done.17.refs_2_, ...), custom_call_target="tpu_custom_call" | custom-call | tf_op jit(solution)/shard_map/inner/pallas_call | solution.py:841
  129.9 0.1 collective-permute-start.18
  129.9 1.1 collective-permute-done.18
  131.1 0.8 collective-permute-start.19
  131.9 2.8 %collective-permute-done.19 = f32[1,512]{1,0:T(1,128)S(1)} collective-permute-done((f32[1,512]{1,0:T(1,128)S(1)}, f32[1,512]{1,0:T(1,128)S(1)}, u32[]{:S(2)}, u32[]{:S(2)}) %collective-permute-start.19) | collective-permute-done | bytes 2080 | tf_op jit(solution)/shard_map/ppermute | solution.py:689
  134.7 0.5 collective-permute-start.20
  135.2 3.1 %collective-permute-done.20 = f32[1,512]{1,0:T(1,128)S(1)} collective-permute-done((f32[1,512]{1,0:T(1,128)S(1)}, f32[1,512]{1,0:T(1,128)S(1)}, u32[]{:S(2)}, u32[]{:S(2)}) %collective-permute-start.20) | collective-permute-done | bytes 2080 | tf_op jit(solution)/shard_map/ppermute | solution.py:689
  138.3 0.0 collective-permute-start.21
  138.3 3.6 %collective-permute-done.21 = f32[1,512]{1,0:T(1,128)S(1)} collective-permute-done((f32[1,512]{1,0:T(1,128)S(1)}, f32[1,512]{1,0:T(1,128)S(1)}, u32[]{:S(2)}, u32[]{:S(2)}) %collective-permute-start.21) | collective-permute-done | bytes 2080 | tf_op jit(solution)/shard_map/ppermute | solution.py:689
  141.8 1.8 %collective-permute-start.22 = (f32[1,512]{1,0:T(1,128)S(1)}, f32[1,512]{1,0:T(1,128)S(1)}, u32[]{:S(2)}, u32[]{:S(2)}) collective-permute-start(f32[1,512]{1,0:T(1,128)S(1)} %add.64), channel_id=1, source_target_pairs={{0,8},{1,9},{2,10},{3,11},{4,12},{5,13},{6,14},{7,15},{8,0},{9,1},... | collective-permute-start | bytes 6152 | tf_op jit(solution)/shard_map/ppermute | solution.py:689
  143.6 2.7 %collective-permute-done.22 = f32[1,512]{1,0:T(1,128)S(1)} collective-permute-done((f32[1,512]{1,0:T(1,128)S(1)}, f32[1,512]{1,0:T(1,128)S(1)}, u32[]{:S(2)}, u32[]{:S(2)}) %collective-permute-start.22) | collective-permute-done | bytes 2080 | tf_op jit(solution)/shard_map/ppermute | solution.py:689
  146.4 17.5 %update.1 = (f32[3]{0:T(128)}, f32[1]{0:T(128)}, f32[2,200]{1,0:T(2,128)}, f32[312,128]{1,0:T(8,128)}, f32[312,128]{1,0:T(8,128)}, /*index=5*/f32[312,128]{1,0:T(8,128)}) custom-call(s32[2]{0:T(128)S(1)} %copy-done.13, f32[1,512]{1,0:T(1,128)S(1)} %add.65.sums, bf16[400,39936]{1,0:T(8,128)(2,1)} %bitcast.28, f32[312,128]{1,0:T(8,128)S(1)} %get-tuple-element.55.grad, ...), custom_call_target="tpu_custom_call" | custom-call | tf_op jit(solution)/shard_map/update/pallas_call | solution.py:854
  (30 shorter events, 0.1 us)
Async XLA Ops:
  3.5 9.6 %collective-permute-start.1 = (bf16[320,128]{1,0:T(8,128)(2,1)S(1)}, bf16[320,128]{1,0:T(8,128)(2,1)S(1)}, u32[]{:S(2)}, u32[]{:S(2)}) collective-permute-start(bf16[320,128]{1,0:T(8,128)(2,1)S(1)} %get-tuple-element.71), channel_id=1, source_target_pairs={{0,8},{1,9},{2,10},{3,11},{4,12},{5,13},{6,14},{7,15},{8,0},{9,1},... | collective-permute-start | bytes 245768 | tf_op jit(solution)/shard_map/ppermute | solution.py:675
  7.6 6.7 %collective-permute-start = (bf16[320,128]{1,0:T(8,128)(2,1)S(1)}, bf16[320,128]{1,0:T(8,128)(2,1)S(1)}, u32[]{:S(2)}, u32[]{:S(2)}) collective-permute-start(bf16[320,128]{1,0:T(8,128)(2,1)S(1)} %get-tuple-element.71), channel_id=1, source_target_pairs={{0,4},{1,5},{2,6},{3,7},{4,8},{5,9},{6,10},{7,11},{8,12},{9,13},{1... | collective-permute-start | bytes 245768 | tf_op jit(solution)/shard_map/ppermute | solution.py:675
  9.2 5.8 %collective-permute-start.2 = (bf16[320,128]{1,0:T(8,128)(2,1)S(1)}, bf16[320,128]{1,0:T(8,128)(2,1)S(1)}, u32[]{:S(2)}, u32[]{:S(2)}) collective-permute-start(bf16[320,128]{1,0:T(8,128)(2,1)S(1)} %get-tuple-element.71), channel_id=1, source_target_pairs={{0,12},{1,13},{2,14},{3,15},{4,0},{5,1},{6,2},{7,3},{8,4},{9,5},{1... | collective-permute-start | bytes 245768 | tf_op jit(solution)/shard_map/ppermute | solution.py:675
  15.1 11.6 %collective-permute-start.5 = (bf16[4,320,128]{2,1,0:T(8,128)(2,1)S(1)}, bf16[4,320,128]{2,1,0:T(8,128)(2,1)S(1)}, u32[]{:S(2)}, u32[]{:S(2)}) collective-permute-start(bf16[4,320,128]{2,1,0:T(8,128)(2,1)S(1)} %pad_maximum_fusion.refs_0_), channel_id=1, source_target_pairs={{0,3},{1,2},{2,1},{3,0},{4,7},{5,6},{6,5},{7,4},{8,11},{9,10},{10,... | collective-permute-start | bytes 983048 | tf_op jit(solution)/shard_map/ppermute | solution.py:675
  17.8 14.4 %collective-permute-start.4 = (bf16[4,320,128]{2,1,0:T(8,128)(2,1)S(1)}, bf16[4,320,128]{2,1,0:T(8,128)(2,1)S(1)}, u32[]{:S(2)}, u32[]{:S(2)}) collective-permute-start(bf16[4,320,128]{2,1,0:T(8,128)(2,1)S(1)} %pad_maximum_fusion.refs_0_), channel_id=1, source_target_pairs={{0,2},{1,3},{2,0},{3,1},{4,6},{5,7},{6,4},{7,5},{8,10},{9,11},{10,... | collective-permute-start | bytes 983048 | tf_op jit(solution)/shard_map/ppermute | solution.py:675
  18.3 14.2 %collective-permute-start.3 = (bf16[4,320,128]{2,1,0:T(8,128)(2,1)S(1)}, bf16[4,320,128]{2,1,0:T(8,128)(2,1)S(1)}, u32[]{:S(2)}, u32[]{:S(2)}) collective-permute-start(bf16[4,320,128]{2,1,0:T(8,128)(2,1)S(1)} %pad_maximum_fusion.refs_0_), channel_id=1, source_target_pairs={{0,1},{1,0},{2,3},{3,2},{4,5},{5,4},{6,7},{7,6},{8,9},{9,8},{10,11... | collective-permute-start | bytes 983048 | tf_op jit(solution)/shard_map/ppermute | solution.py:675
  18.6 16.3 %collective-permute-start.6 = (bf16[4,320,128]{2,1,0:T(8,128)(2,1)S(1)}, bf16[4,320,128]{2,1,0:T(8,128)(2,1)S(1)}, u32[]{:S(2)}, u32[]{:S(2)}) collective-permute-start(bf16[4,320,128]{2,1,0:T(8,128)(2,1)S(1)} %pad_maximum_fusion.refs_0_), channel_id=1, source_target_pairs={{0,16},{1,17},{2,18},{3,19},{4,20},{5,21},{6,22},{7,23},{8,24},{9,... | collective-permute-start | bytes 983048 | tf_op jit(solution)/shard_map/ppermute | solution.py:675
  26.7 8.2 %collective-permute-start.9 = (bf16[4,320,128]{2,1,0:T(8,128)(2,1)S(1)}, bf16[4,320,128]{2,1,0:T(8,128)(2,1)S(1)}, u32[]{:S(2)}, u32[]{:S(2)}) collective-permute-start(bf16[4,320,128]{2,1,0:T(8,128)(2,1)S(1)} %collective-permute-done.5.refs_3_), channel_id=1, source_target_pairs={{0,16},{1,17},{2,18},{3,19},{4,20},{5,21},{6,22},{7,23},{8,24},{9,... | collective-permute-start | bytes 983048 | tf_op jit(solution)/shard_map/ppermute | solution.py:675
  32.2 2.8 %collective-permute-start.8 = (bf16[4,320,128]{2,1,0:T(8,128)(2,1)S(1)}, bf16[4,320,128]{2,1,0:T(8,128)(2,1)S(1)}, u32[]{:S(2)}, u32[]{:S(2)}) collective-permute-start(bf16[4,320,128]{2,1,0:T(8,128)(2,1)S(1)} %collective-permute-done.4.refs_2_), channel_id=1, source_target_pairs={{0,16},{1,17},{2,18},{3,19},{4,20},{5,21},{6,22},{7,23},{8,24},{9,... | collective-permute-start | bytes 983048 | tf_op jit(solution)/shard_map/ppermute | solution.py:675
  32.4 2.5 %collective-permute-start.7 = (bf16[4,320,128]{2,1,0:T(8,128)(2,1)S(1)}, bf16[4,320,128]{2,1,0:T(8,128)(2,1)S(1)}, u32[]{:S(2)}, u32[]{:S(2)}) collective-permute-start(bf16[4,320,128]{2,1,0:T(8,128)(2,1)S(1)} %collective-permute-done.3.refs_1_), channel_id=1, source_target_pairs={{0,16},{1,17},{2,18},{3,19},{4,20},{5,21},{6,22},{7,23},{8,24},{9,... | collective-permute-start | bytes 983048 | tf_op jit(solution)/shard_map/ppermute | solution.py:675
  34.8 12.2 %copy-start = (bf16[8,196,768]{2,1,0:T(8,128)(2,1)}, bf16[8,196,768]{2,1,0:T(8,128)(2,1)S(1)}, u32[]{:S(2)}) copy-start(bf16[8,196,768]{2,1,0:T(8,128)(2,1)S(1)} %copy.15.refs_8_.refs_10_) | copy-start | bytes 7225348
  34.9 13.2 %copy-start.10 = (f32[8,1000]{1,0:T(8,128)S(1)}, f32[8,1000]{1,0:T(8,128)}, u32[]{:S(2)}) copy-start(f32[8,1000]{1,0:T(8,128)} %refs_9_.1) | copy-start | bytes 96004
  34.9 13.2 %copy-start.11 = (s32[8]{0:T(128)S(1)}, s32[8]{0:T(128)}, u32[]{:S(2)}) copy-start(s32[8]{0:T(128)} %labels.1) | copy-start | bytes 100
  34.9 13.2 %copy-start.12 = (s32[8]{0:T(128)S(1)}, s32[8]{0:T(128)}, u32[]{:S(2)}) copy-start(s32[8]{0:T(128)} %replay.1) | copy-start | bytes 100
  35.0 12.1 %copy-start.2 = (bf16[4,320,128]{2,1,0:T(8,128)(2,1)}, bf16[4,320,128]{2,1,0:T(8,128)(2,1)S(1)}, u32[]{:S(2)}) copy-start(bf16[4,320,128]{2,1,0:T(8,128)(2,1)S(1)} %collective-permute-done.8.refs_6_) | copy-start | bytes 983044
  35.0 12.1 %copy-start.4 = (bf16[4,320,128]{2,1,0:T(8,128)(2,1)}, bf16[4,320,128]{2,1,0:T(8,128)(2,1)S(1)}, u32[]{:S(2)}) copy-start(bf16[4,320,128]{2,1,0:T(8,128)(2,1)S(1)} %collective-permute-done.7.refs_5_) | copy-start | bytes 983044
  47.1 1.1 copy-start.6
  48.1 10.2 %copy-start.1 = (f32[2496,208]{1,0:T(8,128)}, f32[2496,208]{1,0:T(8,128)S(1)}, u32[]{:S(2)}) copy-start(f32[2496,208]{1,0:T(8,128)S(1)} %get-tuple-element.40.refs_5_) | copy-start | bytes 6230020
  48.1 1.2 copy-start.3
  49.4 1.0 copy-start.5
  73.6 5.5 %collective-permute-start.10 = (bf16[16,320,128]{2,1,0:T(8,128)(2,1)}, bf16[16,320,128]{2,1,0:T(8,128)(2,1)S(1)}, u32[]{:S(2)}, u32[]{:S(2)}) collective-permute-start(bf16[16,320,128]{2,1,0:T(8,128)(2,1)} %back.1), channel_id=1, source_target_pairs={{16,0},{17,1},{18,2},{19,3},{20,4},{21,5},{22,6},{23,7},{24,8},{25... | collective-permute-start | bytes 3932168 | tf_op jit(solution)/shard_map/ppermute | solution.py:675
  74.9 5.9 %collective-permute-start.11 = (bf16[16,320,128]{2,1,0:T(8,128)(2,1)S(1)}, bf16[16,320,128]{2,1,0:T(8,128)(2,1)}, u32[]{:S(2)}, u32[]{:S(2)}) collective-permute-start(bf16[16,320,128]{2,1,0:T(8,128)(2,1)S(1)} %get-tuple-element.52), channel_id=1, source_target_pairs={{0,16},{1,17},{2,18},{3,19},{4,20},{5,21},{6,22},{7,23},{8,24},{9,... | collective-permute-start | bytes 3932168 | tf_op jit(solution)/shard_map/ppermute | solution.py:675
  82.8 10.6 %collective-permute-start.12 = (bf16[4,320,128]{2,1,0:T(8,128)(2,1)S(1)}, bf16[4,320,128]{2,1,0:T(8,128)(2,1)S(1)}, u32[]{:S(2)}, u32[]{:S(2)}) collective-permute-start(bf16[4,320,128]{2,1,0:T(8,128)(2,1)S(1)} %get-tuple-element.64), channel_id=1, source_target_pairs={{0,1},{1,0},{2,3},{3,2},{4,5},{5,4},{6,7},{7,6},{8,9},{9,8},{10,11... | collective-permute-start | bytes 983048 | tf_op jit(solution)/shard_map/ppermute | solution.py:675
  84.5 16.6 %collective-permute-start.14 = (bf16[4,320,128]{2,1,0:T(8,128)(2,1)S(1)}, bf16[4,320,128]{2,1,0:T(8,128)(2,1)S(1)}, u32[]{:S(2)}, u32[]{:S(2)}) collective-permute-start(bf16[4,320,128]{2,1,0:T(8,128)(2,1)S(1)} %get-tuple-element.65), channel_id=1, source_target_pairs={{0,3},{1,2},{2,1},{3,0},{4,7},{5,6},{6,5},{7,4},{8,11},{9,10},{10,... | collective-permute-start | bytes 983048 | tf_op jit(solution)/shard_map/ppermute | solution.py:675
  86.0 16.4 %collective-permute-start.13 = (bf16[4,320,128]{2,1,0:T(8,128)(2,1)S(1)}, bf16[4,320,128]{2,1,0:T(8,128)(2,1)S(1)}, u32[]{:S(2)}, u32[]{:S(2)}) collective-permute-start(bf16[4,320,128]{2,1,0:T(8,128)(2,1)S(1)} %get-tuple-element.66), channel_id=1, source_target_pairs={{0,2},{1,3},{2,0},{3,1},{4,6},{5,7},{6,4},{7,5},{8,10},{9,11},{10,... | collective-permute-start | bytes 983048 | tf_op jit(solution)/shard_map/ppermute | solution.py:675
  103.9 5.4 %collective-permute-start.17 = (bf16[320,128]{1,0:T(8,128)(2,1)S(1)}, bf16[320,128]{1,0:T(8,128)(2,1)S(1)}, u32[]{:S(2)}, u32[]{:S(2)}) collective-permute-start(bf16[320,128]{1,0:T(8,128)(2,1)S(1)} %get-tuple-element.67), channel_id=1, source_target_pairs={{0,12},{1,13},{2,14},{3,15},{4,0},{5,1},{6,2},{7,3},{8,4},{9,5},{1... | collective-permute-start | bytes 245768 | tf_op jit(solution)/shard_map/ppermute | solution.py:675
  105.7 8.3 %collective-permute-start.16 = (bf16[320,128]{1,0:T(8,128)(2,1)S(1)}, bf16[320,128]{1,0:T(8,128)(2,1)S(1)}, u32[]{:S(2)}, u32[]{:S(2)}) collective-permute-start(bf16[320,128]{1,0:T(8,128)(2,1)S(1)} %get-tuple-element.68), channel_id=1, source_target_pairs={{0,8},{1,9},{2,10},{3,11},{4,12},{5,13},{6,14},{7,15},{8,0},{9,1},... | collective-permute-start | bytes 245768 | tf_op jit(solution)/shard_map/ppermute | solution.py:675
  107.2 6.8 %collective-permute-start.15 = (bf16[320,128]{1,0:T(8,128)(2,1)S(1)}, bf16[320,128]{1,0:T(8,128)(2,1)S(1)}, u32[]{:S(2)}, u32[]{:S(2)}) collective-permute-start(bf16[320,128]{1,0:T(8,128)(2,1)S(1)} %get-tuple-element.69), channel_id=1, source_target_pairs={{0,4},{1,5},{2,6},{3,7},{4,8},{5,9},{6,10},{7,11},{8,12},{9,13},{1... | collective-permute-start | bytes 245768 | tf_op jit(solution)/shard_map/ppermute | solution.py:675
  114.0 32.4 %copy-start.7 = (f32[1,39936]{1,0:T(1,128)S(1)}, f32[1,39936]{1,0:T(1,128)}, u32[]{:S(2)}) copy-start(f32[1,39936]{1,0:T(1,128)} %param.14) | copy-start | bytes 479236
  114.0 32.4 %copy-start.8 = (f32[1,39936]{1,0:T(1,128)S(1)}, f32[1,39936]{1,0:T(1,128)}, u32[]{:S(2)}) copy-start(f32[1,39936]{1,0:T(1,128)} %param.15) | copy-start | bytes 479236
  114.0 32.4 %copy-start.9 = (f32[1,39936]{1,0:T(1,128)S(1)}, f32[1,39936]{1,0:T(1,128)}, u32[]{:S(2)}) copy-start(f32[1,39936]{1,0:T(1,128)} %param.16) | copy-start | bytes 479236
  114.0 32.4 %copy-start.13 = (s32[2]{0:T(128)S(1)}, s32[2]{0:T(128)}, u32[]{:S(2)}) copy-start(s32[2]{0:T(128)} %counts.1) | copy-start | bytes 28
  129.9 1.2 collective-permute-start.18
  131.1 3.6 %collective-permute-start.19 = (f32[1,512]{1,0:T(1,128)S(1)}, f32[1,512]{1,0:T(1,128)S(1)}, u32[]{:S(2)}, u32[]{:S(2)}) collective-permute-start(f32[1,512]{1,0:T(1,128)S(1)} %add.61), channel_id=1, source_target_pairs={{0,1},{1,0},{2,3},{3,2},{4,5},{5,4},{6,7},{7,6},{8,9},{9,8},{10,11... | collective-permute-start | bytes 6152 | tf_op jit(solution)/shard_map/ppermute | solution.py:689
  134.7 3.6 %collective-permute-start.20 = (f32[1,512]{1,0:T(1,128)S(1)}, f32[1,512]{1,0:T(1,128)S(1)}, u32[]{:S(2)}, u32[]{:S(2)}) collective-permute-start(f32[1,512]{1,0:T(1,128)S(1)} %add.62), channel_id=1, source_target_pairs={{0,2},{1,3},{2,0},{3,1},{4,6},{5,7},{6,4},{7,5},{8,10},{9,11},{10,... | collective-permute-start | bytes 6152 | tf_op jit(solution)/shard_map/ppermute | solution.py:689
  138.3 3.6 %collective-permute-start.21 = (f32[1,512]{1,0:T(1,128)S(1)}, f32[1,512]{1,0:T(1,128)S(1)}, u32[]{:S(2)}, u32[]{:S(2)}) collective-permute-start(f32[1,512]{1,0:T(1,128)S(1)} %add.63), channel_id=1, source_target_pairs={{0,4},{1,5},{2,6},{3,7},{4,0},{5,1},{6,2},{7,3},{8,12},{9,13},{10,... | collective-permute-start | bytes 6152 | tf_op jit(solution)/shard_map/ppermute | solution.py:689
  141.8 4.5 %collective-permute-start.22 = (f32[1,512]{1,0:T(1,128)S(1)}, f32[1,512]{1,0:T(1,128)S(1)}, u32[]{:S(2)}, u32[]{:S(2)}) collective-permute-start(f32[1,512]{1,0:T(1,128)S(1)} %add.64), channel_id=1, source_target_pairs={{0,8},{1,9},{2,10},{3,11},{4,12},{5,13},{6,14},{7,15},{8,0},{9,1},... | collective-permute-start | bytes 6152 | tf_op jit(solution)/shard_map/ppermute | solution.py:689

commit v2 on v1

--- a/solution.py
+++ b/solution.py
@@ -22,6 +22,7 @@
 TASKS = 2
 KMAX = 200
 KB = TASKS * KMAX
+UPPER = 208
 STEP = 10
 LANES = 128
 HALF = 64
@@ -572,87 +573,108 @@
         send_out(place, info, flat, grad_out)
 
 
-def inner_kernel(blocks, first, *refs):
-    pieces, basis, loss, grad_out, sums_out, total = refs[:-5], *refs[-5:]
-    step = pl.program_id(0)
+def fetch_kernel(first, last, _, basis, kept, sem):
+    copy = pltpu.make_async_copy(basis.at[pl.ds(first, last - first)], kept, sem)
+    copy.start()
+    copy.wait()
+
+
+def add_kernel(left, right, _, __, total):
+    total[...] = left[...] + right[...]
+
+
+def plane_kernel(depth, info, early, early_here, late, late_here, _, *refs):
+    arrived, (whole_out, *outs) = refs[:-depth], refs[-depth:]
+    for d in range(depth):
+        first = early[d].astype(f32) + early_here[d].astype(f32)
+        second = late[d].astype(f32) + late_here[d].astype(f32)
+        total = jnp.where(info[0] == 0, first, second)
+        for ref in arrived:
+            total = total + ref[d].astype(f32)
+        if d == 0:
+            whole_out[...] = total
+        else:
+            outs[d - 1][...] = total.astype(bf16)
+
+
+def inner_kernel(blocks, *refs):
+    first, pieces, (upper, lower, loss, grad_out, sums_out, total) = refs[0], refs[1:-6], refs[-6:]
     shard_rows = grad_out.shape[0]
-
-    @pl.when(step == 0)
-    def _():
-        value = first[...]
-        for ref in pieces:
-            value = value + ref[...].astype(f32)
-        grad_out[...] = value[:shard_rows]
-        total[...] = jnp.zeros(total.shape, f32)
-
-    base = step * blocks
-    for at in range(0, KB, 16):
-        acc = jnp.zeros((16, LANES), f32)
+    value = first[...]
+    for ref in pieces:
+        value = value + ref[...].astype(f32)
+    grad_out[...] = value[:shard_rows]
+    total[...] = jnp.zeros(total.shape, f32)
+
+    def step(i, carry):
+        base = i * blocks
+        rows = [jnp.broadcast_to(grad_out[pl.ds(base + j, 1), :], (8, LANES)) for j in range(blocks)]
+        start = pl.multiple_of(base * LANES, LANES)
+        for at in range(0, KB, 16):
+            basis, row = (upper, at) if at < UPPER else (lower, at - UPPER)
+            part = basis[row : row + 16, pl.ds(start, blocks * LANES)].astype(f32)
+            for half in range(0, 16, 8):
+                acc = total[at + half : at + half + 8, :]
+                for j in range(blocks):
+                    acc = acc + part[half : half + 8, j * LANES : (j + 1) * LANES] * rows[j]
+                total[at + half : at + half + 8, :] = acc
+        return carry
+
+    lax.fori_loop(0, shard_rows // blocks, step, 0)
+    coefs = jnp.sum(total[...].T, 0, keepdims=True)
+    grad = grad_out[...]
+    squares = jnp.sum(jnp.sum(grad * grad, 0, keepdims=True), 1, keepdims=True)
+    lane = lax.broadcasted_iota(jnp.int32, (1, SUMS - KB), 1)
+    rest = jnp.where(lane == 0, squares, 0.0)
+    rest = rest + jnp.where(lane == 1, loss[0:1, 0:1], 0.0) + jnp.where(lane == 2, loss[0:1, 1:2], 0.0)
+    sums_out[:, 0:KB] = coefs
+    sums_out[:, KB:SUMS] = rest
+
+
+def update_kernel(blocks, whole_len, counts, sums, upper, lower, grad, loss, master, first, second, *refs):
+    loss_out, norm_out, coef_out, master_out, first_out, second_out, removed = refs
+    norm = jnp.sqrt(sums[0:1, KB : KB + 1])
+    factor = jnp.minimum(1.0, CLIP_NORM / (norm + 1e-06))
+    lane = lax.broadcasted_iota(jnp.int32, (1, KB), 1)
+    limit = jnp.where(lane < KMAX, counts[0], counts[1] + KMAX)
+    row = jnp.where(lane < limit, sums[:, 0:KB] * factor, 0.0)
+    coef_out[0:1, :] = row[:, 0:KMAX]
+    coef_out[1:2, :] = row[:, KMAX:KB]
+    norm_out[0] = jnp.sum(norm)
+    loss_out[0] = jnp.sum(sums[0:1, KB + 1 : KB + 2])
+    loss_out[1] = jnp.sum(sums[0:1, KB + 2 : KB + 3])
+    loss_out[2] = jnp.sum(loss[0:1, 2:3])
+    high = row.astype(bf16).astype(f32)
+    mid = (row - high).astype(bf16).astype(f32)
+    low = row - high - mid
+    place = lax.broadcasted_iota(jnp.int32, (16, KB), 0)
+    split = jnp.where(place == 0, high, jnp.where(place == 1, mid, jnp.where(place == 2, low, 0.0)))
+    split = split.astype(bf16)
+    rows = grad.shape[0]
+
+    def step(i, carry):
+        base = i * blocks
+        start = pl.multiple_of(base * LANES, LANES)
+        part = dot(split[:, :UPPER], upper[:, pl.ds(start, blocks * LANES)])
+        part = part + dot(split[:, UPPER:], lower[:, pl.ds(start, blocks * LANES)])
+        part = jnp.sum(part, 0, keepdims=True)
         for j in range(blocks):
-            part = basis[at : at + 16, j * LANES : (j + 1) * LANES].astype(f32)
-            acc = acc + part * grad_out[pl.ds(base + j, 1), :]
-        total[at : at + 16, :] += acc
-
-    @pl.when(step == pl.num_programs(0) - 1)
-    def _():
-        coefs = jnp.sum(total[...].T, 0, keepdims=True)
-        grad = grad_out[...]
-        squares = jnp.sum(jnp.sum(grad * grad, 0, keepdims=True), 1, keepdims=True)
-        lane = lax.broadcasted_iota(jnp.int32, (1, SUMS - KB), 1)
-        rest = jnp.where(lane == 0, squares, 0.0)
-        rest = rest + jnp.where(lane == 1, loss[0:1, 0:1], 0.0) + jnp.where(lane == 2, loss[0:1, 1:2], 0.0)
-        sums_out[:, 0:KB] = coefs
-        sums_out[:, KB:SUMS] = rest
-
-
-def update_kernel(blocks, whole_len, counts, sums, basis, grad, loss, master, first, second, *refs):
-    loss_out, norm_out, coef_out, master_out, first_out, second_out, coef, removed = refs
-    step = pl.program_id(0)
-
-    def clip_factor():
-        norm = jnp.sqrt(sums[0:1, KB : KB + 1])
-        return norm, jnp.minimum(1.0, CLIP_NORM / (norm + 1e-06))
-
-    @pl.when(step == 0)
-    def _():
-        norm, factor = clip_factor()
-        lane = lax.broadcasted_iota(jnp.int32, (1, KB), 1)
-        limit = jnp.where(lane < KMAX, counts[0], counts[1] + KMAX)
-        row = jnp.where(lane < limit, sums[:, 0:KB] * factor, 0.0)
-        coef_out[0:1, :] = row[:, 0:KMAX]
-        coef_out[1:2, :] = row[:, KMAX:KB]
-        coef[...] = jnp.broadcast_to(row, (LANES, KB)).T
-        norm_out[0] = jnp.sum(norm)
-        loss_out[0] = jnp.sum(sums[0:1, KB + 1 : KB + 2])
-        loss_out[1] = jnp.sum(sums[0:1, KB + 2 : KB + 3])
-        loss_out[2] = jnp.sum(loss[0:1, 2:3])
-
-    acc = [jnp.zeros((8, LANES), f32) for _ in range(blocks)]
-    for at in range(0, KB, 16):
-        weight = coef[at : at + 16, :]
-        for j in range(blocks):
-            part = basis[at : at + 16, j * LANES : (j + 1) * LANES].astype(f32) * weight
-            acc[j] = acc[j] + (part[0:8] + part[8:16])
-    base = step * blocks
-    for j in range(blocks):
-        removed[pl.ds(base + j, 1), :] = jnp.sum(acc[j], 0, keepdims=True)
-
-    @pl.when(step == pl.num_programs(0) - 1)
-    def _():
-        _, factor = clip_factor()
-        rows = grad.shape[0]
-        projected = grad[...] * factor - removed[0:rows, :] * (1.0 / whole_len)
-        new_first = BETA_ONE * first[...] + (1.0 - BETA_ONE) * projected
-        new_second = BETA_TWO * second[...] + (1.0 - BETA_TWO) * projected * projected
-        ratio = (
-            new_first
-            / (1.0 - BETA_ONE**STEP)
-            / (jnp.sqrt(new_second / (1.0 - BETA_TWO**STEP)) + ADAM_EPS)
-        )
-        old = master[...]
-        master_out[...] = old - LEARN_RATE * (ratio + WEIGHT_DECAY * old)
-        first_out[...] = new_first
-        second_out[...] = new_second
+            removed[pl.ds(base + j, 1), :] = part[:, j * LANES : (j + 1) * LANES]
+        return carry
+
+    lax.fori_loop(0, rows // blocks, step, 0)
+    projected = grad[...] * factor - removed[0:rows, :] * (1.0 / whole_len)
+    new_first = BETA_ONE * first[...] + (1.0 - BETA_ONE) * projected
+    new_second = BETA_TWO * second[...] + (1.0 - BETA_TWO) * projected * projected
+    ratio = (
+        new_first
+        / (1.0 - BETA_ONE**STEP)
+        / (jnp.sqrt(new_second / (1.0 - BETA_TWO**STEP)) + ADAM_EPS)
+    )
+    old = master[...]
+    master_out[...] = old - LEARN_RATE * (ratio + WEIGHT_DECAY * old)
+    first_out[...] = new_first
+    second_out[...] = new_second
 
 
 def dp_dims(count):
@@ -675,8 +697,20 @@
     return lax.ppermute(value, ("section", "dp"), pairs)
 
 
-def butterfly(value, place):
-    value = value + moved(value, place, core=1)
+def add(left, right, resident):
+    vmem = pl.BlockSpec(memory_space=pltpu.VMEM)
+    return pl.pallas_call(
+        add_kernel,
+        in_specs=[vmem, vmem] + [pl.BlockSpec(memory_space=pl.ANY)] * 2,
+        out_specs=vmem,
+        out_shape=jax.ShapeDtypeStruct(left.shape, left.dtype),
+        compiler_params=pltpu.CompilerParams(vmem_limit_bytes=2 * 1024 * 1024),
+        name="add",
+    )(left, right, *resident)
+
+
+def butterfly(value, place, resident):
+    value = add(value, moved(value, place, core=1), resident)
     for axis, size in ((2, place.x), (1, place.y), (0, place.z)):
         span = 1
         while span < size:
@@ -686,7 +720,7 @@
                 at = [rest // (place.y * place.x), rest // place.x % place.y, rest % place.x]
                 at[axis] ^= span
                 pairs.append((index, section * place.count + (at[0] * place.y + at[1]) * place.x + at[2]))
-            value = value + lax.ppermute(value, ("section", "dp"), pairs)
+            value = add(value, lax.ppermute(value, ("section", "dp"), pairs), resident)
             span *= 2
     return value
 
@@ -825,53 +859,70 @@
         late = late_grad[cut].astype(f32) + late_here[cut].astype(f32)
         return jnp.where(section == 0, early, late)
 
-    summed = paired(0)
-    arrived = [
-        moved(paired(turn).astype(bf16), place, (0, a, b)) for turn, (a, b) in enumerate(turns) if turn
-    ]
-    for piece in arrived:
-        summed = summed + piece.astype(f32)
-    pieces = [moved(summed[d].astype(bf16), place, (d, 0, 0)) for d in range(1, place.z)]
-
-    rows_basis = basis.reshape(KB, shard_len)
-    blocks = max(n for n in range(1, 27) if shard_rows % n == 0)
-    steps = shard_rows // blocks
-    basis_spec = pl.BlockSpec((KB, blocks * LANES), lambda i, *_: (0, i))
+    leaving = [paired(turn).astype(bf16) for turn in range(1, len(turns))]
+    rows_basis = pltpu.with_memory_space_constraint(basis.reshape(KB, shard_len), pltpu.HBM)
+    hbm = pl.BlockSpec(memory_space=pl.ANY)
+
+    def fetch(first, last, after):
+        return pl.pallas_call(
+            functools.partial(fetch_kernel, first, last),
+            in_specs=[hbm, pl.BlockSpec(memory_space=pltpu.HBM)],
+            out_specs=hbm,
+            out_shape=pltpu.VMEM((last - first, shard_len), bf16),
+            scratch_shapes=[pltpu.SemaphoreType.DMA],
+            compiler_params=pltpu.CompilerParams(vmem_limit_bytes=2 * 1024 * 1024),
+            cost_estimate=pl.CostEstimate(
+                flops=0, bytes_accessed=4 * (last - first) * shard_len, transcendentals=0
+            ),
+            name="fetch",
+        )(after, rows_basis)
+
+    upper = fetch(0, UPPER, leaving[0])
+    arrived = [moved(leaving[turn - 1], place, (0, *turns[turn])) for turn in range(1, len(turns))]
+    piece_shape = (place.sent_rows, LANES)
+    first, *rest = pl.pallas_call(
+        functools.partial(plane_kernel, place.z),
+        in_specs=[smem] + [vmem] * 4 + [hbm] + [vmem] * (len(turns) - 1),
+        out_specs=[vmem] * place.z,
+        out_shape=[jax.ShapeDtypeStruct(piece_shape, bf16 if d else f32) for d in range(place.z)],
+        compiler_params=pltpu.CompilerParams(vmem_limit_bytes=2 * 1024 * 1024),
+        name="plane",
+    )(info, early_grad, early_here, late_grad, late_here, upper, *arrived)
+    resident = (upper, fetch(UPPER, KB, rest[0]))
+    pieces = [moved(rest[d - 1], place, (d, 0, 0)) for d in range(1, place.z)]
+
+    def divisor(most):
+        return max(n for n in range(1, most + 1) if shard_rows % n == 0)
+
     flat_kind = jax.ShapeDtypeStruct((shard_rows, LANES), f32)
     grad, sums = pl.pallas_call(
-        functools.partial(inner_kernel, blocks),
-        grid=(steps,),
-        in_specs=[whole((place.sent_rows, LANES))] * place.z + [basis_spec, whole((1, LANES))],
-        out_specs=[whole((shard_rows, LANES)), whole((1, SUMS))],
+        functools.partial(inner_kernel, divisor(26)),
+        in_specs=[vmem] * (place.z + 3),
+        out_specs=[vmem] * 2,
         out_shape=[flat_kind, jax.ShapeDtypeStruct((1, SUMS), f32)],
         scratch_shapes=[pltpu.VMEM((KB, LANES), f32)],
-        compiler_params=params(24),
+        compiler_params=pltpu.CompilerParams(vmem_limit_bytes=2 * 1024 * 1024),
         name="inner",
-    )(summed[0], *pieces, rows_basis, loss)
-    sums = butterfly(sums, place)
-    flat_spec = whole((shard_rows, LANES))
+    )(first, *pieces, *resident, loss)
+    sums = butterfly(sums, place, resident)
     padded_rows = -(-shard_rows // 8) * 8
     loss_parts, norm, coefficients, new_master, new_first, new_second = pl.pallas_call(
-        functools.partial(update_kernel, blocks, float(2 * shard_len * chips)),
-        grid_spec=pltpu.PrefetchScalarGridSpec(
-            num_scalar_prefetch=1,
-            grid=(steps,),
-            in_specs=[whole((1, SUMS)), basis_spec, flat_spec, whole((1, LANES))] + [flat_spec] * 3,
-            out_specs=[smem, smem, whole((TASKS, KMAX))] + [flat_spec] * 3,
-            scratch_shapes=[pltpu.VMEM((KB, LANES), f32), pltpu.VMEM((padded_rows, LANES), f32)],
-        ),
+        functools.partial(update_kernel, divisor(78), float(2 * shard_len * chips)),
+        in_specs=[smem] + [vmem] * 8,
+        out_specs=[smem, smem] + [vmem] * 4,
         out_shape=[
             jax.ShapeDtypeStruct((3,), f32),
             jax.ShapeDtypeStruct((1,), f32),
             jax.ShapeDtypeStruct((TASKS, KMAX), f32),
         ]
         + [flat_kind] * 3,
-        compiler_params=params(24),
+        scratch_shapes=[pltpu.VMEM((padded_rows, LANES), f32)],
+        compiler_params=pltpu.CompilerParams(vmem_limit_bytes=2 * 1024 * 1024),
         name="update",
     )(
         basis_count,
         sums,
-        rows_basis,
+        *resident,
         grad,
         loss,
         master.reshape(shard_rows, LANES),

time: 165 us -> 144 us (0.87)
  waiting for transfers between devices: 53.3 us -> 39.2 us
  Pallas kernels: 68.7 us -> 61.3 us
  starting transfers between devices: 29.2 us -> 31.2 us
    ppermute x19, waiting for transfers between devices: 41.1 us -> 29 us  [moved(): return lax.ppermute(value, ('section', 'dp'), pairs)]
    pallas_call x2 -> x10, Pallas kernels: 33.3 us -> 26 us  [the longest x2 11.2 us: fetch(): pl.pallas_call(functools.partial(fetch_kernel, first, last), in_specs=[hb...]
    ppermute x4, starting transfers between devices: 3.05 us -> 5.05 us  [butterfly(): value = add(value, lax.ppermute(value, ('section', 'dp'), pairs), resident)]
    ppermute x4, waiting for transfers between devices: 12.2 us -> 10.3 us  [butterfly(): value = add(value, lax.ppermute(value, ('section', 'dp'), pairs), resident)]
    unnamed x29 -> x31, local copies, waits for them, and re-layouts: 5.41 us -> 5.88 us
  transfers between devices with their start and end apart: 23 -> 23, of which waited for: 17 -> 15; matrix products, arithmetic and copies ran while one was open for 1% -> 2% of each run, Pallas kernels for 0% -> 8%
where the time goes in v2:
time: 144 us
  Pallas kernels  61.3 us (43%)
  waiting for transfers between devices  39.2 us (27%)
  starting transfers between devices  31.2 us (22%)
  local copies, waits for them, and re-layouts  5.89 us (4%)
  other arithmetic  4.34 us (3%)
  between operations  1.72 us (1%)
    ppermute x19, waiting for transfers between devices, moved(): return lax.ppermute(value, ('section', 'dp'), pairs)  29 us
    ppermute x19, starting transfers between devices, moved(): return lax.ppermute(value, ('section', 'dp'), pairs)  26.2 us
    pallas_call x1, Pallas kernels, body(): pl.pallas_call(functools.partial(back_kernel, place), grid_spec=pltpu.Pre...  15.2 us
    pallas_call x1, Pallas kernels, body(): pl.pallas_call(functools.partial(front_kernel, place), grid_spec=pltpu.Pr...  12.1 us
    pallas_call x2, Pallas kernels, fetch(): pl.pallas_call(functools.partial(fetch_kernel, first, last), in_specs=[hb...  11.2 us
    ppermute x4, waiting for transfers between devices, butterfly(): value = add(value, lax.ppermute(value, ('section', 'dp'), pairs), resident)  10.3 us
    pallas_call x1, Pallas kernels, body(): pl.pallas_call(functools.partial(late_kernel, place, per, float(images *...  8.02 us
    pallas_call x1, Pallas kernels, body(): pl.pallas_call(functools.partial(inner_kernel, divisor(26)), in_specs=[vm...  6.73 us
  transfers between devices with their start and end apart: 23, of which 15 were waited for; matrix products, arithmetic and copies ran while one was open for 2% of the time, Pallas kernels for 8%

profile of v2, /device:TPU:0, one launch (start us, length us, event | category | flops | bytes accessed | tf_op | source)
XLA Modules:
  0.0 143.7 jit_solution(5438033373188190019)
XLA Ops:
  0.6 1.3 reduce_sum.9
  2.6 0.9 convert_element_type.52
  3.5 4.1 %collective-permute-start.1 = (bf16[320,128]{1,0:T(8,128)(2,1)S(1)}, bf16[320,128]{1,0:T(8,128)(2,1)S(1)}, u32[]{:S(2)}, u32[]{:S(2)}) collective-permute-start(bf16[320,128]{1,0:T(8,128)(2,1)S(1)} %get-tuple-element.74), channel_id=1, source_target_pairs={{0,8},{1,9},{2,10},{3,11},{4,12},{5,13},{6,14},{7,15},{8,0},{9,1},... | collective-permute-start | bytes 245768 | tf_op jit(solution)/shard_map/ppermute | solution.py:697
  7.6 1.6 %collective-permute-start = (bf16[320,128]{1,0:T(8,128)(2,1)S(1)}, bf16[320,128]{1,0:T(8,128)(2,1)S(1)}, u32[]{:S(2)}, u32[]{:S(2)}) collective-permute-start(bf16[320,128]{1,0:T(8,128)(2,1)S(1)} %get-tuple-element.74), channel_id=1, source_target_pairs={{0,4},{1,5},{2,6},{3,7},{4,8},{5,9},{6,10},{7,11},{8,12},{9,13},{1... | collective-permute-start | bytes 245768 | tf_op jit(solution)/shard_map/ppermute | solution.py:697
  9.2 2.2 %collective-permute-start.2 = (bf16[320,128]{1,0:T(8,128)(2,1)S(1)}, bf16[320,128]{1,0:T(8,128)(2,1)S(1)}, u32[]{:S(2)}, u32[]{:S(2)}) collective-permute-start(bf16[320,128]{1,0:T(8,128)(2,1)S(1)} %get-tuple-element.74), channel_id=1, source_target_pairs={{0,12},{1,13},{2,14},{3,15},{4,0},{5,1},{6,2},{7,3},{8,4},{9,5},{1... | collective-permute-start | bytes 245768 | tf_op jit(solution)/shard_map/ppermute | solution.py:697
  11.5 1.6 %collective-permute-done.1 = bf16[320,128]{1,0:T(8,128)(2,1)S(1)} collective-permute-done((bf16[320,128]{1,0:T(8,128)(2,1)S(1)}, bf16[320,128]{1,0:T(8,128)(2,1)S(1)}, u32[]{:S(2)}, u32[]{:S(2)}) %collective-permute-start.1) | collective-permute-done | bytes 81952 | tf_op jit(solution)/shard_map/ppermute | solution.py:697
  13.1 1.3 collective-permute-done
  14.4 0.7 collective-permute-done.2
  15.1 2.7 %collective-permute-start.5 = (bf16[4,320,128]{2,1,0:T(8,128)(2,1)S(1)}, bf16[4,320,128]{2,1,0:T(8,128)(2,1)S(1)}, u32[]{:S(2)}, u32[]{:S(2)}) collective-permute-start(bf16[4,320,128]{2,1,0:T(8,128)(2,1)S(1)} %pad_maximum_fusion.refs_0_), channel_id=1, source_target_pairs={{0,3},{1,2},{2,1},{3,0},{4,7},{5,6},{6,5},{7,4},{8,11},{9,10},{10,... | collective-permute-start | bytes 983048 | tf_op jit(solution)/shard_map/ppermute | solution.py:697
  17.8 0.5 collective-permute-start.4
  18.3 0.3 collective-permute-start.3
  18.6 0.0 collective-permute-start.6
  18.6 8.1 %collective-permute-done.5.refs_3_ = bf16[4,320,128]{2,1,0:T(8,128)(2,1)S(1)} collective-permute-done((bf16[4,320,128]{2,1,0:T(8,128)(2,1)S(1)}, bf16[4,320,128]{2,1,0:T(8,128)(2,1)S(1)}, u32[]{:S(2)}, u32[]{:S(2)}) %collective-permute-start.5) | collective-permute-done | bytes 327712 | tf_op jit(solution)/shard_map/ppermute | solution.py:697
  26.7 0.0 collective-permute-start.9
  26.7 5.5 %collective-permute-done.4.refs_2_ = bf16[4,320,128]{2,1,0:T(8,128)(2,1)S(1)} collective-permute-done((bf16[4,320,128]{2,1,0:T(8,128)(2,1)S(1)}, bf16[4,320,128]{2,1,0:T(8,128)(2,1)S(1)}, u32[]{:S(2)}, u32[]{:S(2)}) %collective-permute-start.4) | collective-permute-done | bytes 327712 | tf_op jit(solution)/shard_map/ppermute | solution.py:697
  32.2 0.0 collective-permute-start.8
  32.2 0.2 collective-permute-done.3.refs_1_
  32.4 0.3 collective-permute-start.7
  32.7 2.1 %copy.15.refs_8_.refs_10_ = bf16[8,196,768]{2,1,0:T(8,128)(2,1)S(1)} copy(bf16[8,196,768]{2,0,1:T(8,128)(2,1)} %param.9) | data formatting | bytes 4816896 | tf_op args[0]
  34.8 0.1 pad_add_fusion.info
  34.9 0.0 collective-permute-done.6.refs_4_
  34.9 0.0 collective-permute-done.9.refs_7_
  35.0 0.0 collective-permute-done.8.refs_6_
  35.0 0.0 collective-permute-done.7.refs_5_
  35.0 12.1 %front.1 = (f32[832,192]{1,0:T(8,128)S(1)}, bf16[832,192]{1,0:T(8,128)(2,1)S(1)}, bf16[832,192]{1,0:T(8,128)(2,1)S(1)}, bf16[832,192]{1,0:T(8,128)(2,1)S(1)}, f3...) custom-call(s32[2]{0:T(128)S(1)} %pad_add_fusion.info, ...), custom_call_target="tpu_custom_call" | custom-call | tf_op jit(solution)/shard_map/front/pallas_call | solution.py:781
  47.1 1.5 %copy-done.2 = f32[2496,208]{1,0:T(8,128)} copy-done((f32[2496,208]{1,0:T(8,128)}, f32[2496,208]{1,0:T(8,128)S(1)}, u32[]{:S(2)}) %copy-start.2) | copy-done | bytes 2076696
  48.6 1.2 copy-done.4
  49.8 1.0 copy-done.6
  50.8 8.0 %late.1 = (bf16[832,192]{1,0:T(8,128)(2,1)S(1)}, bf16[16,320,128]{2,1,0:T(8,128)(2,1)S(1)}, f32[1,128]{1,0:T(1,128)S(1)}) custom-call(s32[2]{0:T(128)S(1)} %pad_add_fusion.info, s32[8]{0:T(128)S(1)} %copy-done.12, s32[8]{0:T(128)S(1)} %copy-done.13, bf16[4,320,128]{2,1,0:T(8,128)(2,1)S(1)} %pad_maximum_fusion.refs_0_, ...), custom_call_target="tpu_custom_call" | custom-call | tf_op jit(solution)/shard_map/late/pallas_call | solution.py:807
  58.8 15.2 %back.1.early = bf16[16,320,128]{2,1,0:T(8,128)(2,1)} custom-call(s32[2]{0:T(128)S(1)} %pad_add_fusion.info, bf16[832,192]{1,0:T(8,128)(2,1)S(1)} %get-tuple-element.39.refs_0_, f32[832,192]{1,0:T(8,128)S(1)} %get-tuple-element.40.refs_1_, bf16[832,192]{1,0:T(8,128)(2,1)S(1)} %get-tuple-element.41.refs_2_, bf16[832,192]{1,0:T(8,128)(2,1)S(1)} %get-tuple-element.42.refs_3_, ...), custom_call_target="tpu_custom_call" | custom-call | tf_op jit(solution)/shard_map/back/pallas_call | solution.py:830
  74.0 1.3 collective-permute-start.10
  75.3 4.2 %collective-permute-start.11 = (bf16[16,320,128]{2,1,0:T(8,128)(2,1)S(1)}, bf16[16,320,128]{2,1,0:T(8,128)(2,1)}, u32[]{:S(2)}, u32[]{:S(2)}) collective-permute-start(bf16[16,320,128]{2,1,0:T(8,128)(2,1)S(1)} %get-tuple-element.56.late), channel_id=1, source_target_pairs={{0,16},{1,17},{2,18},{3,19},{4,20},{5,21},{6,22},{7,23},{8,24},{9,... | collective-permute-start | bytes 3932168 | tf_op jit(solution)/shard_map/ppermute | solution.py:697
  79.5 0.0 collective-permute-done.10.early_here
  79.5 1.7 %collective-permute-done.11.late_here = bf16[16,320,128]{2,1,0:T(8,128)(2,1)} collective-permute-done((bf16[16,320,128]{2,1,0:T(8,128)(2,1)S(1)}, bf16[16,320,128]{2,1,0:T(8,128)(2,1)}, u32[]{:S(2)}, u32[]{:S(2)}) %collective-permute-start.11) | collective-permute-done | bytes 1310752 | tf_op jit(solution)/shard_map/ppermute | solution.py:697
  81.2 2.0 %select_convert_fusion = (bf16[4,320,128]{2,1,0:T(8,128)(2,1)S(1)}, bf16[4,320,128]{2,1,0:T(8,128)(2,1)S(1)}, bf16[4,320,128]{2,1,0:T(8,128)(2,1)S(1)}) fusion(bf16[16,320,128]{2,1,0:T(8,128)(2,1)} %collective-permute-done.11.late_here, bf16[16,320,128]{2,1,0:T(8,128)(2,1)S(1)} %collective-permute-done.10.early_here, bf16[16,320,128]{2,1,0:T(8,128)(2,1)} %back.1.early, ...), kind=kLoop, calls=%fused_computation | loop fusion | flops 3932160 | bytes 4915201 | tf_op jit(solution)/shard_map/convert_element_type | solution.py:862
  83.2 1.9 %collective-permute-start.14 = (bf16[4,320,128]{2,1,0:T(8,128)(2,1)S(1)}, bf16[4,320,128]{2,1,0:T(8,128)(2,1)S(1)}, u32[]{:S(2)}, u32[]{:S(2)}) collective-permute-start(bf16[4,320,128]{2,1,0:T(8,128)(2,1)S(1)} %get-tuple-element.70), channel_id=1, source_target_pairs={{0,3},{1,2},{2,1},{3,0},{4,7},{5,6},{6,5},{7,4},{8,11},{9,10},{10,... | collective-permute-start | bytes 983048 | tf_op jit(solution)/shard_map/ppermute | solution.py:697
  85.0 1.3 collective-permute-start.13
  86.4 0.4 collective-permute-start.12
  86.8 5.8 %fetch.2._.refs_4_.upper = bf16[208,39936]{1,0:T(8,128)(2,1)S(1)} custom-call(bf16[4,320,128]{2,1,0:T(8,128)(2,1)S(1)} %get-tuple-element.72._, bf16[400,39936]{1,0:T(8,128)(2,1)} %bitcast.19), custom_call_target="tpu_custom_call" | custom-call | bytes 33226752 | tf_op jit(solution)/shard_map/fetch/pallas_call | solution.py:867
  92.6 2.1 %collective-permute-done.14.refs_2_ = bf16[4,320,128]{2,1,0:T(8,128)(2,1)S(1)} collective-permute-done((bf16[4,320,128]{2,1,0:T(8,128)(2,1)S(1)}, bf16[4,320,128]{2,1,0:T(8,128)(2,1)S(1)}, u32[]{:S(2)}, u32[]{:S(2)}) %collective-permute-start.14) | collective-permute-done | bytes 327712 | tf_op jit(solution)/shard_map/ppermute | solution.py:697
  94.7 6.4 %collective-permute-done.13.refs_1_ = bf16[4,320,128]{2,1,0:T(8,128)(2,1)S(1)} collective-permute-done((bf16[4,320,128]{2,1,0:T(8,128)(2,1)S(1)}, bf16[4,320,128]{2,1,0:T(8,128)(2,1)S(1)}, u32[]{:S(2)}, u32[]{:S(2)}) %collective-permute-start.13) | collective-permute-done | bytes 327712 | tf_op jit(solution)/shard_map/ppermute | solution.py:697
  101.2 0.3 collective-permute-done.12.refs_0_
  101.4 1.6 %plane.1 = (f32[320,128]{1,0:T(8,128)S(1)}, bf16[320,128]{1,0:T(8,128)(2,1)S(1)}, bf16[320,128]{1,0:T(8,128)(2,1)S(1)}, bf16[320,128]{1,0:T(8,128)(2,1)S(1)}) custom-call(s32[2]{0:T(128)S(1)} %pad_add_fusion.info, bf16[16,320,128]{2,1,0:T(8,128)(2,1)S(1)} %copy-done.1, bf16[16,320,128]{2,1,0:T(8,128)(2,1)S(1)} %collective-permute-done.10.early_here, ...), custom_call_target="tpu_custom_call" | custom-call | tf_op jit(solution)/shard_map/plane/pallas_call | solution.py:883
  103.0 3.2 %collective-permute-start.16 = (bf16[320,128]{1,0:T(8,128)(2,1)S(1)}, bf16[320,128]{1,0:T(8,128)(2,1)S(1)}, u32[]{:S(2)}, u32[]{:S(2)}) collective-permute-start(bf16[320,128]{1,0:T(8,128)(2,1)S(1)} %get-tuple-element.59), channel_id=1, source_target_pairs={{0,8},{1,9},{2,10},{3,11},{4,12},{5,13},{6,14},{7,15},{8,0},{9,1},... | collective-permute-start | bytes 245768 | tf_op jit(solution)/shard_map/ppermute | solution.py:697
  106.3 0.4 collective-permute-start.17
  106.7 1.6 %collective-permute-start.15 = (bf16[320,128]{1,0:T(8,128)(2,1)S(1)}, bf16[320,128]{1,0:T(8,128)(2,1)S(1)}, u32[]{:S(2)}, u32[]{:S(2)}) collective-permute-start(bf16[320,128]{1,0:T(8,128)(2,1)S(1)} %get-tuple-element.58._), channel_id=1, source_target_pairs={{0,4},{1,5},{2,6},{3,7},{4,8},{5,9},{6,10},{7,11},{8,12},{9,13},{1... | collective-permute-start | bytes 245768 | tf_op jit(solution)/shard_map/ppermute | solution.py:697
  108.3 5.4 %fetch.3.refs_5_.__.lower = bf16[192,39936]{1,0:T(8,128)(2,1)S(1)} custom-call(bf16[320,128]{1,0:T(8,128)(2,1)S(1)} %get-tuple-element.58._, bf16[400,39936]{1,0:T(8,128)(2,1)} %bitcast.20), custom_call_target="tpu_custom_call" | custom-call | bytes 30670848 | tf_op jit(solution)/shard_map/fetch/pallas_call | solution.py:867
  113.7 0.0 collective-permute-done.16.refs_2_
  113.7 0.0 collective-permute-done.17.refs_3_
  113.7 0.0 collective-permute-done.15.refs_1_
  113.7 6.7 %inner.1 = (f32[312,128]{1,0:T(8,128)S(1)}, f32[1,512]{1,0:T(1,128)S(1)}) custom-call(f32[320,128]{1,0:T(8,128)S(1)} %get-tuple-element.57.refs_0_, bf16[320,128]{1,0:T(8,128)(2,1)S(1)} %collective-permute-done.15.refs_1_, bf16[320,128]{1,0:T(8,128)(2,1)S(1)} %collective-permute-done.16.refs_2_, bf16[320,128]{1,0:T(8,128)(2,1)S(1)} %collective-permute-done.17.refs_3_, ...), custom_call_target="tpu_custom_call" | custom-call | tf_op jit(solution)/shard_map/inner/pallas_call | solution.py:898
  120.4 0.1 collective-permute-start.18
  120.5 1.1 collective-permute-done.18.right
  121.7 1.4 collective-permute-start.19
  123.1 2.2 %collective-permute-done.19.right = f32[1,512]{1,0:T(1,128)S(1)} collective-permute-done((f32[1,512]{1,0:T(1,128)S(1)}, f32[1,512]{1,0:T(1,128)S(1)}, u32[]{:S(2)}, u32[]{:S(2)}) %collective-permute-start.19) | collective-permute-done | bytes 2080 | tf_op jit(solution)/shard_map/ppermute | solution.py:723
  125.3 1.4 collective-permute-start.20
  126.7 2.2 %collective-permute-done.20.right = f32[1,512]{1,0:T(1,128)S(1)} collective-permute-done((f32[1,512]{1,0:T(1,128)S(1)}, f32[1,512]{1,0:T(1,128)S(1)}, u32[]{:S(2)}, u32[]{:S(2)}) %collective-permute-start.20) | collective-permute-done | bytes 2080 | tf_op jit(solution)/shard_map/ppermute | solution.py:723
  128.8 0.9 collective-permute-start.21
  129.8 2.7 %collective-permute-done.21.right = f32[1,512]{1,0:T(1,128)S(1)} collective-permute-done((f32[1,512]{1,0:T(1,128)S(1)}, f32[1,512]{1,0:T(1,128)S(1)}, u32[]{:S(2)}, u32[]{:S(2)}) %collective-permute-start.21) | collective-permute-done | bytes 2080 | tf_op jit(solution)/shard_map/ppermute | solution.py:723
  132.4 0.0 copy-start.10
  132.5 0.0 copy-start.14
  132.5 1.3 collective-permute-start.22
  133.8 3.2 %collective-permute-done.22.right = f32[1,512]{1,0:T(1,128)S(1)} collective-permute-done((f32[1,512]{1,0:T(1,128)S(1)}, f32[1,512]{1,0:T(1,128)S(1)}, u32[]{:S(2)}, u32[]{:S(2)}) %collective-permute-start.22) | collective-permute-done | bytes 2080 | tf_op jit(solution)/shard_map/ppermute | solution.py:723
  137.0 6.5 %update.1 = (f32[3]{0:T(128)}, f32[1]{0:T(128)}, f32[2,200]{1,0:T(2,128)}, f32[312,128]{1,0:T(8,128)}, f32[312,128]{1,0:T(8,128)}, /*index=5*/f32[312,128]{1,0:T(8,128)}) custom-call(s32[2]{0:T(128)S(1)} %copy-done.14, f32[1,512]{1,0:T(1,128)S(1)} %add.43.sums, bf16[208,39936]{1,0:T(8,128)(2,1)S(1)} %fetch.2._.refs_4_.upper, ...), custom_call_target="tpu_custom_call" | custom-call | tf_op jit(solution)/shard_map/update/pallas_call | solution.py:909
  (32 shorter events, 0.1 us)
Async XLA Ops:
  3.5 9.6 %collective-permute-start.1 = (bf16[320,128]{1,0:T(8,128)(2,1)S(1)}, bf16[320,128]{1,0:T(8,128)(2,1)S(1)}, u32[]{:S(2)}, u32[]{:S(2)}) collective-permute-start(bf16[320,128]{1,0:T(8,128)(2,1)S(1)} %get-tuple-element.74), channel_id=1, source_target_pairs={{0,8},{1,9},{2,10},{3,11},{4,12},{5,13},{6,14},{7,15},{8,0},{9,1},... | collective-permute-start | bytes 245768 | tf_op jit(solution)/shard_map/ppermute | solution.py:697
  7.6 6.7 %collective-permute-start = (bf16[320,128]{1,0:T(8,128)(2,1)S(1)}, bf16[320,128]{1,0:T(8,128)(2,1)S(1)}, u32[]{:S(2)}, u32[]{:S(2)}) collective-permute-start(bf16[320,128]{1,0:T(8,128)(2,1)S(1)} %get-tuple-element.74), channel_id=1, source_target_pairs={{0,4},{1,5},{2,6},{3,7},{4,8},{5,9},{6,10},{7,11},{8,12},{9,13},{1... | collective-permute-start | bytes 245768 | tf_op jit(solution)/shard_map/ppermute | solution.py:697
  9.2 5.8 %collective-permute-start.2 = (bf16[320,128]{1,0:T(8,128)(2,1)S(1)}, bf16[320,128]{1,0:T(8,128)(2,1)S(1)}, u32[]{:S(2)}, u32[]{:S(2)}) collective-permute-start(bf16[320,128]{1,0:T(8,128)(2,1)S(1)} %get-tuple-element.74), channel_id=1, source_target_pairs={{0,12},{1,13},{2,14},{3,15},{4,0},{5,1},{6,2},{7,3},{8,4},{9,5},{1... | collective-permute-start | bytes 245768 | tf_op jit(solution)/shard_map/ppermute | solution.py:697
  15.1 11.6 %collective-permute-start.5 = (bf16[4,320,128]{2,1,0:T(8,128)(2,1)S(1)}, bf16[4,320,128]{2,1,0:T(8,128)(2,1)S(1)}, u32[]{:S(2)}, u32[]{:S(2)}) collective-permute-start(bf16[4,320,128]{2,1,0:T(8,128)(2,1)S(1)} %pad_maximum_fusion.refs_0_), channel_id=1, source_target_pairs={{0,3},{1,2},{2,1},{3,0},{4,7},{5,6},{6,5},{7,4},{8,11},{9,10},{10,... | collective-permute-start | bytes 983048 | tf_op jit(solution)/shard_map/ppermute | solution.py:697
  17.8 14.4 %collective-permute-start.4 = (bf16[4,320,128]{2,1,0:T(8,128)(2,1)S(1)}, bf16[4,320,128]{2,1,0:T(8,128)(2,1)S(1)}, u32[]{:S(2)}, u32[]{:S(2)}) collective-permute-start(bf16[4,320,128]{2,1,0:T(8,128)(2,1)S(1)} %pad_maximum_fusion.refs_0_), channel_id=1, source_target_pairs={{0,2},{1,3},{2,0},{3,1},{4,6},{5,7},{6,4},{7,5},{8,10},{9,11},{10,... | collective-permute-start | bytes 983048 | tf_op jit(solution)/shard_map/ppermute | solution.py:697
  18.3 14.2 %collective-permute-start.3 = (bf16[4,320,128]{2,1,0:T(8,128)(2,1)S(1)}, bf16[4,320,128]{2,1,0:T(8,128)(2,1)S(1)}, u32[]{:S(2)}, u32[]{:S(2)}) collective-permute-start(bf16[4,320,128]{2,1,0:T(8,128)(2,1)S(1)} %pad_maximum_fusion.refs_0_), channel_id=1, source_target_pairs={{0,1},{1,0},{2,3},{3,2},{4,5},{5,4},{6,7},{7,6},{8,9},{9,8},{10,11... | collective-permute-start | bytes 983048 | tf_op jit(solution)/shard_map/ppermute | solution.py:697
  18.6 16.3 %collective-permute-start.6 = (bf16[4,320,128]{2,1,0:T(8,128)(2,1)S(1)}, bf16[4,320,128]{2,1,0:T(8,128)(2,1)S(1)}, u32[]{:S(2)}, u32[]{:S(2)}) collective-permute-start(bf16[4,320,128]{2,1,0:T(8,128)(2,1)S(1)} %pad_maximum_fusion.refs_0_), channel_id=1, source_target_pairs={{0,16},{1,17},{2,18},{3,19},{4,20},{5,21},{6,22},{7,23},{8,24},{9,... | collective-permute-start | bytes 983048 | tf_op jit(solution)/shard_map/ppermute | solution.py:697
  26.7 8.2 %collective-permute-start.9 = (bf16[4,320,128]{2,1,0:T(8,128)(2,1)S(1)}, bf16[4,320,128]{2,1,0:T(8,128)(2,1)S(1)}, u32[]{:S(2)}, u32[]{:S(2)}) collective-permute-start(bf16[4,320,128]{2,1,0:T(8,128)(2,1)S(1)} %collective-permute-done.5.refs_3_), channel_id=1, source_target_pairs={{0,16},{1,17},{2,18},{3,19},{4,20},{5,21},{6,22},{7,23},{8,24},{9,... | collective-permute-start | bytes 983048 | tf_op jit(solution)/shard_map/ppermute | solution.py:697
  32.2 2.8 %collective-permute-start.8 = (bf16[4,320,128]{2,1,0:T(8,128)(2,1)S(1)}, bf16[4,320,128]{2,1,0:T(8,128)(2,1)S(1)}, u32[]{:S(2)}, u32[]{:S(2)}) collective-permute-start(bf16[4,320,128]{2,1,0:T(8,128)(2,1)S(1)} %collective-permute-done.4.refs_2_), channel_id=1, source_target_pairs={{0,16},{1,17},{2,18},{3,19},{4,20},{5,21},{6,22},{7,23},{8,24},{9,... | collective-permute-start | bytes 983048 | tf_op jit(solution)/shard_map/ppermute | solution.py:697
  32.4 2.5 %collective-permute-start.7 = (bf16[4,320,128]{2,1,0:T(8,128)(2,1)S(1)}, bf16[4,320,128]{2,1,0:T(8,128)(2,1)S(1)}, u32[]{:S(2)}, u32[]{:S(2)}) collective-permute-start(bf16[4,320,128]{2,1,0:T(8,128)(2,1)S(1)} %collective-permute-done.3.refs_1_), channel_id=1, source_target_pairs={{0,16},{1,17},{2,18},{3,19},{4,20},{5,21},{6,22},{7,23},{8,24},{9,... | collective-permute-start | bytes 983048 | tf_op jit(solution)/shard_map/ppermute | solution.py:697
  34.8 12.2 %copy-start = (bf16[8,196,768]{2,1,0:T(8,128)(2,1)}, bf16[8,196,768]{2,1,0:T(8,128)(2,1)S(1)}, u32[]{:S(2)}) copy-start(bf16[8,196,768]{2,1,0:T(8,128)(2,1)S(1)} %copy.15.refs_8_.refs_10_) | copy-start | bytes 7225348
  34.9 13.7 %copy-start.11 = (f32[8,1000]{1,0:T(8,128)S(1)}, f32[8,1000]{1,0:T(8,128)}, u32[]{:S(2)}) copy-start(f32[8,1000]{1,0:T(8,128)} %refs_9_.1) | copy-start | bytes 96004
  34.9 13.7 %copy-start.12 = (s32[8]{0:T(128)S(1)}, s32[8]{0:T(128)}, u32[]{:S(2)}) copy-start(s32[8]{0:T(128)} %labels.1) | copy-start | bytes 100
  34.9 13.7 %copy-start.13 = (s32[8]{0:T(128)S(1)}, s32[8]{0:T(128)}, u32[]{:S(2)}) copy-start(s32[8]{0:T(128)} %replay.1) | copy-start | bytes 100
  35.0 12.1 %copy-start.3 = (bf16[4,320,128]{2,1,0:T(8,128)(2,1)}, bf16[4,320,128]{2,1,0:T(8,128)(2,1)S(1)}, u32[]{:S(2)}) copy-start(bf16[4,320,128]{2,1,0:T(8,128)(2,1)S(1)} %collective-permute-done.8.refs_6_) | copy-start | bytes 983044
  35.0 12.1 %copy-start.5 = (bf16[4,320,128]{2,1,0:T(8,128)(2,1)}, bf16[4,320,128]{2,1,0:T(8,128)(2,1)S(1)}, u32[]{:S(2)}) copy-start(bf16[4,320,128]{2,1,0:T(8,128)(2,1)S(1)} %collective-permute-done.7.refs_5_) | copy-start | bytes 983044
  47.1 1.5 %copy-start.2 = (f32[2496,208]{1,0:T(8,128)}, f32[2496,208]{1,0:T(8,128)S(1)}, u32[]{:S(2)}) copy-start(f32[2496,208]{1,0:T(8,128)S(1)} %get-tuple-element.44.refs_5_) | copy-start | bytes 6230020
  48.6 10.2 %copy-start.7 = (bf16[832,768]{1,0:T(8,128)(2,1)}, bf16[832,768]{1,0:T(8,128)(2,1)S(1)}, u32[]{:S(2)}) copy-start(bf16[832,768]{1,0:T(8,128)(2,1)S(1)} %get-tuple-element.47.refs_8_) | copy-start | bytes 3833860
  48.6 1.2 copy-start.4
  49.8 1.0 copy-start.6
  74.0 5.5 %collective-permute-start.10 = (bf16[16,320,128]{2,1,0:T(8,128)(2,1)}, bf16[16,320,128]{2,1,0:T(8,128)(2,1)S(1)}, u32[]{:S(2)}, u32[]{:S(2)}) collective-permute-start(bf16[16,320,128]{2,1,0:T(8,128)(2,1)} %back.1.early), channel_id=1, source_target_pairs={{16,0},{17,1},{18,2},{19,3},{20,4},{21,5},{22,6},{23,7},{24,8},{25... | collective-permute-start | bytes 3932168 | tf_op jit(solution)/shard_map/ppermute | solution.py:697
  75.3 5.9 %collective-permute-start.11 = (bf16[16,320,128]{2,1,0:T(8,128)(2,1)S(1)}, bf16[16,320,128]{2,1,0:T(8,128)(2,1)}, u32[]{:S(2)}, u32[]{:S(2)}) collective-permute-start(bf16[16,320,128]{2,1,0:T(8,128)(2,1)S(1)} %get-tuple-element.56.late), channel_id=1, source_target_pairs={{0,16},{1,17},{2,18},{3,19},{4,20},{5,21},{6,22},{7,23},{8,24},{9,... | collective-permute-start | bytes 3932168 | tf_op jit(solution)/shard_map/ppermute | solution.py:697
  83.2 11.6 %collective-permute-start.14 = (bf16[4,320,128]{2,1,0:T(8,128)(2,1)S(1)}, bf16[4,320,128]{2,1,0:T(8,128)(2,1)S(1)}, u32[]{:S(2)}, u32[]{:S(2)}) collective-permute-start(bf16[4,320,128]{2,1,0:T(8,128)(2,1)S(1)} %get-tuple-element.70), channel_id=1, source_target_pairs={{0,3},{1,2},{2,1},{3,0},{4,7},{5,6},{6,5},{7,4},{8,11},{9,10},{10,... | collective-permute-start | bytes 983048 | tf_op jit(solution)/shard_map/ppermute | solution.py:697
  85.0 16.1 %collective-permute-start.13 = (bf16[4,320,128]{2,1,0:T(8,128)(2,1)S(1)}, bf16[4,320,128]{2,1,0:T(8,128)(2,1)S(1)}, u32[]{:S(2)}, u32[]{:S(2)}) collective-permute-start(bf16[4,320,128]{2,1,0:T(8,128)(2,1)S(1)} %get-tuple-element.71), channel_id=1, source_target_pairs={{0,2},{1,3},{2,0},{3,1},{4,6},{5,7},{6,4},{7,5},{8,10},{9,11},{10,... | collective-permute-start | bytes 983048 | tf_op jit(solution)/shard_map/ppermute | solution.py:697
  86.4 15.0 %collective-permute-start.12 = (bf16[4,320,128]{2,1,0:T(8,128)(2,1)S(1)}, bf16[4,320,128]{2,1,0:T(8,128)(2,1)S(1)}, u32[]{:S(2)}, u32[]{:S(2)}) collective-permute-start(bf16[4,320,128]{2,1,0:T(8,128)(2,1)S(1)} %get-tuple-element.72._), channel_id=1, source_target_pairs={{0,1},{1,0},{2,3},{3,2},{4,5},{5,4},{6,7},{7,6},{8,9},{9,8},{10,11... | collective-permute-start | bytes 983048 | tf_op jit(solution)/shard_map/ppermute | solution.py:697
  86.8 14.7 %copy-start.1 = (bf16[16,320,128]{2,1,0:T(8,128)(2,1)S(1)}, bf16[16,320,128]{2,1,0:T(8,128)(2,1)}, u32[]{:S(2)}) copy-start(bf16[16,320,128]{2,1,0:T(8,128)(2,1)} %back.1.early) | copy-start | bytes 3932164
  103.0 10.6 %collective-permute-start.16 = (bf16[320,128]{1,0:T(8,128)(2,1)S(1)}, bf16[320,128]{1,0:T(8,128)(2,1)S(1)}, u32[]{:S(2)}, u32[]{:S(2)}) collective-permute-start(bf16[320,128]{1,0:T(8,128)(2,1)S(1)} %get-tuple-element.59), channel_id=1, source_target_pairs={{0,8},{1,9},{2,10},{3,11},{4,12},{5,13},{6,14},{7,15},{8,0},{9,1},... | collective-permute-start | bytes 245768 | tf_op jit(solution)/shard_map/ppermute | solution.py:697
  106.3 7.4 %collective-permute-start.17 = (bf16[320,128]{1,0:T(8,128)(2,1)S(1)}, bf16[320,128]{1,0:T(8,128)(2,1)S(1)}, u32[]{:S(2)}, u32[]{:S(2)}) collective-permute-start(bf16[320,128]{1,0:T(8,128)(2,1)S(1)} %get-tuple-element.60), channel_id=1, source_target_pairs={{0,12},{1,13},{2,14},{3,15},{4,0},{5,1},{6,2},{7,3},{8,4},{9,5},{1... | collective-permute-start | bytes 245768 | tf_op jit(solution)/shard_map/ppermute | solution.py:697
  106.7 7.0 %collective-permute-start.15 = (bf16[320,128]{1,0:T(8,128)(2,1)S(1)}, bf16[320,128]{1,0:T(8,128)(2,1)S(1)}, u32[]{:S(2)}, u32[]{:S(2)}) collective-permute-start(bf16[320,128]{1,0:T(8,128)(2,1)S(1)} %get-tuple-element.58._), channel_id=1, source_target_pairs={{0,4},{1,5},{2,6},{3,7},{4,8},{5,9},{6,10},{7,11},{8,12},{9,13},{1... | collective-permute-start | bytes 245768 | tf_op jit(solution)/shard_map/ppermute | solution.py:697
  120.4 1.2 collective-permute-start.18
  121.7 3.6 %collective-permute-start.19 = (f32[1,512]{1,0:T(1,128)S(1)}, f32[1,512]{1,0:T(1,128)S(1)}, u32[]{:S(2)}, u32[]{:S(2)}) collective-permute-start(f32[1,512]{1,0:T(1,128)S(1)} %add.39.left), channel_id=1, source_target_pairs={{0,1},{1,0},{2,3},{3,2},{4,5},{5,4},{6,7},{7,6},{8,9},{9,8},{10,11... | collective-permute-start | bytes 6152 | tf_op jit(solution)/shard_map/ppermute | solution.py:723
  125.3 3.6 %collective-permute-start.20 = (f32[1,512]{1,0:T(1,128)S(1)}, f32[1,512]{1,0:T(1,128)S(1)}, u32[]{:S(2)}, u32[]{:S(2)}) collective-permute-start(f32[1,512]{1,0:T(1,128)S(1)} %add.40.left), channel_id=1, source_target_pairs={{0,2},{1,3},{2,0},{3,1},{4,6},{5,7},{6,4},{7,5},{8,10},{9,11},{10,... | collective-permute-start | bytes 6152 | tf_op jit(solution)/shard_map/ppermute | solution.py:723
  128.8 3.6 %collective-permute-start.21 = (f32[1,512]{1,0:T(1,128)S(1)}, f32[1,512]{1,0:T(1,128)S(1)}, u32[]{:S(2)}, u32[]{:S(2)}) collective-permute-start(f32[1,512]{1,0:T(1,128)S(1)} %add.41.left), channel_id=1, source_target_pairs={{0,4},{1,5},{2,6},{3,7},{4,0},{5,1},{6,2},{7,3},{8,12},{9,13},{10,... | collective-permute-start | bytes 6152 | tf_op jit(solution)/shard_map/ppermute | solution.py:723
  132.4 4.6 %copy-start.8 = (f32[1,39936]{1,0:T(1,128)S(1)}, f32[1,39936]{1,0:T(1,128)}, u32[]{:S(2)}) copy-start(f32[1,39936]{1,0:T(1,128)} %param.14) | copy-start | bytes 479236
  132.4 4.6 %copy-start.9 = (f32[1,39936]{1,0:T(1,128)S(1)}, f32[1,39936]{1,0:T(1,128)}, u32[]{:S(2)}) copy-start(f32[1,39936]{1,0:T(1,128)} %param.15) | copy-start | bytes 479236
  132.4 4.6 %copy-start.10 = (f32[1,39936]{1,0:T(1,128)S(1)}, f32[1,39936]{1,0:T(1,128)}, u32[]{:S(2)}) copy-start(f32[1,39936]{1,0:T(1,128)} %param.16) | copy-start | bytes 479236
  132.5 4.6 %copy-start.14 = (s32[2]{0:T(128)S(1)}, s32[2]{0:T(128)}, u32[]{:S(2)}) copy-start(s32[2]{0:T(128)} %counts.1) | copy-start | bytes 28
  132.5 4.5 %collective-permute-start.22 = (f32[1,512]{1,0:T(1,128)S(1)}, f32[1,512]{1,0:T(1,128)S(1)}, u32[]{:S(2)}, u32[]{:S(2)}) collective-permute-start(f32[1,512]{1,0:T(1,128)S(1)} %add.42.left), channel_id=1, source_target_pairs={{0,8},{1,9},{2,10},{3,11},{4,12},{5,13},{6,14},{7,15},{8,0},{9,1},... | collective-permute-start | bytes 6152 | tf_op jit(solution)/shard_map/ppermute | solution.py:723

commit v3 on v2

--- a/solution.py
+++ b/solution.py
@@ -17,6 +17,7 @@
 TOKENS = PATCHES + 1
 ROWS = 208
 CLS = PATCHES
+GROUP = 2
 CLASSES = 1000
 CPAD = 1024
 TASKS = 2
@@ -130,9 +131,9 @@
     def shift(self):
         step = 192
         for at in range(0, self.rows, step):
-            here = swap_halves(self.even[at : at + step, :])
-            after = swap_halves(self.even[at + 1 : at + 1 + step, :])
-            self.odd[at : at + step, :] = jnp.where(low_lanes(here.shape), here, after)
+            here = self.even[at : at + step, :]
+            after = self.even[at + 1 : at + 1 + step, :]
+            self.odd[at : at + step, :] = swap_halves(jnp.where(low_lanes(here.shape), after, here))
 
     def rows_at(self, half, count, stride):
         return strided(self.odd if half % 2 else self.even, half // 2, count, stride)
@@ -185,9 +186,10 @@
                 self.put_rows(start + width, pairs, width, self.mix[pl.ds(1, pairs, stride=2), :])
 
     def merged(self, at, count):
-        here = swap_halves(self.odd[at + 8 : at + 8 + count, :])
-        before = swap_halves(self.odd[at + 7 : at + 7 + count, :])
-        return self.even[at : at + count, :] + jnp.where(low_lanes(here.shape), before, here)
+        here = self.odd[at + 8 : at + 8 + count, :]
+        before = self.odd[at + 7 : at + 7 + count, :]
+        moved_back = swap_halves(jnp.where(low_lanes(here.shape), here, before))
+        return self.even[at : at + count, :] + moved_back
 
 
 class Place:
@@ -196,6 +198,7 @@
         self.count = self.z * self.y * self.x
         self.shard_rows = shard_rows
         self.sent_rows = -(-(shard_rows + 1) // 16) * 16
+        self.first_rows = self.sent_rows * 13 // 20 // 16 * 16
 
     def split(self, index):
         plane = self.y * self.x
@@ -205,10 +208,10 @@
         return [(a, b) for a in range(self.y) for b in range(self.x)]
 
 
-def load_section(place, info, pieces, wanted, flat):
+def load_section(place, pieces, wanted, flat):
     own, other = pieces
-    section = info[0]
-    zed, why, ex = place.split(info[1])
+    section = lax.axis_index("section")
+    zed, why, ex = place.split(lax.axis_index("dp"))
     rows = place.shard_rows
 
     def copy(refs):
@@ -220,8 +223,13 @@
                 start = shard * rows
                 if rows % 8 == 0:
                     start = pl.multiple_of(start, 8)
-                value = refs[turn][d].astype(f32)
-                flat.even[pl.ds(start, rows), :] = value[:rows]
+                cut = place.first_rows
+                flat.even[pl.ds(start, cut), :] = refs[turn][d].astype(f32)
+                value = refs[len(place.turns()) + d][turn].astype(f32)
+                after = start + cut
+                if rows % 8 == 0:
+                    after = pl.multiple_of(after, 8)
+                flat.even[pl.ds(after, rows - cut), :] = value[: rows - cut]
 
     @pl.when(section == wanted)
     def _():
@@ -259,8 +267,8 @@
         flat.write(value, starts[name], 2, value.shape[1])
 
 
-def send_out(place, info, flat, out_ref):
-    zed, why, ex = place.split(info[1])
+def send_out(place, flat, write):
+    zed, why, ex = place.split(lax.axis_index("dp"))
     rows, spare = place.shard_rows, place.sent_rows - place.shard_rows
     for shard in range(place.count):
         zk, yk, xk = shard // (place.y * place.x), shard // place.x % place.y, shard % place.x
@@ -269,12 +277,20 @@
         b = lax.rem(xk + place.x - ex, place.x)
         value = flat.merged(shard * rows, rows)
         value = jnp.concatenate([value, jnp.zeros((spare, LANES), f32)], 0)
-        out_ref[(a * place.x + b) * place.z + d] = value.astype(bf16)
-
-
-def front_kernel(place, info, *refs):
-    turns = len(place.turns())
-    own, other, refs = refs[:turns], refs[turns : 2 * turns], refs[2 * turns :]
+        write((a * place.x + b) * place.z + d, value.astype(bf16))
+
+
+def shard_kernel(replay, master, out):
+    rows = master.shape[0]
+    count = sum(replay[i].astype(f32) for i in range(replay.shape[0]))
+    tail = jnp.full((out.shape[0] - rows, LANES), count, f32)
+    out[...] = jnp.concatenate([master[...], tail], 0).astype(bf16)
+
+
+def front_kernel(place, *refs):
+    section = lax.axis_index("section")
+    parts = len(place.turns()) + place.z
+    own, other, refs = refs[:parts], refs[parts : 2 * parts], refs[2 * parts :]
     patches, refs = refs[0], refs[1:]
     (x_out, q_out, k_out, v_out, probs_out, mixed_out, hidden_out, act_out, slope_out, middle_out) = refs[:10]
     w_q, w_k, w_v, w_out, w_up, w_down, vec = refs[10:17]
@@ -283,7 +299,7 @@
 
     @pl.when(pl.program_id(0) == 0)
     def _():
-        load_section(place, info, (own, other), 0, flat)
+        load_section(place, (own, other), 0, flat)
         read_block(flat, (w_q, w_k, w_v, w_out, w_up, w_down), vec)
         flat.read(w_patch, W_PATCH, 3, PDIM, D)
         flat.read_row(vec, 9, B_PATCH, D)
@@ -293,10 +309,14 @@
         for at, wide, value in flat.blocks(POS_EMBED, 3, TOKENS + 1, D):
             bias = vec[9:10, at : at + wide]
             token = vec[10:11, at : at + wide]
-            added[0:PATCHES, at : at + wide] = value[1:TOKENS, :wide] + bias
-            added[CLS : CLS + 1, at : at + wide] = value[0:1, :wide] + token
-
-    tokens[0:PATCHES, :] = dot(patches[...], w_patch[...])
+            for top in range(0, added.shape[0], ROWS):
+                added[top : top + PATCHES, at : at + wide] = value[1:TOKENS, :wide] + bias
+                added[top + CLS : top + CLS + 1, at : at + wide] = value[0:1, :wide] + token
+
+    group = patches.shape[0]
+    spans = [slice(i * ROWS, (i + 1) * ROWS) for i in range(group)]
+    for i in range(group):
+        tokens[i * ROWS : i * ROWS + PATCHES, :] = dot(patches[i], w_patch[...])
     x = tokens[...] + added[...]
     x_out[...] = x
     unit, _ = normalise(x)
@@ -305,13 +325,16 @@
     k = dot(normed, w_k[...]).astype(bf16)
     v = (dot(normed, w_v[...]) + vector(vec, "b_v")).astype(bf16)
     q_out[...], k_out[...], v_out[...] = q, k, v
-    scores = dot(by_head(q.astype(f32) * SCALE).astype(bf16), k, 1, 1)
-    column = lax.broadcasted_iota(jnp.int32, scores.shape, 1)
-    scores = jnp.where(column < TOKENS, scores, MASKED)
-    raised = jnp.exp(scores - jnp.max(scores, -1, keepdims=True))
-    probs = raised / jnp.sum(raised, -1, keepdims=True)
-    probs_out[...] = probs
-    mixed = from_heads(dot(probs.astype(bf16), v)).astype(bf16)
+    q_scaled = q.astype(f32) * SCALE
+    column = lax.broadcasted_iota(jnp.int32, (1, ROWS), 1)
+    scores = [dot(by_head(q_scaled[at]).astype(bf16), k[at], 1, 1) for at in spans]
+    scores = [jnp.where(column < TOKENS, value, MASKED) for value in scores]
+    raised = [jnp.exp(value - jnp.max(value, -1, keepdims=True)) for value in scores]
+    probs = [value * (1.0 / jnp.sum(value, -1, keepdims=True)) for value in raised]
+    for i, value in enumerate(probs):
+        probs_out[i * HEADS * ROWS : (i + 1) * HEADS * ROWS, :] = value
+    mixed = [from_heads(dot(value.astype(bf16), v[at])) for value, at in zip(probs, spans)]
+    mixed = jnp.concatenate(mixed, 0).astype(bf16)
     mixed_out[...] = mixed
     hidden = x + dot(mixed, w_out[...]) + vector(vec, "b_out")
     hidden_out[...] = hidden
@@ -367,22 +390,24 @@
         flat.even[row : row + 1, :] += grad_b[:, j * LANES : (j + 1) * LANES]
 
 
-def late_kernel(place, per, image_total, info, labels, replay, *refs):
-    turns = len(place.turns())
-    own, other, refs = refs[:turns], refs[turns : 2 * turns], refs[2 * turns :]
+def late_kernel(place, per, image_total, labels, replay, *refs):
+    section = lax.axis_index("section")
+    parts = len(place.turns()) + place.z
+    own, other, refs = refs[:parts], refs[parts : 2 * parts], refs[2 * parts :]
     middle, old_logits, back_out, grad_out, loss_out = refs[:5]
     even, odd, mix, wide, w_q, w_k, w_v, w_out, w_up, w_down, vec, w_head, b_head, few, many = refs[5:]
     flat = Flat(even, odd, mix, place.count * place.shard_rows)
-    load_section(place, info, (own, other), 1, flat)
+    load_section(place, (own, other), 1, flat)
     read_block(flat, (w_q, w_k, w_v, w_out, w_up, w_down), vec)
     flat.read_row(vec, 9, GAIN_LAST, D)
     flat.read_row(vec, 10, BIAS_LAST, D)
     read_head(flat, wide, w_head, b_head)
     gain_last, bias_last = vec[9:10, 0:D], vec[10:11, 0:D]
     carried = jnp.zeros((1, LANES), f32)
-    for ref in own:
-        for d in range(place.z):
-            carried = carried + ref[d].astype(f32)[place.shard_rows : place.shard_rows + 1]
+    carrier = place.shard_rows - place.first_rows
+    for ref in own[len(place.turns()) :]:
+        for turn in range(len(place.turns())):
+            carried = carried + ref[turn].astype(f32)[carrier : carrier + 1]
     replay_count = carried[:, 0:1]
 
     x = middle[...].astype(f32)
@@ -412,7 +437,7 @@
     scores = jnp.where(inside, scores, MASKED)
     raised = jnp.where(inside, jnp.exp(scores - jnp.max(scores, -1, keepdims=True)), 0.0)
     total = jnp.sum(raised, -1, keepdims=True)
-    probs = raised / jnp.where(total > 0.0, total, 1.0)
+    probs = raised * (1.0 / jnp.where(total > 0.0, total, 1.0))
     probs_low = probs.astype(bf16)
     mixed = from_heads(dot(probs_low, v)).astype(bf16)
     hidden = x_top + dot(mixed, w_out[...]) + vector(vec, "b_out")
@@ -432,11 +457,11 @@
     label = jnp.zeros((eight, 1), jnp.int32)
     again = jnp.zeros((eight, 1), f32)
     for i in range(per):
-        label = jnp.where(image == i, labels[info[0] * per + i], label)
-        again = jnp.where(image == i, replay[info[0] * per + i].astype(f32), again)
+        label = jnp.where(image == i, labels[section * per + i], label)
+        again = jnp.where(image == i, replay[section * per + i].astype(f32), again)
     picked = jnp.logical_and(classes == label, real)
     entropy = jnp.where(real, log_total, 0.0) - jnp.sum(jnp.where(picked, logits, 0.0), -1, keepdims=True)
-    wanted = jnp.where(info[0] == 0, old_logits[0:per, :], old_logits[per : 2 * per, :])
+    wanted = jnp.where(section == 0, old_logits[0:per, :], old_logits[per : 2 * per, :])
     if per < eight:
         wanted = jnp.concatenate([wanted, jnp.zeros((eight - per, CLASSES), f32)], 0)
     wanted = jnp.concatenate([wanted, jnp.zeros((eight, CPAD - CLASSES), f32)], 1)
@@ -494,13 +519,17 @@
         many[i * ROWS + CLS : i * ROWS + CLS + 1, :] += grad_hidden[i : i + 1, :]
     back_out[...] = many[...].astype(bf16)
     write_vectors(flat, sums)
-    send_out(place, info, flat, grad_out)
-
-
-def back_kernel(place, info, *refs):
+
+    def store(at, value):
+        grad_out[at] = value
+
+    send_out(place, flat, store)
+
+
+def back_kernel(place, *refs):
     (grad_in, x_in, q_in, k_in, v_in, probs_in, mixed_in, hidden_in, act_in, slope_in, patches) = refs[:11]
-    w_q, w_k, w_v, w_out, w_up, w_down, vec, grad_out = refs[11:19]
-    even, odd, mix, g_q, g_k, g_v, g_out, g_up, g_down, g_patch, g_pos, rows = refs[19:]
+    w_q, w_k, w_v, w_out, w_up, w_down, vec, late_grad, keep_out, give_out = refs[11:21]
+    even, odd, mix, g_q, g_k, g_v, g_out, g_up, g_down, g_patch, g_pos, rows = refs[21:]
     step = pl.program_id(0)
     sums_at = {name: row for row, name in enumerate(VECTORS)}
 
@@ -527,15 +556,20 @@
     branch = grad_hidden.astype(bf16)
     g_out[...] += dot(mixed_in[...], branch, 0, 0)
     add_row(sums_at["b_out"], column_sums(branch))
-    mixed_heads = by_head(dot(branch, w_out[...], 1, 1).astype(bf16).astype(f32)).astype(bf16)
-    q_heads = by_head(q_in[...].astype(f32) * SCALE).astype(bf16)
-    probs = probs_in[...]
-    grad_probs = dot(mixed_heads, v_in[...], 1, 1)
-    grad_v = dot(probs.astype(bf16), mixed_heads, 0, 0).astype(bf16)
-    inner = jnp.sum(grad_probs * probs, -1, keepdims=True)
-    grad_scores = (probs * (grad_probs - inner)).astype(bf16)
-    grad_q = (from_heads(dot(grad_scores, k_in[...])) * SCALE).astype(bf16)
-    grad_k = dot(grad_scores, q_heads, 0, 0).astype(bf16)
+    group = patches.shape[0]
+    spans = [slice(i * ROWS, (i + 1) * ROWS) for i in range(group)]
+    grad_mixed = dot(branch, w_out[...], 1, 1).astype(bf16).astype(f32)
+    mixed_heads = [by_head(grad_mixed[at]).astype(bf16) for at in spans]
+    q_scaled = q_in[...].astype(f32) * SCALE
+    q_heads = [by_head(q_scaled[at]).astype(bf16) for at in spans]
+    probs = [probs_in[i * HEADS * ROWS : (i + 1) * HEADS * ROWS, :] for i in range(group)]
+    grad_probs = [dot(value, v_in[at, :], 1, 1) for value, at in zip(mixed_heads, spans)]
+    grad_v = [dot(value.astype(bf16), right, 0, 0) for value, right in zip(probs, mixed_heads)]
+    inner = [jnp.sum(one * two, -1, keepdims=True) for one, two in zip(grad_probs, probs)]
+    grad_scores = [(two * (one - less)).astype(bf16) for one, two, less in zip(grad_probs, probs, inner)]
+    grad_q = [from_heads(dot(value, k_in[at, :])) * SCALE for value, at in zip(grad_scores, spans)]
+    grad_k = [dot(value, right, 0, 0) for value, right in zip(grad_scores, q_heads)]
+    grad_q, grad_k, grad_v = [jnp.concatenate(value, 0).astype(bf16) for value in (grad_q, grad_k, grad_v)]
     unit, scale = normalise(x_in[...])
     normed = (unit * vector(vec, "gain_one") + vector(vec, "bias_one")).astype(bf16)
     g_q[...] += dot(normed, grad_q, 0, 0)
@@ -547,10 +581,11 @@
     add_row(sums_at["gain_one"], column_sums(grad_one * unit))
     add_row(sums_at["bias_one"], column_sums(grad_one))
     grad_x = grad_hidden + normalise_back(grad_one, vector(vec, "gain_one"), unit, scale)
-    g_pos[...] += grad_x
-    grad_emb = grad_x[0:PATCHES].astype(bf16)
-    g_patch[...] += dot(patches[...], grad_emb, 0, 0)
-    add_row(9, column_sums(grad_emb))
+    grad_emb = [grad_x[at.start : at.start + PATCHES].astype(bf16) for at in spans]
+    for i, at in enumerate(spans):
+        g_pos[...] += grad_x[at]
+        g_patch[...] += dot(patches[i], grad_emb[i], 0, 0)
+        add_row(9, column_sums(grad_emb[i]))
 
     @pl.when(step == pl.num_programs(0) - 1)
     def _():
@@ -570,7 +605,24 @@
         flat.write(token, CLS_TOKEN, 2, D)
         natural = jnp.concatenate([token, g_pos[0:PATCHES, :], jnp.zeros((1, D), f32)], 0)
         flat.write(natural, POS_EMBED, 3, D)
-        send_out(place, info, flat, grad_out)
+
+        section = lax.axis_index("section")
+
+        @pl.when(section == 0)
+        def _():
+            def store(at, value):
+                keep_out[at] = value
+                give_out[at] = late_grad[at]
+
+            send_out(place, flat, store)
+
+        @pl.when(section != 0)
+        def _():
+            def store(at, value):
+                give_out[at] = value
+                keep_out[at] = late_grad[at]
+
+            send_out(place, flat, store)
 
 
 def fetch_kernel(first, last, _, basis, kept, sem):
@@ -583,12 +635,10 @@
     total[...] = left[...] + right[...]
 
 
-def plane_kernel(depth, info, early, early_here, late, late_here, _, *refs):
+def plane_kernel(depth, own, _, *refs):
     arrived, (whole_out, *outs) = refs[:-depth], refs[-depth:]
     for d in range(depth):
-        first = early[d].astype(f32) + early_here[d].astype(f32)
-        second = late[d].astype(f32) + late_here[d].astype(f32)
-        total = jnp.where(info[0] == 0, first, second)
+        total = own[d]
         for ref in arrived:
             total = total + ref[d].astype(f32)
         if d == 0:
@@ -735,6 +785,129 @@
     )
 
 
+BLOCK_SHAPES = [(D, D)] * 4 + [(D, FF), (FF, D)]
+SAVED = [
+    ((ROWS, D), f32),
+    ((ROWS, D), bf16),
+    ((ROWS, D), bf16),
+    ((ROWS, D), bf16),
+    ((HEADS * ROWS, ROWS), f32),
+    ((ROWS, D), bf16),
+    ((ROWS, D), f32),
+    ((ROWS, FF), bf16),
+    ((ROWS, FF), f32),
+]
+MIDDLE = ((ROWS, D), bf16)
+WORK = pl.CostEstimate(flops=3_000_000_000, bytes_accessed=30_000_000, transcendentals=1_000_000)
+VMEM = pl.BlockSpec(memory_space=pltpu.VMEM)
+SMEM = pl.BlockSpec(memory_space=pltpu.SMEM)
+ANY = pl.BlockSpec(memory_space=pl.ANY)
+
+
+def group_of(per):
+    return GROUP if per % GROUP == 0 else 1
+
+
+def row_block(shape, per):
+    return pl.BlockSpec((group_of(per) * shape[0], shape[1]), lambda i, *_: (i, 0))
+
+
+def flat_scratch(place):
+    flat_rows = place.count * place.shard_rows + SPARE
+    return [
+        pltpu.VMEM((flat_rows, LANES), f32),
+        pltpu.VMEM((flat_rows, LANES), f32),
+        pltpu.VMEM((FF + 32, LANES), f32),
+    ]
+
+
+def patch_block(per):
+    return pl.BlockSpec((group_of(per), PATCHES, PDIM), lambda i, *_: (i, 0, 0))
+
+
+def front(place, per, own, other, patches):
+    outs = pl.pallas_call(
+        functools.partial(front_kernel, place),
+        grid_spec=pltpu.PrefetchScalarGridSpec(
+            num_scalar_prefetch=0,
+            grid=(per // group_of(per),),
+            in_specs=[whole(piece.shape) for piece in own + other] + [patch_block(per)],
+            out_specs=[row_block(shape, per) for shape, _ in SAVED + [MIDDLE]]
+            + [whole(shape) for shape in BLOCK_SHAPES]
+            + [whole((VEC_ROWS, FF))],
+            scratch_shapes=flat_scratch(place)
+            + [pltpu.VMEM((PDIM, D), bf16)]
+            + [pltpu.VMEM((group_of(per) * ROWS, D), f32)] * 2,
+        ),
+        out_shape=[
+            jax.ShapeDtypeStruct((per * shape[0], shape[1]), kind) for shape, kind in SAVED + [MIDDLE]
+        ]
+        + [jax.ShapeDtypeStruct(shape, bf16) for shape in BLOCK_SHAPES]
+        + [jax.ShapeDtypeStruct((VEC_ROWS, FF), f32)],
+        compiler_params=params(20),
+        cost_estimate=WORK,
+        name="front",
+    )(*own, *other, patches)
+    return outs[:9], outs[9], outs[10:]
+
+
+def grad_kind(place):
+    return jax.ShapeDtypeStruct((place.count, place.sent_rows, LANES), bf16)
+
+
+def late(place, per, image_total, labels, replay, own, other, middle, old_logits):
+    eight = -(-per // 8) * 8
+    return pl.pallas_call(
+        functools.partial(late_kernel, place, per, image_total),
+        in_specs=[SMEM] * 2 + [VMEM] * (len(own) + len(other) + 2),
+        out_specs=[VMEM] * 3,
+        out_shape=[
+            jax.ShapeDtypeStruct((per * ROWS, D), bf16),
+            grad_kind(place),
+            jax.ShapeDtypeStruct((1, LANES), f32),
+        ],
+        scratch_shapes=flat_scratch(place)
+        + [pltpu.VMEM((8, 256, LANES), f32)]
+        + [pltpu.VMEM(shape, bf16) for shape in BLOCK_SHAPES]
+        + [
+            pltpu.VMEM((VEC_ROWS, FF), f32),
+            pltpu.VMEM((D, CPAD), bf16),
+            pltpu.VMEM((1, CPAD), f32),
+            pltpu.VMEM((eight, D), f32),
+            pltpu.VMEM((per * ROWS, D), f32),
+        ],
+        compiler_params=pltpu.CompilerParams(vmem_limit_bytes=16 * 1024 * 1024),
+        cost_estimate=WORK,
+        name="late",
+    )(labels, replay, *own, *other, middle, old_logits)
+
+
+def back(place, per, grad_middle, kept, patches, weights, late_grad):
+    return pl.pallas_call(
+        functools.partial(back_kernel, place),
+        grid_spec=pltpu.PrefetchScalarGridSpec(
+            num_scalar_prefetch=0,
+            grid=(per // group_of(per),),
+            in_specs=[row_block(shape, per) for shape, _ in [MIDDLE] + SAVED]
+            + [patch_block(per)]
+            + [whole(shape) for shape in BLOCK_SHAPES]
+            + [whole((VEC_ROWS, FF)), whole(grad_kind(place).shape)],
+            out_specs=[whole(grad_kind(place).shape)] * 2,
+            scratch_shapes=flat_scratch(place)
+            + [pltpu.VMEM(shape, f32) for shape in BLOCK_SHAPES]
+            + [
+                pltpu.VMEM((PDIM, D), f32),
+                pltpu.VMEM((ROWS, D), f32),
+                pltpu.VMEM((VEC_ROWS, FF), f32),
+            ],
+        ),
+        out_shape=[grad_kind(place)] * 2,
+        compiler_params=params(20),
+        cost_estimate=WORK,
+        name="back",
+    )(grad_middle, *kept, patches, *weights, late_grad)
+
+
 def body(
     patches, labels, replay, old_logits, basis_count, master, first_moment, second_moment, basis
 ):
@@ -745,129 +918,47 @@
     images = patches.shape[0]
     per = images // 2
     section = lax.axis_index("section")
-    info = jnp.stack([section, lax.axis_index("dp")]).astype(jnp.int32)
-    flat_rows = chips * shard_rows + SPARE
     turns = place.turns()
 
-    shard = master[0].astype(bf16).reshape(shard_rows, LANES)
-    count = jnp.sum(replay).astype(bf16)
-    tail = jnp.full((place.sent_rows - shard_rows, LANES), count, bf16)
-    shard = jnp.concatenate([shard, tail], 0)
-    line = jnp.stack([shard] + [moved(shard, place, (d, 0, 0)) for d in range(1, place.z)])
-    own = [moved(line, place, (0, a, b)) if a + b else line for a, b in turns]
+    shard = pl.pallas_call(
+        shard_kernel,
+        grid=(1,),
+        in_specs=[SMEM, whole((shard_rows, LANES))],
+        out_specs=whole((place.sent_rows, LANES)),
+        out_shape=jax.ShapeDtypeStruct((place.sent_rows, LANES), bf16),
+        compiler_params=pltpu.CompilerParams(vmem_limit_bytes=2 * 1024 * 1024),
+        name="shard",
+    )(replay, master.reshape(shard_rows, LANES))
+    mine = lax.dynamic_slice_in_dim(patches, section * per, per, 0)
+    early, late_part = shard[: place.first_rows], shard[place.first_rows :]
+    column = [early] + [moved(early, place, (d, 0, 0)) for d in range(1, place.z)]
+    plane = [moved(late_part, place, (0, a, b)) if a + b else late_part for a, b in turns]
+    column[-1], mine = lax.optimization_barrier((column[-1], mine))
+    column, plane = jnp.stack(column), jnp.stack(plane)
+    own = [moved(column, place, (0, a, b)) if a + b else column for a, b in turns]
+    own += [moved(plane, place, (d, 0, 0)) if d else plane for d in range(place.z)]
     other = [moved(piece, place, core=1) for piece in own]
 
-    flat_scratch = [
-        pltpu.VMEM((flat_rows, LANES), f32),
-        pltpu.VMEM((flat_rows, LANES), f32),
-        pltpu.VMEM((FF + 32, LANES), f32),
-    ]
-    piece_specs = [whole(piece.shape) for piece in own + other]
-    block_shapes = [(D, D)] * 4 + [(D, FF), (FF, D)]
-    row_of = lambda i, *_: (i, 0)
-    saved = [
-        ((ROWS, D), f32),
-        ((ROWS, D), bf16),
-        ((ROWS, D), bf16),
-        ((ROWS, D), bf16),
-        ((HEADS * ROWS, ROWS), f32),
-        ((ROWS, D), bf16),
-        ((ROWS, D), f32),
-        ((ROWS, FF), bf16),
-        ((ROWS, FF), f32),
-    ]
-    middle_kind = ((ROWS, D), bf16)
-    patch_spec = pl.BlockSpec((None, PATCHES, PDIM), lambda i, info: (info[0] * per + i, 0, 0))
-    outs = pl.pallas_call(
-        functools.partial(front_kernel, place),
-        grid_spec=pltpu.PrefetchScalarGridSpec(
-            num_scalar_prefetch=1,
-            grid=(per,),
-            in_specs=piece_specs + [patch_spec],
-            out_specs=[pl.BlockSpec(shape, row_of) for shape, _ in saved + [middle_kind]]
-            + [whole(shape) for shape in block_shapes]
-            + [whole((VEC_ROWS, FF))],
-            scratch_shapes=flat_scratch
-            + [pltpu.VMEM((PDIM, D), bf16), pltpu.VMEM((ROWS, D), f32), pltpu.VMEM((ROWS, D), f32)],
-        ),
-        out_shape=[
-            jax.ShapeDtypeStruct((per * shape[0], shape[1]), kind) for shape, kind in saved + [middle_kind]
-        ]
-        + [jax.ShapeDtypeStruct(shape, bf16) for shape in block_shapes]
-        + [jax.ShapeDtypeStruct((VEC_ROWS, FF), f32)],
-        compiler_params=params(40),
-        name="front",
-    )(info, *own, *other, patches)
-    kept, middle, weights = outs[:9], outs[9], outs[10:]
-
-    grad_shape = jax.ShapeDtypeStruct((chips, place.sent_rows, LANES), bf16)
-    smem = pl.BlockSpec(memory_space=pltpu.SMEM)
-    vmem = pl.BlockSpec(memory_space=pltpu.VMEM)
-    eight = -(-per // 8) * 8
-    back, late_grad, loss = pl.pallas_call(
-        functools.partial(late_kernel, place, per, float(images * chips)),
-        in_specs=[smem] * 3 + [vmem] * (2 * len(turns) + 2),
-        out_specs=[vmem] * 3,
-        out_shape=[
-            jax.ShapeDtypeStruct((per * ROWS, D), bf16),
-            grad_shape,
-            jax.ShapeDtypeStruct((1, LANES), f32),
-        ],
-        scratch_shapes=flat_scratch
-        + [pltpu.VMEM((8, 256, LANES), f32)]
-        + [pltpu.VMEM(shape, bf16) for shape in block_shapes]
-        + [
-            pltpu.VMEM((VEC_ROWS, FF), f32),
-            pltpu.VMEM((D, CPAD), bf16),
-            pltpu.VMEM((1, CPAD), f32),
-            pltpu.VMEM((eight, D), f32),
-            pltpu.VMEM((per * ROWS, D), f32),
-        ],
-        compiler_params=pltpu.CompilerParams(vmem_limit_bytes=40 * 1024 * 1024),
-        name="late",
-    )(info, labels, replay, *own, *other, middle, old_logits)
-
-    early_grad = pl.pallas_call(
-        functools.partial(back_kernel, place),
-        grid_spec=pltpu.PrefetchScalarGridSpec(
-            num_scalar_prefetch=1,
-            grid=(per,),
-            in_specs=[pl.BlockSpec(shape, row_of) for shape, _ in [middle_kind] + saved]
-            + [patch_spec]
-            + [whole(shape) for shape in block_shapes]
-            + [whole((VEC_ROWS, FF))],
-            out_specs=whole(grad_shape.shape),
-            scratch_shapes=flat_scratch
-            + [pltpu.VMEM(shape, f32) for shape in block_shapes]
-            + [
-                pltpu.VMEM((PDIM, D), f32),
-                pltpu.VMEM((ROWS, D), f32),
-                pltpu.VMEM((VEC_ROWS, FF), f32),
-            ],
-        ),
-        out_shape=grad_shape,
-        compiler_params=params(48),
-        name="back",
-    )(info, back, *kept, patches, *weights)
-
-    late_here = moved(late_grad, place, core=1, sections=(0,))
-    early_here = moved(early_grad, place, core=1, sections=(1,))
+    kept, middle, weights = front(place, per, own, other, mine)
+    grad_middle, late_grad, loss = late(
+        place, per, float(images * chips), labels, replay, own, other, middle, old_logits
+    )
+    keep, give = back(place, per, grad_middle, kept, mine, weights, late_grad)
+
+    given = moved(give, place, core=1)
 
     def paired(turn):
         cut = slice(turn * place.z, (turn + 1) * place.z)
-        early = early_grad[cut].astype(f32) + early_here[cut].astype(f32)
-        late = late_grad[cut].astype(f32) + late_here[cut].astype(f32)
-        return jnp.where(section == 0, early, late)
-
-    leaving = [paired(turn).astype(bf16) for turn in range(1, len(turns))]
+        return keep[cut].astype(f32) + given[cut].astype(f32)
+
+    staying, leaving = paired(0), [paired(turn).astype(bf16) for turn in range(1, len(turns))]
     rows_basis = pltpu.with_memory_space_constraint(basis.reshape(KB, shard_len), pltpu.HBM)
-    hbm = pl.BlockSpec(memory_space=pl.ANY)
 
     def fetch(first, last, after):
         return pl.pallas_call(
             functools.partial(fetch_kernel, first, last),
-            in_specs=[hbm, pl.BlockSpec(memory_space=pltpu.HBM)],
-            out_specs=hbm,
+            in_specs=[ANY, ANY],
+            out_specs=ANY,
             out_shape=pltpu.VMEM((last - first, shard_len), bf16),
             scratch_shapes=[pltpu.SemaphoreType.DMA],
             compiler_params=pltpu.CompilerParams(vmem_limit_bytes=2 * 1024 * 1024),
@@ -882,12 +973,12 @@
     piece_shape = (place.sent_rows, LANES)
     first, *rest = pl.pallas_call(
         functools.partial(plane_kernel, place.z),
-        in_specs=[smem] + [vmem] * 4 + [hbm] + [vmem] * (len(turns) - 1),
-        out_specs=[vmem] * place.z,
+        in_specs=[VMEM, ANY] + [VMEM] * (len(turns) - 1),
+        out_specs=[VMEM] * place.z,
         out_shape=[jax.ShapeDtypeStruct(piece_shape, bf16 if d else f32) for d in range(place.z)],
         compiler_params=pltpu.CompilerParams(vmem_limit_bytes=2 * 1024 * 1024),
         name="plane",
-    )(info, early_grad, early_here, late_grad, late_here, upper, *arrived)
+    )(staying, upper, *arrived)
     resident = (upper, fetch(UPPER, KB, rest[0]))
     pieces = [moved(rest[d - 1], place, (d, 0, 0)) for d in range(1, place.z)]
 
@@ -897,8 +988,8 @@
     flat_kind = jax.ShapeDtypeStruct((shard_rows, LANES), f32)
     grad, sums = pl.pallas_call(
         functools.partial(inner_kernel, divisor(26)),
-        in_specs=[vmem] * (place.z + 3),
-        out_specs=[vmem] * 2,
+        in_specs=[VMEM] * (place.z + 3),
+        out_specs=[VMEM] * 2,
         out_shape=[flat_kind, jax.ShapeDtypeStruct((1, SUMS), f32)],
         scratch_shapes=[pltpu.VMEM((KB, LANES), f32)],
         compiler_params=pltpu.CompilerParams(vmem_limit_bytes=2 * 1024 * 1024),
@@ -908,8 +999,8 @@
     padded_rows = -(-shard_rows // 8) * 8
     loss_parts, norm, coefficients, new_master, new_first, new_second = pl.pallas_call(
         functools.partial(update_kernel, divisor(78), float(2 * shard_len * chips)),
-        in_specs=[smem] + [vmem] * 8,
-        out_specs=[smem, smem] + [vmem] * 4,
+        in_specs=[SMEM] + [VMEM] * 8,
+        out_specs=[SMEM, SMEM] + [VMEM] * 4,
         out_shape=[
             jax.ShapeDtypeStruct((3,), f32),
             jax.ShapeDtypeStruct((1,), f32),

time: 144 us -> 118 us (0.82)
  Pallas kernels: 61.3 us -> 48.9 us
  waiting for transfers between devices: 39.2 us -> 29.5 us
  starting transfers between devices: 31.2 us -> 35.3 us
  other arithmetic: 4.34 us -> 0.37 us
  local copies, waits for them, and re-layouts: 5.89 us -> 2.54 us
    pallas_call x7 -> x8, Pallas kernels: 54.8 us -> 42.4 us  [the longest x2 11.1 us: fetch(): pl.pallas_call(functools.partial(fetch_kernel, first, last), in_specs=[AN...]
    ppermute x19 -> x28, waiting for transfers between devices: 29 us -> 19.2 us  [moved(): return lax.ppermute(value, ('section', 'dp'), pairs)]
    ppermute x19 -> x28, starting transfers between devices: 26.2 us -> 30.4 us  [moved(): return lax.ppermute(value, ('section', 'dp'), pairs)]
    unnamed x31 -> x22, local copies, waits for them, and re-layouts: 5.88 us -> 1.77 us
    convert_element_type x2 -> x1, other arithmetic: 2.92 us -> 0.32 us  [body(): paired(turn).astype(bf16)]
  transfers between devices with their start and end apart: 23 -> 32, of which waited for: 15 -> 15; matrix products, arithmetic and copies ran while one was open for 2% -> 1% of each run, Pallas kernels for 8% -> 9%
where the time goes in v3:
time: 118 us
  Pallas kernels  48.9 us (41%)
  starting transfers between devices  35.3 us (30%)
  waiting for transfers between devices  29.5 us (25%)
  local copies, waits for them, and re-layouts  2.54 us (2%)
    ppermute x28, starting transfers between devices, moved(): return lax.ppermute(value, ('section', 'dp'), pairs)  30.4 us
    ppermute x28, waiting for transfers between devices, moved(): return lax.ppermute(value, ('section', 'dp'), pairs)  19.2 us
    pallas_call x2, Pallas kernels, fetch(): pl.pallas_call(functools.partial(fetch_kernel, first, last), in_specs=[AN...  11.1 us
    ppermute x4, waiting for transfers between devices, butterfly(): value = add(value, lax.ppermute(value, ('section', 'dp'), pairs), resident)  10.4 us
    pallas_call x1, Pallas kernels, back(): pl.pallas_call(functools.partial(back_kernel, place), grid_spec=pltpu.Pre...  9.34 us
    pallas_call x1, Pallas kernels, late(): pl.pallas_call(functools.partial(late_kernel, place, per, image_total), i...  7.77 us
    pallas_call x1, Pallas kernels, body(): pl.pallas_call(functools.partial(inner_kernel, divisor(26)), in_specs=[VM...  6.75 us
    pallas_call x1, Pallas kernels, front(): pl.pallas_call(functools.partial(front_kernel, place), grid_spec=pltpu.Pr...  6.7 us
  transfers between devices with their start and end apart: 32, of which 15 were waited for; matrix products, arithmetic and copies ran while one was open for 1% of the time, Pallas kernels for 9%

profile of v3, /device:TPU:0, one launch (start us, length us, event | category | flops | bytes accessed | tf_op | source)
XLA Modules:
  0.0 117.7 jit_solution(9120566284253050298)
XLA Ops:
  0.6 0.0 copy-start
  0.6 0.0 copy-start.2
  0.7 1.1 copy-done.2
  1.7 0.7 copy-done.6
  2.4 0.6 shard.1
  2.9 3.0 %collective-permute-start.7 = (bf16[112,128]{1,0:T(8,128)(2,1)S(1)}, bf16[112,128]{1,0:T(8,128)(2,1)S(1)}, u32[]{:S(2)}, u32[]{:S(2)}) collective-permute-start(bf16[112,128]{1,0:T(8,128)(2,1)S(1)} %get-tuple-element.83), channel_id=1, source_target_pairs={{0,2},{1,3},{2,0},{3,1},{4,6},{5,7},{6,4},{7,5},{8,10},{9,11},{10,... | collective-permute-start | bytes 86024 | tf_op jit(solution)/shard_map/ppermute | solution.py:747
  6.0 1.5 %collective-permute-start.6 = (bf16[112,128]{1,0:T(8,128)(2,1)S(1)}, bf16[112,128]{1,0:T(8,128)(2,1)S(1)}, u32[]{:S(2)}, u32[]{:S(2)}) collective-permute-start(bf16[112,128]{1,0:T(8,128)(2,1)S(1)} %get-tuple-element.83), channel_id=1, source_target_pairs={{0,1},{1,0},{2,3},{3,2},{4,5},{5,4},{6,7},{7,6},{8,9},{9,8},{10,11... | collective-permute-start | bytes 86024 | tf_op jit(solution)/shard_map/ppermute | solution.py:747
  7.5 0.0 collective-permute-start.8
  7.5 3.1 %collective-permute-start.1 = (bf16[208,128]{1,0:T(8,128)(2,1)S(1)}, bf16[208,128]{1,0:T(8,128)(2,1)S(1)}, u32[]{:S(2)}, u32[]{:S(2)}) collective-permute-start(bf16[208,128]{1,0:T(8,128)(2,1)S(1)} %get-tuple-element.85), channel_id=1, source_target_pairs={{0,8},{1,9},{2,10},{3,11},{4,12},{5,13},{6,14},{7,15},{8,0},{9,1},... | collective-permute-start | bytes 159752 | tf_op jit(solution)/shard_map/ppermute | solution.py:747
  10.6 1.6 %collective-permute-start = (bf16[208,128]{1,0:T(8,128)(2,1)S(1)}, bf16[208,128]{1,0:T(8,128)(2,1)S(1)}, u32[]{:S(2)}, u32[]{:S(2)}) collective-permute-start(bf16[208,128]{1,0:T(8,128)(2,1)S(1)} %get-tuple-element.85), channel_id=1, source_target_pairs={{0,4},{1,5},{2,6},{3,7},{4,8},{5,9},{6,10},{7,11},{8,12},{9,13},{1... | collective-permute-start | bytes 159752 | tf_op jit(solution)/shard_map/ppermute | solution.py:747
  12.2 0.6 constant_dynamic-slice_fusion
  12.8 0.1 copy.16.refs_16_.refs_10_
  13.0 2.3 %collective-permute-start.2 = (bf16[208,128]{1,0:T(8,128)(2,1)S(1)}, bf16[208,128]{1,0:T(8,128)(2,1)S(1)}, u32[]{:S(2)}, u32[]{:S(2)}) collective-permute-start(bf16[208,128]{1,0:T(8,128)(2,1)S(1)} %get-tuple-element.85), channel_id=1, source_target_pairs={{0,12},{1,13},{2,14},{3,15},{4,0},{5,1},{6,2},{7,3},{8,4},{9,5},{1... | collective-permute-start | bytes 159752 | tf_op jit(solution)/shard_map/ppermute | solution.py:747
  15.3 0.1 collective-permute-start.16
  15.4 0.6 collective-permute-start.11
  16.0 1.3 %collective-permute-done.2 = bf16[208,128]{1,0:T(8,128)(2,1)S(1)} collective-permute-done((bf16[208,128]{1,0:T(8,128)(2,1)S(1)}, bf16[208,128]{1,0:T(8,128)(2,1)S(1)}, u32[]{:S(2)}, u32[]{:S(2)}) %collective-permute-start.2) | collective-permute-done | bytes 53280 | tf_op jit(solution)/shard_map/ppermute | solution.py:747
  17.3 0.7 collective-permute-start.10
  18.0 0.0 copy-start.7
  18.0 0.0 copy-start.9
  18.0 0.0 copy-start.10
  18.0 2.8 %collective-permute-start.5 = (bf16[4,208,128]{2,1,0:T(8,128)(2,1)S(1)}, bf16[4,208,128]{2,1,0:T(8,128)(2,1)S(1)}, u32[]{:S(2)}, u32[]{:S(2)}) collective-permute-start(bf16[4,208,128]{2,1,0:T(8,128)(2,1)S(1)} %pad_maximum_fusion.refs_0_), channel_id=1, source_target_pairs={{0,3},{1,2},{2,1},{3,0},{4,7},{5,6},{6,5},{7,4},{8,11},{9,10},{10,... | collective-permute-start | bytes 638984 | tf_op jit(solution)/shard_map/ppermute | solution.py:747
  20.8 0.5 collective-permute-start.4
  21.3 0.3 collective-permute-start.3
  21.6 4.2 %collective-permute-start.9 = (bf16[4,112,128]{2,1,0:T(8,128)(2,1)S(1)}, bf16[4,112,128]{2,1,0:T(8,128)(2,1)S(1)}, u32[]{:S(2)}, u32[]{:S(2)}) collective-permute-start(bf16[4,112,128]{2,1,0:T(8,128)(2,1)S(1)} %pad_maximum_fusion.1.refs_4_), channel_id=1, source_target_pairs={{0,4},{1,5},{2,6},{3,7},{4,8},{5,9},{6,10},{7,11},{8,12},{9,13},{1... | collective-permute-start | bytes 344072 | tf_op jit(solution)/shard_map/ppermute | solution.py:747
  25.8 2.4 %collective-permute-done.9.refs_5_ = bf16[4,112,128]{2,1,0:T(8,128)(2,1)S(1)} collective-permute-done((bf16[4,112,128]{2,1,0:T(8,128)(2,1)S(1)}, bf16[4,112,128]{2,1,0:T(8,128)(2,1)S(1)}, u32[]{:S(2)}, u32[]{:S(2)}) %collective-permute-start.9) | collective-permute-done | bytes 114720 | tf_op jit(solution)/shard_map/ppermute | solution.py:747
  28.2 0.5 collective-permute-start.12
  28.7 0.1 collective-permute-start.15
  28.8 0.6 collective-permute-done.4.refs_2_
  29.3 0.1 collective-permute-done.3.refs_1_
  29.4 0.4 collective-permute-start.13
  29.8 0.1 collective-permute-start.17
  29.9 1.3 %collective-permute-done.17.refs_13_ = bf16[4,112,128]{2,1,0:T(8,128)(2,1)S(1)} collective-permute-done((bf16[4,112,128]{2,1,0:T(8,128)(2,1)S(1)}, bf16[4,112,128]{2,1,0:T(8,128)(2,1)S(1)}, u32[]{:S(2)}, u32[]{:S(2)}) %collective-permute-start.17) | collective-permute-done | bytes 114720 | tf_op jit(solution)/shard_map/ppermute | solution.py:747
  31.3 6.7 %front.1 = (f32[832,192]{1,0:T(8,128)S(1)}, bf16[832,192]{1,0:T(8,128)(2,1)S(1)}, bf16[832,192]{1,0:T(8,128)(2,1)S(1)}, bf16[832,192]{1,0:T(8,128)(2,1)S(1)}, f3...) custom-call(bf16[4,208,128]{2,1,0:T(8,128)(2,1)S(1)} %pad_maximum_fu, ...), custom_call_target="tpu_custom_call" | custom-call | flops 3000000000 | bytes 30000000 | tf_op jit(solution)/shard_map/front/pallas_call | solution.py:829
  38.0 7.8 %late.1 = (bf16[832,192]{1,0:T(8,128)(2,1)S(1)}, bf16[16,320,128]{2,1,0:T(8,128)(2,1)S(1)}, f32[1,128]{1,0:T(1,128)S(1)}) custom-call(s32[8]{0:T(128)S(1)} %copy-done.10, s32[8]{0:T(128)S(1)} %copy-done.7, bf16[4,208,128]{2,1,0:T(8,128)(2,1)S(1)} %pad_maximum_fusion.refs_0_, bf16[4,208,128]{2,1,0:T(8,128)(2,1)S(1)} %collective-permute-done.3.refs_1_, ...), custom_call_target="tpu_custom_call" | custom-call | flops 3000000000 | bytes 30000000 | tf_op jit(solution)/shard_map/late/pallas_call | solution.py:860
  45.8 9.3 %back.1 = (bf16[16,320,128]{2,1,0:T(8,128)(2,1)S(1)}, bf16[16,320,128]{2,1,0:T(8,128)(2,1)S(1)}) custom-call(bf16[832,192]{1,0:T(8,128)(2,1)S(1)} %get-tuple-element.45.refs_0_, f32[832,192]{1,0:T(8,128)S(1)} %get-tuple-element.46.refs_1_, bf16[832,192]{1,0:T(8,128)(2,1)S(1)} %get-tuple-element.47.refs_2_, bf16[832,192]{1,0:T(8,128)(2,1)S(1)} %get-tuple-element.48.refs_3_, ...), custom_call_target="tpu_custom_call" | custom-call | flops 3000000000 | bytes 30000000 | tf_op jit(solution)/shard_map/back/pallas_call | solution.py:886
  55.1 0.3 collective-permute-start.20
  55.4 2.8 %collective-permute-done.20 = bf16[16,320,128]{2,1,0:T(8,128)(2,1)S(1)} collective-permute-done((bf16[16,320,128]{2,1,0:T(8,128)(2,1)S(1)}, bf16[16,320,128]{2,1,0:T(8,128)(2,1)S(1)}, u32[]{:S(2)}, u32[]{:S(2)}) %collective-permute-start.20) | collective-permute-done | bytes 1310752 | tf_op jit(solution)/shard_map/ppermute | solution.py:747
  58.2 0.3 add_convert_fusion
  58.6 2.4 %collective-permute-start.23 = (bf16[4,320,128]{2,1,0:T(8,128)(2,1)S(1)}, bf16[4,320,128]{2,1,0:T(8,128)(2,1)S(1)}, u32[]{:S(2)}, u32[]{:S(2)}) collective-permute-start(bf16[4,320,128]{2,1,0:T(8,128)(2,1)S(1)} %get-tuple-element.78), channel_id=1, source_target_pairs={{0,3},{1,2},{2,1},{3,0},{4,7},{5,6},{6,5},{7,4},{8,11},{9,10},{10,... | collective-permute-start | bytes 983048 | tf_op jit(solution)/shard_map/ppermute | solution.py:747
  61.0 0.6 collective-permute-start.22
  61.6 0.5 collective-permute-start.21
  62.1 5.7 %fetch.2._.refs_4_.upper = bf16[208,39936]{1,0:T(8,128)(2,1)S(1)} custom-call(bf16[4,320,128]{2,1,0:T(8,128)(2,1)S(1)} %get-tuple-element.80._, bf16[400,39936]{1,0:T(8,128)(2,1)} %bitcast.22), custom_call_target="tpu_custom_call" | custom-call | bytes 33226752 | tf_op jit(solution)/shard_map/fetch/pallas_call | solution.py:958
  67.9 2.3 %collective-permute-done.23.refs_2_ = bf16[4,320,128]{2,1,0:T(8,128)(2,1)S(1)} collective-permute-done((bf16[4,320,128]{2,1,0:T(8,128)(2,1)S(1)}, bf16[4,320,128]{2,1,0:T(8,128)(2,1)S(1)}, u32[]{:S(2)}, u32[]{:S(2)}) %collective-permute-start.23) | collective-permute-done | bytes 327712 | tf_op jit(solution)/shard_map/ppermute | solution.py:747
  70.1 6.3 %collective-permute-done.22.refs_1_ = bf16[4,320,128]{2,1,0:T(8,128)(2,1)S(1)} collective-permute-done((bf16[4,320,128]{2,1,0:T(8,128)(2,1)S(1)}, bf16[4,320,128]{2,1,0:T(8,128)(2,1)S(1)}, u32[]{:S(2)}, u32[]{:S(2)}) %collective-permute-start.22) | collective-permute-done | bytes 327712 | tf_op jit(solution)/shard_map/ppermute | solution.py:747
  76.4 0.1 collective-permute-done.21.refs_0_
  76.5 0.1 plane.1
  76.7 2.2 %collective-permute-start.25 = (bf16[320,128]{1,0:T(8,128)(2,1)S(1)}, bf16[320,128]{1,0:T(8,128)(2,1)S(1)}, u32[]{:S(2)}, u32[]{:S(2)}) collective-permute-start(bf16[320,128]{1,0:T(8,128)(2,1)S(1)} %get-tuple-element.67), channel_id=1, source_target_pairs={{0,8},{1,9},{2,10},{3,11},{4,12},{5,13},{6,14},{7,15},{8,0},{9,1},... | collective-permute-start | bytes 245768 | tf_op jit(solution)/shard_map/ppermute | solution.py:747
  78.9 2.6 %collective-permute-start.26 = (bf16[320,128]{1,0:T(8,128)(2,1)S(1)}, bf16[320,128]{1,0:T(8,128)(2,1)S(1)}, u32[]{:S(2)}, u32[]{:S(2)}) collective-permute-start(bf16[320,128]{1,0:T(8,128)(2,1)S(1)} %get-tuple-element.68), channel_id=1, source_target_pairs={{0,12},{1,13},{2,14},{3,15},{4,0},{5,1},{6,2},{7,3},{8,4},{9,5},{1... | collective-permute-start | bytes 245768 | tf_op jit(solution)/shard_map/ppermute | solution.py:747
  81.4 5.4 %fetch.3.refs_5_.__.lower = bf16[192,39936]{1,0:T(8,128)(2,1)S(1)} custom-call(bf16[320,128]{1,0:T(8,128)(2,1)S(1)} %get-tuple-element.66._, bf16[400,39936]{1,0:T(8,128)(2,1)} %bitcast.23), custom_call_target="tpu_custom_call" | custom-call | bytes 30670848 | tf_op jit(solution)/shard_map/fetch/pallas_call | solution.py:958
  86.8 0.8 collective-permute-done.24.refs_1_
  87.7 6.8 %inner.1 = (f32[312,128]{1,0:T(8,128)S(1)}, f32[1,512]{1,0:T(1,128)S(1)}) custom-call(f32[320,128]{1,0:T(8,128)S(1)} %get-tuple-element.65.refs_0_, bf16[320,128]{1,0:T(8,128)(2,1)S(1)} %collective-permute-done.24.refs_1_, bf16[320,128]{1,0:T(8,128)(2,1)S(1)} %collective-permute-done.25.refs_2_, bf16[320,128]{1,0:T(8,128)(2,1)S(1)} %collective-permute-done.26.refs_3_, ...), custom_call_target="tpu_custom_call" | custom-call | tf_op jit(solution)/shard_map/inner/pallas_call | solution.py:989
  94.4 0.1 collective-permute-start.27
  94.5 1.1 collective-permute-done.27.right
  95.6 1.5 %collective-permute-start.28 = (f32[1,512]{1,0:T(1,128)S(1)}, f32[1,512]{1,0:T(1,128)S(1)}, u32[]{:S(2)}, u32[]{:S(2)}) collective-permute-start(f32[1,512]{1,0:T(1,128)S(1)} %add.29.left), channel_id=1, source_target_pairs={{0,1},{1,0},{2,3},{3,2},{4,5},{5,4},{6,7},{7,6},{8,9},{9,8},{10,11... | collective-permute-start | bytes 6152 | tf_op jit(solution)/shard_map/ppermute | solution.py:773
  97.1 2.1 %collective-permute-done.28.right = f32[1,512]{1,0:T(1,128)S(1)} collective-permute-done((f32[1,512]{1,0:T(1,128)S(1)}, f32[1,512]{1,0:T(1,128)S(1)}, u32[]{:S(2)}, u32[]{:S(2)}) %collective-permute-start.28) | collective-permute-done | bytes 2080 | tf_op jit(solution)/shard_map/ppermute | solution.py:773
  99.2 1.4 %collective-permute-start.29 = (f32[1,512]{1,0:T(1,128)S(1)}, f32[1,512]{1,0:T(1,128)S(1)}, u32[]{:S(2)}, u32[]{:S(2)}) collective-permute-start(f32[1,512]{1,0:T(1,128)S(1)} %add.30.left), channel_id=1, source_target_pairs={{0,2},{1,3},{2,0},{3,1},{4,6},{5,7},{6,4},{7,5},{8,10},{9,11},{10,... | collective-permute-start | bytes 6152 | tf_op jit(solution)/shard_map/ppermute | solution.py:773
  100.7 2.2 %collective-permute-done.29.right = f32[1,512]{1,0:T(1,128)S(1)} collective-permute-done((f32[1,512]{1,0:T(1,128)S(1)}, f32[1,512]{1,0:T(1,128)S(1)}, u32[]{:S(2)}, u32[]{:S(2)}) %collective-permute-start.29) | collective-permute-done | bytes 2080 | tf_op jit(solution)/shard_map/ppermute | solution.py:773
  102.8 0.2 collective-permute-start.30
  103.0 3.4 %collective-permute-done.30.right = f32[1,512]{1,0:T(1,128)S(1)} collective-permute-done((f32[1,512]{1,0:T(1,128)S(1)}, f32[1,512]{1,0:T(1,128)S(1)}, u32[]{:S(2)}, u32[]{:S(2)}) %collective-permute-start.30) | collective-permute-done | bytes 2080 | tf_op jit(solution)/shard_map/ppermute | solution.py:773
  106.4 0.0 copy-start.5
  106.4 1.8 %collective-permute-start.31 = (f32[1,512]{1,0:T(1,128)S(1)}, f32[1,512]{1,0:T(1,128)S(1)}, u32[]{:S(2)}, u32[]{:S(2)}) collective-permute-start(f32[1,512]{1,0:T(1,128)S(1)} %add.32.left), channel_id=1, source_target_pairs={{0,8},{1,9},{2,10},{3,11},{4,12},{5,13},{6,14},{7,15},{8,0},{9,1},... | collective-permute-start | bytes 6152 | tf_op jit(solution)/shard_map/ppermute | solution.py:773
  108.3 2.7 %collective-permute-done.31.right = f32[1,512]{1,0:T(1,128)S(1)} collective-permute-done((f32[1,512]{1,0:T(1,128)S(1)}, f32[1,512]{1,0:T(1,128)S(1)}, u32[]{:S(2)}, u32[]{:S(2)}) %collective-permute-start.31) | collective-permute-done | bytes 2080 | tf_op jit(solution)/shard_map/ppermute | solution.py:773
  111.0 0.0 copy-start.1
  111.0 6.5 %update.1 = (f32[3]{0:T(128)}, f32[1]{0:T(128)}, f32[2,200]{1,0:T(2,128)}, f32[312,128]{1,0:T(8,128)}, f32[312,128]{1,0:T(8,128)}, /*index=5*/f32[312,128]{1,0:T(8,128)}) custom-call(s32[2]{0:T(128)S(1)} %copy-done.8, f32[1,512]{1,0:T(1,128)S(1)} %add.33.sums, bf16[208,39936]{1,0:T(8,128)(2,1)S(1)} %fetch.2._.refs_4_.upper, ...), custom_call_target="tpu_custom_call" | custom-call | tf_op jit(solution)/shard_map/update/pallas_call | solution.py:1000
  (43 shorter events, 0.2 us)
Async XLA Ops:
  0.6 11.6 %copy-start = (bf16[8,196,768]{2,0,1:T(8,128)(2,1)S(1)}, bf16[8,196,768]{2,0,1:T(8,128)(2,1)}, u32[]{:S(2)}) copy-start(bf16[8,196,768]{2,0,1:T(8,128)(2,1)} %param.9) | copy-start | bytes 7225348
  0.6 1.1 copy-start.2
  1.7 0.7 copy-start.6
  2.9 10.0 %collective-permute-start.7 = (bf16[112,128]{1,0:T(8,128)(2,1)S(1)}, bf16[112,128]{1,0:T(8,128)(2,1)S(1)}, u32[]{:S(2)}, u32[]{:S(2)}) collective-permute-start(bf16[112,128]{1,0:T(8,128)(2,1)S(1)} %get-tuple-element.83), channel_id=1, source_target_pairs={{0,2},{1,3},{2,0},{3,1},{4,6},{5,7},{6,4},{7,5},{8,10},{9,11},{10,... | collective-permute-start | bytes 86024 | tf_op jit(solution)/shard_map/ppermute | solution.py:747
  6.0 9.3 %collective-permute-start.6 = (bf16[112,128]{1,0:T(8,128)(2,1)S(1)}, bf16[112,128]{1,0:T(8,128)(2,1)S(1)}, u32[]{:S(2)}, u32[]{:S(2)}) collective-permute-start(bf16[112,128]{1,0:T(8,128)(2,1)S(1)} %get-tuple-element.83), channel_id=1, source_target_pairs={{0,1},{1,0},{2,3},{3,2},{4,5},{5,4},{6,7},{7,6},{8,9},{9,8},{10,11... | collective-permute-start | bytes 86024 | tf_op jit(solution)/shard_map/ppermute | solution.py:747
  7.5 7.8 %collective-permute-start.8 = (bf16[112,128]{1,0:T(8,128)(2,1)S(1)}, bf16[112,128]{1,0:T(8,128)(2,1)S(1)}, u32[]{:S(2)}, u32[]{:S(2)}) collective-permute-start(bf16[112,128]{1,0:T(8,128)(2,1)S(1)} %get-tuple-element.83), channel_id=1, source_target_pairs={{0,3},{1,2},{2,1},{3,0},{4,7},{5,6},{6,5},{7,4},{8,11},{9,10},{10,... | collective-permute-start | bytes 86024 | tf_op jit(solution)/shard_map/ppermute | solution.py:747
  7.5 10.4 %collective-permute-start.1 = (bf16[208,128]{1,0:T(8,128)(2,1)S(1)}, bf16[208,128]{1,0:T(8,128)(2,1)S(1)}, u32[]{:S(2)}, u32[]{:S(2)}) collective-permute-start(bf16[208,128]{1,0:T(8,128)(2,1)S(1)} %get-tuple-element.85), channel_id=1, source_target_pairs={{0,8},{1,9},{2,10},{3,11},{4,12},{5,13},{6,14},{7,15},{8,0},{9,1},... | collective-permute-start | bytes 159752 | tf_op jit(solution)/shard_map/ppermute | solution.py:747
  10.6 7.3 %collective-permute-start = (bf16[208,128]{1,0:T(8,128)(2,1)S(1)}, bf16[208,128]{1,0:T(8,128)(2,1)S(1)}, u32[]{:S(2)}, u32[]{:S(2)}) collective-permute-start(bf16[208,128]{1,0:T(8,128)(2,1)S(1)} %get-tuple-element.85), channel_id=1, source_target_pairs={{0,4},{1,5},{2,6},{3,7},{4,8},{5,9},{6,10},{7,11},{8,12},{9,13},{1... | collective-permute-start | bytes 159752 | tf_op jit(solution)/shard_map/ppermute | solution.py:747
  13.0 4.3 %collective-permute-start.2 = (bf16[208,128]{1,0:T(8,128)(2,1)S(1)}, bf16[208,128]{1,0:T(8,128)(2,1)S(1)}, u32[]{:S(2)}, u32[]{:S(2)}) collective-permute-start(bf16[208,128]{1,0:T(8,128)(2,1)S(1)} %get-tuple-element.85), channel_id=1, source_target_pairs={{0,12},{1,13},{2,14},{3,15},{4,0},{5,1},{6,2},{7,3},{8,4},{9,5},{1... | collective-permute-start | bytes 159752 | tf_op jit(solution)/shard_map/ppermute | solution.py:747
  15.3 6.0 %collective-permute-start.16 = (bf16[4,112,128]{2,1,0:T(8,128)(2,1)S(1)}, bf16[4,112,128]{2,1,0:T(8,128)(2,1)S(1)}, u32[]{:S(2)}, u32[]{:S(2)}) collective-permute-start(bf16[4,112,128]{2,1,0:T(8,128)(2,1)S(1)} %pad_maximum_fusion.1.refs_4_), channel_id=1, source_target_pairs={{0,16},{1,17},{2,18},{3,19},{4,20},{5,21},{6,22},{7,23},{8,24},{9,... | collective-permute-start | bytes 344072 | tf_op jit(solution)/shard_map/ppermute | solution.py:747
  15.4 6.2 %collective-permute-start.11 = (bf16[4,112,128]{2,1,0:T(8,128)(2,1)S(1)}, bf16[4,112,128]{2,1,0:T(8,128)(2,1)S(1)}, u32[]{:S(2)}, u32[]{:S(2)}) collective-permute-start(bf16[4,112,128]{2,1,0:T(8,128)(2,1)S(1)} %pad_maximum_fusion.1.refs_4_), channel_id=1, source_target_pairs={{0,12},{1,13},{2,14},{3,15},{4,0},{5,1},{6,2},{7,3},{8,4},{9,5},{1... | collective-permute-start | bytes 344072 | tf_op jit(solution)/shard_map/ppermute | solution.py:747
  17.3 8.5 %collective-permute-start.10 = (bf16[4,112,128]{2,1,0:T(8,128)(2,1)S(1)}, bf16[4,112,128]{2,1,0:T(8,128)(2,1)S(1)}, u32[]{:S(2)}, u32[]{:S(2)}) collective-permute-start(bf16[4,112,128]{2,1,0:T(8,128)(2,1)S(1)} %pad_maximum_fusion.1.refs_4_), channel_id=1, source_target_pairs={{0,8},{1,9},{2,10},{3,11},{4,12},{5,13},{6,14},{7,15},{8,0},{9,1},... | collective-permute-start | bytes 344072 | tf_op jit(solution)/shard_map/ppermute | solution.py:747
  18.0 20.0 %copy-start.7 = (s32[8]{0:T(128)S(1)}, s32[8]{0:T(128)}, u32[]{:S(2)}) copy-start(s32[8]{0:T(128)} %replay.3) | copy-start | bytes 100
  18.0 20.0 %copy-start.9 = (f32[8,1000]{1,0:T(8,128)S(1)}, f32[8,1000]{1,0:T(8,128)}, u32[]{:S(2)}) copy-start(f32[8,1000]{1,0:T(8,128)} %refs_17_.1) | copy-start | bytes 96004
  18.0 20.0 %copy-start.10 = (s32[8]{0:T(128)S(1)}, s32[8]{0:T(128)}, u32[]{:S(2)}) copy-start(s32[8]{0:T(128)} %labels.1) | copy-start | bytes 100
  18.0 10.7 %collective-permute-start.5 = (bf16[4,208,128]{2,1,0:T(8,128)(2,1)S(1)}, bf16[4,208,128]{2,1,0:T(8,128)(2,1)S(1)}, u32[]{:S(2)}, u32[]{:S(2)}) collective-permute-start(bf16[4,208,128]{2,1,0:T(8,128)(2,1)S(1)} %pad_maximum_fusion.refs_0_), channel_id=1, source_target_pairs={{0,3},{1,2},{2,1},{3,0},{4,7},{5,6},{6,5},{7,4},{8,11},{9,10},{10,... | collective-permute-start | bytes 638984 | tf_op jit(solution)/shard_map/ppermute | solution.py:747
  20.8 8.5 %collective-permute-start.4 = (bf16[4,208,128]{2,1,0:T(8,128)(2,1)S(1)}, bf16[4,208,128]{2,1,0:T(8,128)(2,1)S(1)}, u32[]{:S(2)}, u32[]{:S(2)}) collective-permute-start(bf16[4,208,128]{2,1,0:T(8,128)(2,1)S(1)} %pad_maximum_fusion.refs_0_), channel_id=1, source_target_pairs={{0,2},{1,3},{2,0},{3,1},{4,6},{5,7},{6,4},{7,5},{8,10},{9,11},{10,... | collective-permute-start | bytes 638984 | tf_op jit(solution)/shard_map/ppermute | solution.py:747
  21.3 8.1 %collective-permute-start.3 = (bf16[4,208,128]{2,1,0:T(8,128)(2,1)S(1)}, bf16[4,208,128]{2,1,0:T(8,128)(2,1)S(1)}, u32[]{:S(2)}, u32[]{:S(2)}) collective-permute-start(bf16[4,208,128]{2,1,0:T(8,128)(2,1)S(1)} %pad_maximum_fusion.refs_0_), channel_id=1, source_target_pairs={{0,1},{1,0},{2,3},{3,2},{4,5},{5,4},{6,7},{7,6},{8,9},{9,8},{10,11... | collective-permute-start | bytes 638984 | tf_op jit(solution)/shard_map/ppermute | solution.py:747
  21.6 6.6 %collective-permute-start.9 = (bf16[4,112,128]{2,1,0:T(8,128)(2,1)S(1)}, bf16[4,112,128]{2,1,0:T(8,128)(2,1)S(1)}, u32[]{:S(2)}, u32[]{:S(2)}) collective-permute-start(bf16[4,112,128]{2,1,0:T(8,128)(2,1)S(1)} %pad_maximum_fusion.1.refs_4_), channel_id=1, source_target_pairs={{0,4},{1,5},{2,6},{3,7},{4,8},{5,9},{6,10},{7,11},{8,12},{9,13},{1... | collective-permute-start | bytes 344072 | tf_op jit(solution)/shard_map/ppermute | solution.py:747
  25.8 2.4 %collective-permute-start.19 = (bf16[4,112,128]{2,1,0:T(8,128)(2,1)S(1)}, bf16[4,112,128]{2,1,0:T(8,128)(2,1)S(1)}, u32[]{:S(2)}, u32[]{:S(2)}) collective-permute-start(bf16[4,112,128]{2,1,0:T(8,128)(2,1)S(1)} %collective-permute-done.11.refs_7_), channel_id=1, source_target_pairs={{0,16},{1,17},{2,18},{3,19},{4,20},{5,21},{6,22},{7,23},{8,24},{9,... | collective-permute-start | bytes 344072 | tf_op jit(solution)/shard_map/ppermute | solution.py:747
  28.2 1.7 %collective-permute-start.18 = (bf16[4,112,128]{2,1,0:T(8,128)(2,1)S(1)}, bf16[4,112,128]{2,1,0:T(8,128)(2,1)S(1)}, u32[]{:S(2)}, u32[]{:S(2)}) collective-permute-start(bf16[4,112,128]{2,1,0:T(8,128)(2,1)S(1)} %collective-permute-done.10.refs_6_), channel_id=1, source_target_pairs={{0,16},{1,17},{2,18},{3,19},{4,20},{5,21},{6,22},{7,23},{8,24},{9,... | collective-permute-start | bytes 344072 | tf_op jit(solution)/shard_map/ppermute | solution.py:747
  28.2 3.1 %collective-permute-start.12 = (bf16[4,208,128]{2,1,0:T(8,128)(2,1)S(1)}, bf16[4,208,128]{2,1,0:T(8,128)(2,1)S(1)}, u32[]{:S(2)}, u32[]{:S(2)}) collective-permute-start(bf16[4,208,128]{2,1,0:T(8,128)(2,1)S(1)} %pad_maximum_fusion.refs_0_), channel_id=1, source_target_pairs={{0,16},{1,17},{2,18},{3,19},{4,20},{5,21},{6,22},{7,23},{8,24},{9,... | collective-permute-start | bytes 638984 | tf_op jit(solution)/shard_map/ppermute | solution.py:747
  28.7 2.6 %collective-permute-start.15 = (bf16[4,208,128]{2,1,0:T(8,128)(2,1)S(1)}, bf16[4,208,128]{2,1,0:T(8,128)(2,1)S(1)}, u32[]{:S(2)}, u32[]{:S(2)}) collective-permute-start(bf16[4,208,128]{2,1,0:T(8,128)(2,1)S(1)} %collective-permute-done.5.refs_3_), channel_id=1, source_target_pairs={{0,16},{1,17},{2,18},{3,19},{4,20},{5,21},{6,22},{7,23},{8,24},{9,... | collective-permute-start | bytes 638984 | tf_op jit(solution)/shard_map/ppermute | solution.py:747
  29.3 1.9 %collective-permute-start.14 = (bf16[4,208,128]{2,1,0:T(8,128)(2,1)S(1)}, bf16[4,208,128]{2,1,0:T(8,128)(2,1)S(1)}, u32[]{:S(2)}, u32[]{:S(2)}) collective-permute-start(bf16[4,208,128]{2,1,0:T(8,128)(2,1)S(1)} %collective-permute-done.4.refs_2_), channel_id=1, source_target_pairs={{0,16},{1,17},{2,18},{3,19},{4,20},{5,21},{6,22},{7,23},{8,24},{9,... | collective-permute-start | bytes 638984 | tf_op jit(solution)/shard_map/ppermute | solution.py:747
  29.4 1.8 %collective-permute-start.13 = (bf16[4,208,128]{2,1,0:T(8,128)(2,1)S(1)}, bf16[4,208,128]{2,1,0:T(8,128)(2,1)S(1)}, u32[]{:S(2)}, u32[]{:S(2)}) collective-permute-start(bf16[4,208,128]{2,1,0:T(8,128)(2,1)S(1)} %collective-permute-done.3.refs_1_), channel_id=1, source_target_pairs={{0,16},{1,17},{2,18},{3,19},{4,20},{5,21},{6,22},{7,23},{8,24},{9,... | collective-permute-start | bytes 638984 | tf_op jit(solution)/shard_map/ppermute | solution.py:747
  29.8 1.4 %collective-permute-start.17 = (bf16[4,112,128]{2,1,0:T(8,128)(2,1)S(1)}, bf16[4,112,128]{2,1,0:T(8,128)(2,1)S(1)}, u32[]{:S(2)}, u32[]{:S(2)}) collective-permute-start(bf16[4,112,128]{2,1,0:T(8,128)(2,1)S(1)} %collective-permute-done.9.refs_5_), channel_id=1, source_target_pairs={{0,16},{1,17},{2,18},{3,19},{4,20},{5,21},{6,22},{7,23},{8,24},{9,... | collective-permute-start | bytes 344072 | tf_op jit(solution)/shard_map/ppermute | solution.py:747
  55.1 3.1 %collective-permute-start.20 = (bf16[16,320,128]{2,1,0:T(8,128)(2,1)S(1)}, bf16[16,320,128]{2,1,0:T(8,128)(2,1)S(1)}, u32[]{:S(2)}, u32[]{:S(2)}) collective-permute-start(bf16[16,320,128]{2,1,0:T(8,128)(2,1)S(1)} %get-tuple-element.64), channel_id=1, source_target_pairs={{0,16},{1,17},{2,18},{3,19},{4,20},{5,21},{6,22},{7,23},{8,24},{9,... | collective-permute-start | bytes 3932168 | tf_op jit(solution)/shard_map/ppermute | solution.py:747
  58.6 11.6 %collective-permute-start.23 = (bf16[4,320,128]{2,1,0:T(8,128)(2,1)S(1)}, bf16[4,320,128]{2,1,0:T(8,128)(2,1)S(1)}, u32[]{:S(2)}, u32[]{:S(2)}) collective-permute-start(bf16[4,320,128]{2,1,0:T(8,128)(2,1)S(1)} %get-tuple-element.78), channel_id=1, source_target_pairs={{0,3},{1,2},{2,1},{3,0},{4,7},{5,6},{6,5},{7,4},{8,11},{9,10},{10,... | collective-permute-start | bytes 983048 | tf_op jit(solution)/shard_map/ppermute | solution.py:747
  61.0 15.4 %collective-permute-start.22 = (bf16[4,320,128]{2,1,0:T(8,128)(2,1)S(1)}, bf16[4,320,128]{2,1,0:T(8,128)(2,1)S(1)}, u32[]{:S(2)}, u32[]{:S(2)}) collective-permute-start(bf16[4,320,128]{2,1,0:T(8,128)(2,1)S(1)} %get-tuple-element.79), channel_id=1, source_target_pairs={{0,2},{1,3},{2,0},{3,1},{4,6},{5,7},{6,4},{7,5},{8,10},{9,11},{10,... | collective-permute-start | bytes 983048 | tf_op jit(solution)/shard_map/ppermute | solution.py:747
  61.6 14.9 %collective-permute-start.21 = (bf16[4,320,128]{2,1,0:T(8,128)(2,1)S(1)}, bf16[4,320,128]{2,1,0:T(8,128)(2,1)S(1)}, u32[]{:S(2)}, u32[]{:S(2)}) collective-permute-start(bf16[4,320,128]{2,1,0:T(8,128)(2,1)S(1)} %get-tuple-element.80._), channel_id=1, source_target_pairs={{0,1},{1,0},{2,3},{3,2},{4,5},{5,4},{6,7},{7,6},{8,9},{9,8},{10,11... | collective-permute-start | bytes 983048 | tf_op jit(solution)/shard_map/ppermute | solution.py:747
  76.7 10.1 %collective-permute-start.25 = (bf16[320,128]{1,0:T(8,128)(2,1)S(1)}, bf16[320,128]{1,0:T(8,128)(2,1)S(1)}, u32[]{:S(2)}, u32[]{:S(2)}) collective-permute-start(bf16[320,128]{1,0:T(8,128)(2,1)S(1)} %get-tuple-element.67), channel_id=1, source_target_pairs={{0,8},{1,9},{2,10},{3,11},{4,12},{5,13},{6,14},{7,15},{8,0},{9,1},... | collective-permute-start | bytes 245768 | tf_op jit(solution)/shard_map/ppermute | solution.py:747
  78.9 8.0 %collective-permute-start.26 = (bf16[320,128]{1,0:T(8,128)(2,1)S(1)}, bf16[320,128]{1,0:T(8,128)(2,1)S(1)}, u32[]{:S(2)}, u32[]{:S(2)}) collective-permute-start(bf16[320,128]{1,0:T(8,128)(2,1)S(1)} %get-tuple-element.68), channel_id=1, source_target_pairs={{0,12},{1,13},{2,14},{3,15},{4,0},{5,1},{6,2},{7,3},{8,4},{9,5},{1... | collective-permute-start | bytes 245768 | tf_op jit(solution)/shard_map/ppermute | solution.py:747
  81.4 6.2 %collective-permute-start.24 = (bf16[320,128]{1,0:T(8,128)(2,1)S(1)}, bf16[320,128]{1,0:T(8,128)(2,1)S(1)}, u32[]{:S(2)}, u32[]{:S(2)}) collective-permute-start(bf16[320,128]{1,0:T(8,128)(2,1)S(1)} %get-tuple-element.66._), channel_id=1, source_target_pairs={{0,4},{1,5},{2,6},{3,7},{4,8},{5,9},{6,10},{7,11},{8,12},{9,13},{1... | collective-permute-start | bytes 245768 | tf_op jit(solution)/shard_map/ppermute | solution.py:747
  94.4 1.2 %collective-permute-start.27 = (f32[1,512]{1,0:T(1,128)S(1)}, f32[1,512]{1,0:T(1,128)S(1)}, u32[]{:S(2)}, u32[]{:S(2)}) collective-permute-start(f32[1,512]{1,0:T(1,128)S(1)} %get-tuple-element.70.left), channel_id=1, source_target_pairs={{0,16},{1,17},{2,18},{3,19},{4,20},{5,21},{6,22},{7,23},{8,24},{9,... | collective-permute-start | bytes 6152 | tf_op jit(solution)/shard_map/ppermute | solution.py:747
  95.6 3.6 %collective-permute-start.28 = (f32[1,512]{1,0:T(1,128)S(1)}, f32[1,512]{1,0:T(1,128)S(1)}, u32[]{:S(2)}, u32[]{:S(2)}) collective-permute-start(f32[1,512]{1,0:T(1,128)S(1)} %add.29.left), channel_id=1, source_target_pairs={{0,1},{1,0},{2,3},{3,2},{4,5},{5,4},{6,7},{7,6},{8,9},{9,8},{10,11... | collective-permute-start | bytes 6152 | tf_op jit(solution)/shard_map/ppermute | solution.py:773
  99.2 3.6 %collective-permute-start.29 = (f32[1,512]{1,0:T(1,128)S(1)}, f32[1,512]{1,0:T(1,128)S(1)}, u32[]{:S(2)}, u32[]{:S(2)}) collective-permute-start(f32[1,512]{1,0:T(1,128)S(1)} %add.30.left), channel_id=1, source_target_pairs={{0,2},{1,3},{2,0},{3,1},{4,6},{5,7},{6,4},{7,5},{8,10},{9,11},{10,... | collective-permute-start | bytes 6152 | tf_op jit(solution)/shard_map/ppermute | solution.py:773
  102.8 3.6 %collective-permute-start.30 = (f32[1,512]{1,0:T(1,128)S(1)}, f32[1,512]{1,0:T(1,128)S(1)}, u32[]{:S(2)}, u32[]{:S(2)}) collective-permute-start(f32[1,512]{1,0:T(1,128)S(1)} %add.31.left), channel_id=1, source_target_pairs={{0,4},{1,5},{2,6},{3,7},{4,0},{5,1},{6,2},{7,3},{8,12},{9,13},{10,... | collective-permute-start | bytes 6152 | tf_op jit(solution)/shard_map/ppermute | solution.py:773
  106.4 4.6 %copy-start.3 = (f32[1,39936]{1,0:T(1,128)S(1)}, f32[1,39936]{1,0:T(1,128)}, u32[]{:S(2)}) copy-start(f32[1,39936]{1,0:T(1,128)} %param.14) | copy-start | bytes 479236
  106.4 4.6 %copy-start.4 = (f32[1,39936]{1,0:T(1,128)S(1)}, f32[1,39936]{1,0:T(1,128)}, u32[]{:S(2)}) copy-start(f32[1,39936]{1,0:T(1,128)} %param.15) | copy-start | bytes 479236
  106.4 4.6 %copy-start.5 = (f32[1,39936]{1,0:T(1,128)S(1)}, f32[1,39936]{1,0:T(1,128)}, u32[]{:S(2)}) copy-start(f32[1,39936]{1,0:T(1,128)} %param.16) | copy-start | bytes 479236
  106.4 4.6 %copy-start.8 = (s32[2]{0:T(128)S(1)}, s32[2]{0:T(128)}, u32[]{:S(2)}) copy-start(s32[2]{0:T(128)} %counts.1) | copy-start | bytes 28
  106.4 4.5 %collective-permute-start.31 = (f32[1,512]{1,0:T(1,128)S(1)}, f32[1,512]{1,0:T(1,128)S(1)}, u32[]{:S(2)}, u32[]{:S(2)}) collective-permute-start(f32[1,512]{1,0:T(1,128)S(1)} %add.32.left), channel_id=1, source_target_pairs={{0,8},{1,9},{2,10},{3,11},{4,12},{5,13},{6,14},{7,15},{8,0},{9,1},... | collective-permute-start | bytes 6152 | tf_op jit(solution)/shard_map/ppermute | solution.py:773
  111.0 6.5 %copy-start.1 = (bf16[8,196,768]{2,0,1:T(8,128)(2,1)S(1)}, bf16[8,196,768]{2,0,1:T(8,128)(2,1)}, u32[]{:S(2)}) copy-start(bf16[8,196,768]{2,0,1:T(8,128)(2,1)} %param.9) | copy-start | bytes 7225348

commit v4 on v3

--- a/solution.py
+++ b/solution.py
@@ -17,7 +17,7 @@
 TOKENS = PATCHES + 1
 ROWS = 208
 CLS = PATCHES
-GROUP = 2
+GROUP = 4
 CLASSES = 1000
 CPAD = 1024
 TASKS = 2
@@ -192,6 +192,10 @@
         return self.even[at : at + count, :] + moved_back
 
 
+def paired(size):
+    return size & (size - 1) == 0
+
+
 class Place:
     def __init__(self, dims, shard_rows):
         self.z, self.y, self.x = dims
@@ -199,6 +203,8 @@
         self.shard_rows = shard_rows
         self.sent_rows = -(-(shard_rows + 1) // 16) * 16
         self.first_rows = self.sent_rows * 13 // 20 // 16 * 16
+
+        self.half_rows = self.sent_rows // 32 * 16
 
     def split(self, index):
         plane = self.y * self.x
@@ -272,9 +278,8 @@
     rows, spare = place.shard_rows, place.sent_rows - place.shard_rows
     for shard in range(place.count):
         zk, yk, xk = shard // (place.y * place.x), shard // place.x % place.y, shard % place.x
-        d = lax.rem(zk + place.z - zed, place.z)
-        a = lax.rem(yk + place.y - why, place.y)
-        b = lax.rem(xk + place.x - ex, place.x)
+        there = ((zk, zed, place.z), (yk, why, place.y), (xk, ex, place.x))
+        d, a, b = [to ^ at if paired(size) else lax.rem(to + size - at, size) for to, at, size in there]
         value = flat.merged(shard * rows, rows)
         value = jnp.concatenate([value, jnp.zeros((spare, LANES), f32)], 0)
         write((a * place.x + b) * place.z + d, value.astype(bf16))
@@ -287,44 +292,44 @@
     out[...] = jnp.concatenate([master[...], tail], 0).astype(bf16)
 
 
-def front_kernel(place, *refs):
-    section = lax.axis_index("section")
+def front_kernel(place, per, *refs):
     parts = len(place.turns()) + place.z
     own, other, refs = refs[:parts], refs[parts : 2 * parts], refs[2 * parts :]
-    patches, refs = refs[0], refs[1:]
-    (x_out, q_out, k_out, v_out, probs_out, mixed_out, hidden_out, act_out, slope_out, middle_out) = refs[:10]
-    w_q, w_k, w_v, w_out, w_up, w_down, vec = refs[10:17]
-    even, odd, mix, w_patch, added, tokens = refs[17:]
+    patches, kept, middle_out, weights = refs[0], refs[1:10], refs[10], refs[11:18]
+    even, odd, mix, w_patch, added, tokens = refs[18:]
+    vec = weights[-1]
     flat = Flat(even, odd, mix, place.count * place.shard_rows)
-
-    @pl.when(pl.program_id(0) == 0)
-    def _():
-        load_section(place, (own, other), 0, flat)
-        read_block(flat, (w_q, w_k, w_v, w_out, w_up, w_down), vec)
-        flat.read(w_patch, W_PATCH, 3, PDIM, D)
-        flat.read_row(vec, 9, B_PATCH, D)
-        flat.read_row(vec, 10, CLS_TOKEN, D)
-        added[...] = jnp.zeros(added.shape, f32)
-        tokens[...] = jnp.zeros(tokens.shape, f32)
-        for at, wide, value in flat.blocks(POS_EMBED, 3, TOKENS + 1, D):
-            bias = vec[9:10, at : at + wide]
-            token = vec[10:11, at : at + wide]
-            for top in range(0, added.shape[0], ROWS):
-                added[top : top + PATCHES, at : at + wide] = value[1:TOKENS, :wide] + bias
-                added[top + CLS : top + CLS + 1, at : at + wide] = value[0:1, :wide] + token
-
-    group = patches.shape[0]
+    load_section(place, (own, other), 0, flat)
+    read_block(flat, weights[:-1], vec)
+    flat.read(w_patch, W_PATCH, 3, PDIM, D)
+    flat.read_row(vec, 9, B_PATCH, D)
+    flat.read_row(vec, 10, CLS_TOKEN, D)
+    added[...] = jnp.zeros(added.shape, f32)
+    tokens[...] = jnp.zeros(tokens.shape, f32)
+    for at, wide, value in flat.blocks(POS_EMBED, 3, TOKENS + 1, D):
+        added[0:PATCHES, at : at + wide] = value[1:TOKENS, :wide] + vec[9:10, at : at + wide]
+        added[CLS : CLS + 1, at : at + wide] = value[0:1, :wide] + vec[10:11, at : at + wide]
+    group = group_of(per)
+    for step in range(0, per, group):
+        cut = slice(step * ROWS, (step + group) * ROWS)
+        front_images(step, cut, patches, kept, middle_out, weights, w_patch, added, tokens)
+
+
+def front_images(step, cut, patches, kept, middle_out, weights, w_patch, added, tokens):
+    x_out, q_out, k_out, v_out, probs_out, mixed_out, hidden_out, act_out, slope_out = kept
+    w_q, w_k, w_v, w_out, w_up, w_down, vec = weights
+    group = (cut.stop - cut.start) // ROWS
     spans = [slice(i * ROWS, (i + 1) * ROWS) for i in range(group)]
-    for i in range(group):
-        tokens[i * ROWS : i * ROWS + PATCHES, :] = dot(patches[i], w_patch[...])
-    x = tokens[...] + added[...]
-    x_out[...] = x
+    for i, at in enumerate(spans):
+        tokens[cut.start + at.start : cut.start + at.start + PATCHES, :] = dot(patches[step + i], w_patch[...])
+    x = tokens[cut, :] + jnp.concatenate([added[...]] * group, 0)
+    x_out[cut, :] = x
     unit, _ = normalise(x)
     normed = (unit * vector(vec, "gain_one") + vector(vec, "bias_one")).astype(bf16)
     q = (dot(normed, w_q[...]) + vector(vec, "b_q")).astype(bf16)
     k = dot(normed, w_k[...]).astype(bf16)
     v = (dot(normed, w_v[...]) + vector(vec, "b_v")).astype(bf16)
-    q_out[...], k_out[...], v_out[...] = q, k, v
+    q_out[cut, :], k_out[cut, :], v_out[cut, :] = q, k, v
     q_scaled = q.astype(f32) * SCALE
     column = lax.broadcasted_iota(jnp.int32, (1, ROWS), 1)
     scores = [dot(by_head(q_scaled[at]).astype(bf16), k[at], 1, 1) for at in spans]
@@ -332,20 +337,20 @@
     raised = [jnp.exp(value - jnp.max(value, -1, keepdims=True)) for value in scores]
     probs = [value * (1.0 / jnp.sum(value, -1, keepdims=True)) for value in raised]
     for i, value in enumerate(probs):
-        probs_out[i * HEADS * ROWS : (i + 1) * HEADS * ROWS, :] = value
+        probs_out[(step + i) * HEADS * ROWS : (step + i + 1) * HEADS * ROWS, :] = value
     mixed = [from_heads(dot(value.astype(bf16), v[at])) for value, at in zip(probs, spans)]
     mixed = jnp.concatenate(mixed, 0).astype(bf16)
-    mixed_out[...] = mixed
+    mixed_out[cut, :] = mixed
     hidden = x + dot(mixed, w_out[...]) + vector(vec, "b_out")
-    hidden_out[...] = hidden
+    hidden_out[cut, :] = hidden
     unit, _ = normalise(hidden)
     normed = (unit * vector(vec, "gain_two") + vector(vec, "bias_two")).astype(bf16)
     pre = dot(normed, w_up[...]) + vector(vec, "b_up")
     act, slope = gelu_parts(pre)
     act = act.astype(bf16)
-    act_out[...], slope_out[...] = act, slope
+    act_out[cut, :], slope_out[cut, :] = act, slope
     middle = hidden + dot(act, w_down[...]) + vector(vec, "b_down")
-    middle_out[...] = middle.astype(bf16)
+    middle_out[cut, :] = middle.astype(bf16)
 
 
 def read_head(flat, wide, w_head, b_head):
@@ -526,103 +531,102 @@
     send_out(place, flat, store)
 
 
-def back_kernel(place, *refs):
-    (grad_in, x_in, q_in, k_in, v_in, probs_in, mixed_in, hidden_in, act_in, slope_in, patches) = refs[:11]
-    w_q, w_k, w_v, w_out, w_up, w_down, vec, late_grad, keep_out, give_out = refs[11:21]
-    even, odd, mix, g_q, g_k, g_v, g_out, g_up, g_down, g_patch, g_pos, rows = refs[21:]
-    step = pl.program_id(0)
-    sums_at = {name: row for row, name in enumerate(VECTORS)}
-
-    @pl.when(step == 0)
+def back_kernel(place, per, *refs):
+    grad_in, kept, patches, weights = refs[0], refs[1:10], refs[10], refs[11:18]
+    late_grad, keep_out, give_out = refs[18:21]
+    even, odd, mix, *operands = refs[21:]
+    s_normed, s_q, s_k, s_v, s_branch, s_two, s_up = operands
+    vec = weights[-1]
+    group = group_of(per)
+    sums = {}
+    embedded = []
+    positions = jnp.zeros((ROWS, D), f32)
+    for step in range(0, per, group):
+        cut = slice(step * ROWS, (step + group) * ROWS)
+        vectors, grad_x = back_images(step, cut, grad_in, kept, weights, operands)
+        sums = {name: sums[name] + value if sums else value for name, value in vectors.items()}
+        for i in range(group):
+            embedded.append(grad_x[i * ROWS : i * ROWS + PATCHES].astype(bf16))
+            positions = positions + grad_x[i * ROWS : (i + 1) * ROWS]
+
+    at = BLOCK_AT
+    flat = Flat(even, odd, mix, place.count * place.shard_rows)
+    flat.clear()
+    normed = s_normed[...]
+    for part, ref in enumerate((s_q, s_k, s_v)):
+        flat.write(dot(normed, ref[...], 0, 0), at["w_qkv"] + 3 * part, 9, D)
+    flat.write(dot(kept[5][...], s_branch[...], 0, 0), at["w_out"], 3, D)
+    flat.write(dot(s_two[...], s_up[...], 0, 0), at["w_up"], 12, FF)
+    flat.write(dot(kept[7][...], grad_in[...], 0, 0), at["w_down"], 3, D)
+    grad_patch = sum(dot(patches[i], value, 0, 0) for i, value in enumerate(embedded))
+    flat.write(grad_patch, W_PATCH, 3, D)
+    sums["b_q"], sums["b_v"] = column_sums(s_q[...]), column_sums(s_v[...])
+    sums["b_out"], sums["b_up"] = column_sums(s_branch[...]), column_sums(s_up[...])
+    sums["b_down"] = column_sums(grad_in[...])
+    write_vectors(flat, sums)
+    flat.write(sum(column_sums(value) for value in embedded), B_PATCH, 2, D)
+    token = positions[CLS : CLS + 1, :]
+    flat.write(token, CLS_TOKEN, 2, D)
+    natural = jnp.concatenate([token, positions[0:PATCHES, :], jnp.zeros((1, D), f32)], 0)
+    flat.write(natural, POS_EMBED, 3, D)
+
+    section = lax.axis_index("section")
+
+    @pl.when(section == 0)
     def _():
-        for ref in (g_q, g_k, g_v, g_out, g_up, g_down, g_patch, g_pos, rows):
-            ref[...] = jnp.zeros(ref.shape, f32)
-
-    def add_row(row, value):
-        rows[row : row + 1, 0 : value.shape[1]] += value
-
-    grad_low = grad_in[...]
-    g_down[...] += dot(act_in[...], grad_low, 0, 0)
-    add_row(sums_at["b_down"], column_sums(grad_low))
-    grad_up = (dot(grad_low, w_down[...], 1, 1) * slope_in[...]).astype(bf16)
-    unit, scale = normalise(hidden_in[...])
-    normed = (unit * vector(vec, "gain_two") + vector(vec, "bias_two")).astype(bf16)
-    g_up[...] += dot(normed, grad_up, 0, 0)
-    add_row(sums_at["b_up"], column_sums(grad_up))
+        def store(at, value):
+            keep_out[at] = value
+            give_out[at] = late_grad[at]
+
+        send_out(place, flat, store)
+
+    @pl.when(section != 0)
+    def _():
+        def store(at, value):
+            give_out[at] = value
+            keep_out[at] = late_grad[at]
+
+        send_out(place, flat, store)
+
+
+def back_images(step, cut, grad_in, kept, weights, operands):
+    x_in, q_in, k_in, v_in, probs_in, mixed_in, hidden_in, act_in, slope_in = kept
+    w_q, w_k, w_v, w_out, w_up, w_down, vec = weights
+    s_normed, s_q, s_k, s_v, s_branch, s_two, s_up = operands
+    group = (cut.stop - cut.start) // ROWS
+    spans = [slice(i * ROWS, (i + 1) * ROWS) for i in range(group)]
+    sums = {}
+    grad_low = grad_in[cut, :]
+    grad_up = (dot(grad_low, w_down[...], 1, 1) * slope_in[cut, :]).astype(bf16)
+    s_up[cut, :] = grad_up
+    unit, scale = normalise(hidden_in[cut, :])
+    s_two[cut, :] = (unit * vector(vec, "gain_two") + vector(vec, "bias_two")).astype(bf16)
     grad_two = dot(grad_up, w_up[...], 1, 1)
-    add_row(sums_at["gain_two"], column_sums(grad_two * unit))
-    add_row(sums_at["bias_two"], column_sums(grad_two))
+    sums["gain_two"], sums["bias_two"] = column_sums(grad_two * unit), column_sums(grad_two)
     grad_hidden = grad_low.astype(f32) + normalise_back(grad_two, vector(vec, "gain_two"), unit, scale)
     branch = grad_hidden.astype(bf16)
-    g_out[...] += dot(mixed_in[...], branch, 0, 0)
-    add_row(sums_at["b_out"], column_sums(branch))
-    group = patches.shape[0]
-    spans = [slice(i * ROWS, (i + 1) * ROWS) for i in range(group)]
+    s_branch[cut, :] = branch
     grad_mixed = dot(branch, w_out[...], 1, 1).astype(bf16).astype(f32)
     mixed_heads = [by_head(grad_mixed[at]).astype(bf16) for at in spans]
-    q_scaled = q_in[...].astype(f32) * SCALE
+    q_scaled = q_in[cut, :].astype(f32) * SCALE
     q_heads = [by_head(q_scaled[at]).astype(bf16) for at in spans]
-    probs = [probs_in[i * HEADS * ROWS : (i + 1) * HEADS * ROWS, :] for i in range(group)]
-    grad_probs = [dot(value, v_in[at, :], 1, 1) for value, at in zip(mixed_heads, spans)]
+    k, v = k_in[cut, :], v_in[cut, :]
+    probs = [
+        probs_in[(step + i) * HEADS * ROWS : (step + i + 1) * HEADS * ROWS, :] for i in range(group)
+    ]
+    grad_probs = [dot(value, v[at], 1, 1) for value, at in zip(mixed_heads, spans)]
     grad_v = [dot(value.astype(bf16), right, 0, 0) for value, right in zip(probs, mixed_heads)]
     inner = [jnp.sum(one * two, -1, keepdims=True) for one, two in zip(grad_probs, probs)]
     grad_scores = [(two * (one - less)).astype(bf16) for one, two, less in zip(grad_probs, probs, inner)]
-    grad_q = [from_heads(dot(value, k_in[at, :])) * SCALE for value, at in zip(grad_scores, spans)]
+    grad_q = [from_heads(dot(value, k[at])) * SCALE for value, at in zip(grad_scores, spans)]
     grad_k = [dot(value, right, 0, 0) for value, right in zip(grad_scores, q_heads)]
     grad_q, grad_k, grad_v = [jnp.concatenate(value, 0).astype(bf16) for value in (grad_q, grad_k, grad_v)]
-    unit, scale = normalise(x_in[...])
-    normed = (unit * vector(vec, "gain_one") + vector(vec, "bias_one")).astype(bf16)
-    g_q[...] += dot(normed, grad_q, 0, 0)
-    g_k[...] += dot(normed, grad_k, 0, 0)
-    g_v[...] += dot(normed, grad_v, 0, 0)
-    add_row(sums_at["b_q"], column_sums(grad_q))
-    add_row(sums_at["b_v"], column_sums(grad_v))
+    s_q[cut, :], s_k[cut, :], s_v[cut, :] = grad_q, grad_k, grad_v
+    unit, scale = normalise(x_in[cut, :])
+    s_normed[cut, :] = (unit * vector(vec, "gain_one") + vector(vec, "bias_one")).astype(bf16)
     grad_one = dot(grad_q, w_q[...], 1, 1) + dot(grad_k, w_k[...], 1, 1) + dot(grad_v, w_v[...], 1, 1)
-    add_row(sums_at["gain_one"], column_sums(grad_one * unit))
-    add_row(sums_at["bias_one"], column_sums(grad_one))
-    grad_x = grad_hidden + normalise_back(grad_one, vector(vec, "gain_one"), unit, scale)
-    grad_emb = [grad_x[at.start : at.start + PATCHES].astype(bf16) for at in spans]
-    for i, at in enumerate(spans):
-        g_pos[...] += grad_x[at]
-        g_patch[...] += dot(patches[i], grad_emb[i], 0, 0)
-        add_row(9, column_sums(grad_emb[i]))
-
-    @pl.when(step == pl.num_programs(0) - 1)
-    def _():
-        at = BLOCK_AT
-        flat = Flat(even, odd, mix, place.count * place.shard_rows)
-        flat.clear()
-        for part, ref in enumerate((g_q, g_k, g_v)):
-            flat.write(ref[...], at["w_qkv"] + 3 * part, 9, D)
-        flat.write(g_out[...], at["w_out"], 3, D)
-        flat.write(g_up[...], at["w_up"], 12, FF)
-        flat.write(g_down[...], at["w_down"], 3, D)
-        flat.write(g_patch[...], W_PATCH, 3, D)
-        names = {name: rows[row : row + 1, 0 : FF if name == "b_up" else D] for name, row in sums_at.items()}
-        write_vectors(flat, names)
-        flat.write(rows[9:10, 0:D], B_PATCH, 2, D)
-        token = g_pos[CLS : CLS + 1, :]
-        flat.write(token, CLS_TOKEN, 2, D)
-        natural = jnp.concatenate([token, g_pos[0:PATCHES, :], jnp.zeros((1, D), f32)], 0)
-        flat.write(natural, POS_EMBED, 3, D)
-
-        section = lax.axis_index("section")
-
-        @pl.when(section == 0)
-        def _():
-            def store(at, value):
-                keep_out[at] = value
-                give_out[at] = late_grad[at]
-
-            send_out(place, flat, store)
-
-        @pl.when(section != 0)
-        def _():
-            def store(at, value):
-                give_out[at] = value
-                keep_out[at] = late_grad[at]
-
-            send_out(place, flat, store)
+    sums["gain_one"], sums["bias_one"] = column_sums(grad_one * unit), column_sums(grad_one)
+    return sums, grad_hidden + normalise_back(grad_one, vector(vec, "gain_one"), unit, scale)
 
 
 def fetch_kernel(first, last, _, basis, kept, sem):
@@ -635,16 +639,44 @@
     total[...] = left[...] + right[...]
 
 
-def plane_kernel(depth, own, _, *refs):
-    arrived, (whole_out, *outs) = refs[:-depth], refs[-depth:]
-    for d in range(depth):
-        total = own[d]
-        for ref in arrived:
-            total = total + ref[d].astype(f32)
-        if d == 0:
-            whole_out[...] = total
-        else:
-            outs[d - 1][...] = total.astype(bf16)
+def split_kernel(place, keep, given, *outs):
+    cut = place.half_rows
+    for place_y in range(place.y):
+        for place_x in range(place.x):
+            for d in range(place.z):
+                at = (place_y * place.x + place_x) * place.z + d
+                total = keep[at].astype(f32) + given[at].astype(f32)
+                one, two = outs[place_y], outs[place.y + place_x]
+                one[place_x, d] = total[:cut].astype(one.dtype)
+                two[place_y, d] = total[cut:].astype(two.dtype)
+
+
+def turn_kernel(place, one, two, _, *refs):
+    count = place.y + place.x
+    arrived, outs = refs[: count - 2], refs[count - 2 :]
+    for own, came, parts in (
+        (one, arrived[: place.y - 1], outs[: place.x]),
+        (two, arrived[place.y - 1 :], outs[place.x :]),
+    ):
+        for step, out in enumerate(parts):
+            for d in range(place.z):
+                total = own[step, d]
+                for ref in came:
+                    total = total + ref[step, d].astype(f32)
+                out[d] = total.astype(out.dtype)
+
+
+def plane_kernel(place, one, two, _, *refs):
+    arrived, (whole_out, *outs) = refs[: -place.z], refs[-place.z :]
+    for d in range(place.z):
+        upper, lower = one[d], two[d]
+        for ref in arrived[: place.x - 1]:
+            upper = upper + ref[d].astype(f32)
+        for ref in arrived[place.x - 1 :]:
+            lower = lower + ref[d].astype(f32)
+        out = outs[d - 1] if d else whole_out
+        out[0 : place.half_rows, :] = upper.astype(out.dtype)
+        out[place.half_rows :, :] = lower.astype(out.dtype)
 
 
 def inner_kernel(blocks, *refs):
@@ -734,16 +766,19 @@
     return zed, plane // ex, ex
 
 
-def moved(value, place, turn=(0, 0, 0), core=0, sections=(0, 1)):
+def moved(value, place, turn=(0, 0, 0), core=0, pairs_too=False):
+    def step(index, by, size):
+        return index ^ by if pairs_too and paired(size) else (index + by) % size
+
     pairs = []
-    for section in sections:
+    for section in range(2):
         for zed in range(place.z):
             for why in range(place.y):
                 for ex in range(place.x):
                     source = (section * place.z + zed) * place.y * place.x + why * place.x + ex
-                    there = ((section + core) % 2) * place.z + (zed + turn[0]) % place.z
-                    target = (there * place.y + (why + turn[1]) % place.y) * place.x
-                    pairs.append((source, target + (ex + turn[2]) % place.x))
+                    there = ((section + core) % 2) * place.z + step(zed, turn[0], place.z)
+                    target = (there * place.y + step(why, turn[1], place.y)) * place.x
+                    pairs.append((source, target + step(ex, turn[2], place.x)))
     return lax.ppermute(value, ("section", "dp"), pairs)
 
 
@@ -808,10 +843,6 @@
     return GROUP if per % GROUP == 0 else 1
 
 
-def row_block(shape, per):
-    return pl.BlockSpec((group_of(per) * shape[0], shape[1]), lambda i, *_: (i, 0))
-
-
 def flat_scratch(place):
     flat_rows = place.count * place.shard_rows + SPARE
     return [
@@ -821,30 +852,19 @@
     ]
 
 
-def patch_block(per):
-    return pl.BlockSpec((group_of(per), PATCHES, PDIM), lambda i, *_: (i, 0, 0))
-
-
 def front(place, per, own, other, patches):
     outs = pl.pallas_call(
-        functools.partial(front_kernel, place),
-        grid_spec=pltpu.PrefetchScalarGridSpec(
-            num_scalar_prefetch=0,
-            grid=(per // group_of(per),),
-            in_specs=[whole(piece.shape) for piece in own + other] + [patch_block(per)],
-            out_specs=[row_block(shape, per) for shape, _ in SAVED + [MIDDLE]]
-            + [whole(shape) for shape in BLOCK_SHAPES]
-            + [whole((VEC_ROWS, FF))],
-            scratch_shapes=flat_scratch(place)
-            + [pltpu.VMEM((PDIM, D), bf16)]
-            + [pltpu.VMEM((group_of(per) * ROWS, D), f32)] * 2,
-        ),
+        functools.partial(front_kernel, place, per),
+        in_specs=[VMEM] * (len(own) + len(other) + 1),
+        out_specs=[VMEM] * (len(SAVED) + 1 + len(BLOCK_SHAPES) + 1),
         out_shape=[
             jax.ShapeDtypeStruct((per * shape[0], shape[1]), kind) for shape, kind in SAVED + [MIDDLE]
         ]
         + [jax.ShapeDtypeStruct(shape, bf16) for shape in BLOCK_SHAPES]
         + [jax.ShapeDtypeStruct((VEC_ROWS, FF), f32)],
-        compiler_params=params(20),
+        scratch_shapes=flat_scratch(place)
+        + [pltpu.VMEM((PDIM, D), bf16), pltpu.VMEM((ROWS, D), f32), pltpu.VMEM((per * ROWS, D), f32)],
+        compiler_params=pltpu.CompilerParams(vmem_limit_bytes=20 * 1024 * 1024),
         cost_estimate=WORK,
         name="front",
     )(*own, *other, patches)
@@ -884,25 +904,14 @@
 
 def back(place, per, grad_middle, kept, patches, weights, late_grad):
     return pl.pallas_call(
-        functools.partial(back_kernel, place),
-        grid_spec=pltpu.PrefetchScalarGridSpec(
-            num_scalar_prefetch=0,
-            grid=(per // group_of(per),),
-            in_specs=[row_block(shape, per) for shape, _ in [MIDDLE] + SAVED]
-            + [patch_block(per)]
-            + [whole(shape) for shape in BLOCK_SHAPES]
-            + [whole((VEC_ROWS, FF)), whole(grad_kind(place).shape)],
-            out_specs=[whole(grad_kind(place).shape)] * 2,
-            scratch_shapes=flat_scratch(place)
-            + [pltpu.VMEM(shape, f32) for shape in BLOCK_SHAPES]
-            + [
-                pltpu.VMEM((PDIM, D), f32),
-                pltpu.VMEM((ROWS, D), f32),
-                pltpu.VMEM((VEC_ROWS, FF), f32),
-            ],
-        ),
+        functools.partial(back_kernel, place, per),
+        in_specs=[VMEM] * (1 + len(kept) + 1 + len(weights) + 1),
+        out_specs=[VMEM] * 2,
         out_shape=[grad_kind(place)] * 2,
-        compiler_params=params(20),
+        scratch_shapes=flat_scratch(place)
+        + [pltpu.VMEM((per * ROWS, D), bf16)] * 6
+        + [pltpu.VMEM((per * ROWS, FF), bf16)],
+        compiler_params=pltpu.CompilerParams(vmem_limit_bytes=20 * 1024 * 1024),
         cost_estimate=WORK,
         name="back",
     )(grad_middle, *kept, patches, *weights, late_grad)
@@ -928,7 +937,10 @@
         out_shape=jax.ShapeDtypeStruct((place.sent_rows, LANES), bf16),
         compiler_params=pltpu.CompilerParams(vmem_limit_bytes=2 * 1024 * 1024),
         name="shard",
-    )(replay, master.reshape(shard_rows, LANES))
+    )(
+        pltpu.with_memory_space_constraint(replay, pltpu.HBM),
+        pltpu.with_memory_space_constraint(master.reshape(shard_rows, LANES), pltpu.HBM),
+    )
     mine = lax.dynamic_slice_in_dim(patches, section * per, per, 0)
     early, late_part = shard[: place.first_rows], shard[place.first_rows :]
     column = [early] + [moved(early, place, (d, 0, 0)) for d in range(1, place.z)]
@@ -947,11 +959,20 @@
 
     given = moved(give, place, core=1)
 
-    def paired(turn):
-        cut = slice(turn * place.z, (turn + 1) * place.z)
-        return keep[cut].astype(f32) + given[cut].astype(f32)
-
-    staying, leaving = paired(0), [paired(turn).astype(bf16) for turn in range(1, len(turns))]
+    def kinds(lead, rows, count):
+        shape = (*lead, place.z, rows, LANES)
+        return [jax.ShapeDtypeStruct(shape, bf16 if i else f32) for i in range(count)]
+
+    one_rows, two_rows = place.half_rows, place.sent_rows - place.half_rows
+    parts = pl.pallas_call(
+        functools.partial(split_kernel, place),
+        in_specs=[VMEM] * 2,
+        out_specs=[VMEM] * (place.y + place.x),
+        out_shape=kinds((place.x,), one_rows, place.y) + kinds((place.y,), two_rows, place.x),
+        compiler_params=pltpu.CompilerParams(vmem_limit_bytes=12 * 1024 * 1024),
+        name="split",
+    )(keep, given)
+    ones, twos = parts[: place.y], parts[place.y :]
     rows_basis = pltpu.with_memory_space_constraint(basis.reshape(KB, shard_len), pltpu.HBM)
 
     def fetch(first, last, after):
@@ -968,19 +989,36 @@
             name="fetch",
         )(after, rows_basis)
 
-    upper = fetch(0, UPPER, leaving[0])
-    arrived = [moved(leaving[turn - 1], place, (0, *turns[turn])) for turn in range(1, len(turns))]
+    upper = fetch(0, UPPER, ones[-1])
+
+    def along_y(values):
+        return [moved(values[i], place, (0, i, 0), pairs_too=True) for i in range(1, place.y)]
+
+    def along_x(values):
+        return [moved(values[i], place, (0, 0, i), pairs_too=True) for i in range(1, place.x)]
+
+    arrived = along_y(ones) + along_x(twos)
+    parts = pl.pallas_call(
+        functools.partial(turn_kernel, place),
+        in_specs=[VMEM, VMEM, ANY] + [VMEM] * len(arrived),
+        out_specs=[VMEM] * (place.y + place.x),
+        out_shape=kinds((), one_rows, place.x) + kinds((), two_rows, place.y),
+        compiler_params=pltpu.CompilerParams(vmem_limit_bytes=2 * 1024 * 1024),
+        name="turn",
+    )(ones[0], twos[0], upper, *arrived)
+    ones, twos = parts[: place.x], parts[place.x :]
+    arrived = along_x(ones) + along_y(twos)
     piece_shape = (place.sent_rows, LANES)
     first, *rest = pl.pallas_call(
-        functools.partial(plane_kernel, place.z),
-        in_specs=[VMEM, ANY] + [VMEM] * (len(turns) - 1),
+        functools.partial(plane_kernel, place),
+        in_specs=[VMEM, VMEM, ANY] + [VMEM] * len(arrived),
         out_specs=[VMEM] * place.z,
         out_shape=[jax.ShapeDtypeStruct(piece_shape, bf16 if d else f32) for d in range(place.z)],
         compiler_params=pltpu.CompilerParams(vmem_limit_bytes=2 * 1024 * 1024),
         name="plane",
-    )(staying, upper, *arrived)
+    )(ones[0], twos[0], upper, *arrived)
     resident = (upper, fetch(UPPER, KB, rest[0]))
-    pieces = [moved(rest[d - 1], place, (d, 0, 0)) for d in range(1, place.z)]
+    pieces = [moved(rest[d - 1], place, (d, 0, 0), pairs_too=True) for d in range(1, place.z)]
 
     def divisor(most):
         return max(n for n in range(1, most + 1) if shard_rows % n == 0)

time: 118 us -> 112 us (0.949)
  waiting for transfers between devices: 29.5 us -> 24.3 us
  starting transfers between devices: 35.3 us -> 38.9 us
  Pallas kernels: 48.9 us -> 46.4 us
  local copies, waits for them, and re-layouts: 2.54 us -> 0.82 us
    ppermute x28 -> x29, waiting for transfers between devices: 19.2 us -> 15.8 us  [moved(): return lax.ppermute(value, ('section', 'dp'), pairs)]
    pallas_call x3 -> x5, Pallas kernels: 16.2 us -> 13.2 us  [the longest x1 7.28 us: back(): pl.pallas_call(functools.partial(back_kernel, place, per), in_specs=[VMEM...]
    ppermute x4, starting transfers between devices: 4.94 us -> 6.84 us  [butterfly(): value = add(value, lax.ppermute(value, ('section', 'dp'), pairs), resident)]
    ppermute x4, waiting for transfers between devices: 10.4 us -> 8.46 us  [butterfly(): value = add(value, lax.ppermute(value, ('section', 'dp'), pairs), resident)]
    unnamed x22 -> x18, local copies, waits for them, and re-layouts: 1.77 us -> 0.06 us
    ppermute x28 -> x29, starting transfers between devices: 30.4 us -> 32 us  [moved(): return lax.ppermute(value, ('section', 'dp'), pairs)]
  transfers between devices with their start and end apart: 32 -> 33, of which waited for: 15 -> 15; matrix products, arithmetic and copies ran while one was open for 1% -> 1% of each run, Pallas kernels for 9% -> 10%
where the time goes in v4:
time: 112 us
  Pallas kernels  46.4 us (41%)
  starting transfers between devices  38.9 us (35%)
  waiting for transfers between devices  24.3 us (22%)
    ppermute x29, starting transfers between devices, moved(): return lax.ppermute(value, ('section', 'dp'), pairs)  32 us
    ppermute x29, waiting for transfers between devices, moved(): return lax.ppermute(value, ('section', 'dp'), pairs)  15.8 us
    pallas_call x2, Pallas kernels, fetch(): pl.pallas_call(functools.partial(fetch_kernel, first, last), in_specs=[AN...  11.1 us
    ppermute x4, waiting for transfers between devices, butterfly(): value = add(value, lax.ppermute(value, ('section', 'dp'), pairs), resident)  8.46 us
    pallas_call x1, Pallas kernels, late(): pl.pallas_call(functools.partial(late_kernel, place, per, image_total), i...  7.77 us
    pallas_call x1, Pallas kernels, back(): pl.pallas_call(functools.partial(back_kernel, place, per), in_specs=[VMEM...  7.28 us
    ppermute x4, starting transfers between devices, butterfly(): value = add(value, lax.ppermute(value, ('section', 'dp'), pairs), resident)  6.84 us
    pallas_call x1, Pallas kernels, body(): pl.pallas_call(functools.partial(inner_kernel, divisor(26)), in_specs=[VM...  6.75 us
  transfers between devices with their start and end apart: 33, of which 15 were waited for; matrix products, arithmetic and copies ran while one was open for 1% of the time, Pallas kernels for 10%

profile of v4, /device:TPU:0, one launch (start us, length us, event | category | flops | bytes accessed | tf_op | source)
XLA Modules:
  0.0 111.6 jit_solution(1394577187543989264)
XLA Ops:
  0.6 0.0 copy-start
  0.6 1.1 shard.1
  1.8 3.0 %collective-permute-start.7 = (bf16[112,128]{1,0:T(8,128)(2,1)S(1)}, bf16[112,128]{1,0:T(8,128)(2,1)S(1)}, u32[]{:S(2)}, u32[]{:S(2)}) collective-permute-start(bf16[112,128]{1,0:T(8,128)(2,1)S(1)} %get-tuple-element.95), channel_id=1, source_target_pairs={{0,2},{1,3},{2,0},{3,1},{4,6},{5,7},{6,4},{7,5},{8,10},{9,11},{10,... | collective-permute-start | bytes 86024 | tf_op jit(solution)/shard_map/ppermute | solution.py:782
  4.8 1.5 %collective-permute-start.6 = (bf16[112,128]{1,0:T(8,128)(2,1)S(1)}, bf16[112,128]{1,0:T(8,128)(2,1)S(1)}, u32[]{:S(2)}, u32[]{:S(2)}) collective-permute-start(bf16[112,128]{1,0:T(8,128)(2,1)S(1)} %get-tuple-element.95), channel_id=1, source_target_pairs={{0,1},{1,0},{2,3},{3,2},{4,5},{5,4},{6,7},{7,6},{8,9},{9,8},{10,11... | collective-permute-start | bytes 86024 | tf_op jit(solution)/shard_map/ppermute | solution.py:782
  6.3 0.0 collective-permute-start.8
  6.3 3.1 %collective-permute-start.1 = (bf16[208,128]{1,0:T(8,128)(2,1)S(1)}, bf16[208,128]{1,0:T(8,128)(2,1)S(1)}, u32[]{:S(2)}, u32[]{:S(2)}) collective-permute-start(bf16[208,128]{1,0:T(8,128)(2,1)S(1)} %get-tuple-element.97), channel_id=1, source_target_pairs={{0,8},{1,9},{2,10},{3,11},{4,12},{5,13},{6,14},{7,15},{8,0},{9,1},... | collective-permute-start | bytes 159752 | tf_op jit(solution)/shard_map/ppermute | solution.py:782
  9.4 1.6 %collective-permute-start = (bf16[208,128]{1,0:T(8,128)(2,1)S(1)}, bf16[208,128]{1,0:T(8,128)(2,1)S(1)}, u32[]{:S(2)}, u32[]{:S(2)}) collective-permute-start(bf16[208,128]{1,0:T(8,128)(2,1)S(1)} %get-tuple-element.97), channel_id=1, source_target_pairs={{0,4},{1,5},{2,6},{3,7},{4,8},{5,9},{6,10},{7,11},{8,12},{9,13},{1... | collective-permute-start | bytes 159752 | tf_op jit(solution)/shard_map/ppermute | solution.py:782
  11.0 0.6 constant_dynamic-slice_fusion
  11.6 0.1 copy.16.refs_16_.refs_10_
  11.8 2.3 %collective-permute-start.2 = (bf16[208,128]{1,0:T(8,128)(2,1)S(1)}, bf16[208,128]{1,0:T(8,128)(2,1)S(1)}, u32[]{:S(2)}, u32[]{:S(2)}) collective-permute-start(bf16[208,128]{1,0:T(8,128)(2,1)S(1)} %get-tuple-element.97), channel_id=1, source_target_pairs={{0,12},{1,13},{2,14},{3,15},{4,0},{5,1},{6,2},{7,3},{8,4},{9,5},{1... | collective-permute-start | bytes 159752 | tf_op jit(solution)/shard_map/ppermute | solution.py:782
  14.1 0.1 collective-permute-start.16
  14.2 0.6 collective-permute-start.11
  14.8 1.3 %collective-permute-done.2 = bf16[208,128]{1,0:T(8,128)(2,1)S(1)} collective-permute-done((bf16[208,128]{1,0:T(8,128)(2,1)S(1)}, bf16[208,128]{1,0:T(8,128)(2,1)S(1)}, u32[]{:S(2)}, u32[]{:S(2)}) %collective-permute-start.2) | collective-permute-done | bytes 53280 | tf_op jit(solution)/shard_map/ppermute | solution.py:782
  16.1 0.7 collective-permute-start.10
  16.8 0.0 copy-start.5
  16.8 0.0 copy-start.7
  16.8 0.0 copy-start.8
  16.8 2.8 %collective-permute-start.5 = (bf16[4,208,128]{2,1,0:T(8,128)(2,1)S(1)}, bf16[4,208,128]{2,1,0:T(8,128)(2,1)S(1)}, u32[]{:S(2)}, u32[]{:S(2)}) collective-permute-start(bf16[4,208,128]{2,1,0:T(8,128)(2,1)S(1)} %pad_maximum_fusion.refs_0_), channel_id=1, source_target_pairs={{0,3},{1,2},{2,1},{3,0},{4,7},{5,6},{6,5},{7,4},{8,11},{9,10},{10,... | collective-permute-start | bytes 638984 | tf_op jit(solution)/shard_map/ppermute | solution.py:782
  19.6 0.5 collective-permute-start.4
  20.1 0.3 collective-permute-start.3
  20.4 4.2 %collective-permute-start.9 = (bf16[4,112,128]{2,1,0:T(8,128)(2,1)S(1)}, bf16[4,112,128]{2,1,0:T(8,128)(2,1)S(1)}, u32[]{:S(2)}, u32[]{:S(2)}) collective-permute-start(bf16[4,112,128]{2,1,0:T(8,128)(2,1)S(1)} %pad_maximum_fusion.1.refs_4_), channel_id=1, source_target_pairs={{0,4},{1,5},{2,6},{3,7},{4,8},{5,9},{6,10},{7,11},{8,12},{9,13},{1... | collective-permute-start | bytes 344072 | tf_op jit(solution)/shard_map/ppermute | solution.py:782
  24.6 2.4 %collective-permute-done.9.refs_5_ = bf16[4,112,128]{2,1,0:T(8,128)(2,1)S(1)} collective-permute-done((bf16[4,112,128]{2,1,0:T(8,128)(2,1)S(1)}, bf16[4,112,128]{2,1,0:T(8,128)(2,1)S(1)}, u32[]{:S(2)}, u32[]{:S(2)}) %collective-permute-start.9) | collective-permute-done | bytes 114720 | tf_op jit(solution)/shard_map/ppermute | solution.py:782
  27.0 0.5 collective-permute-start.12
  27.5 0.1 collective-permute-start.15
  27.6 0.6 collective-permute-done.4.refs_2_
  28.1 0.1 collective-permute-done.3.refs_1_
  28.2 0.4 collective-permute-start.13
  28.7 0.1 collective-permute-start.17
  28.7 1.3 %collective-permute-done.17.refs_13_ = bf16[4,112,128]{2,1,0:T(8,128)(2,1)S(1)} collective-permute-done((bf16[4,112,128]{2,1,0:T(8,128)(2,1)S(1)}, bf16[4,112,128]{2,1,0:T(8,128)(2,1)S(1)}, u32[]{:S(2)}, u32[]{:S(2)}) %collective-permute-start.17) | collective-permute-done | bytes 114720 | tf_op jit(solution)/shard_map/ppermute | solution.py:782
  30.1 5.5 %front.1 = (f32[832,192]{1,0:T(8,128)S(1)}, bf16[832,192]{1,0:T(8,128)(2,1)S(1)}, bf16[832,192]{1,0:T(8,128)(2,1)S(1)}, bf16[832,192]{1,0:T(8,128)(2,1)S(1)}, f3...) custom-call(bf16[4,208,128]{2,1,0:T(8,128)(2,1)S(1)} %pad_maximum_fu, ...), custom_call_target="tpu_custom_call" | custom-call | flops 3000000000 | bytes 30000000 | tf_op jit(solution)/shard_map/front/pallas_call | solution.py:856
  35.6 7.8 %late.1 = (bf16[832,192]{1,0:T(8,128)(2,1)S(1)}, bf16[16,320,128]{2,1,0:T(8,128)(2,1)S(1)}, f32[1,128]{1,0:T(1,128)S(1)}) custom-call(s32[8]{0:T(128)S(1)} %copy-done.8, s32[8]{0:T(128)S(1)} %copy-done.5, bf16[4,208,128]{2,1,0:T(8,128)(2,1)S(1)} %pad_maximum_fusion.refs_0_, bf16[4,208,128]{2,1,0:T(8,128)(2,1)S(1)} %collective-permute-done.3.refs_1_, ...), custom_call_target="tpu_custom_call" | custom-call | flops 3000000000 | bytes 30000000 | tf_op jit(solution)/shard_map/late/pallas_call | solution.py:880
  43.4 7.3 %back.1 = (bf16[16,320,128]{2,1,0:T(8,128)(2,1)S(1)}, bf16[16,320,128]{2,1,0:T(8,128)(2,1)S(1)}) custom-call(bf16[832,192]{1,0:T(8,128)(2,1)S(1)} %get-tuple-element.53.refs_0_, f32[832,192]{1,0:T(8,128)S(1)} %get-tuple-element.54.refs_1_, bf16[832,192]{1,0:T(8,128)(2,1)S(1)} %get-tuple-element.55.refs_2_, bf16[832,192]{1,0:T(8,128)(2,1)S(1)} %get-tuple-element.56.refs_3_, ...), custom_call_target="tpu_custom_call" | custom-call | flops 3000000000 | bytes 30000000 | tf_op jit(solution)/shard_map/back/pallas_call | solution.py:906
  50.7 0.3 collective-permute-start.20
  51.0 2.8 %collective-permute-done.20.given = bf16[16,320,128]{2,1,0:T(8,128)(2,1)S(1)} collective-permute-done((bf16[16,320,128]{2,1,0:T(8,128)(2,1)S(1)}, bf16[16,320,128]{2,1,0:T(8,128)(2,1)S(1)}, u32[]{:S(2)}, u32[]{:S(2)}) %collective-permute-start.20) | collective-permute-done | bytes 1310752 | tf_op jit(solution)/shard_map/ppermute | solution.py:782
  53.8 0.3 split.1
  54.1 1.6 %collective-permute-start.22 = (bf16[2,4,160,128]{3,2,1,0:T(8,128)(2,1)S(1)}, bf16[2,4,160,128]{3,2,1,0:T(8,128)(2,1)S(1)}, u32[]{:S(2)}, u32[]{:S(2)}) collective-permute-start(bf16[2,4,160,128]{3,2,1,0:T(8,128)(2,1)S(1)} %get-tuple-element.76), channel_id=1, source_target_pairs={{0,1},{1,0},{2,3},{3,2},{4,5},{5,4},{6,7},{7,6},{8,9},{9,8},{10,11... | collective-permute-start | bytes 983048 | tf_op jit(solution)/shard_map/ppermute | solution.py:782
  55.6 1.5 %collective-permute-start.21 = (bf16[2,4,160,128]{3,2,1,0:T(8,128)(2,1)S(1)}, bf16[2,4,160,128]{3,2,1,0:T(8,128)(2,1)S(1)}, u32[]{:S(2)}, u32[]{:S(2)}) collective-permute-start(bf16[2,4,160,128]{3,2,1,0:T(8,128)(2,1)S(1)} %get-tuple-element.75._), channel_id=1, source_target_pairs={{0,2},{1,3},{2,0},{3,1},{4,6},{5,7},{6,4},{7,5},{8,10},{9,11},{10,... | collective-permute-start | bytes 983048 | tf_op jit(solution)/shard_map/ppermute | solution.py:782
  57.1 5.7 %fetch.2._.refs_4_.upper = bf16[208,39936]{1,0:T(8,128)(2,1)S(1)} custom-call(bf16[2,4,160,128]{3,2,1,0:T(8,128)(2,1)S(1)} %get-tuple-element.75._, bf16[400,39936]{1,0:T(8,128)(2,1)} %bitcast.22), custom_call_target="tpu_custom_call" | custom-call | bytes 33226752 | tf_op jit(solution)/shard_map/fetch/pallas_call | solution.py:979
  62.8 1.1 %collective-permute-done.22.refs_1_ = bf16[2,4,160,128]{3,2,1,0:T(8,128)(2,1)S(1)} collective-permute-done((bf16[2,4,160,128]{3,2,1,0:T(8,128)(2,1)S(1)}, bf16[2,4,160,128]{3,2,1,0:T(8,128)(2,1)S(1)}, u32[]{:S(2)}, u32[]{:S(2)}) %collective-permute-start.22) | collective-permute-done | bytes 327712 | tf_op jit(solution)/shard_map/ppermute | solution.py:782
  64.0 1.2 %collective-permute-done.21.refs_0_ = bf16[2,4,160,128]{3,2,1,0:T(8,128)(2,1)S(1)} collective-permute-done((bf16[2,4,160,128]{3,2,1,0:T(8,128)(2,1)S(1)}, bf16[2,4,160,128]{3,2,1,0:T(8,128)(2,1)S(1)}, u32[]{:S(2)}, u32[]{:S(2)}) %collective-permute-start.21) | collective-permute-done | bytes 327712 | tf_op jit(solution)/shard_map/ppermute | solution.py:782
  65.2 0.1 turn.1
  65.3 0.6 collective-permute-start.23
  65.9 1.6 %collective-permute-start.24 = (bf16[4,160,128]{2,1,0:T(8,128)(2,1)S(1)}, bf16[4,160,128]{2,1,0:T(8,128)(2,1)S(1)}, u32[]{:S(2)}, u32[]{:S(2)}) collective-permute-start(bf16[4,160,128]{2,1,0:T(8,128)(2,1)S(1)} %get-tuple-element.80), channel_id=1, source_target_pairs={{0,2},{1,3},{2,0},{3,1},{4,6},{5,7},{6,4},{7,5},{8,10},{9,11},{10,... | collective-permute-start | bytes 491528 | tf_op jit(solution)/shard_map/ppermute | solution.py:782
  67.4 3.3 %collective-permute-done.23.refs_0_ = bf16[4,160,128]{2,1,0:T(8,128)(2,1)S(1)} collective-permute-done((bf16[4,160,128]{2,1,0:T(8,128)(2,1)S(1)}, bf16[4,160,128]{2,1,0:T(8,128)(2,1)S(1)}, u32[]{:S(2)}, u32[]{:S(2)}) %collective-permute-start.23) | collective-permute-done | bytes 163872 | tf_op jit(solution)/shard_map/ppermute | solution.py:782
  70.7 0.5 collective-permute-done.24.refs_1_
  71.2 0.1 plane.1
  71.3 2.3 %collective-permute-start.26 = (bf16[320,128]{1,0:T(8,128)(2,1)S(1)}, bf16[320,128]{1,0:T(8,128)(2,1)S(1)}, u32[]{:S(2)}, u32[]{:S(2)}) collective-permute-start(bf16[320,128]{1,0:T(8,128)(2,1)S(1)} %get-tuple-element.83), channel_id=1, source_target_pairs={{0,8},{1,9},{2,10},{3,11},{4,12},{5,13},{6,14},{7,15},{8,0},{9,1},... | collective-permute-start | bytes 245768 | tf_op jit(solution)/shard_map/ppermute | solution.py:782
  73.6 2.5 %collective-permute-start.27 = (bf16[320,128]{1,0:T(8,128)(2,1)S(1)}, bf16[320,128]{1,0:T(8,128)(2,1)S(1)}, u32[]{:S(2)}, u32[]{:S(2)}) collective-permute-start(bf16[320,128]{1,0:T(8,128)(2,1)S(1)} %get-tuple-element.84), channel_id=1, source_target_pairs={{0,12},{1,13},{2,14},{3,15},{4,8},{5,9},{6,10},{7,11},{8,4},{9,5},... | collective-permute-start | bytes 245768 | tf_op jit(solution)/shard_map/ppermute | solution.py:782
  76.1 5.4 %fetch.3.refs_5_.__.lower = bf16[192,39936]{1,0:T(8,128)(2,1)S(1)} custom-call(bf16[320,128]{1,0:T(8,128)(2,1)S(1)} %get-tuple-element.82._, bf16[400,39936]{1,0:T(8,128)(2,1)} %bitcast.23), custom_call_target="tpu_custom_call" | custom-call | bytes 30670848 | tf_op jit(solution)/shard_map/fetch/pallas_call | solution.py:979
  81.5 6.8 %inner.1 = (f32[312,128]{1,0:T(8,128)S(1)}, f32[1,512]{1,0:T(1,128)S(1)}) custom-call(f32[320,128]{1,0:T(8,128)S(1)} %get-tuple-element.81.refs_0_, bf16[320,128]{1,0:T(8,128)(2,1)S(1)} %collective-permute-done.25.refs_1_, bf16[320,128]{1,0:T(8,128)(2,1)S(1)} %collective-permute-done.26.refs_2_, bf16[320,128]{1,0:T(8,128)(2,1)S(1)} %collective-permute-done.27.refs_3_, ...), custom_call_target="tpu_custom_call" | custom-call | tf_op jit(solution)/shard_map/inner/pallas_call | solution.py:1027
  88.3 0.1 collective-permute-start.28
  88.4 1.1 %collective-permute-done.28.right = f32[1,512]{1,0:T(1,128)S(1)} collective-permute-done((f32[1,512]{1,0:T(1,128)S(1)}, f32[1,512]{1,0:T(1,128)S(1)}, u32[]{:S(2)}, u32[]{:S(2)}) %collective-permute-start.28) | collective-permute-done | bytes 2080 | tf_op jit(solution)/shard_map/ppermute | solution.py:782
  89.5 1.4 %collective-permute-start.29 = (f32[1,512]{1,0:T(1,128)S(1)}, f32[1,512]{1,0:T(1,128)S(1)}, u32[]{:S(2)}, u32[]{:S(2)}) collective-permute-start(f32[1,512]{1,0:T(1,128)S(1)} %add.9.left), channel_id=1, source_target_pairs={{0,1},{1,0},{2,3},{3,2},{4,5},{5,4},{6,7},{7,6},{8,9},{9,8},{10,11... | collective-permute-start | bytes 6152 | tf_op jit(solution)/shard_map/ppermute | solution.py:808
  90.9 2.1 %collective-permute-done.29.right = f32[1,512]{1,0:T(1,128)S(1)} collective-permute-done((f32[1,512]{1,0:T(1,128)S(1)}, f32[1,512]{1,0:T(1,128)S(1)}, u32[]{:S(2)}, u32[]{:S(2)}) %collective-permute-start.29) | collective-permute-done | bytes 2080 | tf_op jit(solution)/shard_map/ppermute | solution.py:808
  93.1 1.5 %collective-permute-start.30 = (f32[1,512]{1,0:T(1,128)S(1)}, f32[1,512]{1,0:T(1,128)S(1)}, u32[]{:S(2)}, u32[]{:S(2)}) collective-permute-start(f32[1,512]{1,0:T(1,128)S(1)} %add.10.left), channel_id=1, source_target_pairs={{0,2},{1,3},{2,0},{3,1},{4,6},{5,7},{6,4},{7,5},{8,10},{9,11},{10,... | collective-permute-start | bytes 6152 | tf_op jit(solution)/shard_map/ppermute | solution.py:808
  94.6 2.1 %collective-permute-done.30.right = f32[1,512]{1,0:T(1,128)S(1)} collective-permute-done((f32[1,512]{1,0:T(1,128)S(1)}, f32[1,512]{1,0:T(1,128)S(1)}, u32[]{:S(2)}, u32[]{:S(2)}) %collective-permute-start.30) | collective-permute-done | bytes 2080 | tf_op jit(solution)/shard_map/ppermute | solution.py:808
  96.7 2.0 %collective-permute-start.31 = (f32[1,512]{1,0:T(1,128)S(1)}, f32[1,512]{1,0:T(1,128)S(1)}, u32[]{:S(2)}, u32[]{:S(2)}) collective-permute-start(f32[1,512]{1,0:T(1,128)S(1)} %add.11.left), channel_id=1, source_target_pairs={{0,4},{1,5},{2,6},{3,7},{4,0},{5,1},{6,2},{7,3},{8,12},{9,13},{10,... | collective-permute-start | bytes 6152 | tf_op jit(solution)/shard_map/ppermute | solution.py:808
  98.7 1.6 %collective-permute-done.31.right = f32[1,512]{1,0:T(1,128)S(1)} collective-permute-done((f32[1,512]{1,0:T(1,128)S(1)}, f32[1,512]{1,0:T(1,128)S(1)}, u32[]{:S(2)}, u32[]{:S(2)}) %collective-permute-start.31) | collective-permute-done | bytes 2080 | tf_op jit(solution)/shard_map/ppermute | solution.py:808
  100.3 0.0 copy-start.4
  100.3 0.0 copy-start.6
  100.3 1.9 %collective-permute-start.32 = (f32[1,512]{1,0:T(1,128)S(1)}, f32[1,512]{1,0:T(1,128)S(1)}, u32[]{:S(2)}, u32[]{:S(2)}) collective-permute-start(f32[1,512]{1,0:T(1,128)S(1)} %add.12.left), channel_id=1, source_target_pairs={{0,8},{1,9},{2,10},{3,11},{4,12},{5,13},{6,14},{7,15},{8,0},{9,1},... | collective-permute-start | bytes 6152 | tf_op jit(solution)/shard_map/ppermute | solution.py:808
  102.2 2.6 %collective-permute-done.32.right = f32[1,512]{1,0:T(1,128)S(1)} collective-permute-done((f32[1,512]{1,0:T(1,128)S(1)}, f32[1,512]{1,0:T(1,128)S(1)}, u32[]{:S(2)}, u32[]{:S(2)}) %collective-permute-start.32) | collective-permute-done | bytes 2080 | tf_op jit(solution)/shard_map/ppermute | solution.py:808
  104.9 0.0 copy-start.1
  104.9 6.5 %update.1 = (f32[3]{0:T(128)}, f32[1]{0:T(128)}, f32[2,200]{1,0:T(2,128)}, f32[312,128]{1,0:T(8,128)}, f32[312,128]{1,0:T(8,128)}, /*index=5*/f32[312,128]{1,0:T(8,128)}) custom-call(s32[2]{0:T(128)S(1)} %copy-done.6, f32[1,512]{1,0:T(1,128)S(1)} %add.13.sums, bf16[208,39936]{1,0:T(8,128)(2,1)S(1)} %fetch.2._.refs_4_.upper, ...), custom_call_target="tpu_custom_call" | custom-call | tf_op jit(solution)/shard_map/update/pallas_call | solution.py:1038
  (42 shorter events, 0.2 us)
Async XLA Ops:
  0.6 10.4 %copy-start = (bf16[8,196,768]{2,0,1:T(8,128)(2,1)S(1)}, bf16[8,196,768]{2,0,1:T(8,128)(2,1)}, u32[]{:S(2)}) copy-start(bf16[8,196,768]{2,0,1:T(8,128)(2,1)} %param.9) | copy-start | bytes 7225348
  1.8 10.0 %collective-permute-start.7 = (bf16[112,128]{1,0:T(8,128)(2,1)S(1)}, bf16[112,128]{1,0:T(8,128)(2,1)S(1)}, u32[]{:S(2)}, u32[]{:S(2)}) collective-permute-start(bf16[112,128]{1,0:T(8,128)(2,1)S(1)} %get-tuple-element.95), channel_id=1, source_target_pairs={{0,2},{1,3},{2,0},{3,1},{4,6},{5,7},{6,4},{7,5},{8,10},{9,11},{10,... | collective-permute-start | bytes 86024 | tf_op jit(solution)/shard_map/ppermute | solution.py:782
  4.8 9.3 %collective-permute-start.6 = (bf16[112,128]{1,0:T(8,128)(2,1)S(1)}, bf16[112,128]{1,0:T(8,128)(2,1)S(1)}, u32[]{:S(2)}, u32[]{:S(2)}) collective-permute-start(bf16[112,128]{1,0:T(8,128)(2,1)S(1)} %get-tuple-element.95), channel_id=1, source_target_pairs={{0,1},{1,0},{2,3},{3,2},{4,5},{5,4},{6,7},{7,6},{8,9},{9,8},{10,11... | collective-permute-start | bytes 86024 | tf_op jit(solution)/shard_map/ppermute | solution.py:782
  6.3 7.8 %collective-permute-start.8 = (bf16[112,128]{1,0:T(8,128)(2,1)S(1)}, bf16[112,128]{1,0:T(8,128)(2,1)S(1)}, u32[]{:S(2)}, u32[]{:S(2)}) collective-permute-start(bf16[112,128]{1,0:T(8,128)(2,1)S(1)} %get-tuple-element.95), channel_id=1, source_target_pairs={{0,3},{1,2},{2,1},{3,0},{4,7},{5,6},{6,5},{7,4},{8,11},{9,10},{10,... | collective-permute-start | bytes 86024 | tf_op jit(solution)/shard_map/ppermute | solution.py:782
  6.3 10.4 %collective-permute-start.1 = (bf16[208,128]{1,0:T(8,128)(2,1)S(1)}, bf16[208,128]{1,0:T(8,128)(2,1)S(1)}, u32[]{:S(2)}, u32[]{:S(2)}) collective-permute-start(bf16[208,128]{1,0:T(8,128)(2,1)S(1)} %get-tuple-element.97), channel_id=1, source_target_pairs={{0,8},{1,9},{2,10},{3,11},{4,12},{5,13},{6,14},{7,15},{8,0},{9,1},... | collective-permute-start | bytes 159752 | tf_op jit(solution)/shard_map/ppermute | solution.py:782
  9.4 7.3 %collective-permute-start = (bf16[208,128]{1,0:T(8,128)(2,1)S(1)}, bf16[208,128]{1,0:T(8,128)(2,1)S(1)}, u32[]{:S(2)}, u32[]{:S(2)}) collective-permute-start(bf16[208,128]{1,0:T(8,128)(2,1)S(1)} %get-tuple-element.97), channel_id=1, source_target_pairs={{0,4},{1,5},{2,6},{3,7},{4,8},{5,9},{6,10},{7,11},{8,12},{9,13},{1... | collective-permute-start | bytes 159752 | tf_op jit(solution)/shard_map/ppermute | solution.py:782
  11.8 4.3 %collective-permute-start.2 = (bf16[208,128]{1,0:T(8,128)(2,1)S(1)}, bf16[208,128]{1,0:T(8,128)(2,1)S(1)}, u32[]{:S(2)}, u32[]{:S(2)}) collective-permute-start(bf16[208,128]{1,0:T(8,128)(2,1)S(1)} %get-tuple-element.97), channel_id=1, source_target_pairs={{0,12},{1,13},{2,14},{3,15},{4,0},{5,1},{6,2},{7,3},{8,4},{9,5},{1... | collective-permute-start | bytes 159752 | tf_op jit(solution)/shard_map/ppermute | solution.py:782
  14.1 6.0 %collective-permute-start.16 = (bf16[4,112,128]{2,1,0:T(8,128)(2,1)S(1)}, bf16[4,112,128]{2,1,0:T(8,128)(2,1)S(1)}, u32[]{:S(2)}, u32[]{:S(2)}) collective-permute-start(bf16[4,112,128]{2,1,0:T(8,128)(2,1)S(1)} %pad_maximum_fusion.1.refs_4_), channel_id=1, source_target_pairs={{0,16},{1,17},{2,18},{3,19},{4,20},{5,21},{6,22},{7,23},{8,24},{9,... | collective-permute-start | bytes 344072 | tf_op jit(solution)/shard_map/ppermute | solution.py:782
  14.2 6.2 %collective-permute-start.11 = (bf16[4,112,128]{2,1,0:T(8,128)(2,1)S(1)}, bf16[4,112,128]{2,1,0:T(8,128)(2,1)S(1)}, u32[]{:S(2)}, u32[]{:S(2)}) collective-permute-start(bf16[4,112,128]{2,1,0:T(8,128)(2,1)S(1)} %pad_maximum_fusion.1.refs_4_), channel_id=1, source_target_pairs={{0,12},{1,13},{2,14},{3,15},{4,0},{5,1},{6,2},{7,3},{8,4},{9,5},{1... | collective-permute-start | bytes 344072 | tf_op jit(solution)/shard_map/ppermute | solution.py:782
  16.1 8.5 %collective-permute-start.10 = (bf16[4,112,128]{2,1,0:T(8,128)(2,1)S(1)}, bf16[4,112,128]{2,1,0:T(8,128)(2,1)S(1)}, u32[]{:S(2)}, u32[]{:S(2)}) collective-permute-start(bf16[4,112,128]{2,1,0:T(8,128)(2,1)S(1)} %pad_maximum_fusion.1.refs_4_), channel_id=1, source_target_pairs={{0,8},{1,9},{2,10},{3,11},{4,12},{5,13},{6,14},{7,15},{8,0},{9,1},... | collective-permute-start | bytes 344072 | tf_op jit(solution)/shard_map/ppermute | solution.py:782
  16.8 18.8 %copy-start.5 = (s32[8]{0:T(128)S(1)}, s32[8]{0:T(128)}, u32[]{:S(2)}) copy-start(s32[8]{0:T(128)} %replay.3) | copy-start | bytes 100
  16.8 18.8 %copy-start.7 = (f32[8,1000]{1,0:T(8,128)S(1)}, f32[8,1000]{1,0:T(8,128)}, u32[]{:S(2)}) copy-start(f32[8,1000]{1,0:T(8,128)} %refs_17_.1) | copy-start | bytes 96004
  16.8 18.8 %copy-start.8 = (s32[8]{0:T(128)S(1)}, s32[8]{0:T(128)}, u32[]{:S(2)}) copy-start(s32[8]{0:T(128)} %labels.1) | copy-start | bytes 100
  16.8 10.7 %collective-permute-start.5 = (bf16[4,208,128]{2,1,0:T(8,128)(2,1)S(1)}, bf16[4,208,128]{2,1,0:T(8,128)(2,1)S(1)}, u32[]{:S(2)}, u32[]{:S(2)}) collective-permute-start(bf16[4,208,128]{2,1,0:T(8,128)(2,1)S(1)} %pad_maximum_fusion.refs_0_), channel_id=1, source_target_pairs={{0,3},{1,2},{2,1},{3,0},{4,7},{5,6},{6,5},{7,4},{8,11},{9,10},{10,... | collective-permute-start | bytes 638984 | tf_op jit(solution)/shard_map/ppermute | solution.py:782
  19.6 8.5 %collective-permute-start.4 = (bf16[4,208,128]{2,1,0:T(8,128)(2,1)S(1)}, bf16[4,208,128]{2,1,0:T(8,128)(2,1)S(1)}, u32[]{:S(2)}, u32[]{:S(2)}) collective-permute-start(bf16[4,208,128]{2,1,0:T(8,128)(2,1)S(1)} %pad_maximum_fusion.refs_0_), channel_id=1, source_target_pairs={{0,2},{1,3},{2,0},{3,1},{4,6},{5,7},{6,4},{7,5},{8,10},{9,11},{10,... | collective-permute-start | bytes 638984 | tf_op jit(solution)/shard_map/ppermute | solution.py:782
  20.1 8.1 %collective-permute-start.3 = (bf16[4,208,128]{2,1,0:T(8,128)(2,1)S(1)}, bf16[4,208,128]{2,1,0:T(8,128)(2,1)S(1)}, u32[]{:S(2)}, u32[]{:S(2)}) collective-permute-start(bf16[4,208,128]{2,1,0:T(8,128)(2,1)S(1)} %pad_maximum_fusion.refs_0_), channel_id=1, source_target_pairs={{0,1},{1,0},{2,3},{3,2},{4,5},{5,4},{6,7},{7,6},{8,9},{9,8},{10,11... | collective-permute-start | bytes 638984 | tf_op jit(solution)/shard_map/ppermute | solution.py:782
  20.4 6.6 %collective-permute-start.9 = (bf16[4,112,128]{2,1,0:T(8,128)(2,1)S(1)}, bf16[4,112,128]{2,1,0:T(8,128)(2,1)S(1)}, u32[]{:S(2)}, u32[]{:S(2)}) collective-permute-start(bf16[4,112,128]{2,1,0:T(8,128)(2,1)S(1)} %pad_maximum_fusion.1.refs_4_), channel_id=1, source_target_pairs={{0,4},{1,5},{2,6},{3,7},{4,8},{5,9},{6,10},{7,11},{8,12},{9,13},{1... | collective-permute-start | bytes 344072 | tf_op jit(solution)/shard_map/ppermute | solution.py:782
  24.6 2.4 %collective-permute-start.19 = (bf16[4,112,128]{2,1,0:T(8,128)(2,1)S(1)}, bf16[4,112,128]{2,1,0:T(8,128)(2,1)S(1)}, u32[]{:S(2)}, u32[]{:S(2)}) collective-permute-start(bf16[4,112,128]{2,1,0:T(8,128)(2,1)S(1)} %collective-permute-done.11.refs_7_), channel_id=1, source_target_pairs={{0,16},{1,17},{2,18},{3,19},{4,20},{5,21},{6,22},{7,23},{8,24},{9,... | collective-permute-start | bytes 344072 | tf_op jit(solution)/shard_map/ppermute | solution.py:782
  27.0 1.7 %collective-permute-start.18 = (bf16[4,112,128]{2,1,0:T(8,128)(2,1)S(1)}, bf16[4,112,128]{2,1,0:T(8,128)(2,1)S(1)}, u32[]{:S(2)}, u32[]{:S(2)}) collective-permute-start(bf16[4,112,128]{2,1,0:T(8,128)(2,1)S(1)} %collective-permute-done.10.refs_6_), channel_id=1, source_target_pairs={{0,16},{1,17},{2,18},{3,19},{4,20},{5,21},{6,22},{7,23},{8,24},{9,... | collective-permute-start | bytes 344072 | tf_op jit(solution)/shard_map/ppermute | solution.py:782
  27.0 3.1 %collective-permute-start.12 = (bf16[4,208,128]{2,1,0:T(8,128)(2,1)S(1)}, bf16[4,208,128]{2,1,0:T(8,128)(2,1)S(1)}, u32[]{:S(2)}, u32[]{:S(2)}) collective-permute-start(bf16[4,208,128]{2,1,0:T(8,128)(2,1)S(1)} %pad_maximum_fusion.refs_0_), channel_id=1, source_target_pairs={{0,16},{1,17},{2,18},{3,19},{4,20},{5,21},{6,22},{7,23},{8,24},{9,... | collective-permute-start | bytes 638984 | tf_op jit(solution)/shard_map/ppermute | solution.py:782
  27.5 2.6 %collective-permute-start.15 = (bf16[4,208,128]{2,1,0:T(8,128)(2,1)S(1)}, bf16[4,208,128]{2,1,0:T(8,128)(2,1)S(1)}, u32[]{:S(2)}, u32[]{:S(2)}) collective-permute-start(bf16[4,208,128]{2,1,0:T(8,128)(2,1)S(1)} %collective-permute-done.5.refs_3_), channel_id=1, source_target_pairs={{0,16},{1,17},{2,18},{3,19},{4,20},{5,21},{6,22},{7,23},{8,24},{9,... | collective-permute-start | bytes 638984 | tf_op jit(solution)/shard_map/ppermute | solution.py:782
  28.1 1.9 %collective-permute-start.14 = (bf16[4,208,128]{2,1,0:T(8,128)(2,1)S(1)}, bf16[4,208,128]{2,1,0:T(8,128)(2,1)S(1)}, u32[]{:S(2)}, u32[]{:S(2)}) collective-permute-start(bf16[4,208,128]{2,1,0:T(8,128)(2,1)S(1)} %collective-permute-done.4.refs_2_), channel_id=1, source_target_pairs={{0,16},{1,17},{2,18},{3,19},{4,20},{5,21},{6,22},{7,23},{8,24},{9,... | collective-permute-start | bytes 638984 | tf_op jit(solution)/shard_map/ppermute | solution.py:782
  28.2 1.8 %collective-permute-start.13 = (bf16[4,208,128]{2,1,0:T(8,128)(2,1)S(1)}, bf16[4,208,128]{2,1,0:T(8,128)(2,1)S(1)}, u32[]{:S(2)}, u32[]{:S(2)}) collective-permute-start(bf16[4,208,128]{2,1,0:T(8,128)(2,1)S(1)} %collective-permute-done.3.refs_1_), channel_id=1, source_target_pairs={{0,16},{1,17},{2,18},{3,19},{4,20},{5,21},{6,22},{7,23},{8,24},{9,... | collective-permute-start | bytes 638984 | tf_op jit(solution)/shard_map/ppermute | solution.py:782
  28.7 1.4 %collective-permute-start.17 = (bf16[4,112,128]{2,1,0:T(8,128)(2,1)S(1)}, bf16[4,112,128]{2,1,0:T(8,128)(2,1)S(1)}, u32[]{:S(2)}, u32[]{:S(2)}) collective-permute-start(bf16[4,112,128]{2,1,0:T(8,128)(2,1)S(1)} %collective-permute-done.9.refs_5_), channel_id=1, source_target_pairs={{0,16},{1,17},{2,18},{3,19},{4,20},{5,21},{6,22},{7,23},{8,24},{9,... | collective-permute-start | bytes 344072 | tf_op jit(solution)/shard_map/ppermute | solution.py:782
  50.7 3.1 %collective-permute-start.20 = (bf16[16,320,128]{2,1,0:T(8,128)(2,1)S(1)}, bf16[16,320,128]{2,1,0:T(8,128)(2,1)S(1)}, u32[]{:S(2)}, u32[]{:S(2)}) collective-permute-start(bf16[16,320,128]{2,1,0:T(8,128)(2,1)S(1)} %get-tuple-element.72), channel_id=1, source_target_pairs={{0,16},{1,17},{2,18},{3,19},{4,20},{5,21},{6,22},{7,23},{8,24},{9,... | collective-permute-start | bytes 3932168 | tf_op jit(solution)/shard_map/ppermute | solution.py:782
  54.1 9.9 %collective-permute-start.22 = (bf16[2,4,160,128]{3,2,1,0:T(8,128)(2,1)S(1)}, bf16[2,4,160,128]{3,2,1,0:T(8,128)(2,1)S(1)}, u32[]{:S(2)}, u32[]{:S(2)}) collective-permute-start(bf16[2,4,160,128]{3,2,1,0:T(8,128)(2,1)S(1)} %get-tuple-element.76), channel_id=1, source_target_pairs={{0,1},{1,0},{2,3},{3,2},{4,5},{5,4},{6,7},{7,6},{8,9},{9,8},{10,11... | collective-permute-start | bytes 983048 | tf_op jit(solution)/shard_map/ppermute | solution.py:782
  55.6 9.6 %collective-permute-start.21 = (bf16[2,4,160,128]{3,2,1,0:T(8,128)(2,1)S(1)}, bf16[2,4,160,128]{3,2,1,0:T(8,128)(2,1)S(1)}, u32[]{:S(2)}, u32[]{:S(2)}) collective-permute-start(bf16[2,4,160,128]{3,2,1,0:T(8,128)(2,1)S(1)} %get-tuple-element.75._), channel_id=1, source_target_pairs={{0,2},{1,3},{2,0},{3,1},{4,6},{5,7},{6,4},{7,5},{8,10},{9,11},{10,... | collective-permute-start | bytes 983048 | tf_op jit(solution)/shard_map/ppermute | solution.py:782
  65.3 5.4 %collective-permute-start.23 = (bf16[4,160,128]{2,1,0:T(8,128)(2,1)S(1)}, bf16[4,160,128]{2,1,0:T(8,128)(2,1)S(1)}, u32[]{:S(2)}, u32[]{:S(2)}) collective-permute-start(bf16[4,160,128]{2,1,0:T(8,128)(2,1)S(1)} %get-tuple-element.79), channel_id=1, source_target_pairs={{0,1},{1,0},{2,3},{3,2},{4,5},{5,4},{6,7},{7,6},{8,9},{9,8},{10,11... | collective-permute-start | bytes 491528 | tf_op jit(solution)/shard_map/ppermute | solution.py:782
  65.9 5.3 %collective-permute-start.24 = (bf16[4,160,128]{2,1,0:T(8,128)(2,1)S(1)}, bf16[4,160,128]{2,1,0:T(8,128)(2,1)S(1)}, u32[]{:S(2)}, u32[]{:S(2)}) collective-permute-start(bf16[4,160,128]{2,1,0:T(8,128)(2,1)S(1)} %get-tuple-element.80), channel_id=1, source_target_pairs={{0,2},{1,3},{2,0},{3,1},{4,6},{5,7},{6,4},{7,5},{8,10},{9,11},{10,... | collective-permute-start | bytes 491528 | tf_op jit(solution)/shard_map/ppermute | solution.py:782
  71.3 10.2 %collective-permute-start.26 = (bf16[320,128]{1,0:T(8,128)(2,1)S(1)}, bf16[320,128]{1,0:T(8,128)(2,1)S(1)}, u32[]{:S(2)}, u32[]{:S(2)}) collective-permute-start(bf16[320,128]{1,0:T(8,128)(2,1)S(1)} %get-tuple-element.83), channel_id=1, source_target_pairs={{0,8},{1,9},{2,10},{3,11},{4,12},{5,13},{6,14},{7,15},{8,0},{9,1},... | collective-permute-start | bytes 245768 | tf_op jit(solution)/shard_map/ppermute | solution.py:782
  73.6 7.9 %collective-permute-start.27 = (bf16[320,128]{1,0:T(8,128)(2,1)S(1)}, bf16[320,128]{1,0:T(8,128)(2,1)S(1)}, u32[]{:S(2)}, u32[]{:S(2)}) collective-permute-start(bf16[320,128]{1,0:T(8,128)(2,1)S(1)} %get-tuple-element.84), channel_id=1, source_target_pairs={{0,12},{1,13},{2,14},{3,15},{4,8},{5,9},{6,10},{7,11},{8,4},{9,5},... | collective-permute-start | bytes 245768 | tf_op jit(solution)/shard_map/ppermute | solution.py:782
  76.1 5.4 %collective-permute-start.25 = (bf16[320,128]{1,0:T(8,128)(2,1)S(1)}, bf16[320,128]{1,0:T(8,128)(2,1)S(1)}, u32[]{:S(2)}, u32[]{:S(2)}) collective-permute-start(bf16[320,128]{1,0:T(8,128)(2,1)S(1)} %get-tuple-element.82._), channel_id=1, source_target_pairs={{0,4},{1,5},{2,6},{3,7},{4,0},{5,1},{6,2},{7,3},{8,12},{9,13},{10,... | collective-permute-start | bytes 245768 | tf_op jit(solution)/shard_map/ppermute | solution.py:782
  88.3 1.2 %collective-permute-start.28 = (f32[1,512]{1,0:T(1,128)S(1)}, f32[1,512]{1,0:T(1,128)S(1)}, u32[]{:S(2)}, u32[]{:S(2)}) collective-permute-start(f32[1,512]{1,0:T(1,128)S(1)} %get-tuple-element.86.left), channel_id=1, source_target_pairs={{0,16},{1,17},{2,18},{3,19},{4,20},{5,21},{6,22},{7,23},{8,24},{9,... | collective-permute-start | bytes 6152 | tf_op jit(solution)/shard_map/ppermute | solution.py:782
  89.5 3.6 %collective-permute-start.29 = (f32[1,512]{1,0:T(1,128)S(1)}, f32[1,512]{1,0:T(1,128)S(1)}, u32[]{:S(2)}, u32[]{:S(2)}) collective-permute-start(f32[1,512]{1,0:T(1,128)S(1)} %add.9.left), channel_id=1, source_target_pairs={{0,1},{1,0},{2,3},{3,2},{4,5},{5,4},{6,7},{7,6},{8,9},{9,8},{10,11... | collective-permute-start | bytes 6152 | tf_op jit(solution)/shard_map/ppermute | solution.py:808
  93.1 3.6 %collective-permute-start.30 = (f32[1,512]{1,0:T(1,128)S(1)}, f32[1,512]{1,0:T(1,128)S(1)}, u32[]{:S(2)}, u32[]{:S(2)}) collective-permute-start(f32[1,512]{1,0:T(1,128)S(1)} %add.10.left), channel_id=1, source_target_pairs={{0,2},{1,3},{2,0},{3,1},{4,6},{5,7},{6,4},{7,5},{8,10},{9,11},{10,... | collective-permute-start | bytes 6152 | tf_op jit(solution)/shard_map/ppermute | solution.py:808
  96.7 3.6 %collective-permute-start.31 = (f32[1,512]{1,0:T(1,128)S(1)}, f32[1,512]{1,0:T(1,128)S(1)}, u32[]{:S(2)}, u32[]{:S(2)}) collective-permute-start(f32[1,512]{1,0:T(1,128)S(1)} %add.11.left), channel_id=1, source_target_pairs={{0,4},{1,5},{2,6},{3,7},{4,0},{5,1},{6,2},{7,3},{8,12},{9,13},{10,... | collective-permute-start | bytes 6152 | tf_op jit(solution)/shard_map/ppermute | solution.py:808
  100.3 4.6 %copy-start.2 = (f32[1,39936]{1,0:T(1,128)S(1)}, f32[1,39936]{1,0:T(1,128)}, u32[]{:S(2)}) copy-start(f32[1,39936]{1,0:T(1,128)} %param.14) | copy-start | bytes 479236
  100.3 4.6 %copy-start.3 = (f32[1,39936]{1,0:T(1,128)S(1)}, f32[1,39936]{1,0:T(1,128)}, u32[]{:S(2)}) copy-start(f32[1,39936]{1,0:T(1,128)} %param.15) | copy-start | bytes 479236
  100.3 4.6 %copy-start.4 = (f32[1,39936]{1,0:T(1,128)S(1)}, f32[1,39936]{1,0:T(1,128)}, u32[]{:S(2)}) copy-start(f32[1,39936]{1,0:T(1,128)} %param.16) | copy-start | bytes 479236
  100.3 4.6 %copy-start.6 = (s32[2]{0:T(128)S(1)}, s32[2]{0:T(128)}, u32[]{:S(2)}) copy-start(s32[2]{0:T(128)} %counts.1) | copy-start | bytes 28
  100.3 4.5 %collective-permute-start.32 = (f32[1,512]{1,0:T(1,128)S(1)}, f32[1,512]{1,0:T(1,128)S(1)}, u32[]{:S(2)}, u32[]{:S(2)}) collective-permute-start(f32[1,512]{1,0:T(1,128)S(1)} %add.12.left), channel_id=1, source_target_pairs={{0,8},{1,9},{2,10},{3,11},{4,12},{5,13},{6,14},{7,15},{8,0},{9,1},... | collective-permute-start | bytes 6152 | tf_op jit(solution)/shard_map/ppermute | solution.py:808
  104.9 6.5 %copy-start.1 = (bf16[8,196,768]{2,0,1:T(8,128)(2,1)S(1)}, bf16[8,196,768]{2,0,1:T(8,128)(2,1)}, u32[]{:S(2)}) copy-start(bf16[8,196,768]{2,0,1:T(8,128)(2,1)} %param.9) | copy-start | bytes 7225348

commit v5 on v4

--- a/solution.py
+++ b/solution.py
@@ -23,7 +23,7 @@
 TASKS = 2
 KMAX = 200
 KB = TASKS * KMAX
-UPPER = 208
+UPPER = 256
 STEP = 10
 LANES = 128
 HALF = 64
@@ -1036,7 +1036,7 @@
     sums = butterfly(sums, place, resident)
     padded_rows = -(-shard_rows // 8) * 8
     loss_parts, norm, coefficients, new_master, new_first, new_second = pl.pallas_call(
-        functools.partial(update_kernel, divisor(78), float(2 * shard_len * chips)),
+        functools.partial(update_kernel, divisor(156), float(2 * shard_len * chips)),
         in_specs=[SMEM] + [VMEM] * 8,
         out_specs=[SMEM, SMEM] + [VMEM] * 4,
         out_shape=[

time: 112 us -> 111 us (level)
  no operation moved by 1% of the time
where the time goes in v5:
time: 111 us; the launch traced here: 110 us
  Pallas kernels  46 us (41%)
  starting transfers between devices  38 us (34%)
  waiting for transfers between devices  24.5 us (22%)
    ppermute x29, starting transfers between devices, moved(): return lax.ppermute(value, ('section', 'dp'), pairs)  32 us
    ppermute x29, waiting for transfers between devices, moved(): return lax.ppermute(value, ('section', 'dp'), pairs)  15.1 us
    pallas_call x2, Pallas kernels, fetch(): pl.pallas_call(functools.partial(fetch_kernel, first, last), in_specs=[AN...  11.1 us
    ppermute x4, waiting for transfers between devices, butterfly(): value = add(value, lax.ppermute(value, ('section', 'dp'), pairs), resident)  9.36 us
    pallas_call x1, Pallas kernels, late(): pl.pallas_call(functools.partial(late_kernel, place, per, image_total), i...  7.77 us
    pallas_call x1, Pallas kernels, back(): pl.pallas_call(functools.partial(back_kernel, place, per), in_specs=[VMEM...  7.28 us
    pallas_call x1, Pallas kernels, body(): pl.pallas_call(functools.partial(inner_kernel, divisor(26)), in_specs=[VM...  6.75 us
    pallas_call x1, Pallas kernels, body(): pl.pallas_call(functools.partial(update_kernel, divisor(156), float(2 * s...  6.06 us
  transfers between devices with their start and end apart: 33, of which 15 were waited for; matrix products, arithmetic and copies ran while one was open for 1% of the time, Pallas kernels for 10%

profile of v5, /device:TPU:0, one launch (start us, length us, event | category | flops | bytes accessed | tf_op | source)
XLA Modules:
  0.0 110.5 jit_solution(746289199998904277)
XLA Ops:
  0.6 0.0 copy-start
  0.6 1.1 shard.1
  1.8 3.0 %collective-permute-start.7 = (bf16[112,128]{1,0:T(8,128)(2,1)S(1)}, bf16[112,128]{1,0:T(8,128)(2,1)S(1)}, u32[]{:S(2)}, u32[]{:S(2)}) collective-permute-start(bf16[112,128]{1,0:T(8,128)(2,1)S(1)} %get-tuple-element.95), channel_id=1, source_target_pairs={{0,2},{1,3},{2,0},{3,1},{4,6},{5,7},{6,4},{7,5},{8,10},{9,11},{10,... | collective-permute-start | bytes 86024 | tf_op jit(solution)/shard_map/ppermute | solution.py:782
  4.8 1.5 %collective-permute-start.6 = (bf16[112,128]{1,0:T(8,128)(2,1)S(1)}, bf16[112,128]{1,0:T(8,128)(2,1)S(1)}, u32[]{:S(2)}, u32[]{:S(2)}) collective-permute-start(bf16[112,128]{1,0:T(8,128)(2,1)S(1)} %get-tuple-element.95), channel_id=1, source_target_pairs={{0,1},{1,0},{2,3},{3,2},{4,5},{5,4},{6,7},{7,6},{8,9},{9,8},{10,11... | collective-permute-start | bytes 86024 | tf_op jit(solution)/shard_map/ppermute | solution.py:782
  6.3 0.0 collective-permute-start.8
  6.3 3.1 %collective-permute-start.1 = (bf16[208,128]{1,0:T(8,128)(2,1)S(1)}, bf16[208,128]{1,0:T(8,128)(2,1)S(1)}, u32[]{:S(2)}, u32[]{:S(2)}) collective-permute-start(bf16[208,128]{1,0:T(8,128)(2,1)S(1)} %get-tuple-element.97), channel_id=1, source_target_pairs={{0,8},{1,9},{2,10},{3,11},{4,12},{5,13},{6,14},{7,15},{8,0},{9,1},... | collective-permute-start | bytes 159752 | tf_op jit(solution)/shard_map/ppermute | solution.py:782
  9.4 1.6 %collective-permute-start = (bf16[208,128]{1,0:T(8,128)(2,1)S(1)}, bf16[208,128]{1,0:T(8,128)(2,1)S(1)}, u32[]{:S(2)}, u32[]{:S(2)}) collective-permute-start(bf16[208,128]{1,0:T(8,128)(2,1)S(1)} %get-tuple-element.97), channel_id=1, source_target_pairs={{0,4},{1,5},{2,6},{3,7},{4,8},{5,9},{6,10},{7,11},{8,12},{9,13},{1... | collective-permute-start | bytes 159752 | tf_op jit(solution)/shard_map/ppermute | solution.py:782
  11.0 0.6 constant_dynamic-slice_fusion
  11.6 0.1 copy.16.refs_16_.refs_10_
  11.8 2.3 %collective-permute-start.2 = (bf16[208,128]{1,0:T(8,128)(2,1)S(1)}, bf16[208,128]{1,0:T(8,128)(2,1)S(1)}, u32[]{:S(2)}, u32[]{:S(2)}) collective-permute-start(bf16[208,128]{1,0:T(8,128)(2,1)S(1)} %get-tuple-element.97), channel_id=1, source_target_pairs={{0,12},{1,13},{2,14},{3,15},{4,0},{5,1},{6,2},{7,3},{8,4},{9,5},{1... | collective-permute-start | bytes 159752 | tf_op jit(solution)/shard_map/ppermute | solution.py:782
  14.1 0.1 collective-permute-start.16
  14.2 0.6 collective-permute-start.11
  14.8 1.3 %collective-permute-done.2 = bf16[208,128]{1,0:T(8,128)(2,1)S(1)} collective-permute-done((bf16[208,128]{1,0:T(8,128)(2,1)S(1)}, bf16[208,128]{1,0:T(8,128)(2,1)S(1)}, u32[]{:S(2)}, u32[]{:S(2)}) %collective-permute-start.2) | collective-permute-done | bytes 53280 | tf_op jit(solution)/shard_map/ppermute | solution.py:782
  16.1 0.7 collective-permute-start.10
  16.8 0.0 copy-start.5
  16.8 0.0 copy-start.7
  16.8 0.0 copy-start.8
  16.8 2.8 %collective-permute-start.5 = (bf16[4,208,128]{2,1,0:T(8,128)(2,1)S(1)}, bf16[4,208,128]{2,1,0:T(8,128)(2,1)S(1)}, u32[]{:S(2)}, u32[]{:S(2)}) collective-permute-start(bf16[4,208,128]{2,1,0:T(8,128)(2,1)S(1)} %pad_maximum_fusion.refs_0_), channel_id=1, source_target_pairs={{0,3},{1,2},{2,1},{3,0},{4,7},{5,6},{6,5},{7,4},{8,11},{9,10},{10,... | collective-permute-start | bytes 638984 | tf_op jit(solution)/shard_map/ppermute | solution.py:782
  19.6 0.5 collective-permute-start.4
  20.1 0.3 collective-permute-start.3
  20.4 4.2 %collective-permute-start.9 = (bf16[4,112,128]{2,1,0:T(8,128)(2,1)S(1)}, bf16[4,112,128]{2,1,0:T(8,128)(2,1)S(1)}, u32[]{:S(2)}, u32[]{:S(2)}) collective-permute-start(bf16[4,112,128]{2,1,0:T(8,128)(2,1)S(1)} %pad_maximum_fusion.1.refs_4_), channel_id=1, source_target_pairs={{0,4},{1,5},{2,6},{3,7},{4,8},{5,9},{6,10},{7,11},{8,12},{9,13},{1... | collective-permute-start | bytes 344072 | tf_op jit(solution)/shard_map/ppermute | solution.py:782
  24.6 2.4 %collective-permute-done.9.refs_5_ = bf16[4,112,128]{2,1,0:T(8,128)(2,1)S(1)} collective-permute-done((bf16[4,112,128]{2,1,0:T(8,128)(2,1)S(1)}, bf16[4,112,128]{2,1,0:T(8,128)(2,1)S(1)}, u32[]{:S(2)}, u32[]{:S(2)}) %collective-permute-start.9) | collective-permute-done | bytes 114720 | tf_op jit(solution)/shard_map/ppermute | solution.py:782
  27.0 0.5 collective-permute-start.12
  27.5 0.1 collective-permute-start.15
  27.6 0.6 collective-permute-done.4.refs_2_
  28.1 0.1 collective-permute-done.3.refs_1_
  28.2 0.4 collective-permute-start.13
  28.7 0.1 collective-permute-start.17
  28.7 1.3 %collective-permute-done.17.refs_13_ = bf16[4,112,128]{2,1,0:T(8,128)(2,1)S(1)} collective-permute-done((bf16[4,112,128]{2,1,0:T(8,128)(2,1)S(1)}, bf16[4,112,128]{2,1,0:T(8,128)(2,1)S(1)}, u32[]{:S(2)}, u32[]{:S(2)}) %collective-permute-start.17) | collective-permute-done | bytes 114720 | tf_op jit(solution)/shard_map/ppermute | solution.py:782
  30.1 5.5 %front.1 = (f32[832,192]{1,0:T(8,128)S(1)}, bf16[832,192]{1,0:T(8,128)(2,1)S(1)}, bf16[832,192]{1,0:T(8,128)(2,1)S(1)}, bf16[832,192]{1,0:T(8,128)(2,1)S(1)}, f3...) custom-call(bf16[4,208,128]{2,1,0:T(8,128)(2,1)S(1)} %pad_maximum_fu, ...), custom_call_target="tpu_custom_call" | custom-call | flops 3000000000 | bytes 30000000 | tf_op jit(solution)/shard_map/front/pallas_call | solution.py:856
  35.6 7.8 %late.1 = (bf16[832,192]{1,0:T(8,128)(2,1)S(1)}, bf16[16,320,128]{2,1,0:T(8,128)(2,1)S(1)}, f32[1,128]{1,0:T(1,128)S(1)}) custom-call(s32[8]{0:T(128)S(1)} %copy-done.8, s32[8]{0:T(128)S(1)} %copy-done.5, bf16[4,208,128]{2,1,0:T(8,128)(2,1)S(1)} %pad_maximum_fusion.refs_0_, bf16[4,208,128]{2,1,0:T(8,128)(2,1)S(1)} %collective-permute-done.3.refs_1_, ...), custom_call_target="tpu_custom_call" | custom-call | flops 3000000000 | bytes 30000000 | tf_op jit(solution)/shard_map/late/pallas_call | solution.py:880
  43.4 7.3 %back.1 = (bf16[16,320,128]{2,1,0:T(8,128)(2,1)S(1)}, bf16[16,320,128]{2,1,0:T(8,128)(2,1)S(1)}) custom-call(bf16[832,192]{1,0:T(8,128)(2,1)S(1)} %get-tuple-element.53.refs_0_, f32[832,192]{1,0:T(8,128)S(1)} %get-tuple-element.54.refs_1_, bf16[832,192]{1,0:T(8,128)(2,1)S(1)} %get-tuple-element.55.refs_2_, bf16[832,192]{1,0:T(8,128)(2,1)S(1)} %get-tuple-element.56.refs_3_, ...), custom_call_target="tpu_custom_call" | custom-call | flops 3000000000 | bytes 30000000 | tf_op jit(solution)/shard_map/back/pallas_call | solution.py:906
  50.7 0.3 collective-permute-start.20
  51.0 2.8 %collective-permute-done.20.given = bf16[16,320,128]{2,1,0:T(8,128)(2,1)S(1)} collective-permute-done((bf16[16,320,128]{2,1,0:T(8,128)(2,1)S(1)}, bf16[16,320,128]{2,1,0:T(8,128)(2,1)S(1)}, u32[]{:S(2)}, u32[]{:S(2)}) %collective-permute-start.20) | collective-permute-done | bytes 1310752 | tf_op jit(solution)/shard_map/ppermute | solution.py:782
  53.8 0.3 split.1
  54.1 1.6 %collective-permute-start.22 = (bf16[2,4,160,128]{3,2,1,0:T(8,128)(2,1)S(1)}, bf16[2,4,160,128]{3,2,1,0:T(8,128)(2,1)S(1)}, u32[]{:S(2)}, u32[]{:S(2)}) collective-permute-start(bf16[2,4,160,128]{3,2,1,0:T(8,128)(2,1)S(1)} %get-tuple-element.76), channel_id=1, source_target_pairs={{0,1},{1,0},{2,3},{3,2},{4,5},{5,4},{6,7},{7,6},{8,9},{9,8},{10,11... | collective-permute-start | bytes 983048 | tf_op jit(solution)/shard_map/ppermute | solution.py:782
  55.6 1.5 %collective-permute-start.21 = (bf16[2,4,160,128]{3,2,1,0:T(8,128)(2,1)S(1)}, bf16[2,4,160,128]{3,2,1,0:T(8,128)(2,1)S(1)}, u32[]{:S(2)}, u32[]{:S(2)}) collective-permute-start(bf16[2,4,160,128]{3,2,1,0:T(8,128)(2,1)S(1)} %get-tuple-element.75._), channel_id=1, source_target_pairs={{0,2},{1,3},{2,0},{3,1},{4,6},{5,7},{6,4},{7,5},{8,10},{9,11},{10,... | collective-permute-start | bytes 983048 | tf_op jit(solution)/shard_map/ppermute | solution.py:782
  57.1 6.8 %fetch.2._.refs_4_.upper = bf16[256,39936]{1,0:T(8,128)(2,1)S(1)} custom-call(bf16[2,4,160,128]{3,2,1,0:T(8,128)(2,1)S(1)} %get-tuple-element.75._, bf16[400,39936]{1,0:T(8,128)(2,1)} %bitcast.22), custom_call_target="tpu_custom_call" | custom-call | bytes 40894464 | tf_op jit(solution)/shard_map/fetch/pallas_call | solution.py:979
  63.9 0.0 collective-permute-done.22.refs_1_
  64.0 1.2 %collective-permute-done.21.refs_0_ = bf16[2,4,160,128]{3,2,1,0:T(8,128)(2,1)S(1)} collective-permute-done((bf16[2,4,160,128]{3,2,1,0:T(8,128)(2,1)S(1)}, bf16[2,4,160,128]{3,2,1,0:T(8,128)(2,1)S(1)}, u32[]{:S(2)}, u32[]{:S(2)}) %collective-permute-start.21) | collective-permute-done | bytes 327712 | tf_op jit(solution)/shard_map/ppermute | solution.py:782
  65.2 0.1 turn.1
  65.3 0.6 collective-permute-start.23
  65.9 1.6 %collective-permute-start.24 = (bf16[4,160,128]{2,1,0:T(8,128)(2,1)S(1)}, bf16[4,160,128]{2,1,0:T(8,128)(2,1)S(1)}, u32[]{:S(2)}, u32[]{:S(2)}) collective-permute-start(bf16[4,160,128]{2,1,0:T(8,128)(2,1)S(1)} %get-tuple-element.80), channel_id=1, source_target_pairs={{0,2},{1,3},{2,0},{3,1},{4,6},{5,7},{6,4},{7,5},{8,10},{9,11},{10,... | collective-permute-start | bytes 491528 | tf_op jit(solution)/shard_map/ppermute | solution.py:782
  67.4 3.3 %collective-permute-done.23.refs_0_ = bf16[4,160,128]{2,1,0:T(8,128)(2,1)S(1)} collective-permute-done((bf16[4,160,128]{2,1,0:T(8,128)(2,1)S(1)}, bf16[4,160,128]{2,1,0:T(8,128)(2,1)S(1)}, u32[]{:S(2)}, u32[]{:S(2)}) %collective-permute-start.23) | collective-permute-done | bytes 163872 | tf_op jit(solution)/shard_map/ppermute | solution.py:782
  70.7 0.5 collective-permute-done.24.refs_1_
  71.2 0.1 plane.1
  71.3 2.3 %collective-permute-start.26 = (bf16[320,128]{1,0:T(8,128)(2,1)S(1)}, bf16[320,128]{1,0:T(8,128)(2,1)S(1)}, u32[]{:S(2)}, u32[]{:S(2)}) collective-permute-start(bf16[320,128]{1,0:T(8,128)(2,1)S(1)} %get-tuple-element.83), channel_id=1, source_target_pairs={{0,8},{1,9},{2,10},{3,11},{4,12},{5,13},{6,14},{7,15},{8,0},{9,1},... | collective-permute-start | bytes 245768 | tf_op jit(solution)/shard_map/ppermute | solution.py:782
  73.6 2.5 %collective-permute-start.27 = (bf16[320,128]{1,0:T(8,128)(2,1)S(1)}, bf16[320,128]{1,0:T(8,128)(2,1)S(1)}, u32[]{:S(2)}, u32[]{:S(2)}) collective-permute-start(bf16[320,128]{1,0:T(8,128)(2,1)S(1)} %get-tuple-element.84), channel_id=1, source_target_pairs={{0,12},{1,13},{2,14},{3,15},{4,8},{5,9},{6,10},{7,11},{8,4},{9,5},... | collective-permute-start | bytes 245768 | tf_op jit(solution)/shard_map/ppermute | solution.py:782
  76.1 4.3 %fetch.3.refs_5_.__.lower = bf16[144,39936]{1,0:T(8,128)(2,1)S(1)} custom-call(bf16[320,128]{1,0:T(8,128)(2,1)S(1)} %get-tuple-element.82._, bf16[400,39936]{1,0:T(8,128)(2,1)} %bitcast.23), custom_call_target="tpu_custom_call" | custom-call | bytes 23003136 | tf_op jit(solution)/shard_map/fetch/pallas_call | solution.py:979
  80.4 0.4 collective-permute-done.25.refs_1_
  80.8 6.8 %inner.1 = (f32[312,128]{1,0:T(8,128)S(1)}, f32[1,512]{1,0:T(1,128)S(1)}) custom-call(f32[320,128]{1,0:T(8,128)S(1)} %get-tuple-element.81.refs_0_, bf16[320,128]{1,0:T(8,128)(2,1)S(1)} %collective-permute-done.25.refs_1_, bf16[320,128]{1,0:T(8,128)(2,1)S(1)} %collective-permute-done.26.refs_2_, bf16[320,128]{1,0:T(8,128)(2,1)S(1)} %collective-permute-done.27.refs_3_, ...), custom_call_target="tpu_custom_call" | custom-call | tf_op jit(solution)/shard_map/inner/pallas_call | solution.py:1027
  87.6 0.1 collective-permute-start.28
  87.7 1.1 %collective-permute-done.28.right = f32[1,512]{1,0:T(1,128)S(1)} collective-permute-done((f32[1,512]{1,0:T(1,128)S(1)}, f32[1,512]{1,0:T(1,128)S(1)}, u32[]{:S(2)}, u32[]{:S(2)}) %collective-permute-start.28) | collective-permute-done | bytes 2080 | tf_op jit(solution)/shard_map/ppermute | solution.py:782
  88.8 1.4 %collective-permute-start.29 = (f32[1,512]{1,0:T(1,128)S(1)}, f32[1,512]{1,0:T(1,128)S(1)}, u32[]{:S(2)}, u32[]{:S(2)}) collective-permute-start(f32[1,512]{1,0:T(1,128)S(1)} %add.9.left), channel_id=1, source_target_pairs={{0,1},{1,0},{2,3},{3,2},{4,5},{5,4},{6,7},{7,6},{8,9},{9,8},{10,11... | collective-permute-start | bytes 6152 | tf_op jit(solution)/shard_map/ppermute | solution.py:808
  90.2 2.2 %collective-permute-done.29.right = f32[1,512]{1,0:T(1,128)S(1)} collective-permute-done((f32[1,512]{1,0:T(1,128)S(1)}, f32[1,512]{1,0:T(1,128)S(1)}, u32[]{:S(2)}, u32[]{:S(2)}) %collective-permute-start.29) | collective-permute-done | bytes 2080 | tf_op jit(solution)/shard_map/ppermute | solution.py:808
  92.4 1.4 %collective-permute-start.30 = (f32[1,512]{1,0:T(1,128)S(1)}, f32[1,512]{1,0:T(1,128)S(1)}, u32[]{:S(2)}, u32[]{:S(2)}) collective-permute-start(f32[1,512]{1,0:T(1,128)S(1)} %add.10.left), channel_id=1, source_target_pairs={{0,2},{1,3},{2,0},{3,1},{4,6},{5,7},{6,4},{7,5},{8,10},{9,11},{10,... | collective-permute-start | bytes 6152 | tf_op jit(solution)/shard_map/ppermute | solution.py:808
  93.8 2.2 %collective-permute-done.30.right = f32[1,512]{1,0:T(1,128)S(1)} collective-permute-done((f32[1,512]{1,0:T(1,128)S(1)}, f32[1,512]{1,0:T(1,128)S(1)}, u32[]{:S(2)}, u32[]{:S(2)}) %collective-permute-start.30) | collective-permute-done | bytes 2080 | tf_op jit(solution)/shard_map/ppermute | solution.py:808
  96.0 1.6 %collective-permute-start.31 = (f32[1,512]{1,0:T(1,128)S(1)}, f32[1,512]{1,0:T(1,128)S(1)}, u32[]{:S(2)}, u32[]{:S(2)}) collective-permute-start(f32[1,512]{1,0:T(1,128)S(1)} %add.11.left), channel_id=1, source_target_pairs={{0,4},{1,5},{2,6},{3,7},{4,0},{5,1},{6,2},{7,3},{8,12},{9,13},{10,... | collective-permute-start | bytes 6152 | tf_op jit(solution)/shard_map/ppermute | solution.py:808
  97.6 2.0 %collective-permute-done.31.right = f32[1,512]{1,0:T(1,128)S(1)} collective-permute-done((f32[1,512]{1,0:T(1,128)S(1)}, f32[1,512]{1,0:T(1,128)S(1)}, u32[]{:S(2)}, u32[]{:S(2)}) %collective-permute-start.31) | collective-permute-done | bytes 2080 | tf_op jit(solution)/shard_map/ppermute | solution.py:808
  99.6 0.0 copy-start.4
  99.6 1.5 %collective-permute-start.32 = (f32[1,512]{1,0:T(1,128)S(1)}, f32[1,512]{1,0:T(1,128)S(1)}, u32[]{:S(2)}, u32[]{:S(2)}) collective-permute-start(f32[1,512]{1,0:T(1,128)S(1)} %add.12.left), channel_id=1, source_target_pairs={{0,8},{1,9},{2,10},{3,11},{4,12},{5,13},{6,14},{7,15},{8,0},{9,1},... | collective-permute-start | bytes 6152 | tf_op jit(solution)/shard_map/ppermute | solution.py:808
  101.1 3.0 %collective-permute-done.32.right = f32[1,512]{1,0:T(1,128)S(1)} collective-permute-done((f32[1,512]{1,0:T(1,128)S(1)}, f32[1,512]{1,0:T(1,128)S(1)}, u32[]{:S(2)}, u32[]{:S(2)}) %collective-permute-start.32) | collective-permute-done | bytes 2080 | tf_op jit(solution)/shard_map/ppermute | solution.py:808
  104.2 0.0 copy-start.1
  104.2 6.1 %update.1 = (f32[3]{0:T(128)}, f32[1]{0:T(128)}, f32[2,200]{1,0:T(2,128)}, f32[312,128]{1,0:T(8,128)}, f32[312,128]{1,0:T(8,128)}, /*index=5*/f32[312,128]{1,0:T(8,128)}) custom-call(s32[2]{0:T(128)S(1)} %copy-done.6, f32[1,512]{1,0:T(1,128)S(1)} %add.13.sums, bf16[256,39936]{1,0:T(8,128)(2,1)S(1)} %fetch.2._.refs_4_.upper, ...), custom_call_target="tpu_custom_call" | custom-call | tf_op jit(solution)/shard_map/update/pallas_call | solution.py:1038
  (42 shorter events, 0.2 us)
Async XLA Ops:
  0.6 10.4 %copy-start = (bf16[8,196,768]{2,0,1:T(8,128)(2,1)S(1)}, bf16[8,196,768]{2,0,1:T(8,128)(2,1)}, u32[]{:S(2)}) copy-start(bf16[8,196,768]{2,0,1:T(8,128)(2,1)} %param.9) | copy-start | bytes 7225348
  1.8 10.0 %collective-permute-start.7 = (bf16[112,128]{1,0:T(8,128)(2,1)S(1)}, bf16[112,128]{1,0:T(8,128)(2,1)S(1)}, u32[]{:S(2)}, u32[]{:S(2)}) collective-permute-start(bf16[112,128]{1,0:T(8,128)(2,1)S(1)} %get-tuple-element.95), channel_id=1, source_target_pairs={{0,2},{1,3},{2,0},{3,1},{4,6},{5,7},{6,4},{7,5},{8,10},{9,11},{10,... | collective-permute-start | bytes 86024 | tf_op jit(solution)/shard_map/ppermute | solution.py:782
  4.8 9.3 %collective-permute-start.6 = (bf16[112,128]{1,0:T(8,128)(2,1)S(1)}, bf16[112,128]{1,0:T(8,128)(2,1)S(1)}, u32[]{:S(2)}, u32[]{:S(2)}) collective-permute-start(bf16[112,128]{1,0:T(8,128)(2,1)S(1)} %get-tuple-element.95), channel_id=1, source_target_pairs={{0,1},{1,0},{2,3},{3,2},{4,5},{5,4},{6,7},{7,6},{8,9},{9,8},{10,11... | collective-permute-start | bytes 86024 | tf_op jit(solution)/shard_map/ppermute | solution.py:782
  6.3 7.8 %collective-permute-start.8 = (bf16[112,128]{1,0:T(8,128)(2,1)S(1)}, bf16[112,128]{1,0:T(8,128)(2,1)S(1)}, u32[]{:S(2)}, u32[]{:S(2)}) collective-permute-start(bf16[112,128]{1,0:T(8,128)(2,1)S(1)} %get-tuple-element.95), channel_id=1, source_target_pairs={{0,3},{1,2},{2,1},{3,0},{4,7},{5,6},{6,5},{7,4},{8,11},{9,10},{10,... | collective-permute-start | bytes 86024 | tf_op jit(solution)/shard_map/ppermute | solution.py:782
  6.3 10.4 %collective-permute-start.1 = (bf16[208,128]{1,0:T(8,128)(2,1)S(1)}, bf16[208,128]{1,0:T(8,128)(2,1)S(1)}, u32[]{:S(2)}, u32[]{:S(2)}) collective-permute-start(bf16[208,128]{1,0:T(8,128)(2,1)S(1)} %get-tuple-element.97), channel_id=1, source_target_pairs={{0,8},{1,9},{2,10},{3,11},{4,12},{5,13},{6,14},{7,15},{8,0},{9,1},... | collective-permute-start | bytes 159752 | tf_op jit(solution)/shard_map/ppermute | solution.py:782
  9.4 7.3 %collective-permute-start = (bf16[208,128]{1,0:T(8,128)(2,1)S(1)}, bf16[208,128]{1,0:T(8,128)(2,1)S(1)}, u32[]{:S(2)}, u32[]{:S(2)}) collective-permute-start(bf16[208,128]{1,0:T(8,128)(2,1)S(1)} %get-tuple-element.97), channel_id=1, source_target_pairs={{0,4},{1,5},{2,6},{3,7},{4,8},{5,9},{6,10},{7,11},{8,12},{9,13},{1... | collective-permute-start | bytes 159752 | tf_op jit(solution)/shard_map/ppermute | solution.py:782
  11.8 4.3 %collective-permute-start.2 = (bf16[208,128]{1,0:T(8,128)(2,1)S(1)}, bf16[208,128]{1,0:T(8,128)(2,1)S(1)}, u32[]{:S(2)}, u32[]{:S(2)}) collective-permute-start(bf16[208,128]{1,0:T(8,128)(2,1)S(1)} %get-tuple-element.97), channel_id=1, source_target_pairs={{0,12},{1,13},{2,14},{3,15},{4,0},{5,1},{6,2},{7,3},{8,4},{9,5},{1... | collective-permute-start | bytes 159752 | tf_op jit(solution)/shard_map/ppermute | solution.py:782
  14.1 6.0 %collective-permute-start.16 = (bf16[4,112,128]{2,1,0:T(8,128)(2,1)S(1)}, bf16[4,112,128]{2,1,0:T(8,128)(2,1)S(1)}, u32[]{:S(2)}, u32[]{:S(2)}) collective-permute-start(bf16[4,112,128]{2,1,0:T(8,128)(2,1)S(1)} %pad_maximum_fusion.1.refs_4_), channel_id=1, source_target_pairs={{0,16},{1,17},{2,18},{3,19},{4,20},{5,21},{6,22},{7,23},{8,24},{9,... | collective-permute-start | bytes 344072 | tf_op jit(solution)/shard_map/ppermute | solution.py:782
  14.2 6.2 %collective-permute-start.11 = (bf16[4,112,128]{2,1,0:T(8,128)(2,1)S(1)}, bf16[4,112,128]{2,1,0:T(8,128)(2,1)S(1)}, u32[]{:S(2)}, u32[]{:S(2)}) collective-permute-start(bf16[4,112,128]{2,1,0:T(8,128)(2,1)S(1)} %pad_maximum_fusion.1.refs_4_), channel_id=1, source_target_pairs={{0,12},{1,13},{2,14},{3,15},{4,0},{5,1},{6,2},{7,3},{8,4},{9,5},{1... | collective-permute-start | bytes 344072 | tf_op jit(solution)/shard_map/ppermute | solution.py:782
  16.1 8.5 %collective-permute-start.10 = (bf16[4,112,128]{2,1,0:T(8,128)(2,1)S(1)}, bf16[4,112,128]{2,1,0:T(8,128)(2,1)S(1)}, u32[]{:S(2)}, u32[]{:S(2)}) collective-permute-start(bf16[4,112,128]{2,1,0:T(8,128)(2,1)S(1)} %pad_maximum_fusion.1.refs_4_), channel_id=1, source_target_pairs={{0,8},{1,9},{2,10},{3,11},{4,12},{5,13},{6,14},{7,15},{8,0},{9,1},... | collective-permute-start | bytes 344072 | tf_op jit(solution)/shard_map/ppermute | solution.py:782
  16.8 18.8 %copy-start.5 = (s32[8]{0:T(128)S(1)}, s32[8]{0:T(128)}, u32[]{:S(2)}) copy-start(s32[8]{0:T(128)} %replay.3) | copy-start | bytes 100
  16.8 18.8 %copy-start.7 = (f32[8,1000]{1,0:T(8,128)S(1)}, f32[8,1000]{1,0:T(8,128)}, u32[]{:S(2)}) copy-start(f32[8,1000]{1,0:T(8,128)} %refs_17_.1) | copy-start | bytes 96004
  16.8 18.8 %copy-start.8 = (s32[8]{0:T(128)S(1)}, s32[8]{0:T(128)}, u32[]{:S(2)}) copy-start(s32[8]{0:T(128)} %labels.1) | copy-start | bytes 100
  16.8 10.7 %collective-permute-start.5 = (bf16[4,208,128]{2,1,0:T(8,128)(2,1)S(1)}, bf16[4,208,128]{2,1,0:T(8,128)(2,1)S(1)}, u32[]{:S(2)}, u32[]{:S(2)}) collective-permute-start(bf16[4,208,128]{2,1,0:T(8,128)(2,1)S(1)} %pad_maximum_fusion.refs_0_), channel_id=1, source_target_pairs={{0,3},{1,2},{2,1},{3,0},{4,7},{5,6},{6,5},{7,4},{8,11},{9,10},{10,... | collective-permute-start | bytes 638984 | tf_op jit(solution)/shard_map/ppermute | solution.py:782
  19.6 8.5 %collective-permute-start.4 = (bf16[4,208,128]{2,1,0:T(8,128)(2,1)S(1)}, bf16[4,208,128]{2,1,0:T(8,128)(2,1)S(1)}, u32[]{:S(2)}, u32[]{:S(2)}) collective-permute-start(bf16[4,208,128]{2,1,0:T(8,128)(2,1)S(1)} %pad_maximum_fusion.refs_0_), channel_id=1, source_target_pairs={{0,2},{1,3},{2,0},{3,1},{4,6},{5,7},{6,4},{7,5},{8,10},{9,11},{10,... | collective-permute-start | bytes 638984 | tf_op jit(solution)/shard_map/ppermute | solution.py:782
  20.1 8.1 %collective-permute-start.3 = (bf16[4,208,128]{2,1,0:T(8,128)(2,1)S(1)}, bf16[4,208,128]{2,1,0:T(8,128)(2,1)S(1)}, u32[]{:S(2)}, u32[]{:S(2)}) collective-permute-start(bf16[4,208,128]{2,1,0:T(8,128)(2,1)S(1)} %pad_maximum_fusion.refs_0_), channel_id=1, source_target_pairs={{0,1},{1,0},{2,3},{3,2},{4,5},{5,4},{6,7},{7,6},{8,9},{9,8},{10,11... | collective-permute-start | bytes 638984 | tf_op jit(solution)/shard_map/ppermute | solution.py:782
  20.4 6.6 %collective-permute-start.9 = (bf16[4,112,128]{2,1,0:T(8,128)(2,1)S(1)}, bf16[4,112,128]{2,1,0:T(8,128)(2,1)S(1)}, u32[]{:S(2)}, u32[]{:S(2)}) collective-permute-start(bf16[4,112,128]{2,1,0:T(8,128)(2,1)S(1)} %pad_maximum_fusion.1.refs_4_), channel_id=1, source_target_pairs={{0,4},{1,5},{2,6},{3,7},{4,8},{5,9},{6,10},{7,11},{8,12},{9,13},{1... | collective-permute-start | bytes 344072 | tf_op jit(solution)/shard_map/ppermute | solution.py:782
  24.6 2.4 %collective-permute-start.19 = (bf16[4,112,128]{2,1,0:T(8,128)(2,1)S(1)}, bf16[4,112,128]{2,1,0:T(8,128)(2,1)S(1)}, u32[]{:S(2)}, u32[]{:S(2)}) collective-permute-start(bf16[4,112,128]{2,1,0:T(8,128)(2,1)S(1)} %collective-permute-done.11.refs_7_), channel_id=1, source_target_pairs={{0,16},{1,17},{2,18},{3,19},{4,20},{5,21},{6,22},{7,23},{8,24},{9,... | collective-permute-start | bytes 344072 | tf_op jit(solution)/shard_map/ppermute | solution.py:782
  27.0 1.7 %collective-permute-start.18 = (bf16[4,112,128]{2,1,0:T(8,128)(2,1)S(1)}, bf16[4,112,128]{2,1,0:T(8,128)(2,1)S(1)}, u32[]{:S(2)}, u32[]{:S(2)}) collective-permute-start(bf16[4,112,128]{2,1,0:T(8,128)(2,1)S(1)} %collective-permute-done.10.refs_6_), channel_id=1, source_target_pairs={{0,16},{1,17},{2,18},{3,19},{4,20},{5,21},{6,22},{7,23},{8,24},{9,... | collective-permute-start | bytes 344072 | tf_op jit(solution)/shard_map/ppermute | solution.py:782
  27.0 3.1 %collective-permute-start.12 = (bf16[4,208,128]{2,1,0:T(8,128)(2,1)S(1)}, bf16[4,208,128]{2,1,0:T(8,128)(2,1)S(1)}, u32[]{:S(2)}, u32[]{:S(2)}) collective-permute-start(bf16[4,208,128]{2,1,0:T(8,128)(2,1)S(1)} %pad_maximum_fusion.refs_0_), channel_id=1, source_target_pairs={{0,16},{1,17},{2,18},{3,19},{4,20},{5,21},{6,22},{7,23},{8,24},{9,... | collective-permute-start | bytes 638984 | tf_op jit(solution)/shard_map/ppermute | solution.py:782
  27.5 2.6 %collective-permute-start.15 = (bf16[4,208,128]{2,1,0:T(8,128)(2,1)S(1)}, bf16[4,208,128]{2,1,0:T(8,128)(2,1)S(1)}, u32[]{:S(2)}, u32[]{:S(2)}) collective-permute-start(bf16[4,208,128]{2,1,0:T(8,128)(2,1)S(1)} %collective-permute-done.5.refs_3_), channel_id=1, source_target_pairs={{0,16},{1,17},{2,18},{3,19},{4,20},{5,21},{6,22},{7,23},{8,24},{9,... | collective-permute-start | bytes 638984 | tf_op jit(solution)/shard_map/ppermute | solution.py:782
  28.1 1.9 %collective-permute-start.14 = (bf16[4,208,128]{2,1,0:T(8,128)(2,1)S(1)}, bf16[4,208,128]{2,1,0:T(8,128)(2,1)S(1)}, u32[]{:S(2)}, u32[]{:S(2)}) collective-permute-start(bf16[4,208,128]{2,1,0:T(8,128)(2,1)S(1)} %collective-permute-done.4.refs_2_), channel_id=1, source_target_pairs={{0,16},{1,17},{2,18},{3,19},{4,20},{5,21},{6,22},{7,23},{8,24},{9,... | collective-permute-start | bytes 638984 | tf_op jit(solution)/shard_map/ppermute | solution.py:782
  28.2 1.8 %collective-permute-start.13 = (bf16[4,208,128]{2,1,0:T(8,128)(2,1)S(1)}, bf16[4,208,128]{2,1,0:T(8,128)(2,1)S(1)}, u32[]{:S(2)}, u32[]{:S(2)}) collective-permute-start(bf16[4,208,128]{2,1,0:T(8,128)(2,1)S(1)} %collective-permute-done.3.refs_1_), channel_id=1, source_target_pairs={{0,16},{1,17},{2,18},{3,19},{4,20},{5,21},{6,22},{7,23},{8,24},{9,... | collective-permute-start | bytes 638984 | tf_op jit(solution)/shard_map/ppermute | solution.py:782
  28.7 1.4 %collective-permute-start.17 = (bf16[4,112,128]{2,1,0:T(8,128)(2,1)S(1)}, bf16[4,112,128]{2,1,0:T(8,128)(2,1)S(1)}, u32[]{:S(2)}, u32[]{:S(2)}) collective-permute-start(bf16[4,112,128]{2,1,0:T(8,128)(2,1)S(1)} %collective-permute-done.9.refs_5_), channel_id=1, source_target_pairs={{0,16},{1,17},{2,18},{3,19},{4,20},{5,21},{6,22},{7,23},{8,24},{9,... | collective-permute-start | bytes 344072 | tf_op jit(solution)/shard_map/ppermute | solution.py:782
  50.7 3.1 %collective-permute-start.20 = (bf16[16,320,128]{2,1,0:T(8,128)(2,1)S(1)}, bf16[16,320,128]{2,1,0:T(8,128)(2,1)S(1)}, u32[]{:S(2)}, u32[]{:S(2)}) collective-permute-start(bf16[16,320,128]{2,1,0:T(8,128)(2,1)S(1)} %get-tuple-element.72), channel_id=1, source_target_pairs={{0,16},{1,17},{2,18},{3,19},{4,20},{5,21},{6,22},{7,23},{8,24},{9,... | collective-permute-start | bytes 3932168 | tf_op jit(solution)/shard_map/ppermute | solution.py:782
  54.1 9.9 %collective-permute-start.22 = (bf16[2,4,160,128]{3,2,1,0:T(8,128)(2,1)S(1)}, bf16[2,4,160,128]{3,2,1,0:T(8,128)(2,1)S(1)}, u32[]{:S(2)}, u32[]{:S(2)}) collective-permute-start(bf16[2,4,160,128]{3,2,1,0:T(8,128)(2,1)S(1)} %get-tuple-element.76), channel_id=1, source_target_pairs={{0,1},{1,0},{2,3},{3,2},{4,5},{5,4},{6,7},{7,6},{8,9},{9,8},{10,11... | collective-permute-start | bytes 983048 | tf_op jit(solution)/shard_map/ppermute | solution.py:782
  55.6 9.6 %collective-permute-start.21 = (bf16[2,4,160,128]{3,2,1,0:T(8,128)(2,1)S(1)}, bf16[2,4,160,128]{3,2,1,0:T(8,128)(2,1)S(1)}, u32[]{:S(2)}, u32[]{:S(2)}) collective-permute-start(bf16[2,4,160,128]{3,2,1,0:T(8,128)(2,1)S(1)} %get-tuple-element.75._), channel_id=1, source_target_pairs={{0,2},{1,3},{2,0},{3,1},{4,6},{5,7},{6,4},{7,5},{8,10},{9,11},{10,... | collective-permute-start | bytes 983048 | tf_op jit(solution)/shard_map/ppermute | solution.py:782
  65.3 5.4 %collective-permute-start.23 = (bf16[4,160,128]{2,1,0:T(8,128)(2,1)S(1)}, bf16[4,160,128]{2,1,0:T(8,128)(2,1)S(1)}, u32[]{:S(2)}, u32[]{:S(2)}) collective-permute-start(bf16[4,160,128]{2,1,0:T(8,128)(2,1)S(1)} %get-tuple-element.79), channel_id=1, source_target_pairs={{0,1},{1,0},{2,3},{3,2},{4,5},{5,4},{6,7},{7,6},{8,9},{9,8},{10,11... | collective-permute-start | bytes 491528 | tf_op jit(solution)/shard_map/ppermute | solution.py:782
  65.9 5.3 %collective-permute-start.24 = (bf16[4,160,128]{2,1,0:T(8,128)(2,1)S(1)}, bf16[4,160,128]{2,1,0:T(8,128)(2,1)S(1)}, u32[]{:S(2)}, u32[]{:S(2)}) collective-permute-start(bf16[4,160,128]{2,1,0:T(8,128)(2,1)S(1)} %get-tuple-element.80), channel_id=1, source_target_pairs={{0,2},{1,3},{2,0},{3,1},{4,6},{5,7},{6,4},{7,5},{8,10},{9,11},{10,... | collective-permute-start | bytes 491528 | tf_op jit(solution)/shard_map/ppermute | solution.py:782
  71.3 9.1 %collective-permute-start.26 = (bf16[320,128]{1,0:T(8,128)(2,1)S(1)}, bf16[320,128]{1,0:T(8,128)(2,1)S(1)}, u32[]{:S(2)}, u32[]{:S(2)}) collective-permute-start(bf16[320,128]{1,0:T(8,128)(2,1)S(1)} %get-tuple-element.83), channel_id=1, source_target_pairs={{0,8},{1,9},{2,10},{3,11},{4,12},{5,13},{6,14},{7,15},{8,0},{9,1},... | collective-permute-start | bytes 245768 | tf_op jit(solution)/shard_map/ppermute | solution.py:782
  73.6 6.8 %collective-permute-start.27 = (bf16[320,128]{1,0:T(8,128)(2,1)S(1)}, bf16[320,128]{1,0:T(8,128)(2,1)S(1)}, u32[]{:S(2)}, u32[]{:S(2)}) collective-permute-start(bf16[320,128]{1,0:T(8,128)(2,1)S(1)} %get-tuple-element.84), channel_id=1, source_target_pairs={{0,12},{1,13},{2,14},{3,15},{4,8},{5,9},{6,10},{7,11},{8,4},{9,5},... | collective-permute-start | bytes 245768 | tf_op jit(solution)/shard_map/ppermute | solution.py:782
  76.1 4.7 %collective-permute-start.25 = (bf16[320,128]{1,0:T(8,128)(2,1)S(1)}, bf16[320,128]{1,0:T(8,128)(2,1)S(1)}, u32[]{:S(2)}, u32[]{:S(2)}) collective-permute-start(bf16[320,128]{1,0:T(8,128)(2,1)S(1)} %get-tuple-element.82._), channel_id=1, source_target_pairs={{0,4},{1,5},{2,6},{3,7},{4,0},{5,1},{6,2},{7,3},{8,12},{9,13},{10,... | collective-permute-start | bytes 245768 | tf_op jit(solution)/shard_map/ppermute | solution.py:782
  87.6 1.2 %collective-permute-start.28 = (f32[1,512]{1,0:T(1,128)S(1)}, f32[1,512]{1,0:T(1,128)S(1)}, u32[]{:S(2)}, u32[]{:S(2)}) collective-permute-start(f32[1,512]{1,0:T(1,128)S(1)} %get-tuple-element.86.left), channel_id=1, source_target_pairs={{0,16},{1,17},{2,18},{3,19},{4,20},{5,21},{6,22},{7,23},{8,24},{9,... | collective-permute-start | bytes 6152 | tf_op jit(solution)/shard_map/ppermute | solution.py:782
  88.8 3.6 %collective-permute-start.29 = (f32[1,512]{1,0:T(1,128)S(1)}, f32[1,512]{1,0:T(1,128)S(1)}, u32[]{:S(2)}, u32[]{:S(2)}) collective-permute-start(f32[1,512]{1,0:T(1,128)S(1)} %add.9.left), channel_id=1, source_target_pairs={{0,1},{1,0},{2,3},{3,2},{4,5},{5,4},{6,7},{7,6},{8,9},{9,8},{10,11... | collective-permute-start | bytes 6152 | tf_op jit(solution)/shard_map/ppermute | solution.py:808
  92.4 3.6 %collective-permute-start.30 = (f32[1,512]{1,0:T(1,128)S(1)}, f32[1,512]{1,0:T(1,128)S(1)}, u32[]{:S(2)}, u32[]{:S(2)}) collective-permute-start(f32[1,512]{1,0:T(1,128)S(1)} %add.10.left), channel_id=1, source_target_pairs={{0,2},{1,3},{2,0},{3,1},{4,6},{5,7},{6,4},{7,5},{8,10},{9,11},{10,... | collective-permute-start | bytes 6152 | tf_op jit(solution)/shard_map/ppermute | solution.py:808
  96.0 3.6 %collective-permute-start.31 = (f32[1,512]{1,0:T(1,128)S(1)}, f32[1,512]{1,0:T(1,128)S(1)}, u32[]{:S(2)}, u32[]{:S(2)}) collective-permute-start(f32[1,512]{1,0:T(1,128)S(1)} %add.11.left), channel_id=1, source_target_pairs={{0,4},{1,5},{2,6},{3,7},{4,0},{5,1},{6,2},{7,3},{8,12},{9,13},{10,... | collective-permute-start | bytes 6152 | tf_op jit(solution)/shard_map/ppermute | solution.py:808
  99.6 4.6 %copy-start.2 = (f32[1,39936]{1,0:T(1,128)S(1)}, f32[1,39936]{1,0:T(1,128)}, u32[]{:S(2)}) copy-start(f32[1,39936]{1,0:T(1,128)} %param.14) | copy-start | bytes 479236
  99.6 4.6 %copy-start.3 = (f32[1,39936]{1,0:T(1,128)S(1)}, f32[1,39936]{1,0:T(1,128)}, u32[]{:S(2)}) copy-start(f32[1,39936]{1,0:T(1,128)} %param.15) | copy-start | bytes 479236
  99.6 4.6 %copy-start.4 = (f32[1,39936]{1,0:T(1,128)S(1)}, f32[1,39936]{1,0:T(1,128)}, u32[]{:S(2)}) copy-start(f32[1,39936]{1,0:T(1,128)} %param.16) | copy-start | bytes 479236
  99.6 4.6 %copy-start.6 = (s32[2]{0:T(128)S(1)}, s32[2]{0:T(128)}, u32[]{:S(2)}) copy-start(s32[2]{0:T(128)} %counts.1) | copy-start | bytes 28
  99.6 4.5 %collective-permute-start.32 = (f32[1,512]{1,0:T(1,128)S(1)}, f32[1,512]{1,0:T(1,128)S(1)}, u32[]{:S(2)}, u32[]{:S(2)}) collective-permute-start(f32[1,512]{1,0:T(1,128)S(1)} %add.12.left), channel_id=1, source_target_pairs={{0,8},{1,9},{2,10},{3,11},{4,12},{5,13},{6,14},{7,15},{8,0},{9,1},... | collective-permute-start | bytes 6152 | tf_op jit(solution)/shard_map/ppermute | solution.py:808
  104.2 6.1 %copy-start.1 = (bf16[8,196,768]{2,0,1:T(8,128)(2,1)S(1)}, bf16[8,196,768]{2,0,1:T(8,128)(2,1)}, u32[]{:S(2)}) copy-start(bf16[8,196,768]{2,0,1:T(8,128)(2,1)} %param.9) | copy-start | bytes 7225348

commit v6 on v5

--- a/solution.py
+++ b/solution.py
@@ -125,12 +125,12 @@
 
 
 class Flat:
-    def __init__(self, even, odd, mix, rows):
-        self.even, self.odd, self.mix, self.rows = even, odd, mix, rows
+    def __init__(self, even, odd, mix, odd_rows):
+        self.even, self.odd, self.mix, self.odd_rows = even, odd, mix, odd_rows
 
     def shift(self):
         step = 192
-        for at in range(0, self.rows, step):
+        for at in range(0, self.odd_rows, step):
             here = self.even[at : at + step, :]
             after = self.even[at + 1 : at + 1 + step, :]
             self.odd[at : at + step, :] = swap_halves(jnp.where(low_lanes(here.shape), after, here))
@@ -159,8 +159,9 @@
             dest[row : row + 1, at : at + wide] = value[:, :wide]
 
     def clear(self):
+        rows = self.odd_rows + 16
         self.even[...] = jnp.zeros(self.even.shape, f32)
-        self.odd[...] = jnp.zeros(self.odd.shape, f32)
+        self.odd[0:rows, :] = jnp.zeros((rows, LANES), f32)
 
     def put_rows(self, half, count, stride, value):
         ref, start = (self.odd, half // 2 + 8) if half % 2 else (self.even, half // 2)
@@ -186,6 +187,8 @@
                 self.put_rows(start + width, pairs, width, self.mix[pl.ds(1, pairs, stride=2), :])
 
     def merged(self, at, count):
+        if at >= self.odd_rows:
+            return self.even[at : at + count, :]
         here = self.odd[at + 8 : at + 8 + count, :]
         before = self.odd[at + 7 : at + 7 + count, :]
         moved_back = swap_halves(jnp.where(low_lanes(here.shape), here, before))
@@ -398,10 +401,11 @@
 def late_kernel(place, per, image_total, labels, replay, *refs):
     section = lax.axis_index("section")
     parts = len(place.turns()) + place.z
+    odd_rows = -(-(W_HEAD // 2 + 1) // place.shard_rows) * place.shard_rows
     own, other, refs = refs[:parts], refs[parts : 2 * parts], refs[2 * parts :]
     middle, old_logits, back_out, grad_out, loss_out = refs[:5]
     even, odd, mix, wide, w_q, w_k, w_v, w_out, w_up, w_down, vec, w_head, b_head, few, many = refs[5:]
-    flat = Flat(even, odd, mix, place.count * place.shard_rows)
+    flat = Flat(even, odd, mix, odd_rows)
     load_section(place, (own, other), 1, flat)
     read_block(flat, (w_q, w_k, w_v, w_out, w_up, w_down), vec)
     flat.read_row(vec, 9, GAIN_LAST, D)
@@ -1036,7 +1040,7 @@
     sums = butterfly(sums, place, resident)
     padded_rows = -(-shard_rows // 8) * 8
     loss_parts, norm, coefficients, new_master, new_first, new_second = pl.pallas_call(
-        functools.partial(update_kernel, divisor(156), float(2 * shard_len * chips)),
+        functools.partial(update_kernel, divisor(312), float(2 * shard_len * chips)),
         in_specs=[SMEM] + [VMEM] * 8,
         out_specs=[SMEM, SMEM] + [VMEM] * 4,
         out_shape=[

time: 111 us -> 110 us (level)
  no operation moved by 1% of the time
where the time goes in v6:
time: 110 us
  Pallas kernels  45.6 us (41%)
  starting transfers between devices  38 us (35%)
  waiting for transfers between devices  24.5 us (22%)
  between operations  1.1 us (1%)
    ppermute x29, starting transfers between devices, moved(): return lax.ppermute(value, ('section', 'dp'), pairs)  32 us
    ppermute x29, waiting for transfers between devices, moved(): return lax.ppermute(value, ('section', 'dp'), pairs)  15.1 us
    pallas_call x2, Pallas kernels, fetch(): pl.pallas_call(functools.partial(fetch_kernel, first, last), in_specs=[AN...  11.1 us
    ppermute x4, waiting for transfers between devices, butterfly(): value = add(value, lax.ppermute(value, ('section', 'dp'), pairs), resident)  9.35 us
    pallas_call x1, Pallas kernels, late(): pl.pallas_call(functools.partial(late_kernel, place, per, image_total), i...  7.63 us
    pallas_call x1, Pallas kernels, back(): pl.pallas_call(functools.partial(back_kernel, place, per), in_specs=[VMEM...  7.28 us
    pallas_call x1, Pallas kernels, body(): pl.pallas_call(functools.partial(inner_kernel, divisor(26)), in_specs=[VM...  6.75 us
    ppermute x4, starting transfers between devices, butterfly(): value = add(value, lax.ppermute(value, ('section', 'dp'), pairs), resident)  5.95 us
  transfers between devices with their start and end apart: 33, of which 15 were waited for; matrix products, arithmetic and copies ran while one was open for 1% of the time, Pallas kernels for 10%

profile of v6, /device:TPU:0, one launch (start us, length us, event | category | flops | bytes accessed | tf_op | source)
XLA Modules:
  0.0 110.0 jit_solution(14640371895147886605)
XLA Ops:
  0.6 0.0 copy-start
  0.6 1.1 shard.1
  1.8 3.0 %collective-permute-start.7 = (bf16[112,128]{1,0:T(8,128)(2,1)S(1)}, bf16[112,128]{1,0:T(8,128)(2,1)S(1)}, u32[]{:S(2)}, u32[]{:S(2)}) collective-permute-start(bf16[112,128]{1,0:T(8,128)(2,1)S(1)} %get-tuple-element.95), channel_id=1, source_target_pairs={{0,2},{1,3},{2,0},{3,1},{4,6},{5,7},{6,4},{7,5},{8,10},{9,11},{10,... | collective-permute-start | bytes 86024 | tf_op jit(solution)/shard_map/ppermute | solution.py:786
  4.8 1.5 %collective-permute-start.6 = (bf16[112,128]{1,0:T(8,128)(2,1)S(1)}, bf16[112,128]{1,0:T(8,128)(2,1)S(1)}, u32[]{:S(2)}, u32[]{:S(2)}) collective-permute-start(bf16[112,128]{1,0:T(8,128)(2,1)S(1)} %get-tuple-element.95), channel_id=1, source_target_pairs={{0,1},{1,0},{2,3},{3,2},{4,5},{5,4},{6,7},{7,6},{8,9},{9,8},{10,11... | collective-permute-start | bytes 86024 | tf_op jit(solution)/shard_map/ppermute | solution.py:786
  6.3 0.0 collective-permute-start.8
  6.3 3.1 %collective-permute-start.1 = (bf16[208,128]{1,0:T(8,128)(2,1)S(1)}, bf16[208,128]{1,0:T(8,128)(2,1)S(1)}, u32[]{:S(2)}, u32[]{:S(2)}) collective-permute-start(bf16[208,128]{1,0:T(8,128)(2,1)S(1)} %get-tuple-element.97), channel_id=1, source_target_pairs={{0,8},{1,9},{2,10},{3,11},{4,12},{5,13},{6,14},{7,15},{8,0},{9,1},... | collective-permute-start | bytes 159752 | tf_op jit(solution)/shard_map/ppermute | solution.py:786
  9.4 1.6 %collective-permute-start = (bf16[208,128]{1,0:T(8,128)(2,1)S(1)}, bf16[208,128]{1,0:T(8,128)(2,1)S(1)}, u32[]{:S(2)}, u32[]{:S(2)}) collective-permute-start(bf16[208,128]{1,0:T(8,128)(2,1)S(1)} %get-tuple-element.97), channel_id=1, source_target_pairs={{0,4},{1,5},{2,6},{3,7},{4,8},{5,9},{6,10},{7,11},{8,12},{9,13},{1... | collective-permute-start | bytes 159752 | tf_op jit(solution)/shard_map/ppermute | solution.py:786
  11.0 0.6 constant_dynamic-slice_fusion
  11.6 0.1 copy.16.refs_16_.refs_10_
  11.8 2.3 %collective-permute-start.2 = (bf16[208,128]{1,0:T(8,128)(2,1)S(1)}, bf16[208,128]{1,0:T(8,128)(2,1)S(1)}, u32[]{:S(2)}, u32[]{:S(2)}) collective-permute-start(bf16[208,128]{1,0:T(8,128)(2,1)S(1)} %get-tuple-element.97), channel_id=1, source_target_pairs={{0,12},{1,13},{2,14},{3,15},{4,0},{5,1},{6,2},{7,3},{8,4},{9,5},{1... | collective-permute-start | bytes 159752 | tf_op jit(solution)/shard_map/ppermute | solution.py:786
  14.1 0.1 collective-permute-start.16
  14.2 0.6 collective-permute-start.11
  14.8 1.3 %collective-permute-done.2 = bf16[208,128]{1,0:T(8,128)(2,1)S(1)} collective-permute-done((bf16[208,128]{1,0:T(8,128)(2,1)S(1)}, bf16[208,128]{1,0:T(8,128)(2,1)S(1)}, u32[]{:S(2)}, u32[]{:S(2)}) %collective-permute-start.2) | collective-permute-done | bytes 53280 | tf_op jit(solution)/shard_map/ppermute | solution.py:786
  16.1 0.7 collective-permute-start.10
  16.8 0.0 copy-start.5
  16.8 0.0 copy-start.7
  16.8 0.0 copy-start.8
  16.8 2.8 %collective-permute-start.5 = (bf16[4,208,128]{2,1,0:T(8,128)(2,1)S(1)}, bf16[4,208,128]{2,1,0:T(8,128)(2,1)S(1)}, u32[]{:S(2)}, u32[]{:S(2)}) collective-permute-start(bf16[4,208,128]{2,1,0:T(8,128)(2,1)S(1)} %pad_maximum_fusion.refs_0_), channel_id=1, source_target_pairs={{0,3},{1,2},{2,1},{3,0},{4,7},{5,6},{6,5},{7,4},{8,11},{9,10},{10,... | collective-permute-start | bytes 638984 | tf_op jit(solution)/shard_map/ppermute | solution.py:786
  19.6 0.5 collective-permute-start.4
  20.1 0.3 collective-permute-start.3
  20.4 4.2 %collective-permute-start.9 = (bf16[4,112,128]{2,1,0:T(8,128)(2,1)S(1)}, bf16[4,112,128]{2,1,0:T(8,128)(2,1)S(1)}, u32[]{:S(2)}, u32[]{:S(2)}) collective-permute-start(bf16[4,112,128]{2,1,0:T(8,128)(2,1)S(1)} %pad_maximum_fusion.1.refs_4_), channel_id=1, source_target_pairs={{0,4},{1,5},{2,6},{3,7},{4,8},{5,9},{6,10},{7,11},{8,12},{9,13},{1... | collective-permute-start | bytes 344072 | tf_op jit(solution)/shard_map/ppermute | solution.py:786
  24.6 2.4 %collective-permute-done.9.refs_5_ = bf16[4,112,128]{2,1,0:T(8,128)(2,1)S(1)} collective-permute-done((bf16[4,112,128]{2,1,0:T(8,128)(2,1)S(1)}, bf16[4,112,128]{2,1,0:T(8,128)(2,1)S(1)}, u32[]{:S(2)}, u32[]{:S(2)}) %collective-permute-start.9) | collective-permute-done | bytes 114720 | tf_op jit(solution)/shard_map/ppermute | solution.py:786
  27.0 0.5 collective-permute-start.12
  27.5 0.1 collective-permute-start.15
  27.6 0.6 collective-permute-done.4.refs_2_
  28.1 0.1 collective-permute-done.3.refs_1_
  28.2 0.4 collective-permute-start.13
  28.7 0.1 collective-permute-start.17
  28.7 1.3 %collective-permute-done.17.refs_13_ = bf16[4,112,128]{2,1,0:T(8,128)(2,1)S(1)} collective-permute-done((bf16[4,112,128]{2,1,0:T(8,128)(2,1)S(1)}, bf16[4,112,128]{2,1,0:T(8,128)(2,1)S(1)}, u32[]{:S(2)}, u32[]{:S(2)}) %collective-permute-start.17) | collective-permute-done | bytes 114720 | tf_op jit(solution)/shard_map/ppermute | solution.py:786
  30.1 5.5 %front.1 = (f32[832,192]{1,0:T(8,128)S(1)}, bf16[832,192]{1,0:T(8,128)(2,1)S(1)}, bf16[832,192]{1,0:T(8,128)(2,1)S(1)}, bf16[832,192]{1,0:T(8,128)(2,1)S(1)}, f3...) custom-call(bf16[4,208,128]{2,1,0:T(8,128)(2,1)S(1)} %pad_maximum_fu, ...), custom_call_target="tpu_custom_call" | custom-call | flops 3000000000 | bytes 30000000 | tf_op jit(solution)/shard_map/front/pallas_call | solution.py:860
  35.6 7.6 %late.1 = (bf16[832,192]{1,0:T(8,128)(2,1)S(1)}, bf16[16,320,128]{2,1,0:T(8,128)(2,1)S(1)}, f32[1,128]{1,0:T(1,128)S(1)}) custom-call(s32[8]{0:T(128)S(1)} %copy-done.8, s32[8]{0:T(128)S(1)} %copy-done.5, bf16[4,208,128]{2,1,0:T(8,128)(2,1)S(1)} %pad_maximum_fusion.refs_0_, bf16[4,208,128]{2,1,0:T(8,128)(2,1)S(1)} %collective-permute-done.3.refs_1_, ...), custom_call_target="tpu_custom_call" | custom-call | flops 3000000000 | bytes 30000000 | tf_op jit(solution)/shard_map/late/pallas_call | solution.py:884
  43.3 7.3 %back.1 = (bf16[16,320,128]{2,1,0:T(8,128)(2,1)S(1)}, bf16[16,320,128]{2,1,0:T(8,128)(2,1)S(1)}) custom-call(bf16[832,192]{1,0:T(8,128)(2,1)S(1)} %get-tuple-element.53.refs_0_, f32[832,192]{1,0:T(8,128)S(1)} %get-tuple-element.54.refs_1_, bf16[832,192]{1,0:T(8,128)(2,1)S(1)} %get-tuple-element.55.refs_2_, bf16[832,192]{1,0:T(8,128)(2,1)S(1)} %get-tuple-element.56.refs_3_, ...), custom_call_target="tpu_custom_call" | custom-call | flops 3000000000 | bytes 30000000 | tf_op jit(solution)/shard_map/back/pallas_call | solution.py:910
  50.6 0.3 collective-permute-start.20
  50.8 2.8 %collective-permute-done.20.given = bf16[16,320,128]{2,1,0:T(8,128)(2,1)S(1)} collective-permute-done((bf16[16,320,128]{2,1,0:T(8,128)(2,1)S(1)}, bf16[16,320,128]{2,1,0:T(8,128)(2,1)S(1)}, u32[]{:S(2)}, u32[]{:S(2)}) %collective-permute-start.20) | collective-permute-done | bytes 1310752 | tf_op jit(solution)/shard_map/ppermute | solution.py:786
  53.7 0.3 split.1
  53.9 1.6 %collective-permute-start.22 = (bf16[2,4,160,128]{3,2,1,0:T(8,128)(2,1)S(1)}, bf16[2,4,160,128]{3,2,1,0:T(8,128)(2,1)S(1)}, u32[]{:S(2)}, u32[]{:S(2)}) collective-permute-start(bf16[2,4,160,128]{3,2,1,0:T(8,128)(2,1)S(1)} %get-tuple-element.76), channel_id=1, source_target_pairs={{0,1},{1,0},{2,3},{3,2},{4,5},{5,4},{6,7},{7,6},{8,9},{9,8},{10,11... | collective-permute-start | bytes 983048 | tf_op jit(solution)/shard_map/ppermute | solution.py:786
  55.5 1.5 %collective-permute-start.21 = (bf16[2,4,160,128]{3,2,1,0:T(8,128)(2,1)S(1)}, bf16[2,4,160,128]{3,2,1,0:T(8,128)(2,1)S(1)}, u32[]{:S(2)}, u32[]{:S(2)}) collective-permute-start(bf16[2,4,160,128]{3,2,1,0:T(8,128)(2,1)S(1)} %get-tuple-element.75._), channel_id=1, source_target_pairs={{0,2},{1,3},{2,0},{3,1},{4,6},{5,7},{6,4},{7,5},{8,10},{9,11},{10,... | collective-permute-start | bytes 983048 | tf_op jit(solution)/shard_map/ppermute | solution.py:786
  57.0 6.8 %fetch.2._.refs_4_.upper = bf16[256,39936]{1,0:T(8,128)(2,1)S(1)} custom-call(bf16[2,4,160,128]{3,2,1,0:T(8,128)(2,1)S(1)} %get-tuple-element.75._, bf16[400,39936]{1,0:T(8,128)(2,1)} %bitcast.22), custom_call_target="tpu_custom_call" | custom-call | bytes 40894464 | tf_op jit(solution)/shard_map/fetch/pallas_call | solution.py:983
  63.8 0.0 collective-permute-done.22.refs_1_
  63.8 1.2 %collective-permute-done.21.refs_0_ = bf16[2,4,160,128]{3,2,1,0:T(8,128)(2,1)S(1)} collective-permute-done((bf16[2,4,160,128]{3,2,1,0:T(8,128)(2,1)S(1)}, bf16[2,4,160,128]{3,2,1,0:T(8,128)(2,1)S(1)}, u32[]{:S(2)}, u32[]{:S(2)}) %collective-permute-start.21) | collective-permute-done | bytes 327712 | tf_op jit(solution)/shard_map/ppermute | solution.py:786
  65.1 0.1 turn.1
  65.2 0.6 collective-permute-start.23
  65.7 1.6 %collective-permute-start.24 = (bf16[4,160,128]{2,1,0:T(8,128)(2,1)S(1)}, bf16[4,160,128]{2,1,0:T(8,128)(2,1)S(1)}, u32[]{:S(2)}, u32[]{:S(2)}) collective-permute-start(bf16[4,160,128]{2,1,0:T(8,128)(2,1)S(1)} %get-tuple-element.80), channel_id=1, source_target_pairs={{0,2},{1,3},{2,0},{3,1},{4,6},{5,7},{6,4},{7,5},{8,10},{9,11},{10,... | collective-permute-start | bytes 491528 | tf_op jit(solution)/shard_map/ppermute | solution.py:786
  67.3 3.3 %collective-permute-done.23.refs_0_ = bf16[4,160,128]{2,1,0:T(8,128)(2,1)S(1)} collective-permute-done((bf16[4,160,128]{2,1,0:T(8,128)(2,1)S(1)}, bf16[4,160,128]{2,1,0:T(8,128)(2,1)S(1)}, u32[]{:S(2)}, u32[]{:S(2)}) %collective-permute-start.23) | collective-permute-done | bytes 163872 | tf_op jit(solution)/shard_map/ppermute | solution.py:786
  70.6 0.5 collective-permute-done.24.refs_1_
  71.1 0.1 plane.1
  71.1 2.3 %collective-permute-start.26 = (bf16[320,128]{1,0:T(8,128)(2,1)S(1)}, bf16[320,128]{1,0:T(8,128)(2,1)S(1)}, u32[]{:S(2)}, u32[]{:S(2)}) collective-permute-start(bf16[320,128]{1,0:T(8,128)(2,1)S(1)} %get-tuple-element.83), channel_id=1, source_target_pairs={{0,8},{1,9},{2,10},{3,11},{4,12},{5,13},{6,14},{7,15},{8,0},{9,1},... | collective-permute-start | bytes 245768 | tf_op jit(solution)/shard_map/ppermute | solution.py:786
  73.4 2.5 %collective-permute-start.27 = (bf16[320,128]{1,0:T(8,128)(2,1)S(1)}, bf16[320,128]{1,0:T(8,128)(2,1)S(1)}, u32[]{:S(2)}, u32[]{:S(2)}) collective-permute-start(bf16[320,128]{1,0:T(8,128)(2,1)S(1)} %get-tuple-element.84), channel_id=1, source_target_pairs={{0,12},{1,13},{2,14},{3,15},{4,8},{5,9},{6,10},{7,11},{8,4},{9,5},... | collective-permute-start | bytes 245768 | tf_op jit(solution)/shard_map/ppermute | solution.py:786
  76.0 4.3 %fetch.3.refs_5_.__.lower = bf16[144,39936]{1,0:T(8,128)(2,1)S(1)} custom-call(bf16[320,128]{1,0:T(8,128)(2,1)S(1)} %get-tuple-element.82._, bf16[400,39936]{1,0:T(8,128)(2,1)} %bitcast.23), custom_call_target="tpu_custom_call" | custom-call | bytes 23003136 | tf_op jit(solution)/shard_map/fetch/pallas_call | solution.py:983
  80.3 0.4 collective-permute-done.25.refs_1_
  80.7 6.8 %inner.1 = (f32[312,128]{1,0:T(8,128)S(1)}, f32[1,512]{1,0:T(1,128)S(1)}) custom-call(f32[320,128]{1,0:T(8,128)S(1)} %get-tuple-element.81.refs_0_, bf16[320,128]{1,0:T(8,128)(2,1)S(1)} %collective-permute-done.25.refs_1_, bf16[320,128]{1,0:T(8,128)(2,1)S(1)} %collective-permute-done.26.refs_2_, bf16[320,128]{1,0:T(8,128)(2,1)S(1)} %collective-permute-done.27.refs_3_, ...), custom_call_target="tpu_custom_call" | custom-call | tf_op jit(solution)/shard_map/inner/pallas_call | solution.py:1031
  87.4 0.1 collective-permute-start.28
  87.5 1.1 %collective-permute-done.28.right = f32[1,512]{1,0:T(1,128)S(1)} collective-permute-done((f32[1,512]{1,0:T(1,128)S(1)}, f32[1,512]{1,0:T(1,128)S(1)}, u32[]{:S(2)}, u32[]{:S(2)}) %collective-permute-start.28) | collective-permute-done | bytes 2080 | tf_op jit(solution)/shard_map/ppermute | solution.py:786
  88.7 1.4 %collective-permute-start.29 = (f32[1,512]{1,0:T(1,128)S(1)}, f32[1,512]{1,0:T(1,128)S(1)}, u32[]{:S(2)}, u32[]{:S(2)}) collective-permute-start(f32[1,512]{1,0:T(1,128)S(1)} %add.9.left), channel_id=1, source_target_pairs={{0,1},{1,0},{2,3},{3,2},{4,5},{5,4},{6,7},{7,6},{8,9},{9,8},{10,11... | collective-permute-start | bytes 6152 | tf_op jit(solution)/shard_map/ppermute | solution.py:812
  90.0 2.2 %collective-permute-done.29.right = f32[1,512]{1,0:T(1,128)S(1)} collective-permute-done((f32[1,512]{1,0:T(1,128)S(1)}, f32[1,512]{1,0:T(1,128)S(1)}, u32[]{:S(2)}, u32[]{:S(2)}) %collective-permute-start.29) | collective-permute-done | bytes 2080 | tf_op jit(solution)/shard_map/ppermute | solution.py:812
  92.2 1.4 %collective-permute-start.30 = (f32[1,512]{1,0:T(1,128)S(1)}, f32[1,512]{1,0:T(1,128)S(1)}, u32[]{:S(2)}, u32[]{:S(2)}) collective-permute-start(f32[1,512]{1,0:T(1,128)S(1)} %add.10.left), channel_id=1, source_target_pairs={{0,2},{1,3},{2,0},{3,1},{4,6},{5,7},{6,4},{7,5},{8,10},{9,11},{10,... | collective-permute-start | bytes 6152 | tf_op jit(solution)/shard_map/ppermute | solution.py:812
  93.7 2.2 %collective-permute-done.30.right = f32[1,512]{1,0:T(1,128)S(1)} collective-permute-done((f32[1,512]{1,0:T(1,128)S(1)}, f32[1,512]{1,0:T(1,128)S(1)}, u32[]{:S(2)}, u32[]{:S(2)}) %collective-permute-start.30) | collective-permute-done | bytes 2080 | tf_op jit(solution)/shard_map/ppermute | solution.py:812
  95.8 1.6 %collective-permute-start.31 = (f32[1,512]{1,0:T(1,128)S(1)}, f32[1,512]{1,0:T(1,128)S(1)}, u32[]{:S(2)}, u32[]{:S(2)}) collective-permute-start(f32[1,512]{1,0:T(1,128)S(1)} %add.11.left), channel_id=1, source_target_pairs={{0,4},{1,5},{2,6},{3,7},{4,0},{5,1},{6,2},{7,3},{8,12},{9,13},{10,... | collective-permute-start | bytes 6152 | tf_op jit(solution)/shard_map/ppermute | solution.py:812
  97.5 1.9 %collective-permute-done.31.right = f32[1,512]{1,0:T(1,128)S(1)} collective-permute-done((f32[1,512]{1,0:T(1,128)S(1)}, f32[1,512]{1,0:T(1,128)S(1)}, u32[]{:S(2)}, u32[]{:S(2)}) %collective-permute-start.31) | collective-permute-done | bytes 2080 | tf_op jit(solution)/shard_map/ppermute | solution.py:812
  99.4 0.0 copy-start.4
  99.5 1.5 %collective-permute-start.32 = (f32[1,512]{1,0:T(1,128)S(1)}, f32[1,512]{1,0:T(1,128)S(1)}, u32[]{:S(2)}, u32[]{:S(2)}) collective-permute-start(f32[1,512]{1,0:T(1,128)S(1)} %add.12.left), channel_id=1, source_target_pairs={{0,8},{1,9},{2,10},{3,11},{4,12},{5,13},{6,14},{7,15},{8,0},{9,1},... | collective-permute-start | bytes 6152 | tf_op jit(solution)/shard_map/ppermute | solution.py:812
  101.0 3.0 %collective-permute-done.32.right = f32[1,512]{1,0:T(1,128)S(1)} collective-permute-done((f32[1,512]{1,0:T(1,128)S(1)}, f32[1,512]{1,0:T(1,128)S(1)}, u32[]{:S(2)}, u32[]{:S(2)}) %collective-permute-start.32) | collective-permute-done | bytes 2080 | tf_op jit(solution)/shard_map/ppermute | solution.py:812
  104.0 0.0 copy-start.1
  104.0 5.8 %update.1 = (f32[3]{0:T(128)}, f32[1]{0:T(128)}, f32[2,200]{1,0:T(2,128)}, f32[312,128]{1,0:T(8,128)}, f32[312,128]{1,0:T(8,128)}, /*index=5*/f32[312,128]{1,0:T(8,128)}) custom-call(s32[2]{0:T(128)S(1)} %copy-done.6, f32[1,512]{1,0:T(1,128)S(1)} %add.13.sums, bf16[256,39936]{1,0:T(8,128)(2,1)S(1)} %fetch.2._.refs_4_.upper, ...), custom_call_target="tpu_custom_call" | custom-call | tf_op jit(solution)/shard_map/update/pallas_call | solution.py:1042
  (42 shorter events, 0.2 us)
Async XLA Ops:
  0.6 10.4 %copy-start = (bf16[8,196,768]{2,0,1:T(8,128)(2,1)S(1)}, bf16[8,196,768]{2,0,1:T(8,128)(2,1)}, u32[]{:S(2)}) copy-start(bf16[8,196,768]{2,0,1:T(8,128)(2,1)} %param.9) | copy-start | bytes 7225348
  1.8 10.0 %collective-permute-start.7 = (bf16[112,128]{1,0:T(8,128)(2,1)S(1)}, bf16[112,128]{1,0:T(8,128)(2,1)S(1)}, u32[]{:S(2)}, u32[]{:S(2)}) collective-permute-start(bf16[112,128]{1,0:T(8,128)(2,1)S(1)} %get-tuple-element.95), channel_id=1, source_target_pairs={{0,2},{1,3},{2,0},{3,1},{4,6},{5,7},{6,4},{7,5},{8,10},{9,11},{10,... | collective-permute-start | bytes 86024 | tf_op jit(solution)/shard_map/ppermute | solution.py:786
  4.8 9.3 %collective-permute-start.6 = (bf16[112,128]{1,0:T(8,128)(2,1)S(1)}, bf16[112,128]{1,0:T(8,128)(2,1)S(1)}, u32[]{:S(2)}, u32[]{:S(2)}) collective-permute-start(bf16[112,128]{1,0:T(8,128)(2,1)S(1)} %get-tuple-element.95), channel_id=1, source_target_pairs={{0,1},{1,0},{2,3},{3,2},{4,5},{5,4},{6,7},{7,6},{8,9},{9,8},{10,11... | collective-permute-start | bytes 86024 | tf_op jit(solution)/shard_map/ppermute | solution.py:786
  6.3 7.8 %collective-permute-start.8 = (bf16[112,128]{1,0:T(8,128)(2,1)S(1)}, bf16[112,128]{1,0:T(8,128)(2,1)S(1)}, u32[]{:S(2)}, u32[]{:S(2)}) collective-permute-start(bf16[112,128]{1,0:T(8,128)(2,1)S(1)} %get-tuple-element.95), channel_id=1, source_target_pairs={{0,3},{1,2},{2,1},{3,0},{4,7},{5,6},{6,5},{7,4},{8,11},{9,10},{10,... | collective-permute-start | bytes 86024 | tf_op jit(solution)/shard_map/ppermute | solution.py:786
  6.3 10.4 %collective-permute-start.1 = (bf16[208,128]{1,0:T(8,128)(2,1)S(1)}, bf16[208,128]{1,0:T(8,128)(2,1)S(1)}, u32[]{:S(2)}, u32[]{:S(2)}) collective-permute-start(bf16[208,128]{1,0:T(8,128)(2,1)S(1)} %get-tuple-element.97), channel_id=1, source_target_pairs={{0,8},{1,9},{2,10},{3,11},{4,12},{5,13},{6,14},{7,15},{8,0},{9,1},... | collective-permute-start | bytes 159752 | tf_op jit(solution)/shard_map/ppermute | solution.py:786
  9.4 7.3 %collective-permute-start = (bf16[208,128]{1,0:T(8,128)(2,1)S(1)}, bf16[208,128]{1,0:T(8,128)(2,1)S(1)}, u32[]{:S(2)}, u32[]{:S(2)}) collective-permute-start(bf16[208,128]{1,0:T(8,128)(2,1)S(1)} %get-tuple-element.97), channel_id=1, source_target_pairs={{0,4},{1,5},{2,6},{3,7},{4,8},{5,9},{6,10},{7,11},{8,12},{9,13},{1... | collective-permute-start | bytes 159752 | tf_op jit(solution)/shard_map/ppermute | solution.py:786
  11.8 4.3 %collective-permute-start.2 = (bf16[208,128]{1,0:T(8,128)(2,1)S(1)}, bf16[208,128]{1,0:T(8,128)(2,1)S(1)}, u32[]{:S(2)}, u32[]{:S(2)}) collective-permute-start(bf16[208,128]{1,0:T(8,128)(2,1)S(1)} %get-tuple-element.97), channel_id=1, source_target_pairs={{0,12},{1,13},{2,14},{3,15},{4,0},{5,1},{6,2},{7,3},{8,4},{9,5},{1... | collective-permute-start | bytes 159752 | tf_op jit(solution)/shard_map/ppermute | solution.py:786
  14.1 6.0 %collective-permute-start.16 = (bf16[4,112,128]{2,1,0:T(8,128)(2,1)S(1)}, bf16[4,112,128]{2,1,0:T(8,128)(2,1)S(1)}, u32[]{:S(2)}, u32[]{:S(2)}) collective-permute-start(bf16[4,112,128]{2,1,0:T(8,128)(2,1)S(1)} %pad_maximum_fusion.1.refs_4_), channel_id=1, source_target_pairs={{0,16},{1,17},{2,18},{3,19},{4,20},{5,21},{6,22},{7,23},{8,24},{9,... | collective-permute-start | bytes 344072 | tf_op jit(solution)/shard_map/ppermute | solution.py:786
  14.2 6.2 %collective-permute-start.11 = (bf16[4,112,128]{2,1,0:T(8,128)(2,1)S(1)}, bf16[4,112,128]{2,1,0:T(8,128)(2,1)S(1)}, u32[]{:S(2)}, u32[]{:S(2)}) collective-permute-start(bf16[4,112,128]{2,1,0:T(8,128)(2,1)S(1)} %pad_maximum_fusion.1.refs_4_), channel_id=1, source_target_pairs={{0,12},{1,13},{2,14},{3,15},{4,0},{5,1},{6,2},{7,3},{8,4},{9,5},{1... | collective-permute-start | bytes 344072 | tf_op jit(solution)/shard_map/ppermute | solution.py:786
  16.1 8.5 %collective-permute-start.10 = (bf16[4,112,128]{2,1,0:T(8,128)(2,1)S(1)}, bf16[4,112,128]{2,1,0:T(8,128)(2,1)S(1)}, u32[]{:S(2)}, u32[]{:S(2)}) collective-permute-start(bf16[4,112,128]{2,1,0:T(8,128)(2,1)S(1)} %pad_maximum_fusion.1.refs_4_), channel_id=1, source_target_pairs={{0,8},{1,9},{2,10},{3,11},{4,12},{5,13},{6,14},{7,15},{8,0},{9,1},... | collective-permute-start | bytes 344072 | tf_op jit(solution)/shard_map/ppermute | solution.py:786
  16.8 18.8 %copy-start.5 = (s32[8]{0:T(128)S(1)}, s32[8]{0:T(128)}, u32[]{:S(2)}) copy-start(s32[8]{0:T(128)} %replay.3) | copy-start | bytes 100
  16.8 18.8 %copy-start.7 = (f32[8,1000]{1,0:T(8,128)S(1)}, f32[8,1000]{1,0:T(8,128)}, u32[]{:S(2)}) copy-start(f32[8,1000]{1,0:T(8,128)} %refs_17_.1) | copy-start | bytes 96004
  16.8 18.8 %copy-start.8 = (s32[8]{0:T(128)S(1)}, s32[8]{0:T(128)}, u32[]{:S(2)}) copy-start(s32[8]{0:T(128)} %labels.1) | copy-start | bytes 100
  16.8 10.7 %collective-permute-start.5 = (bf16[4,208,128]{2,1,0:T(8,128)(2,1)S(1)}, bf16[4,208,128]{2,1,0:T(8,128)(2,1)S(1)}, u32[]{:S(2)}, u32[]{:S(2)}) collective-permute-start(bf16[4,208,128]{2,1,0:T(8,128)(2,1)S(1)} %pad_maximum_fusion.refs_0_), channel_id=1, source_target_pairs={{0,3},{1,2},{2,1},{3,0},{4,7},{5,6},{6,5},{7,4},{8,11},{9,10},{10,... | collective-permute-start | bytes 638984 | tf_op jit(solution)/shard_map/ppermute | solution.py:786
  19.6 8.5 %collective-permute-start.4 = (bf16[4,208,128]{2,1,0:T(8,128)(2,1)S(1)}, bf16[4,208,128]{2,1,0:T(8,128)(2,1)S(1)}, u32[]{:S(2)}, u32[]{:S(2)}) collective-permute-start(bf16[4,208,128]{2,1,0:T(8,128)(2,1)S(1)} %pad_maximum_fusion.refs_0_), channel_id=1, source_target_pairs={{0,2},{1,3},{2,0},{3,1},{4,6},{5,7},{6,4},{7,5},{8,10},{9,11},{10,... | collective-permute-start | bytes 638984 | tf_op jit(solution)/shard_map/ppermute | solution.py:786
  20.1 8.1 %collective-permute-start.3 = (bf16[4,208,128]{2,1,0:T(8,128)(2,1)S(1)}, bf16[4,208,128]{2,1,0:T(8,128)(2,1)S(1)}, u32[]{:S(2)}, u32[]{:S(2)}) collective-permute-start(bf16[4,208,128]{2,1,0:T(8,128)(2,1)S(1)} %pad_maximum_fusion.refs_0_), channel_id=1, source_target_pairs={{0,1},{1,0},{2,3},{3,2},{4,5},{5,4},{6,7},{7,6},{8,9},{9,8},{10,11... | collective-permute-start | bytes 638984 | tf_op jit(solution)/shard_map/ppermute | solution.py:786
  20.4 6.6 %collective-permute-start.9 = (bf16[4,112,128]{2,1,0:T(8,128)(2,1)S(1)}, bf16[4,112,128]{2,1,0:T(8,128)(2,1)S(1)}, u32[]{:S(2)}, u32[]{:S(2)}) collective-permute-start(bf16[4,112,128]{2,1,0:T(8,128)(2,1)S(1)} %pad_maximum_fusion.1.refs_4_), channel_id=1, source_target_pairs={{0,4},{1,5},{2,6},{3,7},{4,8},{5,9},{6,10},{7,11},{8,12},{9,13},{1... | collective-permute-start | bytes 344072 | tf_op jit(solution)/shard_map/ppermute | solution.py:786
  24.6 2.4 %collective-permute-start.19 = (bf16[4,112,128]{2,1,0:T(8,128)(2,1)S(1)}, bf16[4,112,128]{2,1,0:T(8,128)(2,1)S(1)}, u32[]{:S(2)}, u32[]{:S(2)}) collective-permute-start(bf16[4,112,128]{2,1,0:T(8,128)(2,1)S(1)} %collective-permute-done.11.refs_7_), channel_id=1, source_target_pairs={{0,16},{1,17},{2,18},{3,19},{4,20},{5,21},{6,22},{7,23},{8,24},{9,... | collective-permute-start | bytes 344072 | tf_op jit(solution)/shard_map/ppermute | solution.py:786
  27.0 1.7 %collective-permute-start.18 = (bf16[4,112,128]{2,1,0:T(8,128)(2,1)S(1)}, bf16[4,112,128]{2,1,0:T(8,128)(2,1)S(1)}, u32[]{:S(2)}, u32[]{:S(2)}) collective-permute-start(bf16[4,112,128]{2,1,0:T(8,128)(2,1)S(1)} %collective-permute-done.10.refs_6_), channel_id=1, source_target_pairs={{0,16},{1,17},{2,18},{3,19},{4,20},{5,21},{6,22},{7,23},{8,24},{9,... | collective-permute-start | bytes 344072 | tf_op jit(solution)/shard_map/ppermute | solution.py:786
  27.0 3.1 %collective-permute-start.12 = (bf16[4,208,128]{2,1,0:T(8,128)(2,1)S(1)}, bf16[4,208,128]{2,1,0:T(8,128)(2,1)S(1)}, u32[]{:S(2)}, u32[]{:S(2)}) collective-permute-start(bf16[4,208,128]{2,1,0:T(8,128)(2,1)S(1)} %pad_maximum_fusion.refs_0_), channel_id=1, source_target_pairs={{0,16},{1,17},{2,18},{3,19},{4,20},{5,21},{6,22},{7,23},{8,24},{9,... | collective-permute-start | bytes 638984 | tf_op jit(solution)/shard_map/ppermute | solution.py:786
  27.5 2.6 %collective-permute-start.15 = (bf16[4,208,128]{2,1,0:T(8,128)(2,1)S(1)}, bf16[4,208,128]{2,1,0:T(8,128)(2,1)S(1)}, u32[]{:S(2)}, u32[]{:S(2)}) collective-permute-start(bf16[4,208,128]{2,1,0:T(8,128)(2,1)S(1)} %collective-permute-done.5.refs_3_), channel_id=1, source_target_pairs={{0,16},{1,17},{2,18},{3,19},{4,20},{5,21},{6,22},{7,23},{8,24},{9,... | collective-permute-start | bytes 638984 | tf_op jit(solution)/shard_map/ppermute | solution.py:786
  28.1 1.9 %collective-permute-start.14 = (bf16[4,208,128]{2,1,0:T(8,128)(2,1)S(1)}, bf16[4,208,128]{2,1,0:T(8,128)(2,1)S(1)}, u32[]{:S(2)}, u32[]{:S(2)}) collective-permute-start(bf16[4,208,128]{2,1,0:T(8,128)(2,1)S(1)} %collective-permute-done.4.refs_2_), channel_id=1, source_target_pairs={{0,16},{1,17},{2,18},{3,19},{4,20},{5,21},{6,22},{7,23},{8,24},{9,... | collective-permute-start | bytes 638984 | tf_op jit(solution)/shard_map/ppermute | solution.py:786
  28.2 1.8 %collective-permute-start.13 = (bf16[4,208,128]{2,1,0:T(8,128)(2,1)S(1)}, bf16[4,208,128]{2,1,0:T(8,128)(2,1)S(1)}, u32[]{:S(2)}, u32[]{:S(2)}) collective-permute-start(bf16[4,208,128]{2,1,0:T(8,128)(2,1)S(1)} %collective-permute-done.3.refs_1_), channel_id=1, source_target_pairs={{0,16},{1,17},{2,18},{3,19},{4,20},{5,21},{6,22},{7,23},{8,24},{9,... | collective-permute-start | bytes 638984 | tf_op jit(solution)/shard_map/ppermute | solution.py:786
  28.7 1.4 %collective-permute-start.17 = (bf16[4,112,128]{2,1,0:T(8,128)(2,1)S(1)}, bf16[4,112,128]{2,1,0:T(8,128)(2,1)S(1)}, u32[]{:S(2)}, u32[]{:S(2)}) collective-permute-start(bf16[4,112,128]{2,1,0:T(8,128)(2,1)S(1)} %collective-permute-done.9.refs_5_), channel_id=1, source_target_pairs={{0,16},{1,17},{2,18},{3,19},{4,20},{5,21},{6,22},{7,23},{8,24},{9,... | collective-permute-start | bytes 344072 | tf_op jit(solution)/shard_map/ppermute | solution.py:786
  50.6 3.1 %collective-permute-start.20 = (bf16[16,320,128]{2,1,0:T(8,128)(2,1)S(1)}, bf16[16,320,128]{2,1,0:T(8,128)(2,1)S(1)}, u32[]{:S(2)}, u32[]{:S(2)}) collective-permute-start(bf16[16,320,128]{2,1,0:T(8,128)(2,1)S(1)} %get-tuple-element.72), channel_id=1, source_target_pairs={{0,16},{1,17},{2,18},{3,19},{4,20},{5,21},{6,22},{7,23},{8,24},{9,... | collective-permute-start | bytes 3932168 | tf_op jit(solution)/shard_map/ppermute | solution.py:786
  53.9 9.9 %collective-permute-start.22 = (bf16[2,4,160,128]{3,2,1,0:T(8,128)(2,1)S(1)}, bf16[2,4,160,128]{3,2,1,0:T(8,128)(2,1)S(1)}, u32[]{:S(2)}, u32[]{:S(2)}) collective-permute-start(bf16[2,4,160,128]{3,2,1,0:T(8,128)(2,1)S(1)} %get-tuple-element.76), channel_id=1, source_target_pairs={{0,1},{1,0},{2,3},{3,2},{4,5},{5,4},{6,7},{7,6},{8,9},{9,8},{10,11... | collective-permute-start | bytes 983048 | tf_op jit(solution)/shard_map/ppermute | solution.py:786
  55.5 9.6 %collective-permute-start.21 = (bf16[2,4,160,128]{3,2,1,0:T(8,128)(2,1)S(1)}, bf16[2,4,160,128]{3,2,1,0:T(8,128)(2,1)S(1)}, u32[]{:S(2)}, u32[]{:S(2)}) collective-permute-start(bf16[2,4,160,128]{3,2,1,0:T(8,128)(2,1)S(1)} %get-tuple-element.75._), channel_id=1, source_target_pairs={{0,2},{1,3},{2,0},{3,1},{4,6},{5,7},{6,4},{7,5},{8,10},{9,11},{10,... | collective-permute-start | bytes 983048 | tf_op jit(solution)/shard_map/ppermute | solution.py:786
  65.2 5.4 %collective-permute-start.23 = (bf16[4,160,128]{2,1,0:T(8,128)(2,1)S(1)}, bf16[4,160,128]{2,1,0:T(8,128)(2,1)S(1)}, u32[]{:S(2)}, u32[]{:S(2)}) collective-permute-start(bf16[4,160,128]{2,1,0:T(8,128)(2,1)S(1)} %get-tuple-element.79), channel_id=1, source_target_pairs={{0,1},{1,0},{2,3},{3,2},{4,5},{5,4},{6,7},{7,6},{8,9},{9,8},{10,11... | collective-permute-start | bytes 491528 | tf_op jit(solution)/shard_map/ppermute | solution.py:786
  65.7 5.3 %collective-permute-start.24 = (bf16[4,160,128]{2,1,0:T(8,128)(2,1)S(1)}, bf16[4,160,128]{2,1,0:T(8,128)(2,1)S(1)}, u32[]{:S(2)}, u32[]{:S(2)}) collective-permute-start(bf16[4,160,128]{2,1,0:T(8,128)(2,1)S(1)} %get-tuple-element.80), channel_id=1, source_target_pairs={{0,2},{1,3},{2,0},{3,1},{4,6},{5,7},{6,4},{7,5},{8,10},{9,11},{10,... | collective-permute-start | bytes 491528 | tf_op jit(solution)/shard_map/ppermute | solution.py:786
  71.1 9.1 %collective-permute-start.26 = (bf16[320,128]{1,0:T(8,128)(2,1)S(1)}, bf16[320,128]{1,0:T(8,128)(2,1)S(1)}, u32[]{:S(2)}, u32[]{:S(2)}) collective-permute-start(bf16[320,128]{1,0:T(8,128)(2,1)S(1)} %get-tuple-element.83), channel_id=1, source_target_pairs={{0,8},{1,9},{2,10},{3,11},{4,12},{5,13},{6,14},{7,15},{8,0},{9,1},... | collective-permute-start | bytes 245768 | tf_op jit(solution)/shard_map/ppermute | solution.py:786
  73.4 6.8 %collective-permute-start.27 = (bf16[320,128]{1,0:T(8,128)(2,1)S(1)}, bf16[320,128]{1,0:T(8,128)(2,1)S(1)}, u32[]{:S(2)}, u32[]{:S(2)}) collective-permute-start(bf16[320,128]{1,0:T(8,128)(2,1)S(1)} %get-tuple-element.84), channel_id=1, source_target_pairs={{0,12},{1,13},{2,14},{3,15},{4,8},{5,9},{6,10},{7,11},{8,4},{9,5},... | collective-permute-start | bytes 245768 | tf_op jit(solution)/shard_map/ppermute | solution.py:786
  76.0 4.7 %collective-permute-start.25 = (bf16[320,128]{1,0:T(8,128)(2,1)S(1)}, bf16[320,128]{1,0:T(8,128)(2,1)S(1)}, u32[]{:S(2)}, u32[]{:S(2)}) collective-permute-start(bf16[320,128]{1,0:T(8,128)(2,1)S(1)} %get-tuple-element.82._), channel_id=1, source_target_pairs={{0,4},{1,5},{2,6},{3,7},{4,0},{5,1},{6,2},{7,3},{8,12},{9,13},{10,... | collective-permute-start | bytes 245768 | tf_op jit(solution)/shard_map/ppermute | solution.py:786
  87.4 1.2 %collective-permute-start.28 = (f32[1,512]{1,0:T(1,128)S(1)}, f32[1,512]{1,0:T(1,128)S(1)}, u32[]{:S(2)}, u32[]{:S(2)}) collective-permute-start(f32[1,512]{1,0:T(1,128)S(1)} %get-tuple-element.86.left), channel_id=1, source_target_pairs={{0,16},{1,17},{2,18},{3,19},{4,20},{5,21},{6,22},{7,23},{8,24},{9,... | collective-permute-start | bytes 6152 | tf_op jit(solution)/shard_map/ppermute | solution.py:786
  88.7 3.6 %collective-permute-start.29 = (f32[1,512]{1,0:T(1,128)S(1)}, f32[1,512]{1,0:T(1,128)S(1)}, u32[]{:S(2)}, u32[]{:S(2)}) collective-permute-start(f32[1,512]{1,0:T(1,128)S(1)} %add.9.left), channel_id=1, source_target_pairs={{0,1},{1,0},{2,3},{3,2},{4,5},{5,4},{6,7},{7,6},{8,9},{9,8},{10,11... | collective-permute-start | bytes 6152 | tf_op jit(solution)/shard_map/ppermute | solution.py:812
  92.2 3.6 %collective-permute-start.30 = (f32[1,512]{1,0:T(1,128)S(1)}, f32[1,512]{1,0:T(1,128)S(1)}, u32[]{:S(2)}, u32[]{:S(2)}) collective-permute-start(f32[1,512]{1,0:T(1,128)S(1)} %add.10.left), channel_id=1, source_target_pairs={{0,2},{1,3},{2,0},{3,1},{4,6},{5,7},{6,4},{7,5},{8,10},{9,11},{10,... | collective-permute-start | bytes 6152 | tf_op jit(solution)/shard_map/ppermute | solution.py:812
  95.8 3.6 %collective-permute-start.31 = (f32[1,512]{1,0:T(1,128)S(1)}, f32[1,512]{1,0:T(1,128)S(1)}, u32[]{:S(2)}, u32[]{:S(2)}) collective-permute-start(f32[1,512]{1,0:T(1,128)S(1)} %add.11.left), channel_id=1, source_target_pairs={{0,4},{1,5},{2,6},{3,7},{4,0},{5,1},{6,2},{7,3},{8,12},{9,13},{10,... | collective-permute-start | bytes 6152 | tf_op jit(solution)/shard_map/ppermute | solution.py:812
  99.4 4.6 %copy-start.2 = (f32[1,39936]{1,0:T(1,128)S(1)}, f32[1,39936]{1,0:T(1,128)}, u32[]{:S(2)}) copy-start(f32[1,39936]{1,0:T(1,128)} %param.14) | copy-start | bytes 479236
  99.4 4.6 %copy-start.3 = (f32[1,39936]{1,0:T(1,128)S(1)}, f32[1,39936]{1,0:T(1,128)}, u32[]{:S(2)}) copy-start(f32[1,39936]{1,0:T(1,128)} %param.15) | copy-start | bytes 479236
  99.4 4.6 %copy-start.4 = (f32[1,39936]{1,0:T(1,128)S(1)}, f32[1,39936]{1,0:T(1,128)}, u32[]{:S(2)}) copy-start(f32[1,39936]{1,0:T(1,128)} %param.16) | copy-start | bytes 479236
  99.4 4.6 %copy-start.6 = (s32[2]{0:T(128)S(1)}, s32[2]{0:T(128)}, u32[]{:S(2)}) copy-start(s32[2]{0:T(128)} %counts.1) | copy-start | bytes 28
  99.5 4.5 %collective-permute-start.32 = (f32[1,512]{1,0:T(1,128)S(1)}, f32[1,512]{1,0:T(1,128)S(1)}, u32[]{:S(2)}, u32[]{:S(2)}) collective-permute-start(f32[1,512]{1,0:T(1,128)S(1)} %add.12.left), channel_id=1, source_target_pairs={{0,8},{1,9},{2,10},{3,11},{4,12},{5,13},{6,14},{7,15},{8,0},{9,1},... | collective-permute-start | bytes 6152 | tf_op jit(solution)/shard_map/ppermute | solution.py:812
  104.0 5.8 %copy-start.1 = (bf16[8,196,768]{2,0,1:T(8,128)(2,1)S(1)}, bf16[8,196,768]{2,0,1:T(8,128)(2,1)}, u32[]{:S(2)}) copy-start(bf16[8,196,768]{2,0,1:T(8,128)(2,1)} %param.9) | copy-start | bytes 7225348

commit v7 on v6

--- a/solution.py
+++ b/solution.py
@@ -949,7 +949,7 @@
     early, late_part = shard[: place.first_rows], shard[place.first_rows :]
     column = [early] + [moved(early, place, (d, 0, 0)) for d in range(1, place.z)]
     plane = [moved(late_part, place, (0, a, b)) if a + b else late_part for a, b in turns]
-    column[-1], mine = lax.optimization_barrier((column[-1], mine))
+    column[1], mine = lax.optimization_barrier((column[1], mine))
     column, plane = jnp.stack(column), jnp.stack(plane)
     own = [moved(column, place, (0, a, b)) if a + b else column for a, b in turns]
     own += [moved(plane, place, (d, 0, 0)) if d else plane for d in range(place.z)]

time: 110 us -> 109 us (level)
  starting transfers between devices: 38 us -> 32.4 us
  waiting for transfers between devices: 24.5 us -> 29.3 us
    ppermute x29, starting transfers between devices: 32 us -> 26.1 us  [moved(): return lax.ppermute(value, ('section', 'dp'), pairs)]
    ppermute x29, waiting for transfers between devices: 15.1 us -> 20.3 us  [moved(): return lax.ppermute(value, ('section', 'dp'), pairs)]
  transfers between devices with their start and end apart: 33 -> 33, of which waited for: 15 -> 20; matrix products, arithmetic and copies ran while one was open for 1% -> 1% of each run, Pallas kernels for 10% -> 10%
where the time goes in v7:
time: 109 us
  Pallas kernels  45.6 us (42%)
  starting transfers between devices  32.4 us (30%)
  waiting for transfers between devices  29.3 us (27%)
  between operations  1.09 us (1%)
    ppermute x29, starting transfers between devices, moved(): return lax.ppermute(value, ('section', 'dp'), pairs)  26.1 us
    ppermute x29, waiting for transfers between devices, moved(): return lax.ppermute(value, ('section', 'dp'), pairs)  20.3 us
    pallas_call x2, Pallas kernels, fetch(): pl.pallas_call(functools.partial(fetch_kernel, first, last), in_specs=[AN...  11.1 us
    ppermute x4, waiting for transfers between devices, butterfly(): value = add(value, lax.ppermute(value, ('section', 'dp'), pairs), resident)  9.02 us
    pallas_call x1, Pallas kernels, late(): pl.pallas_call(functools.partial(late_kernel, place, per, image_total), i...  7.63 us
    pallas_call x1, Pallas kernels, back(): pl.pallas_call(functools.partial(back_kernel, place, per), in_specs=[VMEM...  7.28 us
    pallas_call x1, Pallas kernels, body(): pl.pallas_call(functools.partial(inner_kernel, divisor(26)), in_specs=[VM...  6.75 us
    ppermute x4, starting transfers between devices, butterfly(): value = add(value, lax.ppermute(value, ('section', 'dp'), pairs), resident)  6.29 us
  transfers between devices with their start and end apart: 33, of which 20 were waited for; matrix products, arithmetic and copies ran while one was open for 1% of the time, Pallas kernels for 10%

profile of v7, /device:TPU:0, one launch (start us, length us, event | category | flops | bytes accessed | tf_op | source)
XLA Modules:
  0.0 109.3 jit_solution(725713201065177278)
XLA Ops:
  0.6 0.0 copy-start
  0.6 1.1 shard.1
  1.8 3.0 %collective-permute-start.7 = (bf16[112,128]{1,0:T(8,128)(2,1)S(1)}, bf16[112,128]{1,0:T(8,128)(2,1)S(1)}, u32[]{:S(2)}, u32[]{:S(2)}) collective-permute-start(bf16[112,128]{1,0:T(8,128)(2,1)S(1)} %get-tuple-element.95), channel_id=1, source_target_pairs={{0,2},{1,3},{2,0},{3,1},{4,6},{5,7},{6,4},{7,5},{8,10},{9,11},{10,... | collective-permute-start | bytes 86024 | tf_op jit(solution)/shard_map/ppermute | solution.py:786
  4.8 1.5 %collective-permute-start.6 = (bf16[112,128]{1,0:T(8,128)(2,1)S(1)}, bf16[112,128]{1,0:T(8,128)(2,1)S(1)}, u32[]{:S(2)}, u32[]{:S(2)}) collective-permute-start(bf16[112,128]{1,0:T(8,128)(2,1)S(1)} %get-tuple-element.95), channel_id=1, source_target_pairs={{0,1},{1,0},{2,3},{3,2},{4,5},{5,4},{6,7},{7,6},{8,9},{9,8},{10,11... | collective-permute-start | bytes 86024 | tf_op jit(solution)/shard_map/ppermute | solution.py:786
  6.3 0.0 collective-permute-start.8
  6.3 3.1 %collective-permute-start.1 = (bf16[208,128]{1,0:T(8,128)(2,1)S(1)}, bf16[208,128]{1,0:T(8,128)(2,1)S(1)}, u32[]{:S(2)}, u32[]{:S(2)}) collective-permute-start(bf16[208,128]{1,0:T(8,128)(2,1)S(1)} %get-tuple-element.97), channel_id=1, source_target_pairs={{0,8},{1,9},{2,10},{3,11},{4,12},{5,13},{6,14},{7,15},{8,0},{9,1},... | collective-permute-start | bytes 159752 | tf_op jit(solution)/shard_map/ppermute | solution.py:786
  9.4 1.6 %collective-permute-start = (bf16[208,128]{1,0:T(8,128)(2,1)S(1)}, bf16[208,128]{1,0:T(8,128)(2,1)S(1)}, u32[]{:S(2)}, u32[]{:S(2)}) collective-permute-start(bf16[208,128]{1,0:T(8,128)(2,1)S(1)} %get-tuple-element.97), channel_id=1, source_target_pairs={{0,4},{1,5},{2,6},{3,7},{4,8},{5,9},{6,10},{7,11},{8,12},{9,13},{1... | collective-permute-start | bytes 159752 | tf_op jit(solution)/shard_map/ppermute | solution.py:786
  11.0 0.6 constant_dynamic-slice_fusion
  11.6 0.1 copy.16.refs_16_.refs_10_
  11.8 2.3 %collective-permute-start.2 = (bf16[208,128]{1,0:T(8,128)(2,1)S(1)}, bf16[208,128]{1,0:T(8,128)(2,1)S(1)}, u32[]{:S(2)}, u32[]{:S(2)}) collective-permute-start(bf16[208,128]{1,0:T(8,128)(2,1)S(1)} %get-tuple-element.97), channel_id=1, source_target_pairs={{0,12},{1,13},{2,14},{3,15},{4,0},{5,1},{6,2},{7,3},{8,4},{9,5},{1... | collective-permute-start | bytes 159752 | tf_op jit(solution)/shard_map/ppermute | solution.py:786
  14.1 0.1 collective-permute-start.16
  14.2 0.6 collective-permute-start.11
  14.8 0.6 collective-permute-done
  15.4 0.2 collective-permute-start.10
  15.6 0.5 collective-permute-done.2
  16.1 0.0 copy-start.5
  16.2 2.7 %collective-permute-start.5 = (bf16[4,208,128]{2,1,0:T(8,128)(2,1)S(1)}, bf16[4,208,128]{2,1,0:T(8,128)(2,1)S(1)}, u32[]{:S(2)}, u32[]{:S(2)}) collective-permute-start(bf16[4,208,128]{2,1,0:T(8,128)(2,1)S(1)} %pad_maximum_fusion.refs_0_), channel_id=1, source_target_pairs={{0,3},{1,2},{2,1},{3,0},{4,7},{5,6},{6,5},{7,4},{8,11},{9,10},{10,... | collective-permute-start | bytes 638984 | tf_op jit(solution)/shard_map/ppermute | solution.py:786
  18.9 0.5 collective-permute-start.4
  19.4 0.3 collective-permute-start.3
  19.7 0.5 collective-permute-done.11.refs_7_
  20.3 3.6 %collective-permute-done.10.refs_6_ = bf16[4,112,128]{2,1,0:T(8,128)(2,1)S(1)} collective-permute-done((bf16[4,112,128]{2,1,0:T(8,128)(2,1)S(1)}, bf16[4,112,128]{2,1,0:T(8,128)(2,1)S(1)}, u32[]{:S(2)}, u32[]{:S(2)}) %collective-permute-start.10) | collective-permute-done | bytes 114720 | tf_op jit(solution)/shard_map/ppermute | solution.py:786
  23.9 3.0 %collective-permute-done.9.refs_5_ = bf16[4,112,128]{2,1,0:T(8,128)(2,1)S(1)} collective-permute-done((bf16[4,112,128]{2,1,0:T(8,128)(2,1)S(1)}, bf16[4,112,128]{2,1,0:T(8,128)(2,1)S(1)}, u32[]{:S(2)}, u32[]{:S(2)}) %collective-permute-start.9) | collective-permute-done | bytes 114720 | tf_op jit(solution)/shard_map/ppermute | solution.py:786
  26.9 0.5 collective-permute-start.12
  27.4 0.1 collective-permute-start.15
  27.4 0.7 collective-permute-done.4.refs_2_
  28.1 0.1 collective-permute-done.3.refs_1_
  28.2 0.4 collective-permute-start.13
  28.7 0.1 collective-permute-start.17
  28.7 1.3 %collective-permute-done.17.refs_13_ = bf16[4,112,128]{2,1,0:T(8,128)(2,1)S(1)} collective-permute-done((bf16[4,112,128]{2,1,0:T(8,128)(2,1)S(1)}, bf16[4,112,128]{2,1,0:T(8,128)(2,1)S(1)}, u32[]{:S(2)}, u32[]{:S(2)}) %collective-permute-start.17) | collective-permute-done | bytes 114720 | tf_op jit(solution)/shard_map/ppermute | solution.py:786
  30.1 5.5 %front.1 = (f32[832,192]{1,0:T(8,128)S(1)}, bf16[832,192]{1,0:T(8,128)(2,1)S(1)}, bf16[832,192]{1,0:T(8,128)(2,1)S(1)}, bf16[832,192]{1,0:T(8,128)(2,1)S(1)}, f3...) custom-call(bf16[4,208,128]{2,1,0:T(8,128)(2,1)S(1)} %pad_maximum_fu, ...), custom_call_target="tpu_custom_call" | custom-call | flops 3000000000 | bytes 30000000 | tf_op jit(solution)/shard_map/front/pallas_call | solution.py:860
  35.6 7.6 %late.1 = (bf16[832,192]{1,0:T(8,128)(2,1)S(1)}, bf16[16,320,128]{2,1,0:T(8,128)(2,1)S(1)}, f32[1,128]{1,0:T(1,128)S(1)}) custom-call(s32[8]{0:T(128)S(1)} %copy-done.8, s32[8]{0:T(128)S(1)} %copy-done.5, bf16[4,208,128]{2,1,0:T(8,128)(2,1)S(1)} %pad_maximum_fusion.refs_0_, bf16[4,208,128]{2,1,0:T(8,128)(2,1)S(1)} %collective-permute-done.3.refs_1_, ...), custom_call_target="tpu_custom_call" | custom-call | flops 3000000000 | bytes 30000000 | tf_op jit(solution)/shard_map/late/pallas_call | solution.py:884
  43.3 7.3 %back.1 = (bf16[16,320,128]{2,1,0:T(8,128)(2,1)S(1)}, bf16[16,320,128]{2,1,0:T(8,128)(2,1)S(1)}) custom-call(bf16[832,192]{1,0:T(8,128)(2,1)S(1)} %get-tuple-element.53.refs_0_, f32[832,192]{1,0:T(8,128)S(1)} %get-tuple-element.54.refs_1_, bf16[832,192]{1,0:T(8,128)(2,1)S(1)} %get-tuple-element.55.refs_2_, bf16[832,192]{1,0:T(8,128)(2,1)S(1)} %get-tuple-element.56.refs_3_, ...), custom_call_target="tpu_custom_call" | custom-call | flops 3000000000 | bytes 30000000 | tf_op jit(solution)/shard_map/back/pallas_call | solution.py:910
  50.6 0.3 collective-permute-start.20
  50.8 2.8 %collective-permute-done.20.given = bf16[16,320,128]{2,1,0:T(8,128)(2,1)S(1)} collective-permute-done((bf16[16,320,128]{2,1,0:T(8,128)(2,1)S(1)}, bf16[16,320,128]{2,1,0:T(8,128)(2,1)S(1)}, u32[]{:S(2)}, u32[]{:S(2)}) %collective-permute-start.20) | collective-permute-done | bytes 1310752 | tf_op jit(solution)/shard_map/ppermute | solution.py:786
  53.7 0.3 split.1
  53.9 1.6 %collective-permute-start.22 = (bf16[2,4,160,128]{3,2,1,0:T(8,128)(2,1)S(1)}, bf16[2,4,160,128]{3,2,1,0:T(8,128)(2,1)S(1)}, u32[]{:S(2)}, u32[]{:S(2)}) collective-permute-start(bf16[2,4,160,128]{3,2,1,0:T(8,128)(2,1)S(1)} %get-tuple-element.76), channel_id=1, source_target_pairs={{0,1},{1,0},{2,3},{3,2},{4,5},{5,4},{6,7},{7,6},{8,9},{9,8},{10,11... | collective-permute-start | bytes 983048 | tf_op jit(solution)/shard_map/ppermute | solution.py:786
  55.5 1.3 %collective-permute-start.21 = (bf16[2,4,160,128]{3,2,1,0:T(8,128)(2,1)S(1)}, bf16[2,4,160,128]{3,2,1,0:T(8,128)(2,1)S(1)}, u32[]{:S(2)}, u32[]{:S(2)}) collective-permute-start(bf16[2,4,160,128]{3,2,1,0:T(8,128)(2,1)S(1)} %get-tuple-element.75._), channel_id=1, source_target_pairs={{0,2},{1,3},{2,0},{3,1},{4,6},{5,7},{6,4},{7,5},{8,10},{9,11},{10,... | collective-permute-start | bytes 983048 | tf_op jit(solution)/shard_map/ppermute | solution.py:786
  56.8 6.8 %fetch.2._.refs_4_.upper = bf16[256,39936]{1,0:T(8,128)(2,1)S(1)} custom-call(bf16[2,4,160,128]{3,2,1,0:T(8,128)(2,1)S(1)} %get-tuple-element.75._, bf16[400,39936]{1,0:T(8,128)(2,1)} %bitcast.22), custom_call_target="tpu_custom_call" | custom-call | bytes 40894464 | tf_op jit(solution)/shard_map/fetch/pallas_call | solution.py:983
  63.6 0.2 collective-permute-done.22.refs_1_
  63.8 1.2 %collective-permute-done.21.refs_0_ = bf16[2,4,160,128]{3,2,1,0:T(8,128)(2,1)S(1)} collective-permute-done((bf16[2,4,160,128]{3,2,1,0:T(8,128)(2,1)S(1)}, bf16[2,4,160,128]{3,2,1,0:T(8,128)(2,1)S(1)}, u32[]{:S(2)}, u32[]{:S(2)}) %collective-permute-start.21) | collective-permute-done | bytes 327712 | tf_op jit(solution)/shard_map/ppermute | solution.py:786
  65.0 0.1 turn.1
  65.1 0.6 collective-permute-start.23
  65.7 1.5 %collective-permute-start.24 = (bf16[4,160,128]{2,1,0:T(8,128)(2,1)S(1)}, bf16[4,160,128]{2,1,0:T(8,128)(2,1)S(1)}, u32[]{:S(2)}, u32[]{:S(2)}) collective-permute-start(bf16[4,160,128]{2,1,0:T(8,128)(2,1)S(1)} %get-tuple-element.80), channel_id=1, source_target_pairs={{0,2},{1,3},{2,0},{3,1},{4,6},{5,7},{6,4},{7,5},{8,10},{9,11},{10,... | collective-permute-start | bytes 491528 | tf_op jit(solution)/shard_map/ppermute | solution.py:786
  67.3 3.3 %collective-permute-done.23.refs_0_ = bf16[4,160,128]{2,1,0:T(8,128)(2,1)S(1)} collective-permute-done((bf16[4,160,128]{2,1,0:T(8,128)(2,1)S(1)}, bf16[4,160,128]{2,1,0:T(8,128)(2,1)S(1)}, u32[]{:S(2)}, u32[]{:S(2)}) %collective-permute-start.23) | collective-permute-done | bytes 163872 | tf_op jit(solution)/shard_map/ppermute | solution.py:786
  70.5 0.5 collective-permute-done.24.refs_1_
  71.1 0.1 plane.1
  71.1 2.3 %collective-permute-start.26 = (bf16[320,128]{1,0:T(8,128)(2,1)S(1)}, bf16[320,128]{1,0:T(8,128)(2,1)S(1)}, u32[]{:S(2)}, u32[]{:S(2)}) collective-permute-start(bf16[320,128]{1,0:T(8,128)(2,1)S(1)} %get-tuple-element.83), channel_id=1, source_target_pairs={{0,8},{1,9},{2,10},{3,11},{4,12},{5,13},{6,14},{7,15},{8,0},{9,1},... | collective-permute-start | bytes 245768 | tf_op jit(solution)/shard_map/ppermute | solution.py:786
  73.4 1.2 %collective-permute-start.27 = (bf16[320,128]{1,0:T(8,128)(2,1)S(1)}, bf16[320,128]{1,0:T(8,128)(2,1)S(1)}, u32[]{:S(2)}, u32[]{:S(2)}) collective-permute-start(bf16[320,128]{1,0:T(8,128)(2,1)S(1)} %get-tuple-element.84), channel_id=1, source_target_pairs={{0,12},{1,13},{2,14},{3,15},{4,8},{5,9},{6,10},{7,11},{8,4},{9,5},... | collective-permute-start | bytes 245768 | tf_op jit(solution)/shard_map/ppermute | solution.py:786
  74.6 0.3 collective-permute-start.25
  74.9 4.3 %fetch.3.refs_5_.__.lower = bf16[144,39936]{1,0:T(8,128)(2,1)S(1)} custom-call(bf16[320,128]{1,0:T(8,128)(2,1)S(1)} %get-tuple-element.82._, bf16[400,39936]{1,0:T(8,128)(2,1)} %bitcast.23), custom_call_target="tpu_custom_call" | custom-call | bytes 23003136 | tf_op jit(solution)/shard_map/fetch/pallas_call | solution.py:983
  79.2 0.6 collective-permute-done.27.refs_3_
  79.8 0.1 collective-permute-done.25.refs_1_
  80.0 6.8 %inner.1 = (f32[312,128]{1,0:T(8,128)S(1)}, f32[1,512]{1,0:T(1,128)S(1)}) custom-call(f32[320,128]{1,0:T(8,128)S(1)} %get-tuple-element.81.refs_0_, bf16[320,128]{1,0:T(8,128)(2,1)S(1)} %collective-permute-done.25.refs_1_, bf16[320,128]{1,0:T(8,128)(2,1)S(1)} %collective-permute-done.26.refs_2_, bf16[320,128]{1,0:T(8,128)(2,1)S(1)} %collective-permute-done.27.refs_3_, ...), custom_call_target="tpu_custom_call" | custom-call | tf_op jit(solution)/shard_map/inner/pallas_call | solution.py:1031
  86.7 0.1 collective-permute-start.28
  86.8 1.1 %collective-permute-done.28.right = f32[1,512]{1,0:T(1,128)S(1)} collective-permute-done((f32[1,512]{1,0:T(1,128)S(1)}, f32[1,512]{1,0:T(1,128)S(1)}, u32[]{:S(2)}, u32[]{:S(2)}) %collective-permute-start.28) | collective-permute-done | bytes 2080 | tf_op jit(solution)/shard_map/ppermute | solution.py:786
  87.9 1.5 %collective-permute-start.29 = (f32[1,512]{1,0:T(1,128)S(1)}, f32[1,512]{1,0:T(1,128)S(1)}, u32[]{:S(2)}, u32[]{:S(2)}) collective-permute-start(f32[1,512]{1,0:T(1,128)S(1)} %add.9.left), channel_id=1, source_target_pairs={{0,1},{1,0},{2,3},{3,2},{4,5},{5,4},{6,7},{7,6},{8,9},{9,8},{10,11... | collective-permute-start | bytes 6152 | tf_op jit(solution)/shard_map/ppermute | solution.py:812
  89.4 2.1 %collective-permute-done.29.right = f32[1,512]{1,0:T(1,128)S(1)} collective-permute-done((f32[1,512]{1,0:T(1,128)S(1)}, f32[1,512]{1,0:T(1,128)S(1)}, u32[]{:S(2)}, u32[]{:S(2)}) %collective-permute-start.29) | collective-permute-done | bytes 2080 | tf_op jit(solution)/shard_map/ppermute | solution.py:812
  91.5 1.5 %collective-permute-start.30 = (f32[1,512]{1,0:T(1,128)S(1)}, f32[1,512]{1,0:T(1,128)S(1)}, u32[]{:S(2)}, u32[]{:S(2)}) collective-permute-start(f32[1,512]{1,0:T(1,128)S(1)} %add.10.left), channel_id=1, source_target_pairs={{0,2},{1,3},{2,0},{3,1},{4,6},{5,7},{6,4},{7,5},{8,10},{9,11},{10,... | collective-permute-start | bytes 6152 | tf_op jit(solution)/shard_map/ppermute | solution.py:812
  93.0 2.1 %collective-permute-done.30.right = f32[1,512]{1,0:T(1,128)S(1)} collective-permute-done((f32[1,512]{1,0:T(1,128)S(1)}, f32[1,512]{1,0:T(1,128)S(1)}, u32[]{:S(2)}, u32[]{:S(2)}) %collective-permute-start.30) | collective-permute-done | bytes 2080 | tf_op jit(solution)/shard_map/ppermute | solution.py:812
  95.1 1.0 collective-permute-start.31
  96.1 2.6 %collective-permute-done.31.right = f32[1,512]{1,0:T(1,128)S(1)} collective-permute-done((f32[1,512]{1,0:T(1,128)S(1)}, f32[1,512]{1,0:T(1,128)S(1)}, u32[]{:S(2)}, u32[]{:S(2)}) %collective-permute-start.31) | collective-permute-done | bytes 2080 | tf_op jit(solution)/shard_map/ppermute | solution.py:812
  98.7 2.3 %collective-permute-start.32 = (f32[1,512]{1,0:T(1,128)S(1)}, f32[1,512]{1,0:T(1,128)S(1)}, u32[]{:S(2)}, u32[]{:S(2)}) collective-permute-start(f32[1,512]{1,0:T(1,128)S(1)} %add.12.left), channel_id=1, source_target_pairs={{0,8},{1,9},{2,10},{3,11},{4,12},{5,13},{6,14},{7,15},{8,0},{9,1},... | collective-permute-start | bytes 6152 | tf_op jit(solution)/shard_map/ppermute | solution.py:812
  101.0 2.3 %collective-permute-done.32.right = f32[1,512]{1,0:T(1,128)S(1)} collective-permute-done((f32[1,512]{1,0:T(1,128)S(1)}, f32[1,512]{1,0:T(1,128)S(1)}, u32[]{:S(2)}, u32[]{:S(2)}) %collective-permute-start.32) | collective-permute-done | bytes 2080 | tf_op jit(solution)/shard_map/ppermute | solution.py:812
  103.3 5.8 %update.1 = (f32[3]{0:T(128)}, f32[1]{0:T(128)}, f32[2,200]{1,0:T(2,128)}, f32[312,128]{1,0:T(8,128)}, f32[312,128]{1,0:T(8,128)}, /*index=5*/f32[312,128]{1,0:T(8,128)}) custom-call(s32[2]{0:T(128)S(1)} %copy-done.6, f32[1,512]{1,0:T(1,128)S(1)} %add.13.sums, bf16[256,39936]{1,0:T(8,128)(2,1)S(1)} %fetch.2._.refs_4_.upper, ...), custom_call_target="tpu_custom_call" | custom-call | tf_op jit(solution)/shard_map/update/pallas_call | solution.py:1042
  (42 shorter events, 0.2 us)
Async XLA Ops:
  0.6 10.4 %copy-start = (bf16[8,196,768]{2,0,1:T(8,128)(2,1)S(1)}, bf16[8,196,768]{2,0,1:T(8,128)(2,1)}, u32[]{:S(2)}) copy-start(bf16[8,196,768]{2,0,1:T(8,128)(2,1)} %param.9) | copy-start | bytes 7225348
  1.8 10.0 %collective-permute-start.7 = (bf16[112,128]{1,0:T(8,128)(2,1)S(1)}, bf16[112,128]{1,0:T(8,128)(2,1)S(1)}, u32[]{:S(2)}, u32[]{:S(2)}) collective-permute-start(bf16[112,128]{1,0:T(8,128)(2,1)S(1)} %get-tuple-element.95), channel_id=1, source_target_pairs={{0,2},{1,3},{2,0},{3,1},{4,6},{5,7},{6,4},{7,5},{8,10},{9,11},{10,... | collective-permute-start | bytes 86024 | tf_op jit(solution)/shard_map/ppermute | solution.py:786
  4.8 9.3 %collective-permute-start.6 = (bf16[112,128]{1,0:T(8,128)(2,1)S(1)}, bf16[112,128]{1,0:T(8,128)(2,1)S(1)}, u32[]{:S(2)}, u32[]{:S(2)}) collective-permute-start(bf16[112,128]{1,0:T(8,128)(2,1)S(1)} %get-tuple-element.95), channel_id=1, source_target_pairs={{0,1},{1,0},{2,3},{3,2},{4,5},{5,4},{6,7},{7,6},{8,9},{9,8},{10,11... | collective-permute-start | bytes 86024 | tf_op jit(solution)/shard_map/ppermute | solution.py:786
  6.3 7.8 %collective-permute-start.8 = (bf16[112,128]{1,0:T(8,128)(2,1)S(1)}, bf16[112,128]{1,0:T(8,128)(2,1)S(1)}, u32[]{:S(2)}, u32[]{:S(2)}) collective-permute-start(bf16[112,128]{1,0:T(8,128)(2,1)S(1)} %get-tuple-element.95), channel_id=1, source_target_pairs={{0,3},{1,2},{2,1},{3,0},{4,7},{5,6},{6,5},{7,4},{8,11},{9,10},{10,... | collective-permute-start | bytes 86024 | tf_op jit(solution)/shard_map/ppermute | solution.py:786
  6.3 9.3 %collective-permute-start.1 = (bf16[208,128]{1,0:T(8,128)(2,1)S(1)}, bf16[208,128]{1,0:T(8,128)(2,1)S(1)}, u32[]{:S(2)}, u32[]{:S(2)}) collective-permute-start(bf16[208,128]{1,0:T(8,128)(2,1)S(1)} %get-tuple-element.97), channel_id=1, source_target_pairs={{0,8},{1,9},{2,10},{3,11},{4,12},{5,13},{6,14},{7,15},{8,0},{9,1},... | collective-permute-start | bytes 159752 | tf_op jit(solution)/shard_map/ppermute | solution.py:786
  9.4 6.0 %collective-permute-start = (bf16[208,128]{1,0:T(8,128)(2,1)S(1)}, bf16[208,128]{1,0:T(8,128)(2,1)S(1)}, u32[]{:S(2)}, u32[]{:S(2)}) collective-permute-start(bf16[208,128]{1,0:T(8,128)(2,1)S(1)} %get-tuple-element.97), channel_id=1, source_target_pairs={{0,4},{1,5},{2,6},{3,7},{4,8},{5,9},{6,10},{7,11},{8,12},{9,13},{1... | collective-permute-start | bytes 159752 | tf_op jit(solution)/shard_map/ppermute | solution.py:786
  11.8 4.3 %collective-permute-start.2 = (bf16[208,128]{1,0:T(8,128)(2,1)S(1)}, bf16[208,128]{1,0:T(8,128)(2,1)S(1)}, u32[]{:S(2)}, u32[]{:S(2)}) collective-permute-start(bf16[208,128]{1,0:T(8,128)(2,1)S(1)} %get-tuple-element.97), channel_id=1, source_target_pairs={{0,12},{1,13},{2,14},{3,15},{4,0},{5,1},{6,2},{7,3},{8,4},{9,5},{1... | collective-permute-start | bytes 159752 | tf_op jit(solution)/shard_map/ppermute | solution.py:786
  14.1 5.3 %collective-permute-start.16 = (bf16[4,112,128]{2,1,0:T(8,128)(2,1)S(1)}, bf16[4,112,128]{2,1,0:T(8,128)(2,1)S(1)}, u32[]{:S(2)}, u32[]{:S(2)}) collective-permute-start(bf16[4,112,128]{2,1,0:T(8,128)(2,1)S(1)} %pad_maximum_fusion.1.refs_4_), channel_id=1, source_target_pairs={{0,16},{1,17},{2,18},{3,19},{4,20},{5,21},{6,22},{7,23},{8,24},{9,... | collective-permute-start | bytes 344072 | tf_op jit(solution)/shard_map/ppermute | solution.py:786
  14.2 6.1 %collective-permute-start.11 = (bf16[4,112,128]{2,1,0:T(8,128)(2,1)S(1)}, bf16[4,112,128]{2,1,0:T(8,128)(2,1)S(1)}, u32[]{:S(2)}, u32[]{:S(2)}) collective-permute-start(bf16[4,112,128]{2,1,0:T(8,128)(2,1)S(1)} %pad_maximum_fusion.1.refs_4_), channel_id=1, source_target_pairs={{0,12},{1,13},{2,14},{3,15},{4,0},{5,1},{6,2},{7,3},{8,4},{9,5},{1... | collective-permute-start | bytes 344072 | tf_op jit(solution)/shard_map/ppermute | solution.py:786
  15.4 8.5 %collective-permute-start.10 = (bf16[4,112,128]{2,1,0:T(8,128)(2,1)S(1)}, bf16[4,112,128]{2,1,0:T(8,128)(2,1)S(1)}, u32[]{:S(2)}, u32[]{:S(2)}) collective-permute-start(bf16[4,112,128]{2,1,0:T(8,128)(2,1)S(1)} %pad_maximum_fusion.1.refs_4_), channel_id=1, source_target_pairs={{0,8},{1,9},{2,10},{3,11},{4,12},{5,13},{6,14},{7,15},{8,0},{9,1},... | collective-permute-start | bytes 344072 | tf_op jit(solution)/shard_map/ppermute | solution.py:786
  16.1 19.5 %copy-start.5 = (s32[8]{0:T(128)S(1)}, s32[8]{0:T(128)}, u32[]{:S(2)}) copy-start(s32[8]{0:T(128)} %replay.3) | copy-start | bytes 100
  16.1 19.5 %copy-start.7 = (f32[8,1000]{1,0:T(8,128)S(1)}, f32[8,1000]{1,0:T(8,128)}, u32[]{:S(2)}) copy-start(f32[8,1000]{1,0:T(8,128)} %refs_17_.1) | copy-start | bytes 96004
  16.2 19.5 %copy-start.8 = (s32[8]{0:T(128)S(1)}, s32[8]{0:T(128)}, u32[]{:S(2)}) copy-start(s32[8]{0:T(128)} %labels.1) | copy-start | bytes 100
  16.2 11.2 %collective-permute-start.5 = (bf16[4,208,128]{2,1,0:T(8,128)(2,1)S(1)}, bf16[4,208,128]{2,1,0:T(8,128)(2,1)S(1)}, u32[]{:S(2)}, u32[]{:S(2)}) collective-permute-start(bf16[4,208,128]{2,1,0:T(8,128)(2,1)S(1)} %pad_maximum_fusion.refs_0_), channel_id=1, source_target_pairs={{0,3},{1,2},{2,1},{3,0},{4,7},{5,6},{6,5},{7,4},{8,11},{9,10},{10,... | collective-permute-start | bytes 638984 | tf_op jit(solution)/shard_map/ppermute | solution.py:786
  18.9 9.2 %collective-permute-start.4 = (bf16[4,208,128]{2,1,0:T(8,128)(2,1)S(1)}, bf16[4,208,128]{2,1,0:T(8,128)(2,1)S(1)}, u32[]{:S(2)}, u32[]{:S(2)}) collective-permute-start(bf16[4,208,128]{2,1,0:T(8,128)(2,1)S(1)} %pad_maximum_fusion.refs_0_), channel_id=1, source_target_pairs={{0,2},{1,3},{2,0},{3,1},{4,6},{5,7},{6,4},{7,5},{8,10},{9,11},{10,... | collective-permute-start | bytes 638984 | tf_op jit(solution)/shard_map/ppermute | solution.py:786
  19.4 8.8 %collective-permute-start.3 = (bf16[4,208,128]{2,1,0:T(8,128)(2,1)S(1)}, bf16[4,208,128]{2,1,0:T(8,128)(2,1)S(1)}, u32[]{:S(2)}, u32[]{:S(2)}) collective-permute-start(bf16[4,208,128]{2,1,0:T(8,128)(2,1)S(1)} %pad_maximum_fusion.refs_0_), channel_id=1, source_target_pairs={{0,1},{1,0},{2,3},{3,2},{4,5},{5,4},{6,7},{7,6},{8,9},{9,8},{10,11... | collective-permute-start | bytes 638984 | tf_op jit(solution)/shard_map/ppermute | solution.py:786
  20.3 6.6 %collective-permute-start.9 = (bf16[4,112,128]{2,1,0:T(8,128)(2,1)S(1)}, bf16[4,112,128]{2,1,0:T(8,128)(2,1)S(1)}, u32[]{:S(2)}, u32[]{:S(2)}) collective-permute-start(bf16[4,112,128]{2,1,0:T(8,128)(2,1)S(1)} %pad_maximum_fusion.1.refs_4_), channel_id=1, source_target_pairs={{0,4},{1,5},{2,6},{3,7},{4,8},{5,9},{6,10},{7,11},{8,12},{9,13},{1... | collective-permute-start | bytes 344072 | tf_op jit(solution)/shard_map/ppermute | solution.py:786
  23.9 3.0 %collective-permute-start.19 = (bf16[4,112,128]{2,1,0:T(8,128)(2,1)S(1)}, bf16[4,112,128]{2,1,0:T(8,128)(2,1)S(1)}, u32[]{:S(2)}, u32[]{:S(2)}) collective-permute-start(bf16[4,112,128]{2,1,0:T(8,128)(2,1)S(1)} %collective-permute-done.11.refs_7_), channel_id=1, source_target_pairs={{0,16},{1,17},{2,18},{3,19},{4,20},{5,21},{6,22},{7,23},{8,24},{9,... | collective-permute-start | bytes 344072 | tf_op jit(solution)/shard_map/ppermute | solution.py:786
  26.9 1.8 %collective-permute-start.18 = (bf16[4,112,128]{2,1,0:T(8,128)(2,1)S(1)}, bf16[4,112,128]{2,1,0:T(8,128)(2,1)S(1)}, u32[]{:S(2)}, u32[]{:S(2)}) collective-permute-start(bf16[4,112,128]{2,1,0:T(8,128)(2,1)S(1)} %collective-permute-done.10.refs_6_), channel_id=1, source_target_pairs={{0,16},{1,17},{2,18},{3,19},{4,20},{5,21},{6,22},{7,23},{8,24},{9,... | collective-permute-start | bytes 344072 | tf_op jit(solution)/shard_map/ppermute | solution.py:786
  26.9 3.2 %collective-permute-start.12 = (bf16[4,208,128]{2,1,0:T(8,128)(2,1)S(1)}, bf16[4,208,128]{2,1,0:T(8,128)(2,1)S(1)}, u32[]{:S(2)}, u32[]{:S(2)}) collective-permute-start(bf16[4,208,128]{2,1,0:T(8,128)(2,1)S(1)} %pad_maximum_fusion.refs_0_), channel_id=1, source_target_pairs={{0,16},{1,17},{2,18},{3,19},{4,20},{5,21},{6,22},{7,23},{8,24},{9,... | collective-permute-start | bytes 638984 | tf_op jit(solution)/shard_map/ppermute | solution.py:786
  27.4 2.7 %collective-permute-start.15 = (bf16[4,208,128]{2,1,0:T(8,128)(2,1)S(1)}, bf16[4,208,128]{2,1,0:T(8,128)(2,1)S(1)}, u32[]{:S(2)}, u32[]{:S(2)}) collective-permute-start(bf16[4,208,128]{2,1,0:T(8,128)(2,1)S(1)} %collective-permute-done.5.refs_3_), channel_id=1, source_target_pairs={{0,16},{1,17},{2,18},{3,19},{4,20},{5,21},{6,22},{7,23},{8,24},{9,... | collective-permute-start | bytes 638984 | tf_op jit(solution)/shard_map/ppermute | solution.py:786
  28.1 1.9 %collective-permute-start.14 = (bf16[4,208,128]{2,1,0:T(8,128)(2,1)S(1)}, bf16[4,208,128]{2,1,0:T(8,128)(2,1)S(1)}, u32[]{:S(2)}, u32[]{:S(2)}) collective-permute-start(bf16[4,208,128]{2,1,0:T(8,128)(2,1)S(1)} %collective-permute-done.4.refs_2_), channel_id=1, source_target_pairs={{0,16},{1,17},{2,18},{3,19},{4,20},{5,21},{6,22},{7,23},{8,24},{9,... | collective-permute-start | bytes 638984 | tf_op jit(solution)/shard_map/ppermute | solution.py:786
  28.2 1.8 %collective-permute-start.13 = (bf16[4,208,128]{2,1,0:T(8,128)(2,1)S(1)}, bf16[4,208,128]{2,1,0:T(8,128)(2,1)S(1)}, u32[]{:S(2)}, u32[]{:S(2)}) collective-permute-start(bf16[4,208,128]{2,1,0:T(8,128)(2,1)S(1)} %collective-permute-done.3.refs_1_), channel_id=1, source_target_pairs={{0,16},{1,17},{2,18},{3,19},{4,20},{5,21},{6,22},{7,23},{8,24},{9,... | collective-permute-start | bytes 638984 | tf_op jit(solution)/shard_map/ppermute | solution.py:786
  28.7 1.4 %collective-permute-start.17 = (bf16[4,112,128]{2,1,0:T(8,128)(2,1)S(1)}, bf16[4,112,128]{2,1,0:T(8,128)(2,1)S(1)}, u32[]{:S(2)}, u32[]{:S(2)}) collective-permute-start(bf16[4,112,128]{2,1,0:T(8,128)(2,1)S(1)} %collective-permute-done.9.refs_5_), channel_id=1, source_target_pairs={{0,16},{1,17},{2,18},{3,19},{4,20},{5,21},{6,22},{7,23},{8,24},{9,... | collective-permute-start | bytes 344072 | tf_op jit(solution)/shard_map/ppermute | solution.py:786
  50.6 3.1 %collective-permute-start.20 = (bf16[16,320,128]{2,1,0:T(8,128)(2,1)S(1)}, bf16[16,320,128]{2,1,0:T(8,128)(2,1)S(1)}, u32[]{:S(2)}, u32[]{:S(2)}) collective-permute-start(bf16[16,320,128]{2,1,0:T(8,128)(2,1)S(1)} %get-tuple-element.72), channel_id=1, source_target_pairs={{0,16},{1,17},{2,18},{3,19},{4,20},{5,21},{6,22},{7,23},{8,24},{9,... | collective-permute-start | bytes 3932168 | tf_op jit(solution)/shard_map/ppermute | solution.py:786
  53.9 9.9 %collective-permute-start.22 = (bf16[2,4,160,128]{3,2,1,0:T(8,128)(2,1)S(1)}, bf16[2,4,160,128]{3,2,1,0:T(8,128)(2,1)S(1)}, u32[]{:S(2)}, u32[]{:S(2)}) collective-permute-start(bf16[2,4,160,128]{3,2,1,0:T(8,128)(2,1)S(1)} %get-tuple-element.76), channel_id=1, source_target_pairs={{0,1},{1,0},{2,3},{3,2},{4,5},{5,4},{6,7},{7,6},{8,9},{9,8},{10,11... | collective-permute-start | bytes 983048 | tf_op jit(solution)/shard_map/ppermute | solution.py:786
  55.5 9.5 %collective-permute-start.21 = (bf16[2,4,160,128]{3,2,1,0:T(8,128)(2,1)S(1)}, bf16[2,4,160,128]{3,2,1,0:T(8,128)(2,1)S(1)}, u32[]{:S(2)}, u32[]{:S(2)}) collective-permute-start(bf16[2,4,160,128]{3,2,1,0:T(8,128)(2,1)S(1)} %get-tuple-element.75._), channel_id=1, source_target_pairs={{0,2},{1,3},{2,0},{3,1},{4,6},{5,7},{6,4},{7,5},{8,10},{9,11},{10,... | collective-permute-start | bytes 983048 | tf_op jit(solution)/shard_map/ppermute | solution.py:786
  65.1 5.4 %collective-permute-start.23 = (bf16[4,160,128]{2,1,0:T(8,128)(2,1)S(1)}, bf16[4,160,128]{2,1,0:T(8,128)(2,1)S(1)}, u32[]{:S(2)}, u32[]{:S(2)}) collective-permute-start(bf16[4,160,128]{2,1,0:T(8,128)(2,1)S(1)} %get-tuple-element.79), channel_id=1, source_target_pairs={{0,1},{1,0},{2,3},{3,2},{4,5},{5,4},{6,7},{7,6},{8,9},{9,8},{10,11... | collective-permute-start | bytes 491528 | tf_op jit(solution)/shard_map/ppermute | solution.py:786
  65.7 5.3 %collective-permute-start.24 = (bf16[4,160,128]{2,1,0:T(8,128)(2,1)S(1)}, bf16[4,160,128]{2,1,0:T(8,128)(2,1)S(1)}, u32[]{:S(2)}, u32[]{:S(2)}) collective-permute-start(bf16[4,160,128]{2,1,0:T(8,128)(2,1)S(1)} %get-tuple-element.80), channel_id=1, source_target_pairs={{0,2},{1,3},{2,0},{3,1},{4,6},{5,7},{6,4},{7,5},{8,10},{9,11},{10,... | collective-permute-start | bytes 491528 | tf_op jit(solution)/shard_map/ppermute | solution.py:786
  71.1 8.1 %collective-permute-start.26 = (bf16[320,128]{1,0:T(8,128)(2,1)S(1)}, bf16[320,128]{1,0:T(8,128)(2,1)S(1)}, u32[]{:S(2)}, u32[]{:S(2)}) collective-permute-start(bf16[320,128]{1,0:T(8,128)(2,1)S(1)} %get-tuple-element.83), channel_id=1, source_target_pairs={{0,8},{1,9},{2,10},{3,11},{4,12},{5,13},{6,14},{7,15},{8,0},{9,1},... | collective-permute-start | bytes 245768 | tf_op jit(solution)/shard_map/ppermute | solution.py:786
  73.4 6.4 %collective-permute-start.27 = (bf16[320,128]{1,0:T(8,128)(2,1)S(1)}, bf16[320,128]{1,0:T(8,128)(2,1)S(1)}, u32[]{:S(2)}, u32[]{:S(2)}) collective-permute-start(bf16[320,128]{1,0:T(8,128)(2,1)S(1)} %get-tuple-element.84), channel_id=1, source_target_pairs={{0,12},{1,13},{2,14},{3,15},{4,8},{5,9},{6,10},{7,11},{8,4},{9,5},... | collective-permute-start | bytes 245768 | tf_op jit(solution)/shard_map/ppermute | solution.py:786
  74.6 5.3 %collective-permute-start.25 = (bf16[320,128]{1,0:T(8,128)(2,1)S(1)}, bf16[320,128]{1,0:T(8,128)(2,1)S(1)}, u32[]{:S(2)}, u32[]{:S(2)}) collective-permute-start(bf16[320,128]{1,0:T(8,128)(2,1)S(1)} %get-tuple-element.82._), channel_id=1, source_target_pairs={{0,4},{1,5},{2,6},{3,7},{4,0},{5,1},{6,2},{7,3},{8,12},{9,13},{10,... | collective-permute-start | bytes 245768 | tf_op jit(solution)/shard_map/ppermute | solution.py:786
  86.7 1.2 %collective-permute-start.28 = (f32[1,512]{1,0:T(1,128)S(1)}, f32[1,512]{1,0:T(1,128)S(1)}, u32[]{:S(2)}, u32[]{:S(2)}) collective-permute-start(f32[1,512]{1,0:T(1,128)S(1)} %get-tuple-element.86.left), channel_id=1, source_target_pairs={{0,16},{1,17},{2,18},{3,19},{4,20},{5,21},{6,22},{7,23},{8,24},{9,... | collective-permute-start | bytes 6152 | tf_op jit(solution)/shard_map/ppermute | solution.py:786
  87.9 3.6 %collective-permute-start.29 = (f32[1,512]{1,0:T(1,128)S(1)}, f32[1,512]{1,0:T(1,128)S(1)}, u32[]{:S(2)}, u32[]{:S(2)}) collective-permute-start(f32[1,512]{1,0:T(1,128)S(1)} %add.9.left), channel_id=1, source_target_pairs={{0,1},{1,0},{2,3},{3,2},{4,5},{5,4},{6,7},{7,6},{8,9},{9,8},{10,11... | collective-permute-start | bytes 6152 | tf_op jit(solution)/shard_map/ppermute | solution.py:812
  91.5 3.6 %collective-permute-start.30 = (f32[1,512]{1,0:T(1,128)S(1)}, f32[1,512]{1,0:T(1,128)S(1)}, u32[]{:S(2)}, u32[]{:S(2)}) collective-permute-start(f32[1,512]{1,0:T(1,128)S(1)} %add.10.left), channel_id=1, source_target_pairs={{0,2},{1,3},{2,0},{3,1},{4,6},{5,7},{6,4},{7,5},{8,10},{9,11},{10,... | collective-permute-start | bytes 6152 | tf_op jit(solution)/shard_map/ppermute | solution.py:812
  95.1 3.6 %collective-permute-start.31 = (f32[1,512]{1,0:T(1,128)S(1)}, f32[1,512]{1,0:T(1,128)S(1)}, u32[]{:S(2)}, u32[]{:S(2)}) collective-permute-start(f32[1,512]{1,0:T(1,128)S(1)} %add.11.left), channel_id=1, source_target_pairs={{0,4},{1,5},{2,6},{3,7},{4,0},{5,1},{6,2},{7,3},{8,12},{9,13},{10,... | collective-permute-start | bytes 6152 | tf_op jit(solution)/shard_map/ppermute | solution.py:812
  98.7 4.6 %copy-start.2 = (f32[1,39936]{1,0:T(1,128)S(1)}, f32[1,39936]{1,0:T(1,128)}, u32[]{:S(2)}) copy-start(f32[1,39936]{1,0:T(1,128)} %param.14) | copy-start | bytes 479236
  98.7 4.6 %copy-start.3 = (f32[1,39936]{1,0:T(1,128)S(1)}, f32[1,39936]{1,0:T(1,128)}, u32[]{:S(2)}) copy-start(f32[1,39936]{1,0:T(1,128)} %param.15) | copy-start | bytes 479236
  98.7 4.6 %copy-start.4 = (f32[1,39936]{1,0:T(1,128)S(1)}, f32[1,39936]{1,0:T(1,128)}, u32[]{:S(2)}) copy-start(f32[1,39936]{1,0:T(1,128)} %param.16) | copy-start | bytes 479236
  98.7 4.6 %copy-start.6 = (s32[2]{0:T(128)S(1)}, s32[2]{0:T(128)}, u32[]{:S(2)}) copy-start(s32[2]{0:T(128)} %counts.1) | copy-start | bytes 28
  98.7 4.5 %collective-permute-start.32 = (f32[1,512]{1,0:T(1,128)S(1)}, f32[1,512]{1,0:T(1,128)S(1)}, u32[]{:S(2)}, u32[]{:S(2)}) collective-permute-start(f32[1,512]{1,0:T(1,128)S(1)} %add.12.left), channel_id=1, source_target_pairs={{0,8},{1,9},{2,10},{3,11},{4,12},{5,13},{6,14},{7,15},{8,0},{9,1},... | collective-permute-start | bytes 6152 | tf_op jit(solution)/shard_map/ppermute | solution.py:812
  103.3 5.8 %copy-start.1 = (bf16[8,196,768]{2,0,1:T(8,128)(2,1)S(1)}, bf16[8,196,768]{2,0,1:T(8,128)(2,1)}, u32[]{:S(2)}) copy-start(bf16[8,196,768]{2,0,1:T(8,128)(2,1)} %param.9) | copy-start | bytes 7225348

commit v8 on v7

--- a/solution.py
+++ b/solution.py
@@ -949,7 +949,7 @@
     early, late_part = shard[: place.first_rows], shard[place.first_rows :]
     column = [early] + [moved(early, place, (d, 0, 0)) for d in range(1, place.z)]
     plane = [moved(late_part, place, (0, a, b)) if a + b else late_part for a, b in turns]
-    column[1], mine = lax.optimization_barrier((column[1], mine))
+    plane[1], mine = lax.optimization_barrier((plane[1], mine))
     column, plane = jnp.stack(column), jnp.stack(plane)
     own = [moved(column, place, (0, a, b)) if a + b else column for a, b in turns]
     own += [moved(plane, place, (d, 0, 0)) if d else plane for d in range(place.z)]

time: 109 us -> 109 us (level)
  transfers between devices with their start and end apart: 33 -> 33, of which waited for: 20 -> 19; matrix products, arithmetic and copies ran while one was open for 1% -> 1% of each run, Pallas kernels for 10% -> 10%
where the time goes in v8:
time: 109 us
  Pallas kernels  45.6 us (42%)
  starting transfers between devices  32.9 us (30%)
  waiting for transfers between devices  28.8 us (26%)
  between operations  1.09 us (1%)
    ppermute x29, starting transfers between devices, moved(): return lax.ppermute(value, ('section', 'dp'), pairs)  26.6 us
    ppermute x29, waiting for transfers between devices, moved(): return lax.ppermute(value, ('section', 'dp'), pairs)  19.8 us
    pallas_call x2, Pallas kernels, fetch(): pl.pallas_call(functools.partial(fetch_kernel, first, last), in_specs=[AN...  11.1 us
    ppermute x4, waiting for transfers between devices, butterfly(): value = add(value, lax.ppermute(value, ('section', 'dp'), pairs), resident)  9.02 us
    pallas_call x1, Pallas kernels, late(): pl.pallas_call(functools.partial(late_kernel, place, per, image_total), i...  7.63 us
    pallas_call x1, Pallas kernels, back(): pl.pallas_call(functools.partial(back_kernel, place, per), in_specs=[VMEM...  7.28 us
    pallas_call x1, Pallas kernels, body(): pl.pallas_call(functools.partial(inner_kernel, divisor(26)), in_specs=[VM...  6.75 us
    ppermute x4, starting transfers between devices, butterfly(): value = add(value, lax.ppermute(value, ('section', 'dp'), pairs), resident)  6.29 us
  transfers between devices with their start and end apart: 33, of which 19 were waited for; matrix products, arithmetic and copies ran while one was open for 1% of the time, Pallas kernels for 10%

profile of v8, /device:TPU:0, one launch (start us, length us, event | category | flops | bytes accessed | tf_op | source)
XLA Modules:
  0.0 109.3 jit_solution(14896701313392470454)
XLA Ops:
  0.6 0.0 copy-start
  0.6 1.1 shard.1
  1.8 3.0 %collective-permute-start.7 = (bf16[112,128]{1,0:T(8,128)(2,1)S(1)}, bf16[112,128]{1,0:T(8,128)(2,1)S(1)}, u32[]{:S(2)}, u32[]{:S(2)}) collective-permute-start(bf16[112,128]{1,0:T(8,128)(2,1)S(1)} %get-tuple-element.95), channel_id=1, source_target_pairs={{0,2},{1,3},{2,0},{3,1},{4,6},{5,7},{6,4},{7,5},{8,10},{9,11},{10,... | collective-permute-start | bytes 86024 | tf_op jit(solution)/shard_map/ppermute | solution.py:786
  4.8 1.5 %collective-permute-start.6 = (bf16[112,128]{1,0:T(8,128)(2,1)S(1)}, bf16[112,128]{1,0:T(8,128)(2,1)S(1)}, u32[]{:S(2)}, u32[]{:S(2)}) collective-permute-start(bf16[112,128]{1,0:T(8,128)(2,1)S(1)} %get-tuple-element.95), channel_id=1, source_target_pairs={{0,1},{1,0},{2,3},{3,2},{4,5},{5,4},{6,7},{7,6},{8,9},{9,8},{10,11... | collective-permute-start | bytes 86024 | tf_op jit(solution)/shard_map/ppermute | solution.py:786
  6.3 0.0 collective-permute-start.8
  6.3 3.1 %collective-permute-start.1 = (bf16[208,128]{1,0:T(8,128)(2,1)S(1)}, bf16[208,128]{1,0:T(8,128)(2,1)S(1)}, u32[]{:S(2)}, u32[]{:S(2)}) collective-permute-start(bf16[208,128]{1,0:T(8,128)(2,1)S(1)} %get-tuple-element.97), channel_id=1, source_target_pairs={{0,8},{1,9},{2,10},{3,11},{4,12},{5,13},{6,14},{7,15},{8,0},{9,1},... | collective-permute-start | bytes 159752 | tf_op jit(solution)/shard_map/ppermute | solution.py:786
  9.4 1.6 %collective-permute-start = (bf16[208,128]{1,0:T(8,128)(2,1)S(1)}, bf16[208,128]{1,0:T(8,128)(2,1)S(1)}, u32[]{:S(2)}, u32[]{:S(2)}) collective-permute-start(bf16[208,128]{1,0:T(8,128)(2,1)S(1)} %get-tuple-element.97), channel_id=1, source_target_pairs={{0,4},{1,5},{2,6},{3,7},{4,8},{5,9},{6,10},{7,11},{8,12},{9,13},{1... | collective-permute-start | bytes 159752 | tf_op jit(solution)/shard_map/ppermute | solution.py:786
  11.0 0.6 constant_dynamic-slice_fusion
  11.6 0.1 copy.16.refs_16_.refs_10_
  11.8 2.3 %collective-permute-start.2 = (bf16[208,128]{1,0:T(8,128)(2,1)S(1)}, bf16[208,128]{1,0:T(8,128)(2,1)S(1)}, u32[]{:S(2)}, u32[]{:S(2)}) collective-permute-start(bf16[208,128]{1,0:T(8,128)(2,1)S(1)} %get-tuple-element.97), channel_id=1, source_target_pairs={{0,12},{1,13},{2,14},{3,15},{4,0},{5,1},{6,2},{7,3},{8,4},{9,5},{1... | collective-permute-start | bytes 159752 | tf_op jit(solution)/shard_map/ppermute | solution.py:786
  14.1 0.1 collective-permute-start.16
  14.2 0.6 collective-permute-start.11
  14.8 0.7 collective-permute-start.10
  15.5 0.6 collective-permute-done.2
  16.1 0.0 copy-start.5
  16.1 0.0 copy-start.7
  16.2 2.7 %collective-permute-start.5 = (bf16[4,208,128]{2,1,0:T(8,128)(2,1)S(1)}, bf16[4,208,128]{2,1,0:T(8,128)(2,1)S(1)}, u32[]{:S(2)}, u32[]{:S(2)}) collective-permute-start(bf16[4,208,128]{2,1,0:T(8,128)(2,1)S(1)} %pad_maximum_fusion.refs_0_), channel_id=1, source_target_pairs={{0,3},{1,2},{2,1},{3,0},{4,7},{5,6},{6,5},{7,4},{8,11},{9,10},{10,... | collective-permute-start | bytes 638984 | tf_op jit(solution)/shard_map/ppermute | solution.py:786
  18.9 0.5 collective-permute-start.4
  19.4 0.3 collective-permute-start.3
  19.7 0.5 collective-permute-done.11.refs_7_
  20.3 3.6 %collective-permute-done.10.refs_6_ = bf16[4,112,128]{2,1,0:T(8,128)(2,1)S(1)} collective-permute-done((bf16[4,112,128]{2,1,0:T(8,128)(2,1)S(1)}, bf16[4,112,128]{2,1,0:T(8,128)(2,1)S(1)}, u32[]{:S(2)}, u32[]{:S(2)}) %collective-permute-start.10) | collective-permute-done | bytes 114720 | tf_op jit(solution)/shard_map/ppermute | solution.py:786
  23.9 3.0 %collective-permute-done.9.refs_5_ = bf16[4,112,128]{2,1,0:T(8,128)(2,1)S(1)} collective-permute-done((bf16[4,112,128]{2,1,0:T(8,128)(2,1)S(1)}, bf16[4,112,128]{2,1,0:T(8,128)(2,1)S(1)}, u32[]{:S(2)}, u32[]{:S(2)}) %collective-permute-start.9) | collective-permute-done | bytes 114720 | tf_op jit(solution)/shard_map/ppermute | solution.py:786
  26.9 0.5 collective-permute-start.12
  27.4 0.1 collective-permute-start.15
  27.4 0.7 collective-permute-done.4.refs_2_
  28.1 0.1 collective-permute-done.3.refs_1_
  28.2 0.4 collective-permute-start.13
  28.7 0.1 collective-permute-start.17
  28.7 1.3 %collective-permute-done.17.refs_13_ = bf16[4,112,128]{2,1,0:T(8,128)(2,1)S(1)} collective-permute-done((bf16[4,112,128]{2,1,0:T(8,128)(2,1)S(1)}, bf16[4,112,128]{2,1,0:T(8,128)(2,1)S(1)}, u32[]{:S(2)}, u32[]{:S(2)}) %collective-permute-start.17) | collective-permute-done | bytes 114720 | tf_op jit(solution)/shard_map/ppermute | solution.py:786
  30.1 5.5 %front.1 = (f32[832,192]{1,0:T(8,128)S(1)}, bf16[832,192]{1,0:T(8,128)(2,1)S(1)}, bf16[832,192]{1,0:T(8,128)(2,1)S(1)}, bf16[832,192]{1,0:T(8,128)(2,1)S(1)}, f3...) custom-call(bf16[4,208,128]{2,1,0:T(8,128)(2,1)S(1)} %pad_maximum_fu, ...), custom_call_target="tpu_custom_call" | custom-call | flops 3000000000 | bytes 30000000 | tf_op jit(solution)/shard_map/front/pallas_call | solution.py:860
  35.6 7.6 %late.1 = (bf16[832,192]{1,0:T(8,128)(2,1)S(1)}, bf16[16,320,128]{2,1,0:T(8,128)(2,1)S(1)}, f32[1,128]{1,0:T(1,128)S(1)}) custom-call(s32[8]{0:T(128)S(1)} %copy-done.8, s32[8]{0:T(128)S(1)} %copy-done.5, bf16[4,208,128]{2,1,0:T(8,128)(2,1)S(1)} %pad_maximum_fusion.refs_0_, bf16[4,208,128]{2,1,0:T(8,128)(2,1)S(1)} %collective-permute-done.3.refs_1_, ...), custom_call_target="tpu_custom_call" | custom-call | flops 3000000000 | bytes 30000000 | tf_op jit(solution)/shard_map/late/pallas_call | solution.py:884
  43.3 7.3 %back.1 = (bf16[16,320,128]{2,1,0:T(8,128)(2,1)S(1)}, bf16[16,320,128]{2,1,0:T(8,128)(2,1)S(1)}) custom-call(bf16[832,192]{1,0:T(8,128)(2,1)S(1)} %get-tuple-element.53.refs_0_, f32[832,192]{1,0:T(8,128)S(1)} %get-tuple-element.54.refs_1_, bf16[832,192]{1,0:T(8,128)(2,1)S(1)} %get-tuple-element.55.refs_2_, bf16[832,192]{1,0:T(8,128)(2,1)S(1)} %get-tuple-element.56.refs_3_, ...), custom_call_target="tpu_custom_call" | custom-call | flops 3000000000 | bytes 30000000 | tf_op jit(solution)/shard_map/back/pallas_call | solution.py:910
  50.6 0.3 collective-permute-start.20
  50.8 2.8 %collective-permute-done.20.given = bf16[16,320,128]{2,1,0:T(8,128)(2,1)S(1)} collective-permute-done((bf16[16,320,128]{2,1,0:T(8,128)(2,1)S(1)}, bf16[16,320,128]{2,1,0:T(8,128)(2,1)S(1)}, u32[]{:S(2)}, u32[]{:S(2)}) %collective-permute-start.20) | collective-permute-done | bytes 1310752 | tf_op jit(solution)/shard_map/ppermute | solution.py:786
  53.7 0.3 split.1
  53.9 1.6 %collective-permute-start.22 = (bf16[2,4,160,128]{3,2,1,0:T(8,128)(2,1)S(1)}, bf16[2,4,160,128]{3,2,1,0:T(8,128)(2,1)S(1)}, u32[]{:S(2)}, u32[]{:S(2)}) collective-permute-start(bf16[2,4,160,128]{3,2,1,0:T(8,128)(2,1)S(1)} %get-tuple-element.76), channel_id=1, source_target_pairs={{0,1},{1,0},{2,3},{3,2},{4,5},{5,4},{6,7},{7,6},{8,9},{9,8},{10,11... | collective-permute-start | bytes 983048 | tf_op jit(solution)/shard_map/ppermute | solution.py:786
  55.5 1.3 %collective-permute-start.21 = (bf16[2,4,160,128]{3,2,1,0:T(8,128)(2,1)S(1)}, bf16[2,4,160,128]{3,2,1,0:T(8,128)(2,1)S(1)}, u32[]{:S(2)}, u32[]{:S(2)}) collective-permute-start(bf16[2,4,160,128]{3,2,1,0:T(8,128)(2,1)S(1)} %get-tuple-element.75._), channel_id=1, source_target_pairs={{0,2},{1,3},{2,0},{3,1},{4,6},{5,7},{6,4},{7,5},{8,10},{9,11},{10,... | collective-permute-start | bytes 983048 | tf_op jit(solution)/shard_map/ppermute | solution.py:786
  56.8 6.8 %fetch.2._.refs_4_.upper = bf16[256,39936]{1,0:T(8,128)(2,1)S(1)} custom-call(bf16[2,4,160,128]{3,2,1,0:T(8,128)(2,1)S(1)} %get-tuple-element.75._, bf16[400,39936]{1,0:T(8,128)(2,1)} %bitcast.22), custom_call_target="tpu_custom_call" | custom-call | bytes 40894464 | tf_op jit(solution)/shard_map/fetch/pallas_call | solution.py:983
  63.6 0.2 collective-permute-done.22.refs_1_
  63.8 1.2 %collective-permute-done.21.refs_0_ = bf16[2,4,160,128]{3,2,1,0:T(8,128)(2,1)S(1)} collective-permute-done((bf16[2,4,160,128]{3,2,1,0:T(8,128)(2,1)S(1)}, bf16[2,4,160,128]{3,2,1,0:T(8,128)(2,1)S(1)}, u32[]{:S(2)}, u32[]{:S(2)}) %collective-permute-start.21) | collective-permute-done | bytes 327712 | tf_op jit(solution)/shard_map/ppermute | solution.py:786
  65.0 0.1 turn.1
  65.1 0.6 collective-permute-start.23
  65.7 1.5 %collective-permute-start.24 = (bf16[4,160,128]{2,1,0:T(8,128)(2,1)S(1)}, bf16[4,160,128]{2,1,0:T(8,128)(2,1)S(1)}, u32[]{:S(2)}, u32[]{:S(2)}) collective-permute-start(bf16[4,160,128]{2,1,0:T(8,128)(2,1)S(1)} %get-tuple-element.80), channel_id=1, source_target_pairs={{0,2},{1,3},{2,0},{3,1},{4,6},{5,7},{6,4},{7,5},{8,10},{9,11},{10,... | collective-permute-start | bytes 491528 | tf_op jit(solution)/shard_map/ppermute | solution.py:786
  67.3 3.3 %collective-permute-done.23.refs_0_ = bf16[4,160,128]{2,1,0:T(8,128)(2,1)S(1)} collective-permute-done((bf16[4,160,128]{2,1,0:T(8,128)(2,1)S(1)}, bf16[4,160,128]{2,1,0:T(8,128)(2,1)S(1)}, u32[]{:S(2)}, u32[]{:S(2)}) %collective-permute-start.23) | collective-permute-done | bytes 163872 | tf_op jit(solution)/shard_map/ppermute | solution.py:786
  70.5 0.5 collective-permute-done.24.refs_1_
  71.1 0.1 plane.1
  71.1 2.3 %collective-permute-start.26 = (bf16[320,128]{1,0:T(8,128)(2,1)S(1)}, bf16[320,128]{1,0:T(8,128)(2,1)S(1)}, u32[]{:S(2)}, u32[]{:S(2)}) collective-permute-start(bf16[320,128]{1,0:T(8,128)(2,1)S(1)} %get-tuple-element.83), channel_id=1, source_target_pairs={{0,8},{1,9},{2,10},{3,11},{4,12},{5,13},{6,14},{7,15},{8,0},{9,1},... | collective-permute-start | bytes 245768 | tf_op jit(solution)/shard_map/ppermute | solution.py:786
  73.4 1.2 %collective-permute-start.27 = (bf16[320,128]{1,0:T(8,128)(2,1)S(1)}, bf16[320,128]{1,0:T(8,128)(2,1)S(1)}, u32[]{:S(2)}, u32[]{:S(2)}) collective-permute-start(bf16[320,128]{1,0:T(8,128)(2,1)S(1)} %get-tuple-element.84), channel_id=1, source_target_pairs={{0,12},{1,13},{2,14},{3,15},{4,8},{5,9},{6,10},{7,11},{8,4},{9,5},... | collective-permute-start | bytes 245768 | tf_op jit(solution)/shard_map/ppermute | solution.py:786
  74.6 0.3 collective-permute-start.25
  74.9 4.3 %fetch.3.refs_5_.__.lower = bf16[144,39936]{1,0:T(8,128)(2,1)S(1)} custom-call(bf16[320,128]{1,0:T(8,128)(2,1)S(1)} %get-tuple-element.82._, bf16[400,39936]{1,0:T(8,128)(2,1)} %bitcast.23), custom_call_target="tpu_custom_call" | custom-call | bytes 23003136 | tf_op jit(solution)/shard_map/fetch/pallas_call | solution.py:983
  79.2 0.6 collective-permute-done.27.refs_3_
  79.8 0.1 collective-permute-done.25.refs_1_
  80.0 6.8 %inner.1 = (f32[312,128]{1,0:T(8,128)S(1)}, f32[1,512]{1,0:T(1,128)S(1)}) custom-call(f32[320,128]{1,0:T(8,128)S(1)} %get-tuple-element.81.refs_0_, bf16[320,128]{1,0:T(8,128)(2,1)S(1)} %collective-permute-done.25.refs_1_, bf16[320,128]{1,0:T(8,128)(2,1)S(1)} %collective-permute-done.26.refs_2_, bf16[320,128]{1,0:T(8,128)(2,1)S(1)} %collective-permute-done.27.refs_3_, ...), custom_call_target="tpu_custom_call" | custom-call | tf_op jit(solution)/shard_map/inner/pallas_call | solution.py:1031
  86.7 0.1 collective-permute-start.28
  86.8 1.1 %collective-permute-done.28.right = f32[1,512]{1,0:T(1,128)S(1)} collective-permute-done((f32[1,512]{1,0:T(1,128)S(1)}, f32[1,512]{1,0:T(1,128)S(1)}, u32[]{:S(2)}, u32[]{:S(2)}) %collective-permute-start.28) | collective-permute-done | bytes 2080 | tf_op jit(solution)/shard_map/ppermute | solution.py:786
  87.9 1.5 %collective-permute-start.29 = (f32[1,512]{1,0:T(1,128)S(1)}, f32[1,512]{1,0:T(1,128)S(1)}, u32[]{:S(2)}, u32[]{:S(2)}) collective-permute-start(f32[1,512]{1,0:T(1,128)S(1)} %add.9.left), channel_id=1, source_target_pairs={{0,1},{1,0},{2,3},{3,2},{4,5},{5,4},{6,7},{7,6},{8,9},{9,8},{10,11... | collective-permute-start | bytes 6152 | tf_op jit(solution)/shard_map/ppermute | solution.py:812
  89.4 2.1 %collective-permute-done.29.right = f32[1,512]{1,0:T(1,128)S(1)} collective-permute-done((f32[1,512]{1,0:T(1,128)S(1)}, f32[1,512]{1,0:T(1,128)S(1)}, u32[]{:S(2)}, u32[]{:S(2)}) %collective-permute-start.29) | collective-permute-done | bytes 2080 | tf_op jit(solution)/shard_map/ppermute | solution.py:812
  91.5 1.5 %collective-permute-start.30 = (f32[1,512]{1,0:T(1,128)S(1)}, f32[1,512]{1,0:T(1,128)S(1)}, u32[]{:S(2)}, u32[]{:S(2)}) collective-permute-start(f32[1,512]{1,0:T(1,128)S(1)} %add.10.left), channel_id=1, source_target_pairs={{0,2},{1,3},{2,0},{3,1},{4,6},{5,7},{6,4},{7,5},{8,10},{9,11},{10,... | collective-permute-start | bytes 6152 | tf_op jit(solution)/shard_map/ppermute | solution.py:812
  93.0 2.1 %collective-permute-done.30.right = f32[1,512]{1,0:T(1,128)S(1)} collective-permute-done((f32[1,512]{1,0:T(1,128)S(1)}, f32[1,512]{1,0:T(1,128)S(1)}, u32[]{:S(2)}, u32[]{:S(2)}) %collective-permute-start.30) | collective-permute-done | bytes 2080 | tf_op jit(solution)/shard_map/ppermute | solution.py:812
  95.1 1.0 collective-permute-start.31
  96.1 2.6 %collective-permute-done.31.right = f32[1,512]{1,0:T(1,128)S(1)} collective-permute-done((f32[1,512]{1,0:T(1,128)S(1)}, f32[1,512]{1,0:T(1,128)S(1)}, u32[]{:S(2)}, u32[]{:S(2)}) %collective-permute-start.31) | collective-permute-done | bytes 2080 | tf_op jit(solution)/shard_map/ppermute | solution.py:812
  98.7 2.3 %collective-permute-start.32 = (f32[1,512]{1,0:T(1,128)S(1)}, f32[1,512]{1,0:T(1,128)S(1)}, u32[]{:S(2)}, u32[]{:S(2)}) collective-permute-start(f32[1,512]{1,0:T(1,128)S(1)} %add.12.left), channel_id=1, source_target_pairs={{0,8},{1,9},{2,10},{3,11},{4,12},{5,13},{6,14},{7,15},{8,0},{9,1},... | collective-permute-start | bytes 6152 | tf_op jit(solution)/shard_map/ppermute | solution.py:812
  101.0 2.3 %collective-permute-done.32.right = f32[1,512]{1,0:T(1,128)S(1)} collective-permute-done((f32[1,512]{1,0:T(1,128)S(1)}, f32[1,512]{1,0:T(1,128)S(1)}, u32[]{:S(2)}, u32[]{:S(2)}) %collective-permute-start.32) | collective-permute-done | bytes 2080 | tf_op jit(solution)/shard_map/ppermute | solution.py:812
  103.3 5.8 %update.1 = (f32[3]{0:T(128)}, f32[1]{0:T(128)}, f32[2,200]{1,0:T(2,128)}, f32[312,128]{1,0:T(8,128)}, f32[312,128]{1,0:T(8,128)}, /*index=5*/f32[312,128]{1,0:T(8,128)}) custom-call(s32[2]{0:T(128)S(1)} %copy-done.6, f32[1,512]{1,0:T(1,128)S(1)} %add.13.sums, bf16[256,39936]{1,0:T(8,128)(2,1)S(1)} %fetch.2._.refs_4_.upper, ...), custom_call_target="tpu_custom_call" | custom-call | tf_op jit(solution)/shard_map/update/pallas_call | solution.py:1042
  (42 shorter events, 0.2 us)
Async XLA Ops:
  0.6 10.4 %copy-start = (bf16[8,196,768]{2,0,1:T(8,128)(2,1)S(1)}, bf16[8,196,768]{2,0,1:T(8,128)(2,1)}, u32[]{:S(2)}) copy-start(bf16[8,196,768]{2,0,1:T(8,128)(2,1)} %param.9) | copy-start | bytes 7225348
  1.8 12.3 %collective-permute-start.7 = (bf16[112,128]{1,0:T(8,128)(2,1)S(1)}, bf16[112,128]{1,0:T(8,128)(2,1)S(1)}, u32[]{:S(2)}, u32[]{:S(2)}) collective-permute-start(bf16[112,128]{1,0:T(8,128)(2,1)S(1)} %get-tuple-element.95), channel_id=1, source_target_pairs={{0,2},{1,3},{2,0},{3,1},{4,6},{5,7},{6,4},{7,5},{8,10},{9,11},{10,... | collective-permute-start | bytes 86024 | tf_op jit(solution)/shard_map/ppermute | solution.py:786
  4.8 7.0 %collective-permute-start.6 = (bf16[112,128]{1,0:T(8,128)(2,1)S(1)}, bf16[112,128]{1,0:T(8,128)(2,1)S(1)}, u32[]{:S(2)}, u32[]{:S(2)}) collective-permute-start(bf16[112,128]{1,0:T(8,128)(2,1)S(1)} %get-tuple-element.95), channel_id=1, source_target_pairs={{0,1},{1,0},{2,3},{3,2},{4,5},{5,4},{6,7},{7,6},{8,9},{9,8},{10,11... | collective-permute-start | bytes 86024 | tf_op jit(solution)/shard_map/ppermute | solution.py:786
  6.3 7.8 %collective-permute-start.8 = (bf16[112,128]{1,0:T(8,128)(2,1)S(1)}, bf16[112,128]{1,0:T(8,128)(2,1)S(1)}, u32[]{:S(2)}, u32[]{:S(2)}) collective-permute-start(bf16[112,128]{1,0:T(8,128)(2,1)S(1)} %get-tuple-element.95), channel_id=1, source_target_pairs={{0,3},{1,2},{2,1},{3,0},{4,7},{5,6},{6,5},{7,4},{8,11},{9,10},{10,... | collective-permute-start | bytes 86024 | tf_op jit(solution)/shard_map/ppermute | solution.py:786
  6.3 8.5 %collective-permute-start.1 = (bf16[208,128]{1,0:T(8,128)(2,1)S(1)}, bf16[208,128]{1,0:T(8,128)(2,1)S(1)}, u32[]{:S(2)}, u32[]{:S(2)}) collective-permute-start(bf16[208,128]{1,0:T(8,128)(2,1)S(1)} %get-tuple-element.97), channel_id=1, source_target_pairs={{0,8},{1,9},{2,10},{3,11},{4,12},{5,13},{6,14},{7,15},{8,0},{9,1},... | collective-permute-start | bytes 159752 | tf_op jit(solution)/shard_map/ppermute | solution.py:786
  9.4 6.1 %collective-permute-start = (bf16[208,128]{1,0:T(8,128)(2,1)S(1)}, bf16[208,128]{1,0:T(8,128)(2,1)S(1)}, u32[]{:S(2)}, u32[]{:S(2)}) collective-permute-start(bf16[208,128]{1,0:T(8,128)(2,1)S(1)} %get-tuple-element.97), channel_id=1, source_target_pairs={{0,4},{1,5},{2,6},{3,7},{4,8},{5,9},{6,10},{7,11},{8,12},{9,13},{1... | collective-permute-start | bytes 159752 | tf_op jit(solution)/shard_map/ppermute | solution.py:786
  11.8 4.3 %collective-permute-start.2 = (bf16[208,128]{1,0:T(8,128)(2,1)S(1)}, bf16[208,128]{1,0:T(8,128)(2,1)S(1)}, u32[]{:S(2)}, u32[]{:S(2)}) collective-permute-start(bf16[208,128]{1,0:T(8,128)(2,1)S(1)} %get-tuple-element.97), channel_id=1, source_target_pairs={{0,12},{1,13},{2,14},{3,15},{4,0},{5,1},{6,2},{7,3},{8,4},{9,5},{1... | collective-permute-start | bytes 159752 | tf_op jit(solution)/shard_map/ppermute | solution.py:786
  14.1 5.3 %collective-permute-start.16 = (bf16[4,112,128]{2,1,0:T(8,128)(2,1)S(1)}, bf16[4,112,128]{2,1,0:T(8,128)(2,1)S(1)}, u32[]{:S(2)}, u32[]{:S(2)}) collective-permute-start(bf16[4,112,128]{2,1,0:T(8,128)(2,1)S(1)} %pad_maximum_fusion.1.refs_4_), channel_id=1, source_target_pairs={{0,16},{1,17},{2,18},{3,19},{4,20},{5,21},{6,22},{7,23},{8,24},{9,... | collective-permute-start | bytes 344072 | tf_op jit(solution)/shard_map/ppermute | solution.py:786
  14.2 6.1 %collective-permute-start.11 = (bf16[4,112,128]{2,1,0:T(8,128)(2,1)S(1)}, bf16[4,112,128]{2,1,0:T(8,128)(2,1)S(1)}, u32[]{:S(2)}, u32[]{:S(2)}) collective-permute-start(bf16[4,112,128]{2,1,0:T(8,128)(2,1)S(1)} %pad_maximum_fusion.1.refs_4_), channel_id=1, source_target_pairs={{0,12},{1,13},{2,14},{3,15},{4,0},{5,1},{6,2},{7,3},{8,4},{9,5},{1... | collective-permute-start | bytes 344072 | tf_op jit(solution)/shard_map/ppermute | solution.py:786
  14.8 9.1 %collective-permute-start.10 = (bf16[4,112,128]{2,1,0:T(8,128)(2,1)S(1)}, bf16[4,112,128]{2,1,0:T(8,128)(2,1)S(1)}, u32[]{:S(2)}, u32[]{:S(2)}) collective-permute-start(bf16[4,112,128]{2,1,0:T(8,128)(2,1)S(1)} %pad_maximum_fusion.1.refs_4_), channel_id=1, source_target_pairs={{0,8},{1,9},{2,10},{3,11},{4,12},{5,13},{6,14},{7,15},{8,0},{9,1},... | collective-permute-start | bytes 344072 | tf_op jit(solution)/shard_map/ppermute | solution.py:786
  16.1 19.5 %copy-start.5 = (s32[8]{0:T(128)S(1)}, s32[8]{0:T(128)}, u32[]{:S(2)}) copy-start(s32[8]{0:T(128)} %replay.3) | copy-start | bytes 100
  16.1 19.5 %copy-start.7 = (f32[8,1000]{1,0:T(8,128)S(1)}, f32[8,1000]{1,0:T(8,128)}, u32[]{:S(2)}) copy-start(f32[8,1000]{1,0:T(8,128)} %refs_17_.1) | copy-start | bytes 96004
  16.2 19.5 %copy-start.8 = (s32[8]{0:T(128)S(1)}, s32[8]{0:T(128)}, u32[]{:S(2)}) copy-start(s32[8]{0:T(128)} %labels.1) | copy-start | bytes 100
  16.2 11.2 %collective-permute-start.5 = (bf16[4,208,128]{2,1,0:T(8,128)(2,1)S(1)}, bf16[4,208,128]{2,1,0:T(8,128)(2,1)S(1)}, u32[]{:S(2)}, u32[]{:S(2)}) collective-permute-start(bf16[4,208,128]{2,1,0:T(8,128)(2,1)S(1)} %pad_maximum_fusion.refs_0_), channel_id=1, source_target_pairs={{0,3},{1,2},{2,1},{3,0},{4,7},{5,6},{6,5},{7,4},{8,11},{9,10},{10,... | collective-permute-start | bytes 638984 | tf_op jit(solution)/shard_map/ppermute | solution.py:786
  18.9 9.2 %collective-permute-start.4 = (bf16[4,208,128]{2,1,0:T(8,128)(2,1)S(1)}, bf16[4,208,128]{2,1,0:T(8,128)(2,1)S(1)}, u32[]{:S(2)}, u32[]{:S(2)}) collective-permute-start(bf16[4,208,128]{2,1,0:T(8,128)(2,1)S(1)} %pad_maximum_fusion.refs_0_), channel_id=1, source_target_pairs={{0,2},{1,3},{2,0},{3,1},{4,6},{5,7},{6,4},{7,5},{8,10},{9,11},{10,... | collective-permute-start | bytes 638984 | tf_op jit(solution)/shard_map/ppermute | solution.py:786
  19.4 8.8 %collective-permute-start.3 = (bf16[4,208,128]{2,1,0:T(8,128)(2,1)S(1)}, bf16[4,208,128]{2,1,0:T(8,128)(2,1)S(1)}, u32[]{:S(2)}, u32[]{:S(2)}) collective-permute-start(bf16[4,208,128]{2,1,0:T(8,128)(2,1)S(1)} %pad_maximum_fusion.refs_0_), channel_id=1, source_target_pairs={{0,1},{1,0},{2,3},{3,2},{4,5},{5,4},{6,7},{7,6},{8,9},{9,8},{10,11... | collective-permute-start | bytes 638984 | tf_op jit(solution)/shard_map/ppermute | solution.py:786
  20.3 6.6 %collective-permute-start.9 = (bf16[4,112,128]{2,1,0:T(8,128)(2,1)S(1)}, bf16[4,112,128]{2,1,0:T(8,128)(2,1)S(1)}, u32[]{:S(2)}, u32[]{:S(2)}) collective-permute-start(bf16[4,112,128]{2,1,0:T(8,128)(2,1)S(1)} %pad_maximum_fusion.1.refs_4_), channel_id=1, source_target_pairs={{0,4},{1,5},{2,6},{3,7},{4,8},{5,9},{6,10},{7,11},{8,12},{9,13},{1... | collective-permute-start | bytes 344072 | tf_op jit(solution)/shard_map/ppermute | solution.py:786
  23.9 3.0 %collective-permute-start.19 = (bf16[4,112,128]{2,1,0:T(8,128)(2,1)S(1)}, bf16[4,112,128]{2,1,0:T(8,128)(2,1)S(1)}, u32[]{:S(2)}, u32[]{:S(2)}) collective-permute-start(bf16[4,112,128]{2,1,0:T(8,128)(2,1)S(1)} %collective-permute-done.11.refs_7_), channel_id=1, source_target_pairs={{0,16},{1,17},{2,18},{3,19},{4,20},{5,21},{6,22},{7,23},{8,24},{9,... | collective-permute-start | bytes 344072 | tf_op jit(solution)/shard_map/ppermute | solution.py:786
  26.9 1.8 %collective-permute-start.18 = (bf16[4,112,128]{2,1,0:T(8,128)(2,1)S(1)}, bf16[4,112,128]{2,1,0:T(8,128)(2,1)S(1)}, u32[]{:S(2)}, u32[]{:S(2)}) collective-permute-start(bf16[4,112,128]{2,1,0:T(8,128)(2,1)S(1)} %collective-permute-done.10.refs_6_), channel_id=1, source_target_pairs={{0,16},{1,17},{2,18},{3,19},{4,20},{5,21},{6,22},{7,23},{8,24},{9,... | collective-permute-start | bytes 344072 | tf_op jit(solution)/shard_map/ppermute | solution.py:786
  26.9 3.2 %collective-permute-start.12 = (bf16[4,208,128]{2,1,0:T(8,128)(2,1)S(1)}, bf16[4,208,128]{2,1,0:T(8,128)(2,1)S(1)}, u32[]{:S(2)}, u32[]{:S(2)}) collective-permute-start(bf16[4,208,128]{2,1,0:T(8,128)(2,1)S(1)} %pad_maximum_fusion.refs_0_), channel_id=1, source_target_pairs={{0,16},{1,17},{2,18},{3,19},{4,20},{5,21},{6,22},{7,23},{8,24},{9,... | collective-permute-start | bytes 638984 | tf_op jit(solution)/shard_map/ppermute | solution.py:786
  27.4 2.7 %collective-permute-start.15 = (bf16[4,208,128]{2,1,0:T(8,128)(2,1)S(1)}, bf16[4,208,128]{2,1,0:T(8,128)(2,1)S(1)}, u32[]{:S(2)}, u32[]{:S(2)}) collective-permute-start(bf16[4,208,128]{2,1,0:T(8,128)(2,1)S(1)} %collective-permute-done.5.refs_3_), channel_id=1, source_target_pairs={{0,16},{1,17},{2,18},{3,19},{4,20},{5,21},{6,22},{7,23},{8,24},{9,... | collective-permute-start | bytes 638984 | tf_op jit(solution)/shard_map/ppermute | solution.py:786
  28.1 1.9 %collective-permute-start.14 = (bf16[4,208,128]{2,1,0:T(8,128)(2,1)S(1)}, bf16[4,208,128]{2,1,0:T(8,128)(2,1)S(1)}, u32[]{:S(2)}, u32[]{:S(2)}) collective-permute-start(bf16[4,208,128]{2,1,0:T(8,128)(2,1)S(1)} %collective-permute-done.4.refs_2_), channel_id=1, source_target_pairs={{0,16},{1,17},{2,18},{3,19},{4,20},{5,21},{6,22},{7,23},{8,24},{9,... | collective-permute-start | bytes 638984 | tf_op jit(solution)/shard_map/ppermute | solution.py:786
  28.2 1.8 %collective-permute-start.13 = (bf16[4,208,128]{2,1,0:T(8,128)(2,1)S(1)}, bf16[4,208,128]{2,1,0:T(8,128)(2,1)S(1)}, u32[]{:S(2)}, u32[]{:S(2)}) collective-permute-start(bf16[4,208,128]{2,1,0:T(8,128)(2,1)S(1)} %collective-permute-done.3.refs_1_), channel_id=1, source_target_pairs={{0,16},{1,17},{2,18},{3,19},{4,20},{5,21},{6,22},{7,23},{8,24},{9,... | collective-permute-start | bytes 638984 | tf_op jit(solution)/shard_map/ppermute | solution.py:786
  28.7 1.4 %collective-permute-start.17 = (bf16[4,112,128]{2,1,0:T(8,128)(2,1)S(1)}, bf16[4,112,128]{2,1,0:T(8,128)(2,1)S(1)}, u32[]{:S(2)}, u32[]{:S(2)}) collective-permute-start(bf16[4,112,128]{2,1,0:T(8,128)(2,1)S(1)} %collective-permute-done.9.refs_5_), channel_id=1, source_target_pairs={{0,16},{1,17},{2,18},{3,19},{4,20},{5,21},{6,22},{7,23},{8,24},{9,... | collective-permute-start | bytes 344072 | tf_op jit(solution)/shard_map/ppermute | solution.py:786
  50.6 3.1 %collective-permute-start.20 = (bf16[16,320,128]{2,1,0:T(8,128)(2,1)S(1)}, bf16[16,320,128]{2,1,0:T(8,128)(2,1)S(1)}, u32[]{:S(2)}, u32[]{:S(2)}) collective-permute-start(bf16[16,320,128]{2,1,0:T(8,128)(2,1)S(1)} %get-tuple-element.72), channel_id=1, source_target_pairs={{0,16},{1,17},{2,18},{3,19},{4,20},{5,21},{6,22},{7,23},{8,24},{9,... | collective-permute-start | bytes 3932168 | tf_op jit(solution)/shard_map/ppermute | solution.py:786
  53.9 9.9 %collective-permute-start.22 = (bf16[2,4,160,128]{3,2,1,0:T(8,128)(2,1)S(1)}, bf16[2,4,160,128]{3,2,1,0:T(8,128)(2,1)S(1)}, u32[]{:S(2)}, u32[]{:S(2)}) collective-permute-start(bf16[2,4,160,128]{3,2,1,0:T(8,128)(2,1)S(1)} %get-tuple-element.76), channel_id=1, source_target_pairs={{0,1},{1,0},{2,3},{3,2},{4,5},{5,4},{6,7},{7,6},{8,9},{9,8},{10,11... | collective-permute-start | bytes 983048 | tf_op jit(solution)/shard_map/ppermute | solution.py:786
  55.5 9.5 %collective-permute-start.21 = (bf16[2,4,160,128]{3,2,1,0:T(8,128)(2,1)S(1)}, bf16[2,4,160,128]{3,2,1,0:T(8,128)(2,1)S(1)}, u32[]{:S(2)}, u32[]{:S(2)}) collective-permute-start(bf16[2,4,160,128]{3,2,1,0:T(8,128)(2,1)S(1)} %get-tuple-element.75._), channel_id=1, source_target_pairs={{0,2},{1,3},{2,0},{3,1},{4,6},{5,7},{6,4},{7,5},{8,10},{9,11},{10,... | collective-permute-start | bytes 983048 | tf_op jit(solution)/shard_map/ppermute | solution.py:786
  65.1 5.4 %collective-permute-start.23 = (bf16[4,160,128]{2,1,0:T(8,128)(2,1)S(1)}, bf16[4,160,128]{2,1,0:T(8,128)(2,1)S(1)}, u32[]{:S(2)}, u32[]{:S(2)}) collective-permute-start(bf16[4,160,128]{2,1,0:T(8,128)(2,1)S(1)} %get-tuple-element.79), channel_id=1, source_target_pairs={{0,1},{1,0},{2,3},{3,2},{4,5},{5,4},{6,7},{7,6},{8,9},{9,8},{10,11... | collective-permute-start | bytes 491528 | tf_op jit(solution)/shard_map/ppermute | solution.py:786
  65.7 5.3 %collective-permute-start.24 = (bf16[4,160,128]{2,1,0:T(8,128)(2,1)S(1)}, bf16[4,160,128]{2,1,0:T(8,128)(2,1)S(1)}, u32[]{:S(2)}, u32[]{:S(2)}) collective-permute-start(bf16[4,160,128]{2,1,0:T(8,128)(2,1)S(1)} %get-tuple-element.80), channel_id=1, source_target_pairs={{0,2},{1,3},{2,0},{3,1},{4,6},{5,7},{6,4},{7,5},{8,10},{9,11},{10,... | collective-permute-start | bytes 491528 | tf_op jit(solution)/shard_map/ppermute | solution.py:786
  71.1 8.1 %collective-permute-start.26 = (bf16[320,128]{1,0:T(8,128)(2,1)S(1)}, bf16[320,128]{1,0:T(8,128)(2,1)S(1)}, u32[]{:S(2)}, u32[]{:S(2)}) collective-permute-start(bf16[320,128]{1,0:T(8,128)(2,1)S(1)} %get-tuple-element.83), channel_id=1, source_target_pairs={{0,8},{1,9},{2,10},{3,11},{4,12},{5,13},{6,14},{7,15},{8,0},{9,1},... | collective-permute-start | bytes 245768 | tf_op jit(solution)/shard_map/ppermute | solution.py:786
  73.4 6.4 %collective-permute-start.27 = (bf16[320,128]{1,0:T(8,128)(2,1)S(1)}, bf16[320,128]{1,0:T(8,128)(2,1)S(1)}, u32[]{:S(2)}, u32[]{:S(2)}) collective-permute-start(bf16[320,128]{1,0:T(8,128)(2,1)S(1)} %get-tuple-element.84), channel_id=1, source_target_pairs={{0,12},{1,13},{2,14},{3,15},{4,8},{5,9},{6,10},{7,11},{8,4},{9,5},... | collective-permute-start | bytes 245768 | tf_op jit(solution)/shard_map/ppermute | solution.py:786
  74.6 5.3 %collective-permute-start.25 = (bf16[320,128]{1,0:T(8,128)(2,1)S(1)}, bf16[320,128]{1,0:T(8,128)(2,1)S(1)}, u32[]{:S(2)}, u32[]{:S(2)}) collective-permute-start(bf16[320,128]{1,0:T(8,128)(2,1)S(1)} %get-tuple-element.82._), channel_id=1, source_target_pairs={{0,4},{1,5},{2,6},{3,7},{4,0},{5,1},{6,2},{7,3},{8,12},{9,13},{10,... | collective-permute-start | bytes 245768 | tf_op jit(solution)/shard_map/ppermute | solution.py:786
  86.7 1.2 %collective-permute-start.28 = (f32[1,512]{1,0:T(1,128)S(1)}, f32[1,512]{1,0:T(1,128)S(1)}, u32[]{:S(2)}, u32[]{:S(2)}) collective-permute-start(f32[1,512]{1,0:T(1,128)S(1)} %get-tuple-element.86.left), channel_id=1, source_target_pairs={{0,16},{1,17},{2,18},{3,19},{4,20},{5,21},{6,22},{7,23},{8,24},{9,... | collective-permute-start | bytes 6152 | tf_op jit(solution)/shard_map/ppermute | solution.py:786
  87.9 3.6 %collective-permute-start.29 = (f32[1,512]{1,0:T(1,128)S(1)}, f32[1,512]{1,0:T(1,128)S(1)}, u32[]{:S(2)}, u32[]{:S(2)}) collective-permute-start(f32[1,512]{1,0:T(1,128)S(1)} %add.9.left), channel_id=1, source_target_pairs={{0,1},{1,0},{2,3},{3,2},{4,5},{5,4},{6,7},{7,6},{8,9},{9,8},{10,11... | collective-permute-start | bytes 6152 | tf_op jit(solution)/shard_map/ppermute | solution.py:812
  91.5 3.6 %collective-permute-start.30 = (f32[1,512]{1,0:T(1,128)S(1)}, f32[1,512]{1,0:T(1,128)S(1)}, u32[]{:S(2)}, u32[]{:S(2)}) collective-permute-start(f32[1,512]{1,0:T(1,128)S(1)} %add.10.left), channel_id=1, source_target_pairs={{0,2},{1,3},{2,0},{3,1},{4,6},{5,7},{6,4},{7,5},{8,10},{9,11},{10,... | collective-permute-start | bytes 6152 | tf_op jit(solution)/shard_map/ppermute | solution.py:812
  95.1 3.6 %collective-permute-start.31 = (f32[1,512]{1,0:T(1,128)S(1)}, f32[1,512]{1,0:T(1,128)S(1)}, u32[]{:S(2)}, u32[]{:S(2)}) collective-permute-start(f32[1,512]{1,0:T(1,128)S(1)} %add.11.left), channel_id=1, source_target_pairs={{0,4},{1,5},{2,6},{3,7},{4,0},{5,1},{6,2},{7,3},{8,12},{9,13},{10,... | collective-permute-start | bytes 6152 | tf_op jit(solution)/shard_map/ppermute | solution.py:812
  98.7 4.6 %copy-start.2 = (f32[1,39936]{1,0:T(1,128)S(1)}, f32[1,39936]{1,0:T(1,128)}, u32[]{:S(2)}) copy-start(f32[1,39936]{1,0:T(1,128)} %param.14) | copy-start | bytes 479236
  98.7 4.6 %copy-start.3 = (f32[1,39936]{1,0:T(1,128)S(1)}, f32[1,39936]{1,0:T(1,128)}, u32[]{:S(2)}) copy-start(f32[1,39936]{1,0:T(1,128)} %param.15) | copy-start | bytes 479236
  98.7 4.6 %copy-start.4 = (f32[1,39936]{1,0:T(1,128)S(1)}, f32[1,39936]{1,0:T(1,128)}, u32[]{:S(2)}) copy-start(f32[1,39936]{1,0:T(1,128)} %param.16) | copy-start | bytes 479236
  98.7 4.6 %copy-start.6 = (s32[2]{0:T(128)S(1)}, s32[2]{0:T(128)}, u32[]{:S(2)}) copy-start(s32[2]{0:T(128)} %counts.1) | copy-start | bytes 28
  98.7 4.5 %collective-permute-start.32 = (f32[1,512]{1,0:T(1,128)S(1)}, f32[1,512]{1,0:T(1,128)S(1)}, u32[]{:S(2)}, u32[]{:S(2)}) collective-permute-start(f32[1,512]{1,0:T(1,128)S(1)} %add.12.left), channel_id=1, source_target_pairs={{0,8},{1,9},{2,10},{3,11},{4,12},{5,13},{6,14},{7,15},{8,0},{9,1},... | collective-permute-start | bytes 6152 | tf_op jit(solution)/shard_map/ppermute | solution.py:812
  103.3 5.8 %copy-start.1 = (bf16[8,196,768]{2,0,1:T(8,128)(2,1)S(1)}, bf16[8,196,768]{2,0,1:T(8,128)(2,1)}, u32[]{:S(2)}) copy-start(bf16[8,196,768]{2,0,1:T(8,128)(2,1)} %param.9) | copy-start | bytes 7225348
